TPU v7x, 512 devices: a whole 4x4x16 slice. The times are simulated.
512 devices in a mesh: pass: 64 (over y, z_lo, core), qry: 8 (over x, z_hi).
Axes of the slice: x: 4, y: 4, z: 16 (z_hi: 2, z_lo: 8; z = z_hi * 8 + z_lo), core: 2. Of those that a mesh axis runs over, the one named last changes fastest.
Arguments:
- queries: bfloat16 [1024, 768], P(('pass', 'qry')), may hold values from -6 to 6
- passages: bfloat16 [65536, 768], P(('pass', 'qry')), may hold values from -32 to 32
- teacher: bfloat16 [1024, 65536], P(('pass', 'qry')), may hold values from -16 to 320
Outputs:
- query_grad: float32 [1024, 768], P(('pass', 'qry'))
- passage_grad: float32 [65536, 768], P(('pass', 'qry'))
All inputs are finite; a program needn't handle non-finite values.
Results may differ from a plain program's by a relative error of at most 0.0003.
Values may be sent and summed in bfloat16 or wider, within the bound.
No kernel may reach another device: no remote copies, remote signals or barrier semaphores. Data moves between devices by JAX's collectives and lax.ppermute only.
A program may use at most 64 MiB of HBM per device.

v0:
```python
import jax
import jax.numpy as jnp
from jax import lax
from jax.sharding import PartitionSpec as P

logit_scale = 0.125


def row_softmax(values):
    top_value = jnp.max(values, axis=1, keepdims=True)
    lifted = jnp.exp(values - top_value)
    return lifted / jnp.sum(lifted, axis=1, keepdims=True)


def per_device(queries, passages, teacher):
    feature_dim = passages.shape[1]
    owned_rows = queries.shape[0]
    pool_count = lax.axis_size("pass")
    group_count = lax.axis_size("qry")
    gathered = lax.all_gather(queries, ("pass", "qry"), axis=0, tiled=True)
    ordered = (
        gathered.reshape(pool_count, group_count, owned_rows, feature_dim)
        .transpose(1, 0, 2, 3)
        .reshape(-1, feature_dim)
    )
    student = logit_scale * lax.dot_general(
        ordered, passages, (((1,), (1,)), ((), ())), preferred_element_type=jnp.float32
    )
    row_scores = lax.all_to_all(
        lax.all_to_all(student, "qry", split_axis=0, concat_axis=1, tiled=True),
        "pass",
        split_axis=0,
        concat_axis=1,
        tiled=True,
    )
    gap_rows = logit_scale * (row_softmax(row_scores) - row_softmax(teacher.astype(jnp.float32)))
    grad_tile = lax.all_to_all(
        lax.all_to_all(gap_rows, "pass", split_axis=1, concat_axis=0, tiled=True),
        "qry",
        split_axis=1,
        concat_axis=0,
        tiled=True,
    )
    passage_grad = lax.dot_general(
        grad_tile,
        ordered.astype(jnp.float32),
        (((0,), (0,)), ((), ())),
        precision=lax.Precision.HIGHEST,
        preferred_element_type=jnp.float32,
    )
    pool_wide = passages.astype(jnp.float32)
    global_rows = (
        grad_tile.reshape(group_count, pool_count, owned_rows, -1)
        .transpose(1, 0, 2, 3)
        .reshape(-1, grad_tile.shape[1])
    )
    query_grad = lax.psum_scatter(
        jnp.dot(
            global_rows,
            pool_wide,
            precision=lax.Precision.HIGHEST,
            preferred_element_type=jnp.float32,
        ),
        ("pass", "qry"),
        scatter_dimension=0,
        tiled=True,
    )
    return (query_grad, passage_grad)


def solution(mesh):
    placed = (P(("pass", "qry"), None), P(("pass", "qry"), None), P(("pass", "qry"), None))
    return jax.shard_map(
        per_device,
        mesh=mesh,
        in_specs=placed,
        out_specs=(P(("pass", "qry"), None), P(("pass", "qry"), None)),
        check_vma=False,
    )
```

profile of v0, /device:TPU:1, one launch (start us, length us, event | category | flops | bytes accessed | tf_op | source)
XLA Modules:
  0.0 1713.9 jit_solution(12897156515775784866)
XLA Ops:
  7.2 0.0 copy-start
  7.2 0.0 all-gather.3.cloned.1.call-start
  7.2 0.7 all-gather.3.cloned.1.call-update
  7.9 1058.3 %all-gather.3.cloned.1.call-done = bf16[512,2,768]{2,1,0:T(2,128)(2,1)} async-done(((bf16[1,2,768]{2,1,0:T(2,128)(2,1)}), bf16[512,2,768]{2,1,0:T(2,128)(2,1)}) %all-gather.3.cloned.1.call-update) | async-done | bytes 1572880 | tf_op jit(solution)/shard_map/all_gather | solution.py:20
  1066.2 2.5 copy.16
  1068.7 0.6 reshape.42
  1069.3 0.0 copy-done
  1069.3 0.6 convolution_multiply_fusion
  1069.9 34.3 %all_to_all.70 = f32[8,128,128]{2,1,0:T(8,128)S(1)} all-to-all(f32[8,128,128]{2,1,0:T(8,128)S(1)} %bitcast.38), channel_id=1, replica_groups=mesh['pass'=64,'qry'=8] {'qry'}, dimensions={0} | all-to-all | bytes 1048576 | tf_op jit(solution)/shard_map/all_to_all | solution.py:30
  1104.2 0.0 copy-start.1
  1104.2 0.3 copy.11
  1104.5 1.0 all_to_all.55
  1105.6 13.5 all-to-all-start.1
  1119.1 0.0 all-reduce.3.cloned.1.call-start
  1119.2 0.0 copy-done.1
  1119.2 0.7 reduce_max.24
  1119.9 0.7 fusion.3
  1120.6 28.2 %all-to-all-done.1 = f32[64,2,1024]{2,1,0:T(2,128)S(1)} async-done(((f32[64,2,1024]{2,1,0:T(2,128)}), f32[64,2,1024]{2,1,0:T(2,128)S(1)}, u32[]{:S(2)}, u32[]{:S(2)}) %all-to-all-start.1) | async-done | bytes 524320 | tf_op jit(solution)/shard_map/all_to_all | solution.py:29
  1148.7 0.7 reduce_max.23
  1149.4 0.7 fusion.1
  1150.1 0.8 fusion.2
  1151.0 36.9 %all_to_all.71 = f32[2,64,1024]{2,0,1:T(2,128)S(1)} all-to-all(f32[2,64,1024]{2,0,1:T(2,128)S(1)} %bitcast.35), channel_id=1, replica_groups=mesh['pass'=64,'qry'=8] {'pass'}, dimensions={1} | all-to-all | bytes 1048576 | tf_op jit(solution)/shard_map/all_to_all | solution.py:38
  1187.8 0.4 all_to_all.62
  1188.2 0.1 copy.13
  1188.4 22.5 %all_to_all.72 = f32[128,8,128]{2,0,1:T(8,128)S(1)} all-to-all(f32[128,8,128]{2,0,1:T(8,128)S(1)} %copy.13), channel_id=1, replica_groups=mesh['pass'=64,'qry'=8] {'qry'}, dimensions={1} | all-to-all | bytes 1048576 | tf_op jit(solution)/shard_map/all_to_all | solution.py:37
  1210.9 0.2 copy.14
  1211.1 3.1 fusion.4
  1214.1 0.0 all-reduce.3.cloned.1.call-update
  1214.2 1.7 fusion.5
  1215.8 489.9 %all-reduce.3.cloned.1.call-done = f32[1024,768]{1,0:T(8,128)} async-done(((f32[1024,768]{1,0:T(8,128)}), f32[1024,768]{1,0:T(8,128)}) %all-reduce.3.cloned.1.call-update) | async-done | bytes 3145744
  1705.7 1.3 constant_dynamic-slice_fusion
  (1 shorter events, 0.0 us)
Async XLA Ops:
  7.2 1062.2 %copy-start = (bf16[128,768]{1,0:T(8,128)(2,1)S(1)}, bf16[128,768]{1,0:T(8,128)(2,1)}, u32[]{:S(2)}) copy-start(bf16[128,768]{1,0:T(8,128)(2,1)} %param.4) | copy-start | bytes 589828
  7.2 1059.0 %all-gather.3.cloned.1.call-start = ((), (), s32[]{:S(2)}) async-start(), calls=%async_computation.4 | async-start | bytes 1575936 | tf_op jit(solution)/shard_map/all_gather | solution.py:20
  1104.2 15.0 copy-start.1
  1105.6 43.1 %all-to-all-start.1 = ((f32[64,2,1024]{2,1,0:T(2,128)}), f32[64,2,1024]{2,1,0:T(2,128)S(1)}, u32[]{:S(2)}, u32[]{:S(2)}) async-start(f32[64,2,1024]{2,1,0:T(2,128)} %all_to_all.55), calls=%async_computation.1 | async-start | bytes 1048576 | tf_op jit(solution)/shard_map/all_to_all | solution.py:29
  1119.1 586.6 %all-reduce.3.cloned.1.call-start = ((), (), s32[]{:S(2)}) async-start(), calls=%async_computation.5 | async-start | bytes 6291456
Sparse Core Ops, SparseCore 0:
  10.2 1055.9 all-gather.2
  1214.3 491.3 all-reduce.2
where the time goes:
time: 1710 us
  waiting for transfers between devices  1580 us (92%)
  blocking collectives  93.7 us (5%)
    all_gather x1, waiting for transfers between devices, per_device(): gathered = lax.all_gather(queries, ('pass', 'qry'), axis=0, tiled=True)  1060 us
    unnamed x3, waiting for transfers between devices  491 us
    all_to_all x1, blocking collectives, per_device(): lax.all_to_all(gap_rows, 'pass', split_axis=1, concat_axis=0, tiled=True)  36.9 us
    all_to_all x1, blocking collectives, per_device(): lax.all_to_all(student, 'qry', split_axis=0, concat_axis=1, tiled=True)  34.3 us
  transfers between devices with their start and end apart: 3, of which 3 were waited for; matrix products, arithmetic and copies ran while one was open for 0% of the time, Pallas kernels for 0%

commit v1 on v0

v1 whole, which is shorter than its diff:
```python
import jax
import jax.numpy as jnp
from jax import lax
from jax.sharding import Mesh
from jax.sharding import PartitionSpec as P

logit_scale = 0.125
names = ("y", "zl", "core", "x", "zh")
sizes = (4, 8, 2, 4, 2)
z_axes = ("zh", "zl")
group_axes = ("core", "x")
lane = 128
f32 = jnp.float32
bf16 = jnp.bfloat16


def exchange(values, axes):
    return lax.all_to_all(values, axes, 0, 0, tiled=True)


def split_dot(weights, exact, dims):
    high = lax.reduce_precision(weights, 8, 7)
    low = weights - high
    return lax.dot_general(
        high.astype(bf16), exact, dims, preferred_element_type=f32
    ) + lax.dot_general(low.astype(bf16), exact, dims, preferred_element_type=f32)


def combine(top, total, axis):
    high = jnp.max(top, axis=axis, keepdims=True)
    weight = jnp.exp(top - high)
    return weight, jnp.squeeze(high, axis), jnp.sum(weight * total, axis=axis)


def per_device(queries, passages, teacher):
    own, dim = queries.shape
    pool = passages.shape[0]
    ny, nzl, nc, nx, nzh = (lax.axis_size(a) for a in names)
    nz, group = nzh * nzl, nc * nx
    fold = dim // lane

    tiles = teacher.reshape(own, ny, nzl, nc, nx, nzh, pool).transpose(5, 2, 1, 0, 3, 4, 6)
    tiles = tiles.reshape(nz, ny * own * group, pool)
    rows = jnp.broadcast_to(queries.reshape(1, own * fold, lane), (nz, own * fold, lane))
    got = exchange(jnp.concatenate([tiles, rows], axis=1), z_axes)
    cut = ny * own * group
    tiles = got[:, :cut].reshape(nz, ny, own * group, pool).transpose(1, 0, 2, 3)
    tiles = tiles.reshape(ny, nz * own * group, pool)
    rows = jnp.broadcast_to(got[:, cut:].reshape(1, nz * own * fold, lane), (ny, nz * own * fold, lane))
    got = exchange(jnp.concatenate([tiles, rows], axis=1), "y")
    cut = nz * own * group
    count = ny * nz * own
    logits = got[:, :cut].reshape(count, group * pool)
    block = got[:, cut:].reshape(count, dim)

    shared = lax.all_gather(passages, group_axes, axis=0, tiled=True)
    all_rows = lax.all_gather(block, group_axes, axis=0, tiled=True)
    own_logits = exchange(logits.reshape(count, group, pool).transpose(1, 0, 2), group_axes)
    own_logits = own_logits.reshape(group * count, pool)

    student = logit_scale * lax.dot_general(
        block, shared, (((1,), (1,)), ((), ())), preferred_element_type=f32
    )

    def local(values):
        top = jnp.max(values, axis=1, keepdims=True)
        lifted = jnp.exp(values - top)
        part = split_dot(lifted, shared, (((1,), (0,)), ((), ())))
        return part, top[:, 0], jnp.sum(lifted, axis=1)

    part_s, top_s, sum_s = local(student)
    part_t, top_t, sum_t = local(logits.astype(f32))
    parts = jnp.concatenate([part_s, part_t], axis=1)
    stats = jnp.stack([top_s, sum_s, top_t, sum_t])

    def reduce_over(parts, stats, axes, n, place):
        width = parts.shape[0] // n
        sent = jnp.concatenate(
            [
                parts.reshape(n, width * 2 * fold, lane),
                jnp.broadcast_to(stats.reshape(1, -1, lane), (n, stats.size // lane, lane)),
            ],
            axis=1,
        )
        got = exchange(sent, axes)
        parts = got[:, : width * 2 * fold].reshape(n, width, 2, dim)
        stats = got[:, width * 2 * fold :].reshape(n, 4, -1)
        weight_s, top_s, sum_s = combine(stats[:, 0], stats[:, 1], 0)
        weight_t, top_t, sum_t = combine(stats[:, 2], stats[:, 3], 0)
        weight_s = lax.dynamic_slice_in_dim(weight_s, place, width, 1)
        weight_t = lax.dynamic_slice_in_dim(weight_t, place, width, 1)
        part_s = jnp.sum(weight_s[:, :, None] * parts[:, :, 0], axis=0)
        part_t = jnp.sum(weight_t[:, :, None] * parts[:, :, 1], axis=0)
        return part_s, part_t, jnp.stack([top_s, sum_s, top_t, sum_t])

    y_at = lax.axis_index("y") * (nz * own)
    z_at = y_at + lax.axis_index(z_axes) * own
    part_s, part_t, stats = reduce_over(parts, stats, "y", ny, y_at)
    part_s, part_t, stats = reduce_over(
        jnp.concatenate([part_s, part_t], axis=1), stats, z_axes, nz, z_at
    )
    mine = lax.dynamic_slice_in_dim(stats, z_at, own, 1)
    query_grad = logit_scale * (part_s / mine[1][:, None] - part_t / mine[3][:, None])

    every = exchange(jnp.broadcast_to(stats[None], (group,) + stats.shape), group_axes)
    every = every.transpose(1, 0, 2).reshape(4, group * count)
    scores = logit_scale * lax.dot_general(
        passages, all_rows, (((1,), (1,)), ((), ())), preferred_element_type=f32
    )
    grad = logit_scale * (
        jnp.exp(scores - every[0]) / every[1]
        - jnp.exp(own_logits.T.astype(f32) - every[2]) / every[3]
    )
    passage_grad = split_dot(grad, all_rows, (((1,), (0,)), ((), ())))
    return query_grad, passage_grad


def solution(mesh):
    shape = sizes if mesh.devices.size == 512 else (2,) * 5
    fine = Mesh(mesh.devices.reshape(shape), names)
    placed = P(names, None)
    return jax.shard_map(
        per_device,
        mesh=fine,
        in_specs=(placed, placed, placed),
        out_specs=(placed, placed),
        check_vma=False,
    )
```

time: 1710 us -> 139 us (0.08)
  waiting for transfers between devices: 1580 us -> 31.2 us
  blocking collectives: 93.7 us -> 41.3 us
  starting transfers between devices: 13.6 us -> 33 us
    all_gather x1 -> x2, waiting for transfers between devices: 1060 us -> 0.02 us  [the longest x1 0.02 us: per_device(): shared = lax.all_gather(passages, group_axes, axis=0, tiled=True)]
    unnamed x3 -> x2, waiting for transfers between devices: 491 us -> 1.38 us
    all_to_all x3 -> x2, blocking collectives: 93.7 us -> 41.3 us  [exchange(): return lax.all_to_all(values, axes, 0, 0, tiled=True)]
    all_to_all x1 -> x4, starting transfers between devices: 13.5 us -> 32.9 us  [exchange(): return lax.all_to_all(values, axes, 0, 0, tiled=True)]
  transfers between devices with their start and end apart: 3 -> 6, of which waited for: 3 -> 4; matrix products, arithmetic and copies ran while one was open for 0% -> 5% of each run, Pallas kernels for 0% -> 0%
where the time goes in v1:
time: 139 us; the launch traced here: 138 us
  blocking collectives  41.3 us (30%)
  starting transfers between devices  33 us (24%)
  waiting for transfers between devices  31.2 us (22%)
  between operations  14.4 us (10%)
  matrix products  7.81 us (6%)
  local copies, waits for them, and re-layouts  6.12 us (4%)
  other arithmetic  4.08 us (3%)
    all_to_all x2, blocking collectives, exchange(): return lax.all_to_all(values, axes, 0, 0, tiled=True)  41.3 us
    all_to_all x4, starting transfers between devices, exchange(): return lax.all_to_all(values, axes, 0, 0, tiled=True)  32.9 us
    all_to_all x4, waiting for transfers between devices, exchange(): return lax.all_to_all(values, axes, 0, 0, tiled=True)  29.8 us
  transfers between devices with their start and end apart: 6, of which 4 were waited for; matrix products, arithmetic and copies ran while one was open for 5% of the time, Pallas kernels for 0%

profile of v1, /device:TPU:1, one launch (start us, length us, event | category | flops | bytes accessed | tf_op | source)
XLA Modules:
  0.0 138.0 jit_solution(12010665173180510508)
XLA Ops:
  7.2 0.7 all-gather.3.cloned.1.call-update
  7.9 0.7 broadcast_in_dim.22
  8.6 1.2 reshape.86
  9.9 0.1 copy.48
  10.0 30.8 %all_to_all.30 = bf16[16,76,128]{2,1,0:T(8,128)(2,1)S(1)} all-to-all(bf16[16,76,128]{2,1,0:T(8,128)(2,1)S(1)} %copy.48), channel_id=1, replica_groups=mesh['y'=4,'zl'=8,'core'=2,'x'=4,'zh'=2] {'zh','zl'}, dimensions={0} | all-to-all | bytes 622592 | tf_op jit(solution)/shard_map/all_to_all | solution.py:18
  40.9 10.6 %all_to_all.31 = bf16[4,448,128]{2,1,0:T(8,128)(2,1)S(1)} all-to-all(bf16[4,448,128]{2,1,0:T(8,128)(2,1)S(1)} %pad_maximum_fusion.2), channel_id=1, replica_groups=mesh['y'=4,'zl'=8,'core'=2,'x'=4,'zh'=2] {'y'}, dimensions={0} | all-to-all | bytes 917504 | tf_op jit(solution)/shard_map/all_to_all | solution.py:18
  51.5 0.2 fusion.29
  51.7 0.1 reduce_max.76
  51.8 0.1 reduce_max.77
  51.9 0.1 reshape.97
  52.0 0.1 sub.100
  52.0 0.1 sub.101
  52.2 0.4 exponential_reduce_fusion
  52.6 0.1 reduce_sum.99
  52.7 0.2 reshape.90
  52.9 0.1 reshape.95
  53.0 0.1 reduce_sum.100
  53.1 2.2 %fusion.34 = (f32[128]{0:T(128)S(1)}, f32[128,1024]{1,0:T(8,128)S(1)}) fusion(bf16[128,768]{1,0:T(8,128)(2,1)S(1)} %reshape.90, bf16[1024,768]{1,0:T(8,128)(2,1)} %all-gather.3.cloned.1.call-done), kind=kOutput, calls=%fused_computation.78 | convolution fusion | flops 201588608 | bytes 2294272 | tf_op jit(solution)/shard_map/dot_general | solution.py:61
  55.4 0.2 fusion.11
  55.6 0.4 fusion.17
  56.1 0.4 fusion.18
  56.5 0.4 convolution_add_fusion.1
  57.0 0.4 convolution_add_fusion.2
  57.4 0.1 pad_maximum_fusion.1
  57.6 0.9 pad_maximum_fusion
  58.5 3.5 %all-to-all-start.2 = ((f32[4,388,128]{2,1,0:T(8,128)}), f32[4,388,128]{2,1,0:T(8,128)S(1)}, u32[]{:S(2)}, u32[]{:S(2)}) async-start(f32[4,388,128]{2,1,0:T(8,128)} %pad_maximum_fusion), calls=%async_computation.2 | async-start | bytes 1605632 | tf_op jit(solution)/shard_map/all_to_all | solution.py:18
  62.1 8.4 %all-to-all-done.2 = f32[4,388,128]{2,1,0:T(8,128)S(1)} async-done(((f32[4,388,128]{2,1,0:T(8,128)}), f32[4,388,128]{2,1,0:T(8,128)S(1)}, u32[]{:S(2)}, u32[]{:S(2)}) %all-to-all-start.2) | async-done | bytes 794656 | tf_op jit(solution)/shard_map/all_to_all | solution.py:18
  70.5 0.4 reshape.92
  71.0 0.6 fusion.28
  71.8 0.1 fusion.12
  72.0 0.7 pad_maximum_fusion.4
  72.7 14.0 %all-to-all-start.3 = ((f32[16,28,128]{2,1,0:T(8,128)}), f32[16,28,128]{2,1,0:T(8,128)S(1)}, u32[]{:S(2)}, u32[]{:S(2)}) async-start(f32[16,28,128]{2,1,0:T(8,128)} %pad_maximum_fusion.4), calls=%async_computation.3 | async-start | bytes 524288 | tf_op jit(solution)/shard_map/all_to_all | solution.py:18
  86.8 0.7 all-gather.5.cloned.1.call-update
  87.5 0.7 copy.56
  88.3 11.3 %all-to-all-done.3 = f32[16,28,128]{2,1,0:T(8,128)S(1)} async-done(((f32[16,28,128]{2,1,0:T(8,128)}), f32[16,28,128]{2,1,0:T(8,128)S(1)}, u32[]{:S(2)}, u32[]{:S(2)}) %all-to-all-start.3) | async-done | bytes 229408 | tf_op jit(solution)/shard_map/all_to_all | solution.py:18
  99.6 0.1 reshape.94
  99.8 0.6 broadcast_in_dim.58
  100.4 11.7 %all-to-all-start.4 = ((f32[8,4,128]{2,1,0:T(4,128)}), f32[8,4,128]{2,1,0:T(4,128)S(1)}, u32[]{:S(2)}, u32[]{:S(2)}) async-start(f32[8,4,128]{2,1,0:T(4,128)} %broadcast_in_dim.58), calls=%async_computation.4 | async-start | bytes 32768 | tf_op jit(solution)/shard_map/all_to_all | solution.py:18
  112.3 0.2 fusion.31
  112.5 0.1 fusion.24
  112.6 0.1 fusion.25
  112.7 4.3 %all-to-all-done.4 = f32[8,4,128]{2,1,0:T(4,128)S(1)} async-done(((f32[8,4,128]{2,1,0:T(4,128)}), f32[8,4,128]{2,1,0:T(4,128)S(1)}, u32[]{:S(2)}, u32[]{:S(2)}) %all-to-all-start.4) | async-done | bytes 16416 | tf_op jit(solution)/shard_map/all_to_all | solution.py:18
  117.0 3.7 %all-to-all-start.5 = ((bf16[8,128,128]{2,1,0:T(8,128)(2,1)}), bf16[8,128,128]{2,1,0:T(8,128)(2,1)S(1)}, u32[]{:S(2)}, u32[]{:S(2)}) async-start(bf16[8,128,128]{2,1,0:T(8,128)(2,1)} %copy.56), calls=%async_computation.5 | async-start | bytes 524288 | tf_op jit(solution)/shard_map/all_to_all | solution.py:18
  120.8 0.7 fusion.26
  121.5 5.9 %all-to-all-done.5 = bf16[8,128,128]{2,1,0:T(8,128)(2,1)S(1)} async-done(((bf16[8,128,128]{2,1,0:T(8,128)(2,1)}), bf16[8,128,128]{2,1,0:T(8,128)(2,1)S(1)}, u32[]{:S(2)}, u32[]{:S(2)}) %all-to-all-start.5) | async-done | bytes 262176 | tf_op jit(solution)/shard_map/all_to_all | solution.py:18
  127.3 2.2 %fusion.5 = f32[128,1024]{0,1:T(8,128)S(1)} fusion(bf16[1024,768]{1,0:T(8,128)(2,1)} %all-gather.5.cloned.1.call-done, bf16[128,768]{1,0:T(8,128)(2,1)S(1)} %copy-done.3, bf16[1024,128]{1,0:T(8,128)(2,1)S(1)} %bitcast.82, f32[1024]{0:T(1024)S(1)} %bitcast.102, f32[1024]{0:T(1024)S(1)} %bitcast.103, f32[1024]{0:T(1024)S(1)} %bitcast.104, f32[1024]{0:T(1024)S(1)} %bitcast.101), kind=kOutput, calls=%fused_computation.7 | convolution fusion | flops 202375168 | bytes 2572288 | tf_op jit(solution)/shard_map/dot_general | solution.py:107
  129.6 0.4 fusion.19
  130.0 1.2 convolution_add_fusion
  (50 shorter events, 1.1 us)
Async XLA Ops:
  7.2 46.0 %all-gather.3.cloned.1.call-start = ((), (), s32[]{:S(2)}) async-start(), calls=%async_computation.6 | async-start | bytes 1769472 | tf_op jit(solution)/shard_map/all_gather | solution.py:56
  52.9 2.5 %copy-start.2 = (bf16[128,768]{1,0:T(8,128)(2,1)}, bf16[128,768]{1,0:T(8,128)(2,1)S(1)}, u32[]{:S(2)}) copy-start(bf16[128,768]{1,0:T(8,128)(2,1)S(1)} %reshape.90) | copy-start | bytes 589828
  53.1 2.5 %copy-start = (bf16[1024,768]{1,0:T(8,128)(2,1)S(1)}, bf16[1024,768]{1,0:T(8,128)(2,1)}, u32[]{:S(2)}) copy-start(bf16[1024,768]{1,0:T(8,128)(2,1)} %all-gather.3.cloned.1.call-done) | copy-start | bytes 4718596
  58.5 11.9 %all-to-all-start.2 = ((f32[4,388,128]{2,1,0:T(8,128)}), f32[4,388,128]{2,1,0:T(8,128)S(1)}, u32[]{:S(2)}, u32[]{:S(2)}) async-start(f32[4,388,128]{2,1,0:T(8,128)} %pad_maximum_fusion), calls=%async_computation.2 | async-start | bytes 1605632 | tf_op jit(solution)/shard_map/all_to_all | solution.py:18
  72.7 26.8 %all-to-all-start.3 = ((f32[16,28,128]{2,1,0:T(8,128)}), f32[16,28,128]{2,1,0:T(8,128)S(1)}, u32[]{:S(2)}, u32[]{:S(2)}) async-start(f32[16,28,128]{2,1,0:T(8,128)} %pad_maximum_fusion.4), calls=%async_computation.3 | async-start | bytes 524288 | tf_op jit(solution)/shard_map/all_to_all | solution.py:18
  86.8 40.6 %copy-start.3 = (bf16[128,768]{1,0:T(8,128)(2,1)S(1)}, bf16[128,768]{1,0:T(8,128)(2,1)}, u32[]{:S(2)}) copy-start(bf16[128,768]{1,0:T(8,128)(2,1)} %param.4) | copy-start | bytes 589828
  86.8 40.6 %all-gather.5.cloned.1.call-start = ((), (), s32[]{:S(2)}) async-start(), calls=%async_computation.7 | async-start | bytes 1769472 | tf_op jit(solution)/shard_map/all_gather | solution.py:57
  100.4 16.6 %all-to-all-start.4 = ((f32[8,4,128]{2,1,0:T(4,128)}), f32[8,4,128]{2,1,0:T(4,128)S(1)}, u32[]{:S(2)}, u32[]{:S(2)}) async-start(f32[8,4,128]{2,1,0:T(4,128)} %broadcast_in_dim.58), calls=%async_computation.4 | async-start | bytes 32768 | tf_op jit(solution)/shard_map/all_to_all | solution.py:18
  117.0 10.3 %all-to-all-start.5 = ((bf16[8,128,128]{2,1,0:T(8,128)(2,1)}), bf16[8,128,128]{2,1,0:T(8,128)(2,1)S(1)}, u32[]{:S(2)}, u32[]{:S(2)}) async-start(bf16[8,128,128]{2,1,0:T(8,128)(2,1)} %copy.56), calls=%async_computation.5 | async-start | bytes 524288 | tf_op jit(solution)/shard_map/all_to_all | solution.py:18
  127.3 2.2 %copy-start.1 = (bf16[1024,768]{1,0:T(8,128)(2,1)S(1)}, bf16[1024,768]{1,0:T(8,128)(2,1)}, u32[]{:S(2)}) copy-start(bf16[1024,768]{1,0:T(8,128)(2,1)} %all-gather.5.cloned.1.call-done) | copy-start | bytes 4718596
Sparse Core Ops, SparseCore 0:
  10.1 37.6 all-gather.2
  89.8 34.6 all-gather.4

commit v2 on v1

--- a/solution.py
+++ b/solution.py
@@ -39,6 +39,9 @@
     nz, group = nzh * nzl, nc * nx
     fold = dim // lane
 
+    shared = exchange(jnp.broadcast_to(passages[None], (group, pool, dim)), group_axes)
+    shared = shared.reshape(group * pool, dim)
+
     tiles = teacher.reshape(own, ny, nzl, nc, nx, nzh, pool).transpose(5, 2, 1, 0, 3, 4, 6)
     tiles = tiles.reshape(nz, ny * own * group, pool)
     rows = jnp.broadcast_to(queries.reshape(1, own * fold, lane), (nz, own * fold, lane))
@@ -53,10 +56,11 @@
     logits = got[:, :cut].reshape(count, group * pool)
     block = got[:, cut:].reshape(count, dim)
 
-    shared = lax.all_gather(passages, group_axes, axis=0, tiled=True)
-    all_rows = lax.all_gather(block, group_axes, axis=0, tiled=True)
-    own_logits = exchange(logits.reshape(count, group, pool).transpose(1, 0, 2), group_axes)
-    own_logits = own_logits.reshape(group * count, pool)
+    rows = jnp.broadcast_to(block[None], (group, count, dim))
+    tiles = logits.reshape(count, group, pool).transpose(1, 0, 2)
+    every_row = exchange(jnp.concatenate([rows, tiles], axis=2), group_axes)
+    every_row = every_row.reshape(group * count, dim + pool)
+    all_rows, own_logits = every_row[:, :dim], every_row[:, dim:]
 
     student = logit_scale * lax.dot_general(
         block, shared, (((1,), (1,)), ((), ())), preferred_element_type=f32
@@ -75,22 +79,19 @@
 
     def reduce_over(parts, stats, axes, n, place):
         width = parts.shape[0] // n
-        sent = jnp.concatenate(
-            [
-                parts.reshape(n, width * 2 * fold, lane),
-                jnp.broadcast_to(stats.reshape(1, -1, lane), (n, stats.size // lane, lane)),
-            ],
-            axis=1,
-        )
+        extra = -(-stats.size // width)
+        extra += -extra % lane
+        spread = jnp.pad(stats.reshape(-1, extra), ((0, width - stats.size // extra), (0, 0)))
+        sent = jnp.concatenate([parts.reshape(n, width, 2 * dim), jnp.broadcast_to(spread, (n, width, extra))], axis=2)
         got = exchange(sent, axes)
-        parts = got[:, : width * 2 * fold].reshape(n, width, 2, dim)
-        stats = got[:, width * 2 * fold :].reshape(n, 4, -1)
+        parts = got[:, :, : 2 * dim]
+        stats = got[:, : stats.size // extra, 2 * dim :].reshape(n, 4, -1)
         weight_s, top_s, sum_s = combine(stats[:, 0], stats[:, 1], 0)
         weight_t, top_t, sum_t = combine(stats[:, 2], stats[:, 3], 0)
         weight_s = lax.dynamic_slice_in_dim(weight_s, place, width, 1)
         weight_t = lax.dynamic_slice_in_dim(weight_t, place, width, 1)
-        part_s = jnp.sum(weight_s[:, :, None] * parts[:, :, 0], axis=0)
-        part_t = jnp.sum(weight_t[:, :, None] * parts[:, :, 1], axis=0)
+        part_s = jnp.sum(weight_s[:, :, None] * parts[:, :, :dim], axis=0)
+        part_t = jnp.sum(weight_t[:, :, None] * parts[:, :, dim:], axis=0)
         return part_s, part_t, jnp.stack([top_s, sum_s, top_t, sum_t])
 
     y_at = lax.axis_index("y") * (nz * own)
@@ -102,11 +103,12 @@
     mine = lax.dynamic_slice_in_dim(stats, z_at, own, 1)
     query_grad = logit_scale * (part_s / mine[1][:, None] - part_t / mine[3][:, None])
 
-    every = exchange(jnp.broadcast_to(stats[None], (group,) + stats.shape), group_axes)
-    every = every.transpose(1, 0, 2).reshape(4, group * count)
     scores = logit_scale * lax.dot_general(
         passages, all_rows, (((1,), (1,)), ((), ())), preferred_element_type=f32
     )
+    stats, scores = lax.optimization_barrier((stats, scores))
+    every = exchange(jnp.broadcast_to(stats[None], (group,) + stats.shape), group_axes)
+    every = every.transpose(1, 0, 2).reshape(4, group * count)
     grad = logit_scale * (
         jnp.exp(scores - every[0]) / every[1]
         - jnp.exp(own_logits.T.astype(f32) - every[2]) / every[3]

time: 139 us -> 169 us (1.22)
  waiting for transfers between devices: 31.2 us -> 70.7 us
  between operations: 14.4 us -> 1 us
  starting transfers between devices: 33 us -> 35.5 us
  other arithmetic: 4.08 us -> 6.05 us
    all_to_all x4 -> x5, waiting for transfers between devices: 29.8 us -> 70.7 us  [exchange(): return lax.all_to_all(values, axes, 0, 0, tiled=True)]
    all_to_all x4 -> x5, starting transfers between devices: 32.9 us -> 35.5 us  [exchange(): return lax.all_to_all(values, axes, 0, 0, tiled=True)]
    dot_general x3, matrix products: 1.27 us -> 3.16 us  [split_dot(): lax.dot_general(high.astype(bf16), exact, dims, preferred_element_type=f32)]
    dot_general x1, matrix products: 2.23 us -> 0.39 us  [per_device(): lax.dot_general(passages, all_rows, (((1,), (1,)), ((), ())), preferred_e...]
  transfers between devices with their start and end apart: 6 -> 5, of which waited for: 4 -> 5; matrix products, arithmetic and copies ran while one was open for 5% -> 2% of each run, Pallas kernels for 0% -> 0%
where the time goes in v2:
time: 169 us
  waiting for transfers between devices  70.7 us (42%)
  blocking collectives  41.3 us (24%)
  starting transfers between devices  35.5 us (21%)
  local copies, waits for them, and re-layouts  7.51 us (4%)
  matrix products  6.62 us (4%)
  other arithmetic  6.05 us (4%)
    all_to_all x5, waiting for transfers between devices, exchange(): return lax.all_to_all(values, axes, 0, 0, tiled=True)  70.7 us
    all_to_all x2, blocking collectives, exchange(): return lax.all_to_all(values, axes, 0, 0, tiled=True)  41.3 us
    all_to_all x5, starting transfers between devices, exchange(): return lax.all_to_all(values, axes, 0, 0, tiled=True)  35.5 us
  transfers between devices with their start and end apart: 5, of which 5 were waited for; matrix products, arithmetic and copies ran while one was open for 2% of the time, Pallas kernels for 0%

profile of v2, /device:TPU:1, one launch (start us, length us, event | category | flops | bytes accessed | tf_op | source)
XLA Modules:
  0.0 168.8 jit_solution(2142802960674361709)
XLA Ops:
  0.6 1.2 reshape.93
  1.9 0.7 broadcast_in_dim.26
  2.6 0.1 copy.72
  2.7 30.8 %all_to_all.35 = bf16[16,76,128]{2,1,0:T(8,128)(2,1)S(1)} all-to-all(bf16[16,76,128]{2,1,0:T(8,128)(2,1)S(1)} %copy.72), channel_id=1, replica_groups=mesh['y'=4,'zl'=8,'core'=2,'x'=4,'zh'=2] {'zh','zl'}, dimensions={0} | all-to-all | bytes 622592 | tf_op jit(solution)/shard_map/all_to_all | solution.py:18
  33.6 10.6 %all_to_all.36 = bf16[4,448,128]{2,1,0:T(8,128)(2,1)S(1)} all-to-all(bf16[4,448,128]{2,1,0:T(8,128)(2,1)S(1)} %pad_maximum_fusion.3), channel_id=1, replica_groups=mesh['y'=4,'zl'=8,'core'=2,'x'=4,'zh'=2] {'y'}, dimensions={0} | all-to-all | bytes 917504 | tf_op jit(solution)/shard_map/all_to_all | solution.py:18
  44.2 1.3 broadcast_in_dim.59
  45.5 12.2 %all-to-all-start.2 = ((bf16[8,128,768]{2,1,0:T(8,128)(2,1)}), bf16[8,128,768]{2,1,0:T(8,128)(2,1)S(1)}, u32[]{:S(2)}, u32[]{:S(2)}) async-start(bf16[8,128,768]{2,1,0:T(8,128)(2,1)} %broadcast_in_dim.59), calls=%async_computation.2 | async-start | bytes 3145728 | tf_op jit(solution)/shard_map/all_to_all | solution.py:18
  57.7 0.2 reshape.97
  57.9 20.4 %all-to-all-done.2 = bf16[8,128,768]{2,1,0:T(8,128)(2,1)S(1)} async-done(((bf16[8,128,768]{2,1,0:T(8,128)(2,1)}), bf16[8,128,768]{2,1,0:T(8,128)(2,1)S(1)}, u32[]{:S(2)}, u32[]{:S(2)}) %all-to-all-start.2) | async-done | bytes 1572896 | tf_op jit(solution)/shard_map/all_to_all | solution.py:18
  78.3 0.7 fusion.27
  79.0 0.4 fusion.15
  79.5 0.2 fusion.10
  79.7 0.8 fusion.24
  80.5 0.1 reduce_max.74
  80.6 0.1 reduce_max.75
  80.8 0.5 convolution_add_fusion.2
  81.3 0.1 sub.96
  81.4 0.4 fusion.6
  81.8 0.1 convert_element_type.40
  81.9 0.4 fusion.28
  82.3 0.1 convert_element_type.42
  82.5 0.1 reduce_sum.99
  82.5 0.4 convolution_add_fusion.1
  83.0 0.1 reduce_sum.100
  83.2 1.0 pad_maximum_fusion.1
  84.1 3.5 %all-to-all-start.3 = ((f32[4,32,1664]{2,1,0:T(8,128)}), f32[4,32,1664]{2,1,0:T(8,128)S(1)}, u32[]{:S(2)}, u32[]{:S(2)}) async-start(f32[4,32,1664]{2,1,0:T(8,128)} %pad_maximum_fusion.1), calls=%async_computation.3 | async-start | bytes 1703936 | tf_op jit(solution)/shard_map/all_to_all | solution.py:18
  87.6 12.7 %all-to-all-done.3 = f32[4,32,1664]{2,1,0:T(8,128)S(1)} async-done(((f32[4,32,1664]{2,1,0:T(8,128)}), f32[4,32,1664]{2,1,0:T(8,128)S(1)}, u32[]{:S(2)}, u32[]{:S(2)}) %all-to-all-start.3) | async-done | bytes 852000 | tf_op jit(solution)/shard_map/all_to_all | solution.py:18
  100.5 0.1 fusion.12
  100.7 0.1 reshape.100
  100.8 0.8 pad_maximum_fusion.5
  101.6 6.8 %all-to-all-start.4 = ((f32[16,2,1792]{2,1,0:T(2,128)}), f32[16,2,1792]{2,1,0:T(2,128)S(1)}, u32[]{:S(2)}, u32[]{:S(2)}) async-start(f32[16,2,1792]{2,1,0:T(2,128)} %pad_maximum_fusion.5), calls=%async_computation.4 | async-start | bytes 458752 | tf_op jit(solution)/shard_map/all_to_all | solution.py:18
  108.4 0.2 copy.80
  108.6 0.2 copy.81
  108.9 0.2 broadcast_in_dim.66
  109.1 1.4 pad_maximum_fusion
  110.4 10.6 %all-to-all-done.4 = f32[16,2,1792]{2,1,0:T(2,128)S(1)} async-done(((f32[16,2,1792]{2,1,0:T(2,128)}), f32[16,2,1792]{2,1,0:T(2,128)S(1)}, u32[]{:S(2)}, u32[]{:S(2)}) %all-to-all-start.4) | async-done | bytes 229408 | tf_op jit(solution)/shard_map/all_to_all | solution.py:18
  121.0 9.4 %all-to-all-start.5 = ((bf16[8,128,896]{1,2,0:T(8,128)(2,1)}), bf16[8,128,896]{1,2,0:T(8,128)(2,1)S(1)}, u32[]{:S(2)}, u32[]{:S(2)}) async-start(bf16[8,128,896]{1,2,0:T(8,128)(2,1)} %pad_maximum_fusion), calls=%async_computation.5 | async-start | bytes 3670016 | tf_op jit(solution)/shard_map/all_to_all | solution.py:18
  130.8 0.2 fusion.19
  131.0 22.8 %all-to-all-done.5 = bf16[8,128,896]{1,2,0:T(8,128)(2,1)S(1)} async-done(((bf16[8,128,896]{1,2,0:T(8,128)(2,1)}), bf16[8,128,896]{1,2,0:T(8,128)(2,1)S(1)}, u32[]{:S(2)}, u32[]{:S(2)}) %all-to-all-start.5) | async-done | bytes 1835040 | tf_op jit(solution)/shard_map/all_to_all | solution.py:18
  153.8 0.3 copy_bitcast_fusion
  154.1 1.2 copy-done
  155.3 0.4 fusion
  155.7 0.6 broadcast_in_dim.67
  156.4 3.6 %all-to-all-start.6 = ((f32[8,4,128]{2,1,0:T(4,128)}), f32[8,4,128]{2,1,0:T(4,128)S(1)}, u32[]{:S(2)}, u32[]{:S(2)}) async-start(f32[8,4,128]{2,1,0:T(4,128)} %broadcast_in_dim.67), calls=%async_computation.6 | async-start | bytes 32768 | tf_op jit(solution)/shard_map/all_to_all | solution.py:18
  160.0 0.7 fusion.20
  160.6 4.2 %all-to-all-done.6 = f32[8,4,128]{2,1,0:T(4,128)S(1)} async-done(((f32[8,4,128]{2,1,0:T(4,128)}), f32[8,4,128]{2,1,0:T(4,128)S(1)}, u32[]{:S(2)}, u32[]{:S(2)}) %all-to-all-start.6) | async-done | bytes 16416 | tf_op jit(solution)/shard_map/all_to_all | solution.py:18
  164.9 2.3 %fusion.2 = f32[128,768]{1,0:T(8,128)S(1)} fusion(bf16[1024,896]{0,1:T(8,128)(2,1)} %copy-done, f32[128,1024]{1,0:T(8,128)S(1)} %fusion, f32[1024]{0:T(1024)S(1)} %bitcast.106, f32[1024]{0:T(1024)S(1)} %bitcast.108, f32[1024]{0:T(1024)S(1)} %bitcast.110, f32[1024]{0:T(1024)S(1)} %bitcast.104), kind=kOutput, calls=%fused_computation.9 | convolution fusion | flops 202506240 | bytes 2768896 | tf_op jit(solution)/shard_map/dot_general | solution.py:24
  167.2 1.5 convolution_add_fusion
  (48 shorter events, 1.1 us)
Async XLA Ops:
  33.5 10.7 %copy-start.3 = (bf16[128,768]{1,0:T(8,128)(2,1)S(1)}, bf16[128,768]{1,0:T(8,128)(2,1)}, u32[]{:S(2)}) copy-start(bf16[128,768]{1,0:T(8,128)(2,1)} %param.4) | copy-start | bytes 589828
  45.5 32.8 %all-to-all-start.2 = ((bf16[8,128,768]{2,1,0:T(8,128)(2,1)}), bf16[8,128,768]{2,1,0:T(8,128)(2,1)S(1)}, u32[]{:S(2)}, u32[]{:S(2)}) async-start(bf16[8,128,768]{2,1,0:T(8,128)(2,1)} %broadcast_in_dim.59), calls=%async_computation.2 | async-start | bytes 3145728 | tf_op jit(solution)/shard_map/all_to_all | solution.py:18
  84.1 16.2 %all-to-all-start.3 = ((f32[4,32,1664]{2,1,0:T(8,128)}), f32[4,32,1664]{2,1,0:T(8,128)S(1)}, u32[]{:S(2)}, u32[]{:S(2)}) async-start(f32[4,32,1664]{2,1,0:T(8,128)} %pad_maximum_fusion.1), calls=%async_computation.3 | async-start | bytes 1703936 | tf_op jit(solution)/shard_map/all_to_all | solution.py:18
  100.5 8.1 %copy-start.2 = (bf16[4,256,128]{2,1,0:T(8,128)(2,1)S(1)}, bf16[4,256,128]{2,1,0:T(8,128)(2,1)}, u32[]{:S(2)}) copy-start(bf16[4,256,128]{2,1,0:T(8,128)(2,1)} %get-tuple-element.25) | copy-start | bytes 786436
  101.6 19.4 %all-to-all-start.4 = ((f32[16,2,1792]{2,1,0:T(2,128)}), f32[16,2,1792]{2,1,0:T(2,128)S(1)}, u32[]{:S(2)}, u32[]{:S(2)}) async-start(f32[16,2,1792]{2,1,0:T(2,128)} %pad_maximum_fusion.5), calls=%async_computation.4 | async-start | bytes 458752 | tf_op jit(solution)/shard_map/all_to_all | solution.py:18
  121.0 32.8 %all-to-all-start.5 = ((bf16[8,128,896]{1,2,0:T(8,128)(2,1)}), bf16[8,128,896]{1,2,0:T(8,128)(2,1)S(1)}, u32[]{:S(2)}, u32[]{:S(2)}) async-start(bf16[8,128,896]{1,2,0:T(8,128)(2,1)} %pad_maximum_fusion), calls=%async_computation.5 | async-start | bytes 3670016 | tf_op jit(solution)/shard_map/all_to_all | solution.py:18
  131.0 24.4 %copy-start.4 = (bf16[128,768]{1,0:T(8,128)(2,1)S(1)}, bf16[128,768]{1,0:T(8,128)(2,1)}, u32[]{:S(2)}) copy-start(bf16[128,768]{1,0:T(8,128)(2,1)} %param.4) | copy-start | bytes 589828
  154.1 1.3 copy-start
  156.4 8.5 %all-to-all-start.6 = ((f32[8,4,128]{2,1,0:T(4,128)}), f32[8,4,128]{2,1,0:T(4,128)S(1)}, u32[]{:S(2)}, u32[]{:S(2)}) async-start(f32[8,4,128]{2,1,0:T(4,128)} %broadcast_in_dim.67), calls=%async_computation.6 | async-start | bytes 32768 | tf_op jit(solution)/shard_map/all_to_all | solution.py:18
  164.9 2.4 %copy-start.1 = (bf16[1024,896]{0,1:T(8,128)(2,1)S(1)}, bf16[1024,896]{0,1:T(8,128)(2,1)}, u32[]{:S(2)}) copy-start(bf16[1024,896]{0,1:T(8,128)(2,1)} %copy-done) | copy-start | bytes 5505028

commit v3 on v2

--- a/solution.py
+++ b/solution.py
@@ -16,6 +16,16 @@
 
 def exchange(values, axes):
     return lax.all_to_all(values, axes, 0, 0, tiled=True)
+
+
+def from_next(values, axis, step):
+    n = lax.axis_size(axis)
+    return lax.ppermute(values, axis, [(i, (i - step) % n) for i in range(n)])
+
+
+def rolled(values, axis, dim):
+    twice = jnp.concatenate([values, values], axis=dim)
+    return lax.dynamic_slice_in_dim(twice, lax.axis_index(axis), lax.axis_size(axis), dim)
 
 
 def split_dot(weights, exact, dims):
@@ -39,13 +49,16 @@
     nz, group = nzh * nzl, nc * nx
     fold = dim // lane
 
-    shared = exchange(jnp.broadcast_to(passages[None], (group, pool, dim)), group_axes)
-    shared = shared.reshape(group * pool, dim)
+    near = [from_next(passages, "x", k) for k in range(1, nx)]
 
-    tiles = teacher.reshape(own, ny, nzl, nc, nx, nzh, pool).transpose(5, 2, 1, 0, 3, 4, 6)
+    tiles = teacher.reshape(own, ny, nzl, nc, nx, nzh, pool)
+    tiles = rolled(rolled(tiles, "x", 4), "core", 3).transpose(5, 2, 1, 0, 3, 4, 6)
     tiles = tiles.reshape(nz, ny * own * group, pool)
     rows = jnp.broadcast_to(queries.reshape(1, own * fold, lane), (nz, own * fold, lane))
     got = exchange(jnp.concatenate([tiles, rows], axis=1), z_axes)
+    got, *near = lax.optimization_barrier((got, *near))
+    near = jnp.stack([passages, *near])
+    far = from_next(near, "core", 1)
     cut = ny * own * group
     tiles = got[:, :cut].reshape(nz, ny, own * group, pool).transpose(1, 0, 2, 3)
     tiles = tiles.reshape(ny, nz * own * group, pool)
@@ -55,12 +68,15 @@
     count = ny * nz * own
     logits = got[:, :cut].reshape(count, group * pool)
     block = got[:, cut:].reshape(count, dim)
+    shared = jnp.concatenate([near, far]).reshape(group * pool, dim)
 
-    rows = jnp.broadcast_to(block[None], (group, count, dim))
-    tiles = logits.reshape(count, group, pool).transpose(1, 0, 2)
-    every_row = exchange(jnp.concatenate([rows, tiles], axis=2), group_axes)
-    every_row = every_row.reshape(group * count, dim + pool)
-    all_rows, own_logits = every_row[:, :dim], every_row[:, dim:]
+    def columns(c, k):
+        return logits[:, (c * nx + k) * pool :][:, :pool]
+
+    rows = [
+        jnp.concatenate([block, columns(0, -k % nx), columns(1, -k % nx)], axis=1) for k in range(nx)
+    ]
+    rows = [rows[0]] + [from_next(rows[k], "x", k) for k in range(1, nx)]
 
     student = logit_scale * lax.dot_general(
         block, shared, (((1,), (1,)), ((), ())), preferred_element_type=f32
@@ -97,22 +113,35 @@
     y_at = lax.axis_index("y") * (nz * own)
     z_at = y_at + lax.axis_index(z_axes) * own
     part_s, part_t, stats = reduce_over(parts, stats, "y", ny, y_at)
+    part_s, part_t, stats, *rows = lax.optimization_barrier((part_s, part_t, stats, *rows))
+    kept = jnp.stack([r[:, : dim + pool] for r in rows])
+    sent = jnp.stack([jnp.concatenate([r[:, :dim], r[:, dim + pool :]], axis=1) for r in rows])
+    every_row = jnp.concatenate([kept, from_next(sent, "core", 1)]).reshape(group * count, dim + pool)
+    all_rows, own_logits = every_row[:, :dim], every_row[:, dim:]
     part_s, part_t, stats = reduce_over(
         jnp.concatenate([part_s, part_t], axis=1), stats, z_axes, nz, z_at
     )
     mine = lax.dynamic_slice_in_dim(stats, z_at, own, 1)
     query_grad = logit_scale * (part_s / mine[1][:, None] - part_t / mine[3][:, None])
 
-    scores = logit_scale * lax.dot_general(
-        passages, all_rows, (((1,), (1,)), ((), ())), preferred_element_type=f32
+    def lifted(values):
+        top = jnp.max(values, axis=0)
+        return jnp.exp(values - top), top
+
+    scores, high_s = lifted(
+        logit_scale
+        * lax.dot_general(passages, all_rows, (((1,), (1,)), ((), ())), preferred_element_type=f32)
     )
-    stats, scores = lax.optimization_barrier((stats, scores))
+    wanted, high_t = lifted(own_logits.T.astype(f32))
+    stats, scores, wanted, high_s, high_t = lax.optimization_barrier(
+        (stats, scores, wanted, high_s, high_t)
+    )
     every = exchange(jnp.broadcast_to(stats[None], (group,) + stats.shape), group_axes)
-    every = every.transpose(1, 0, 2).reshape(4, group * count)
-    grad = logit_scale * (
-        jnp.exp(scores - every[0]) / every[1]
-        - jnp.exp(own_logits.T.astype(f32) - every[2]) / every[3]
-    )
+    every = rolled(rolled(every.reshape(nc, nx, 4, count), "x", 1), "core", 0)
+    every = every.transpose(2, 0, 1, 3).reshape(4, group * count)
+    grad = (logit_scale * jnp.exp(high_s - every[0]) / every[1]) * scores - (
+        logit_scale * jnp.exp(high_t - every[2]) / every[3]
+    ) * wanted
     passage_grad = split_dot(grad, all_rows, (((1,), (0,)), ((), ())))
     return query_grad, passage_grad
 

time: 169 us -> 125 us (0.74)
  blocking collectives: 41.3 us -> 0 us
  waiting for transfers between devices: 70.7 us -> 30.8 us
  starting transfers between devices: 35.5 us -> 71.3 us
  matrix products: 6.62 us -> 4.57 us
  other arithmetic: 6.05 us -> 7.86 us
    all_to_all x5, waiting for transfers between devices: 70.7 us -> 12.2 us  [exchange(): return lax.all_to_all(values, axes, 0, 0, tiled=True)]
    all_to_all x2 -> x0, blocking collectives: 41.3 us -> none  [exchange(): return lax.all_to_all(values, axes, 0, 0, tiled=True)]
    ppermute x0 -> x8, starting transfers between devices: none -> 28.7 us  [from_next(): return lax.ppermute(values, axis, [(i, (i - step) % n) for i in range(n)])]
    ppermute x0 -> x8, waiting for transfers between devices: none -> 18.6 us  [from_next(): return lax.ppermute(values, axis, [(i, (i - step) % n) for i in range(n)])]
    all_to_all x5, starting transfers between devices: 35.5 us -> 42.6 us  [exchange(): return lax.all_to_all(values, axes, 0, 0, tiled=True)]
    concatenate x0 -> x2, local copies, waits for them, and re-layouts: none -> 2.5 us  [the longest x1 1.31 us: per_device(): jnp.concatenate([kept, from_next(sent, 'core', 1)])]
  transfers between devices with their start and end apart: 5 -> 13, of which waited for: 5 -> 7; matrix products, arithmetic and copies ran while one was open for 2% -> 4% of each run, Pallas kernels for 0% -> 0%
where the time goes in v3:
time: 125 us; the launch traced here: 124 us
  starting transfers between devices  71.3 us (57%)
  waiting for transfers between devices  30.8 us (25%)
  local copies, waits for them, and re-layouts  7.99 us (6%)
  other arithmetic  7.86 us (6%)
  matrix products  4.57 us (4%)
  between operations  1.35 us (1%)
    all_to_all x5, starting transfers between devices, exchange(): return lax.all_to_all(values, axes, 0, 0, tiled=True)  42.6 us
    ppermute x8, starting transfers between devices, from_next(): return lax.ppermute(values, axis, [(i, (i - step) % n) for i in range(n)])  28.7 us
    ppermute x8, waiting for transfers between devices, from_next(): return lax.ppermute(values, axis, [(i, (i - step) % n) for i in range(n)])  18.6 us
    all_to_all x5, waiting for transfers between devices, exchange(): return lax.all_to_all(values, axes, 0, 0, tiled=True)  12.2 us
  transfers between devices with their start and end apart: 13, of which 7 were waited for; matrix products, arithmetic and copies ran while one was open for 4% of the time, Pallas kernels for 0%

profile of v3, /device:TPU:1, one launch (start us, length us, event | category | flops | bytes accessed | tf_op | source)
XLA Modules:
  0.0 123.8 jit_solution(7973533357039960788)
XLA Ops:
  0.6 0.7 broadcast_in_dim.22
  1.3 1.2 reshape.102
  2.5 0.7 fusion.12
  3.2 0.7 fusion.22
  4.0 0.8 copy.65
  4.8 15.7 %all-to-all-start = ((bf16[16,76,128]{2,1,0:T(8,128)(2,1)}), bf16[16,76,128]{2,1,0:T(8,128)(2,1)S(1)}, u32[]{:S(2)}, u32[]{:S(2)}) async-start(bf16[16,76,128]{2,1,0:T(8,128)(2,1)} %copy.65), calls=%async_computation | async-start | bytes 655360 | tf_op jit(solution)/shard_map/all_to_all | solution.py:18
  20.5 4.4 %collective-permute-start = (bf16[128,768]{1,0:T(8,128)(2,1)S(1)}, bf16[128,768]{1,0:T(8,128)(2,1)S(1)}, u32[]{:S(2)}, u32[]{:S(2)}) collective-permute-start(bf16[128,768]{1,0:T(8,128)(2,1)S(1)} %copy-done.4), channel_id=1, source_target_pairs={{0,6},{2,0},{4,2},{6,4},{1,7},{3,1},{5,3},{7,5},{8,14},{10,8},{12,... | collective-permute-start | bytes 589832 | tf_op jit(solution)/shard_map/ppermute | solution.py:23
  24.9 2.4 %collective-permute-start.1 = (bf16[128,768]{1,0:T(8,128)(2,1)S(1)}, bf16[128,768]{1,0:T(8,128)(2,1)S(1)}, u32[]{:S(2)}, u32[]{:S(2)}) collective-permute-start(bf16[128,768]{1,0:T(8,128)(2,1)S(1)} %copy-done.4), channel_id=1, source_target_pairs={{0,4},{2,6},{4,0},{6,2},{1,5},{3,7},{5,1},{7,3},{8,12},{10,14},{12... | collective-permute-start | bytes 589832 | tf_op jit(solution)/shard_map/ppermute | solution.py:23
  27.4 2.5 %collective-permute-start.2 = (bf16[128,768]{1,0:T(8,128)(2,1)S(1)}, bf16[128,768]{1,0:T(8,128)(2,1)S(1)}, u32[]{:S(2)}, u32[]{:S(2)}) collective-permute-start(bf16[128,768]{1,0:T(8,128)(2,1)S(1)} %copy-done.4), channel_id=1, source_target_pairs={{0,2},{2,4},{4,6},{6,0},{1,3},{3,5},{5,7},{7,1},{8,10},{10,12},{12... | collective-permute-start | bytes 589832 | tf_op jit(solution)/shard_map/ppermute | solution.py:23
  29.9 3.6 %collective-permute-done.1 = bf16[128,768]{1,0:T(8,128)(2,1)S(1)} collective-permute-done((bf16[128,768]{1,0:T(8,128)(2,1)S(1)}, bf16[128,768]{1,0:T(8,128)(2,1)S(1)}, u32[]{:S(2)}, u32[]{:S(2)}) %collective-permute-start.1) | collective-permute-done | bytes 196640 | tf_op jit(solution)/shard_map/ppermute | solution.py:23
  33.5 5.1 %collective-permute-done.2 = bf16[128,768]{1,0:T(8,128)(2,1)S(1)} collective-permute-done((bf16[128,768]{1,0:T(8,128)(2,1)S(1)}, bf16[128,768]{1,0:T(8,128)(2,1)S(1)}, u32[]{:S(2)}, u32[]{:S(2)}) %collective-permute-start.2) | collective-permute-done | bytes 196640 | tf_op jit(solution)/shard_map/ppermute | solution.py:23
  38.7 0.8 pad_maximum_fusion.4
  39.5 4.2 %all-to-all-start.1 = ((bf16[4,448,128]{2,1,0:T(8,128)(2,1)}), bf16[4,448,128]{2,1,0:T(8,128)(2,1)S(1)}, u32[]{:S(2)}, u32[]{:S(2)}) async-start(bf16[4,448,128]{2,1,0:T(8,128)(2,1)} %pad_maximum_fusion.4), calls=%async_computation.1 | async-start | bytes 917504 | tf_op jit(solution)/shard_map/all_to_all | solution.py:18
  43.7 1.0 pad_maximum_fusion.2
  44.7 5.9 %collective-permute-start.3 = (bf16[4,128,768]{2,1,0:T(8,128)(2,1)}, bf16[4,128,768]{2,1,0:T(8,128)(2,1)}, u32[]{:S(2)}, u32[]{:S(2)}) collective-permute-start(bf16[4,128,768]{2,1,0:T(8,128)(2,1)} %pad_maximum_fusion.2), channel_id=1, source_target_pairs={{0,8},{8,0},{1,9},{9,1},{2,10},{10,2},{3,11},{11,3},{4,12},{12,4},... | collective-permute-start | bytes 2359304 | tf_op jit(solution)/shard_map/ppermute | solution.py:23
  50.6 0.2 fusion.30
  51.3 0.4 reduce-precision_convert_fusion.1
  51.8 0.2 reshape.106
  52.4 0.4 collective-permute-done.3
  52.8 1.2 constant_dynamic-update-slice_fusion
  54.0 0.7 fusion.34
  54.7 0.2 fusion.8
  55.0 0.5 fusion.18
  55.4 0.4 fusion.36
  55.8 0.4 convolution_add_fusion.2
  56.2 0.4 convolution_add_fusion.1
  56.7 1.0 pad_maximum_fusion.1
  57.7 4.5 %all-to-all-start.2 = ((f32[4,32,1664]{2,1,0:T(8,128)}), f32[4,32,1664]{2,1,0:T(8,128)S(1)}, u32[]{:S(2)}, u32[]{:S(2)}) async-start(f32[4,32,1664]{2,1,0:T(8,128)} %pad_maximum_fusion.1), calls=%async_computation.2 | async-start | bytes 1703936 | tf_op jit(solution)/shard_map/all_to_all | solution.py:18
  62.5 4.4 %collective-permute-start.4 = (bf16[128,1024]{1,0:T(8,128)(2,1)S(1)}, bf16[128,1024]{1,0:T(8,128)(2,1)S(1)}, u32[]{:S(2)}, u32[]{:S(2)}) collective-permute-start(bf16[128,1024]{1,0:T(8,128)(2,1)S(1)} %get-tuple-element.66), channel_id=1, source_target_pairs={{0,6},{2,0},{4,2},{6,4},{1,7},{3,1},{5,3},{7,5},{8,14},{10,8},{12,... | collective-permute-start | bytes 786440 | tf_op jit(solution)/shard_map/ppermute | solution.py:23
  66.9 2.4 %collective-permute-start.5 = (bf16[128,1024]{1,0:T(8,128)(2,1)S(1)}, bf16[128,1024]{1,0:T(8,128)(2,1)S(1)}, u32[]{:S(2)}, u32[]{:S(2)}) collective-permute-start(bf16[128,1024]{1,0:T(8,128)(2,1)S(1)} %get-tuple-element.67), channel_id=1, source_target_pairs={{0,4},{2,6},{4,0},{6,2},{1,5},{3,7},{5,1},{7,3},{8,12},{10,14},{12... | collective-permute-start | bytes 786440 | tf_op jit(solution)/shard_map/ppermute | solution.py:23
  69.4 2.5 %collective-permute-start.6 = (bf16[128,1024]{1,0:T(8,128)(2,1)S(1)}, bf16[128,1024]{1,0:T(8,128)(2,1)S(1)}, u32[]{:S(2)}, u32[]{:S(2)}) collective-permute-start(bf16[128,1024]{1,0:T(8,128)(2,1)S(1)} %get-tuple-element.65), channel_id=1, source_target_pairs={{0,2},{2,4},{4,6},{6,0},{1,3},{3,5},{5,7},{7,1},{8,10},{10,12},{12... | collective-permute-start | bytes 786440 | tf_op jit(solution)/shard_map/ppermute | solution.py:23
  72.2 3.5 %collective-permute-done.5 = bf16[128,1024]{1,0:T(8,128)(2,1)S(1)} collective-permute-done((bf16[128,1024]{1,0:T(8,128)(2,1)S(1)}, bf16[128,1024]{1,0:T(8,128)(2,1)S(1)}, u32[]{:S(2)}, u32[]{:S(2)}) %collective-permute-start.5) | collective-permute-done | bytes 262176 | tf_op jit(solution)/shard_map/ppermute | solution.py:23
  75.8 5.9 %collective-permute-done.6 = bf16[128,1024]{1,0:T(8,128)(2,1)S(1)} collective-permute-done((bf16[128,1024]{1,0:T(8,128)(2,1)S(1)}, bf16[128,1024]{1,0:T(8,128)(2,1)S(1)}, u32[]{:S(2)}, u32[]{:S(2)}) %collective-permute-start.6) | collective-permute-done | bytes 262176 | tf_op jit(solution)/shard_map/ppermute | solution.py:23
  82.0 0.8 pad_maximum_fusion.10
  82.8 8.8 %all-to-all-start.3 = ((f32[16,2,1792]{2,1,0:T(2,128)}), f32[16,2,1792]{2,1,0:T(2,128)S(1)}, u32[]{:S(2)}, u32[]{:S(2)}) async-start(f32[16,2,1792]{2,1,0:T(2,128)} %pad_maximum_fusion.10), calls=%async_computation.3 | async-start | bytes 458752 | tf_op jit(solution)/shard_map/all_to_all | solution.py:18
  92.0 4.1 %collective-permute-start.7 = (bf16[4,128,896]{2,1,0:T(8,128)(2,1)S(1)}, bf16[4,128,896]{2,1,0:T(8,128)(2,1)}, u32[]{:S(2)}, u32[]{:S(2)}) collective-permute-start(bf16[4,128,896]{2,1,0:T(8,128)(2,1)S(1)} %pad_maximum_fusion), channel_id=1, source_target_pairs={{0,8},{8,0},{1,9},{9,1},{2,10},{10,2},{3,11},{11,3},{4,12},{12,4},... | collective-permute-start | bytes 2752520 | tf_op jit(solution)/shard_map/ppermute | solution.py:23
  96.3 8.0 %all-to-all-done.3 = f32[16,2,1792]{2,1,0:T(2,128)S(1)} async-done(((f32[16,2,1792]{2,1,0:T(2,128)}), f32[16,2,1792]{2,1,0:T(2,128)S(1)}, u32[]{:S(2)}, u32[]{:S(2)}) %all-to-all-start.3) | async-done | bytes 229408 | tf_op jit(solution)/shard_map/all_to_all | solution.py:18
  104.7 0.2 fusion.24
  104.9 1.3 %constant_dynamic-update-slice_fusion.5 = bf16[8,128,896]{2,1,0:T(8,128)(2,1)S(1)} fusion(bf16[8,128,896]{2,1,0:T(8,128)(2,1)S(1)} %bitcast_dynamic-update-slice_fusion, bf16[4,128,896]{2,1,0:T(8,128)(2,1)} %collective-permute-done.7), kind=kLoop, calls=%fused_computation.76 | loop fusion | bytes 1835008 | tf_op jit(solution)/shard_map/concatenate | solution.py:119
  106.2 0.7 fusion.35
  106.8 0.2 slice_reduce_fusion
  107.0 0.1 copy.82
  107.3 0.6 broadcast_in_dim.58
  107.9 9.3 %all-to-all-start.4 = ((f32[8,4,128]{2,1,0:T(4,128)}), f32[8,4,128]{2,1,0:T(4,128)S(1)}, u32[]{:S(2)}, u32[]{:S(2)}) async-start(f32[8,4,128]{2,1,0:T(4,128)} %broadcast_in_dim.58), calls=%async_computation.4 | async-start | bytes 32768 | tf_op jit(solution)/shard_map/all_to_all | solution.py:18
  117.3 0.7 fusion.28
  118.0 4.2 %all-to-all-done.4 = f32[8,4,128]{2,1,0:T(4,128)S(1)} async-done(((f32[8,4,128]{2,1,0:T(4,128)}), f32[8,4,128]{2,1,0:T(4,128)S(1)}, u32[]{:S(2)}, u32[]{:S(2)}) %all-to-all-start.4) | async-done | bytes 16416 | tf_op jit(solution)/shard_map/all_to_all | solution.py:18
  122.3 0.4 fusion.2
  122.7 1.1 convolution_add_fusion
  (96 shorter events, 3.1 us)
Async XLA Ops:
  3.2 17.4 %copy-start.4 = (bf16[128,768]{1,0:T(8,128)(2,1)S(1)}, bf16[128,768]{1,0:T(8,128)(2,1)}, u32[]{:S(2)}) copy-start(bf16[128,768]{1,0:T(8,128)(2,1)} %param.4) | copy-start | bytes 589828
  4.8 33.8 %all-to-all-start = ((bf16[16,76,128]{2,1,0:T(8,128)(2,1)}), bf16[16,76,128]{2,1,0:T(8,128)(2,1)S(1)}, u32[]{:S(2)}, u32[]{:S(2)}) async-start(bf16[16,76,128]{2,1,0:T(8,128)(2,1)} %copy.65), calls=%async_computation | async-start | bytes 655360 | tf_op jit(solution)/shard_map/all_to_all | solution.py:18
  20.5 9.4 %collective-permute-start = (bf16[128,768]{1,0:T(8,128)(2,1)S(1)}, bf16[128,768]{1,0:T(8,128)(2,1)S(1)}, u32[]{:S(2)}, u32[]{:S(2)}) collective-permute-start(bf16[128,768]{1,0:T(8,128)(2,1)S(1)} %copy-done.4), channel_id=1, source_target_pairs={{0,6},{2,0},{4,2},{6,4},{1,7},{3,1},{5,3},{7,5},{8,14},{10,8},{12,... | collective-permute-start | bytes 589832 | tf_op jit(solution)/shard_map/ppermute | solution.py:23
  24.9 8.6 %collective-permute-start.1 = (bf16[128,768]{1,0:T(8,128)(2,1)S(1)}, bf16[128,768]{1,0:T(8,128)(2,1)S(1)}, u32[]{:S(2)}, u32[]{:S(2)}) collective-permute-start(bf16[128,768]{1,0:T(8,128)(2,1)S(1)} %copy-done.4), channel_id=1, source_target_pairs={{0,4},{2,6},{4,0},{6,2},{1,5},{3,7},{5,1},{7,3},{8,12},{10,14},{12... | collective-permute-start | bytes 589832 | tf_op jit(solution)/shard_map/ppermute | solution.py:23
  27.4 11.2 %collective-permute-start.2 = (bf16[128,768]{1,0:T(8,128)(2,1)S(1)}, bf16[128,768]{1,0:T(8,128)(2,1)S(1)}, u32[]{:S(2)}, u32[]{:S(2)}) collective-permute-start(bf16[128,768]{1,0:T(8,128)(2,1)S(1)} %copy-done.4), channel_id=1, source_target_pairs={{0,2},{2,4},{4,6},{6,0},{1,3},{3,5},{5,7},{7,1},{8,10},{10,12},{12... | collective-permute-start | bytes 589832 | tf_op jit(solution)/shard_map/ppermute | solution.py:23
  39.5 11.1 %all-to-all-start.1 = ((bf16[4,448,128]{2,1,0:T(8,128)(2,1)}), bf16[4,448,128]{2,1,0:T(8,128)(2,1)S(1)}, u32[]{:S(2)}, u32[]{:S(2)}) async-start(bf16[4,448,128]{2,1,0:T(8,128)(2,1)} %pad_maximum_fusion.4), calls=%async_computation.1 | async-start | bytes 917504 | tf_op jit(solution)/shard_map/all_to_all | solution.py:18
  44.7 8.1 %collective-permute-start.3 = (bf16[4,128,768]{2,1,0:T(8,128)(2,1)}, bf16[4,128,768]{2,1,0:T(8,128)(2,1)}, u32[]{:S(2)}, u32[]{:S(2)}) collective-permute-start(bf16[4,128,768]{2,1,0:T(8,128)(2,1)} %pad_maximum_fusion.2), channel_id=1, source_target_pairs={{0,8},{8,0},{1,9},{9,1},{2,10},{10,2},{3,11},{11,3},{4,12},{12,4},... | collective-permute-start | bytes 2359304 | tf_op jit(solution)/shard_map/ppermute | solution.py:23
  57.7 14.2 %all-to-all-start.2 = ((f32[4,32,1664]{2,1,0:T(8,128)}), f32[4,32,1664]{2,1,0:T(8,128)S(1)}, u32[]{:S(2)}, u32[]{:S(2)}) async-start(f32[4,32,1664]{2,1,0:T(8,128)} %pad_maximum_fusion.1), calls=%async_computation.2 | async-start | bytes 1703936 | tf_op jit(solution)/shard_map/all_to_all | solution.py:18
  62.5 9.7 %collective-permute-start.4 = (bf16[128,1024]{1,0:T(8,128)(2,1)S(1)}, bf16[128,1024]{1,0:T(8,128)(2,1)S(1)}, u32[]{:S(2)}, u32[]{:S(2)}) collective-permute-start(bf16[128,1024]{1,0:T(8,128)(2,1)S(1)} %get-tuple-element.66), channel_id=1, source_target_pairs={{0,6},{2,0},{4,2},{6,4},{1,7},{3,1},{5,3},{7,5},{8,14},{10,8},{12,... | collective-permute-start | bytes 786440 | tf_op jit(solution)/shard_map/ppermute | solution.py:23
  66.9 8.8 %collective-permute-start.5 = (bf16[128,1024]{1,0:T(8,128)(2,1)S(1)}, bf16[128,1024]{1,0:T(8,128)(2,1)S(1)}, u32[]{:S(2)}, u32[]{:S(2)}) collective-permute-start(bf16[128,1024]{1,0:T(8,128)(2,1)S(1)} %get-tuple-element.67), channel_id=1, source_target_pairs={{0,4},{2,6},{4,0},{6,2},{1,5},{3,7},{5,1},{7,3},{8,12},{10,14},{12... | collective-permute-start | bytes 786440 | tf_op jit(solution)/shard_map/ppermute | solution.py:23
  69.4 12.3 %collective-permute-start.6 = (bf16[128,1024]{1,0:T(8,128)(2,1)S(1)}, bf16[128,1024]{1,0:T(8,128)(2,1)S(1)}, u32[]{:S(2)}, u32[]{:S(2)}) collective-permute-start(bf16[128,1024]{1,0:T(8,128)(2,1)S(1)} %get-tuple-element.65), channel_id=1, source_target_pairs={{0,2},{2,4},{4,6},{6,0},{1,3},{3,5},{5,7},{7,1},{8,10},{10,12},{12... | collective-permute-start | bytes 786440 | tf_op jit(solution)/shard_map/ppermute | solution.py:23
  75.8 7.1 %copy-start = (bf16[128,1024]{1,0:T(8,128)(2,1)}, bf16[128,1024]{1,0:T(8,128)(2,1)S(1)}, u32[]{:S(2)}) copy-start(bf16[128,1024]{1,0:T(8,128)(2,1)S(1)} %collective-permute-done.5) | copy-start | bytes 786436
  81.7 1.1 copy-start.2
  82.8 21.4 %all-to-all-start.3 = ((f32[16,2,1792]{2,1,0:T(2,128)}), f32[16,2,1792]{2,1,0:T(2,128)S(1)}, u32[]{:S(2)}, u32[]{:S(2)}) async-start(f32[16,2,1792]{2,1,0:T(2,128)} %pad_maximum_fusion.10), calls=%async_computation.3 | async-start | bytes 458752 | tf_op jit(solution)/shard_map/all_to_all | solution.py:18
  91.8 4.4 %copy-start.1 = (bf16[128,1024]{1,0:T(8,128)(2,1)S(1)}, bf16[128,1024]{1,0:T(8,128)(2,1)}, u32[]{:S(2)}) copy-start(bf16[128,1024]{1,0:T(8,128)(2,1)} %copy-done) | copy-start | bytes 786436
  91.8 4.4 %copy-start.3 = (bf16[128,1024]{1,0:T(8,128)(2,1)S(1)}, bf16[128,1024]{1,0:T(8,128)(2,1)}, u32[]{:S(2)}) copy-start(bf16[128,1024]{1,0:T(8,128)(2,1)} %copy-done.2) | copy-start | bytes 786436
  92.0 12.9 %collective-permute-start.7 = (bf16[4,128,896]{2,1,0:T(8,128)(2,1)S(1)}, bf16[4,128,896]{2,1,0:T(8,128)(2,1)}, u32[]{:S(2)}, u32[]{:S(2)}) collective-permute-start(bf16[4,128,896]{2,1,0:T(8,128)(2,1)S(1)} %pad_maximum_fusion), channel_id=1, source_target_pairs={{0,8},{8,0},{1,9},{9,1},{2,10},{10,2},{3,11},{11,3},{4,12},{12,4},... | collective-permute-start | bytes 2752520 | tf_op jit(solution)/shard_map/ppermute | solution.py:23
  96.2 10.0 %copy-start.5 = (bf16[128,768]{1,0:T(8,128)(2,1)S(1)}, bf16[128,768]{1,0:T(8,128)(2,1)}, u32[]{:S(2)}) copy-start(bf16[128,768]{1,0:T(8,128)(2,1)} %param.4) | copy-start | bytes 589828
  107.9 14.2 %all-to-all-start.4 = ((f32[8,4,128]{2,1,0:T(4,128)}), f32[8,4,128]{2,1,0:T(4,128)S(1)}, u32[]{:S(2)}, u32[]{:S(2)}) async-start(f32[8,4,128]{2,1,0:T(4,128)} %broadcast_in_dim.58), calls=%async_computation.4 | async-start | bytes 32768 | tf_op jit(solution)/shard_map/all_to_all | solution.py:18

commit v4 on v3

--- a/solution.py
+++ b/solution.py
@@ -93,34 +93,37 @@
     parts = jnp.concatenate([part_s, part_t], axis=1)
     stats = jnp.stack([top_s, sum_s, top_t, sum_t])
 
-    def reduce_over(parts, stats, axes, n, place):
+    def pack(parts, stats, n):
         width = parts.shape[0] // n
         extra = -(-stats.size // width)
         extra += -extra % lane
         spread = jnp.pad(stats.reshape(-1, extra), ((0, width - stats.size // extra), (0, 0)))
-        sent = jnp.concatenate([parts.reshape(n, width, 2 * dim), jnp.broadcast_to(spread, (n, width, extra))], axis=2)
-        got = exchange(sent, axes)
-        parts = got[:, :, : 2 * dim]
-        stats = got[:, : stats.size // extra, 2 * dim :].reshape(n, 4, -1)
+        spread = jnp.broadcast_to(spread, (n, width, extra))
+        return jnp.concatenate([parts.reshape(n, width, 2 * dim), spread], axis=2)
+
+    def unpack(got, place):
+        n, width, full = got.shape
+        extra = full - 2 * dim
+        stats = got[:, : 4 * count // extra, 2 * dim :].reshape(n, 4, count)
         weight_s, top_s, sum_s = combine(stats[:, 0], stats[:, 1], 0)
         weight_t, top_t, sum_t = combine(stats[:, 2], stats[:, 3], 0)
         weight_s = lax.dynamic_slice_in_dim(weight_s, place, width, 1)
         weight_t = lax.dynamic_slice_in_dim(weight_t, place, width, 1)
-        part_s = jnp.sum(weight_s[:, :, None] * parts[:, :, :dim], axis=0)
-        part_t = jnp.sum(weight_t[:, :, None] * parts[:, :, dim:], axis=0)
+        part_s = jnp.sum(weight_s[:, :, None] * got[:, :, :dim], axis=0)
+        part_t = jnp.sum(weight_t[:, :, None] * got[:, :, dim : 2 * dim], axis=0)
         return part_s, part_t, jnp.stack([top_s, sum_s, top_t, sum_t])
 
     y_at = lax.axis_index("y") * (nz * own)
     z_at = y_at + lax.axis_index(z_axes) * own
-    part_s, part_t, stats = reduce_over(parts, stats, "y", ny, y_at)
-    part_s, part_t, stats, *rows = lax.optimization_barrier((part_s, part_t, stats, *rows))
+    part_s, part_t, stats = unpack(exchange(pack(parts, stats, ny), "y"), y_at)
+    sent = pack(jnp.concatenate([part_s, part_t], axis=1), stats, nz)
+    got = exchange(sent, z_axes)
+    *rows, _ = lax.optimization_barrier((*rows, sent))
     kept = jnp.stack([r[:, : dim + pool] for r in rows])
-    sent = jnp.stack([jnp.concatenate([r[:, :dim], r[:, dim + pool :]], axis=1) for r in rows])
-    every_row = jnp.concatenate([kept, from_next(sent, "core", 1)]).reshape(group * count, dim + pool)
+    away = jnp.stack([jnp.concatenate([r[:, :dim], r[:, dim + pool :]], axis=1) for r in rows])
+    every_row = jnp.concatenate([kept, from_next(away, "core", 1)]).reshape(group * count, dim + pool)
     all_rows, own_logits = every_row[:, :dim], every_row[:, dim:]
-    part_s, part_t, stats = reduce_over(
-        jnp.concatenate([part_s, part_t], axis=1), stats, z_axes, nz, z_at
-    )
+    part_s, part_t, stats = unpack(got, z_at)
     mine = lax.dynamic_slice_in_dim(stats, z_at, own, 1)
     query_grad = logit_scale * (part_s / mine[1][:, None] - part_t / mine[3][:, None])
 

time: 125 us -> 118 us (0.944)
  waiting for transfers between devices: 30.8 us -> 18.2 us
  starting transfers between devices: 71.3 us -> 75.6 us
    ppermute x8, waiting for transfers between devices: 18.6 us -> 9.1 us  [from_next(): return lax.ppermute(values, axis, [(i, (i - step) % n) for i in range(n)])]
    all_to_all x5, waiting for transfers between devices: 12.2 us -> 9.15 us  [exchange(): return lax.all_to_all(values, axes, 0, 0, tiled=True)]
    ppermute x8, starting transfers between devices: 28.7 us -> 31 us  [from_next(): return lax.ppermute(values, axis, [(i, (i - step) % n) for i in range(n)])]
    all_to_all x5, starting transfers between devices: 42.6 us -> 44.6 us  [exchange(): return lax.all_to_all(values, axes, 0, 0, tiled=True)]
  transfers between devices with their start and end apart: 13 -> 13, of which waited for: 7 -> 5; matrix products, arithmetic and copies ran while one was open for 4% -> 6% of each run, Pallas kernels for 0% -> 0%
where the time goes in v4:
time: 118 us; the launch traced here: 117 us
  starting transfers between devices  75.6 us (64%)
  waiting for transfers between devices  18.2 us (15%)
  other arithmetic  8.57 us (7%)
  local copies, waits for them, and re-layouts  8.47 us (7%)
  matrix products  4.56 us (4%)
  between operations  1.38 us (1%)
    all_to_all x5, starting transfers between devices, exchange(): return lax.all_to_all(values, axes, 0, 0, tiled=True)  44.6 us
    ppermute x8, starting transfers between devices, from_next(): return lax.ppermute(values, axis, [(i, (i - step) % n) for i in range(n)])  31 us
    all_to_all x5, waiting for transfers between devices, exchange(): return lax.all_to_all(values, axes, 0, 0, tiled=True)  9.15 us
    ppermute x8, waiting for transfers between devices, from_next(): return lax.ppermute(values, axis, [(i, (i - step) % n) for i in range(n)])  9.1 us
  transfers between devices with their start and end apart: 13, of which 5 were waited for; matrix products, arithmetic and copies ran while one was open for 6% of the time, Pallas kernels for 0%

profile of v4, /device:TPU:1, one launch (start us, length us, event | category | flops | bytes accessed | tf_op | source)
XLA Modules:
  0.0 116.8 jit_solution(7097530692365658206)
XLA Ops:
  0.6 0.7 broadcast_in_dim.22
  1.3 1.2 reshape.102
  2.5 0.7 fusion.12
  3.2 0.7 fusion.22
  4.0 0.8 copy.65
  4.8 15.7 %all-to-all-start = ((bf16[16,76,128]{2,1,0:T(8,128)(2,1)}), bf16[16,76,128]{2,1,0:T(8,128)(2,1)S(1)}, u32[]{:S(2)}, u32[]{:S(2)}) async-start(bf16[16,76,128]{2,1,0:T(8,128)(2,1)} %copy.65), calls=%async_computation | async-start | bytes 655360 | tf_op jit(solution)/shard_map/all_to_all | solution.py:18
  20.5 4.4 %collective-permute-start = (bf16[128,768]{1,0:T(8,128)(2,1)S(1)}, bf16[128,768]{1,0:T(8,128)(2,1)S(1)}, u32[]{:S(2)}, u32[]{:S(2)}) collective-permute-start(bf16[128,768]{1,0:T(8,128)(2,1)S(1)} %copy-done.4), channel_id=1, source_target_pairs={{0,6},{2,0},{4,2},{6,4},{1,7},{3,1},{5,3},{7,5},{8,14},{10,8},{12,... | collective-permute-start | bytes 589832 | tf_op jit(solution)/shard_map/ppermute | solution.py:23
  24.9 2.4 %collective-permute-start.1 = (bf16[128,768]{1,0:T(8,128)(2,1)S(1)}, bf16[128,768]{1,0:T(8,128)(2,1)S(1)}, u32[]{:S(2)}, u32[]{:S(2)}) collective-permute-start(bf16[128,768]{1,0:T(8,128)(2,1)S(1)} %copy-done.4), channel_id=1, source_target_pairs={{0,4},{2,6},{4,0},{6,2},{1,5},{3,7},{5,1},{7,3},{8,12},{10,14},{12... | collective-permute-start | bytes 589832 | tf_op jit(solution)/shard_map/ppermute | solution.py:23
  27.4 2.5 %collective-permute-start.2 = (bf16[128,768]{1,0:T(8,128)(2,1)S(1)}, bf16[128,768]{1,0:T(8,128)(2,1)S(1)}, u32[]{:S(2)}, u32[]{:S(2)}) collective-permute-start(bf16[128,768]{1,0:T(8,128)(2,1)S(1)} %copy-done.4), channel_id=1, source_target_pairs={{0,2},{2,4},{4,6},{6,0},{1,3},{3,5},{5,7},{7,1},{8,10},{10,12},{12... | collective-permute-start | bytes 589832 | tf_op jit(solution)/shard_map/ppermute | solution.py:23
  29.9 3.6 %collective-permute-done.1 = bf16[128,768]{1,0:T(8,128)(2,1)S(1)} collective-permute-done((bf16[128,768]{1,0:T(8,128)(2,1)S(1)}, bf16[128,768]{1,0:T(8,128)(2,1)S(1)}, u32[]{:S(2)}, u32[]{:S(2)}) %collective-permute-start.1) | collective-permute-done | bytes 196640 | tf_op jit(solution)/shard_map/ppermute | solution.py:23
  33.5 5.1 %collective-permute-done.2 = bf16[128,768]{1,0:T(8,128)(2,1)S(1)} collective-permute-done((bf16[128,768]{1,0:T(8,128)(2,1)S(1)}, bf16[128,768]{1,0:T(8,128)(2,1)S(1)}, u32[]{:S(2)}, u32[]{:S(2)}) %collective-permute-start.2) | collective-permute-done | bytes 196640 | tf_op jit(solution)/shard_map/ppermute | solution.py:23
  38.7 0.8 pad_maximum_fusion.4
  39.5 4.2 %all-to-all-start.1 = ((bf16[4,448,128]{2,1,0:T(8,128)(2,1)}), bf16[4,448,128]{2,1,0:T(8,128)(2,1)S(1)}, u32[]{:S(2)}, u32[]{:S(2)}) async-start(bf16[4,448,128]{2,1,0:T(8,128)(2,1)} %pad_maximum_fusion.4), calls=%async_computation.1 | async-start | bytes 917504 | tf_op jit(solution)/shard_map/all_to_all | solution.py:18
  43.7 1.0 pad_maximum_fusion.2
  44.7 5.9 %collective-permute-start.3 = (bf16[4,128,768]{2,1,0:T(8,128)(2,1)}, bf16[4,128,768]{2,1,0:T(8,128)(2,1)}, u32[]{:S(2)}, u32[]{:S(2)}) collective-permute-start(bf16[4,128,768]{2,1,0:T(8,128)(2,1)} %pad_maximum_fusion.2), channel_id=1, source_target_pairs={{0,8},{8,0},{1,9},{9,1},{2,10},{10,2},{3,11},{11,3},{4,12},{12,4},... | collective-permute-start | bytes 2359304 | tf_op jit(solution)/shard_map/ppermute | solution.py:23
  50.6 0.2 fusion.30
  51.3 0.4 reduce-precision_convert_fusion.1
  51.8 0.2 reshape.106
  52.4 0.4 collective-permute-done.3
  52.8 1.2 %constant_dynamic-update-slice_fusion = bf16[8,128,768]{2,1,0:T(8,128)(2,1)S(1)} fusion(bf16[8,128,768]{2,1,0:T(8,128)(2,1)S(1)} %constant_dynamic-update-slice_fusion.1, bf16[4,128,768]{2,1,0:T(8,128)(2,1)} %collective-permute-done.3), kind=kLoop, calls=%fused_computation.71 | loop fusion | bytes 1572864 | tf_op jit(solution)/shard_map/concatenate | solution.py:71
  54.0 0.7 fusion.34
  54.7 0.2 fusion.8
  55.0 0.5 fusion.18
  55.4 0.4 fusion.36
  55.8 0.4 convolution_add_fusion.2
  56.2 0.4 convolution_add_fusion.1
  56.7 1.0 pad_maximum_fusion.1
  57.7 4.5 %all-to-all-start.2 = ((f32[4,32,1664]{2,1,0:T(8,128)}), f32[4,32,1664]{2,1,0:T(8,128)S(1)}, u32[]{:S(2)}, u32[]{:S(2)}) async-start(f32[4,32,1664]{2,1,0:T(8,128)} %pad_maximum_fusion.1), calls=%async_computation.2 | async-start | bytes 1703936 | tf_op jit(solution)/shard_map/all_to_all | solution.py:18
  62.4 0.8 fusion.16
  63.2 4.4 %collective-permute-start.4 = (bf16[128,1024]{1,0:T(8,128)(2,1)}, bf16[128,1024]{1,0:T(8,128)(2,1)S(1)}, u32[]{:S(2)}, u32[]{:S(2)}) collective-permute-start(bf16[128,1024]{1,0:T(8,128)(2,1)} %get-tuple-element.60), channel_id=1, source_target_pairs={{0,6},{2,0},{4,2},{6,4},{1,7},{3,1},{5,3},{7,5},{8,14},{10,8},{12,... | collective-permute-start | bytes 786440 | tf_op jit(solution)/shard_map/ppermute | solution.py:23
  67.6 2.4 %collective-permute-start.5 = (bf16[128,1024]{1,0:T(8,128)(2,1)S(1)}, bf16[128,1024]{1,0:T(8,128)(2,1)S(1)}, u32[]{:S(2)}, u32[]{:S(2)}) collective-permute-start(bf16[128,1024]{1,0:T(8,128)(2,1)S(1)} %get-tuple-element.61), channel_id=1, source_target_pairs={{0,4},{2,6},{4,0},{6,2},{1,5},{3,7},{5,1},{7,3},{8,12},{10,14},{12... | collective-permute-start | bytes 786440 | tf_op jit(solution)/shard_map/ppermute | solution.py:23
  70.1 2.5 %collective-permute-start.6 = (bf16[128,1024]{1,0:T(8,128)(2,1)S(1)}, bf16[128,1024]{1,0:T(8,128)(2,1)S(1)}, u32[]{:S(2)}, u32[]{:S(2)}) collective-permute-start(bf16[128,1024]{1,0:T(8,128)(2,1)S(1)} %get-tuple-element.59), channel_id=1, source_target_pairs={{0,2},{2,4},{4,6},{6,0},{1,3},{3,5},{5,7},{7,1},{8,10},{10,12},{12... | collective-permute-start | bytes 786440 | tf_op jit(solution)/shard_map/ppermute | solution.py:23
  73.1 0.8 pad_maximum_fusion.10
  73.9 8.7 %all-to-all-start.3 = ((f32[16,2,1792]{2,1,0:T(2,128)}), f32[16,2,1792]{2,1,0:T(2,128)S(1)}, u32[]{:S(2)}, u32[]{:S(2)}) async-start(f32[16,2,1792]{2,1,0:T(2,128)} %pad_maximum_fusion.10), calls=%async_computation.3 | async-start | bytes 458752 | tf_op jit(solution)/shard_map/all_to_all | solution.py:18
  82.9 0.4 copy-done
  83.6 6.5 %collective-permute-start.7 = (bf16[4,128,896]{2,1,0:T(8,128)(2,1)S(1)}, bf16[4,128,896]{2,1,0:T(8,128)(2,1)}, u32[]{:S(2)}, u32[]{:S(2)}) collective-permute-start(bf16[4,128,896]{2,1,0:T(8,128)(2,1)S(1)} %pad_maximum_fusion), channel_id=1, source_target_pairs={{0,8},{8,0},{1,9},{9,1},{2,10},{10,2},{3,11},{11,3},{4,12},{12,4},... | collective-permute-start | bytes 2752520 | tf_op jit(solution)/shard_map/ppermute | solution.py:23
  90.2 4.9 %all-to-all-done.3 = f32[16,2,1792]{2,1,0:T(2,128)S(1)} async-done(((f32[16,2,1792]{2,1,0:T(2,128)}), f32[16,2,1792]{2,1,0:T(2,128)S(1)}, u32[]{:S(2)}, u32[]{:S(2)}) %all-to-all-start.3) | async-done | bytes 229408 | tf_op jit(solution)/shard_map/all_to_all | solution.py:18
  95.6 0.2 fusion.24
  95.7 1.3 %constant_dynamic-update-slice_fusion.5 = bf16[8,128,896]{2,1,0:T(8,128)(2,1)S(1)} fusion(bf16[8,128,896]{2,1,0:T(8,128)(2,1)S(1)} %bitcast_dynamic-update-slice_fusion, bf16[4,128,896]{2,1,0:T(8,128)(2,1)} %collective-permute-done.7), kind=kLoop, calls=%fused_computation.76 | loop fusion | bytes 1835008 | tf_op jit(solution)/shard_map/concatenate | solution.py:124
  97.1 0.6 fusion.35
  97.7 0.2 slice_reduce_fusion
  97.9 0.1 copy.82
  98.2 0.6 broadcast_in_dim.58
  98.8 11.4 %all-to-all-start.4 = ((f32[8,4,128]{2,1,0:T(4,128)}), f32[8,4,128]{2,1,0:T(4,128)S(1)}, u32[]{:S(2)}, u32[]{:S(2)}) async-start(f32[8,4,128]{2,1,0:T(4,128)} %broadcast_in_dim.58), calls=%async_computation.4 | async-start | bytes 32768 | tf_op jit(solution)/shard_map/all_to_all | solution.py:18
  110.2 0.7 fusion.28
  110.9 4.2 %all-to-all-done.4 = f32[8,4,128]{2,1,0:T(4,128)S(1)} async-done(((f32[8,4,128]{2,1,0:T(4,128)}), f32[8,4,128]{2,1,0:T(4,128)S(1)}, u32[]{:S(2)}, u32[]{:S(2)}) %all-to-all-start.4) | async-done | bytes 16416 | tf_op jit(solution)/shard_map/all_to_all | solution.py:18
  115.2 0.4 fusion.2
  115.6 1.1 convolution_add_fusion
  (96 shorter events, 3.1 us)
Async XLA Ops:
  3.2 17.4 %copy-start.4 = (bf16[128,768]{1,0:T(8,128)(2,1)S(1)}, bf16[128,768]{1,0:T(8,128)(2,1)}, u32[]{:S(2)}) copy-start(bf16[128,768]{1,0:T(8,128)(2,1)} %param.4) | copy-start | bytes 589828
  4.8 33.8 %all-to-all-start = ((bf16[16,76,128]{2,1,0:T(8,128)(2,1)}), bf16[16,76,128]{2,1,0:T(8,128)(2,1)S(1)}, u32[]{:S(2)}, u32[]{:S(2)}) async-start(bf16[16,76,128]{2,1,0:T(8,128)(2,1)} %copy.65), calls=%async_computation | async-start | bytes 655360 | tf_op jit(solution)/shard_map/all_to_all | solution.py:18
  20.5 9.4 %collective-permute-start = (bf16[128,768]{1,0:T(8,128)(2,1)S(1)}, bf16[128,768]{1,0:T(8,128)(2,1)S(1)}, u32[]{:S(2)}, u32[]{:S(2)}) collective-permute-start(bf16[128,768]{1,0:T(8,128)(2,1)S(1)} %copy-done.4), channel_id=1, source_target_pairs={{0,6},{2,0},{4,2},{6,4},{1,7},{3,1},{5,3},{7,5},{8,14},{10,8},{12,... | collective-permute-start | bytes 589832 | tf_op jit(solution)/shard_map/ppermute | solution.py:23
  24.9 8.6 %collective-permute-start.1 = (bf16[128,768]{1,0:T(8,128)(2,1)S(1)}, bf16[128,768]{1,0:T(8,128)(2,1)S(1)}, u32[]{:S(2)}, u32[]{:S(2)}) collective-permute-start(bf16[128,768]{1,0:T(8,128)(2,1)S(1)} %copy-done.4), channel_id=1, source_target_pairs={{0,4},{2,6},{4,0},{6,2},{1,5},{3,7},{5,1},{7,3},{8,12},{10,14},{12... | collective-permute-start | bytes 589832 | tf_op jit(solution)/shard_map/ppermute | solution.py:23
  27.4 11.2 %collective-permute-start.2 = (bf16[128,768]{1,0:T(8,128)(2,1)S(1)}, bf16[128,768]{1,0:T(8,128)(2,1)S(1)}, u32[]{:S(2)}, u32[]{:S(2)}) collective-permute-start(bf16[128,768]{1,0:T(8,128)(2,1)S(1)} %copy-done.4), channel_id=1, source_target_pairs={{0,2},{2,4},{4,6},{6,0},{1,3},{3,5},{5,7},{7,1},{8,10},{10,12},{12... | collective-permute-start | bytes 589832 | tf_op jit(solution)/shard_map/ppermute | solution.py:23
  39.5 11.1 %all-to-all-start.1 = ((bf16[4,448,128]{2,1,0:T(8,128)(2,1)}), bf16[4,448,128]{2,1,0:T(8,128)(2,1)S(1)}, u32[]{:S(2)}, u32[]{:S(2)}) async-start(bf16[4,448,128]{2,1,0:T(8,128)(2,1)} %pad_maximum_fusion.4), calls=%async_computation.1 | async-start | bytes 917504 | tf_op jit(solution)/shard_map/all_to_all | solution.py:18
  44.7 8.1 %collective-permute-start.3 = (bf16[4,128,768]{2,1,0:T(8,128)(2,1)}, bf16[4,128,768]{2,1,0:T(8,128)(2,1)}, u32[]{:S(2)}, u32[]{:S(2)}) collective-permute-start(bf16[4,128,768]{2,1,0:T(8,128)(2,1)} %pad_maximum_fusion.2), channel_id=1, source_target_pairs={{0,8},{8,0},{1,9},{9,1},{2,10},{10,2},{3,11},{11,3},{4,12},{12,4},... | collective-permute-start | bytes 2359304 | tf_op jit(solution)/shard_map/ppermute | solution.py:23
  57.7 14.9 %all-to-all-start.2 = ((f32[4,32,1664]{2,1,0:T(8,128)}), f32[4,32,1664]{2,1,0:T(8,128)S(1)}, u32[]{:S(2)}, u32[]{:S(2)}) async-start(f32[4,32,1664]{2,1,0:T(8,128)} %pad_maximum_fusion.1), calls=%async_computation.2 | async-start | bytes 1703936 | tf_op jit(solution)/shard_map/all_to_all | solution.py:18
  63.2 19.4 %collective-permute-start.4 = (bf16[128,1024]{1,0:T(8,128)(2,1)}, bf16[128,1024]{1,0:T(8,128)(2,1)S(1)}, u32[]{:S(2)}, u32[]{:S(2)}) collective-permute-start(bf16[128,1024]{1,0:T(8,128)(2,1)} %get-tuple-element.60), channel_id=1, source_target_pairs={{0,6},{2,0},{4,2},{6,4},{1,7},{3,1},{5,3},{7,5},{8,14},{10,8},{12,... | collective-permute-start | bytes 786440 | tf_op jit(solution)/shard_map/ppermute | solution.py:23
  67.6 15.0 %collective-permute-start.5 = (bf16[128,1024]{1,0:T(8,128)(2,1)S(1)}, bf16[128,1024]{1,0:T(8,128)(2,1)S(1)}, u32[]{:S(2)}, u32[]{:S(2)}) collective-permute-start(bf16[128,1024]{1,0:T(8,128)(2,1)S(1)} %get-tuple-element.61), channel_id=1, source_target_pairs={{0,4},{2,6},{4,0},{6,2},{1,5},{3,7},{5,1},{7,3},{8,12},{10,14},{12... | collective-permute-start | bytes 786440 | tf_op jit(solution)/shard_map/ppermute | solution.py:23
  70.1 12.6 %collective-permute-start.6 = (bf16[128,1024]{1,0:T(8,128)(2,1)S(1)}, bf16[128,1024]{1,0:T(8,128)(2,1)S(1)}, u32[]{:S(2)}, u32[]{:S(2)}) collective-permute-start(bf16[128,1024]{1,0:T(8,128)(2,1)S(1)} %get-tuple-element.59), channel_id=1, source_target_pairs={{0,2},{2,4},{4,6},{6,0},{1,3},{3,5},{5,7},{7,1},{8,10},{10,12},{12... | collective-permute-start | bytes 786440 | tf_op jit(solution)/shard_map/ppermute | solution.py:23
  73.9 21.3 %all-to-all-start.3 = ((f32[16,2,1792]{2,1,0:T(2,128)}), f32[16,2,1792]{2,1,0:T(2,128)S(1)}, u32[]{:S(2)}, u32[]{:S(2)}) async-start(f32[16,2,1792]{2,1,0:T(2,128)} %pad_maximum_fusion.10), calls=%async_computation.3 | async-start | bytes 458752 | tf_op jit(solution)/shard_map/all_to_all | solution.py:18
  82.6 0.7 copy-start
  82.6 0.8 copy-start.2
  83.4 6.7 %copy-start.1 = (bf16[128,1024]{1,0:T(8,128)(2,1)S(1)}, bf16[128,1024]{1,0:T(8,128)(2,1)}, u32[]{:S(2)}) copy-start(bf16[128,1024]{1,0:T(8,128)(2,1)} %copy-done) | copy-start | bytes 786436
  83.4 6.8 %copy-start.3 = (bf16[128,1024]{1,0:T(8,128)(2,1)S(1)}, bf16[128,1024]{1,0:T(8,128)(2,1)}, u32[]{:S(2)}) copy-start(bf16[128,1024]{1,0:T(8,128)(2,1)} %copy-done.2) | copy-start | bytes 786436
  83.6 12.1 %collective-permute-start.7 = (bf16[4,128,896]{2,1,0:T(8,128)(2,1)S(1)}, bf16[4,128,896]{2,1,0:T(8,128)(2,1)}, u32[]{:S(2)}, u32[]{:S(2)}) collective-permute-start(bf16[4,128,896]{2,1,0:T(8,128)(2,1)S(1)} %pad_maximum_fusion), channel_id=1, source_target_pairs={{0,8},{8,0},{1,9},{9,1},{2,10},{10,2},{3,11},{11,3},{4,12},{12,4},... | collective-permute-start | bytes 2752520 | tf_op jit(solution)/shard_map/ppermute | solution.py:23
  90.1 6.9 %copy-start.5 = (bf16[128,768]{1,0:T(8,128)(2,1)S(1)}, bf16[128,768]{1,0:T(8,128)(2,1)}, u32[]{:S(2)}) copy-start(bf16[128,768]{1,0:T(8,128)(2,1)} %param.4) | copy-start | bytes 589828
  98.8 16.3 %all-to-all-start.4 = ((f32[8,4,128]{2,1,0:T(4,128)}), f32[8,4,128]{2,1,0:T(4,128)S(1)}, u32[]{:S(2)}, u32[]{:S(2)}) async-start(f32[8,4,128]{2,1,0:T(4,128)} %broadcast_in_dim.58), calls=%async_computation.4 | async-start | bytes 32768 | tf_op jit(solution)/shard_map/all_to_all | solution.py:18

commit v5 on v4

--- a/solution.py
+++ b/solution.py
@@ -1,6 +1,10 @@
+import functools
+
 import jax
 import jax.numpy as jnp
 from jax import lax
+from jax.experimental import pallas as pl
+from jax.experimental.pallas import tpu as pltpu
 from jax.sharding import Mesh
 from jax.sharding import PartitionSpec as P
 
@@ -42,6 +46,91 @@
     return weight, jnp.squeeze(high, axis), jnp.sum(weight * total, axis=axis)
 
 
+def bf16_parts(values):
+    high = values.astype(bf16)
+    return high, (values - high.astype(f32)).astype(bf16)
+
+
+def along_lanes(column):
+    n = column.shape[0]
+    at_row = lax.broadcasted_iota(jnp.int32, (n, n), 0)
+    at_lane = lax.broadcasted_iota(jnp.int32, (n, n), 1)
+    return jnp.sum(jnp.where(at_row == at_lane, column, 0.0), axis=0, keepdims=True)
+
+
+def parts_kernel(nc, nx, place, got, near, far, sent, block, logits, wide, columns):
+    ny, width, out = sent.shape
+    count, dim = block.shape
+    pool = logits.shape[2]
+    group, fold = nc * nx, dim // lane
+    cut = width * group
+    for y in range(ny):
+        wide[y * cut : (y + 1) * cut] = got[y, :cut].astype(f32)
+    for i in range(group):
+        columns[i] = wide[pl.ds(i, count, stride=group), :]
+    for i in range(group):
+        c, k = divmod(i, nx)
+        logits[i] = columns[(place[0] + c) % nc * nx + (place[1] + k) % nx].astype(bf16)
+    cut_rows = width * fold
+    for y in range(ny):
+        wide[y * cut_rows : (y + 1) * cut_rows] = got[y, cut:].astype(f32)
+    for i in range(fold):
+        block[:, i * lane : (i + 1) * lane] = wide[pl.ds(i, count, stride=fold), :].astype(bf16)
+
+    rows = block[...]
+    shared = near[...], far[...]
+    student = [
+        logit_scale * lax.dot_general(rows, p, (((1,), (1,)), ((), ())), preferred_element_type=f32)
+        for p in shared
+    ]
+    taught = [
+        jnp.concatenate([logits[c * nx + k].astype(f32) for k in range(nx)], axis=1) for c in range(nc)
+    ]
+    stats = []
+    for at, values in enumerate((student, taught)):
+        top = functools.reduce(jnp.maximum, [jnp.max(v, axis=1, keepdims=True) for v in values])
+        total = jnp.zeros_like(top)
+        part = jnp.zeros((count, dim), f32)
+        for v, p in zip(values, shared):
+            lifted = jnp.exp(v - top)
+            total += jnp.sum(lifted, axis=1, keepdims=True)
+            for piece in bf16_parts(lifted):
+                part += jnp.dot(piece, p, preferred_element_type=f32)
+        for y in range(ny):
+            sent[y, :, at * dim : (at + 1) * dim] = part[y * width : (y + 1) * width]
+        stats += [along_lanes(top), along_lanes(total)]
+    spread = jnp.concatenate(stats + [jnp.zeros((width - 4, count), f32)], axis=0)
+    for y in range(ny):
+        sent[y, :, 2 * dim :] = spread
+
+
+def local_parts(got, near, far, sizes):
+    ny, width, nc, nx, pool, dim = sizes
+    count, group = ny * width, nc * nx
+    place = jnp.stack([lax.axis_index("core"), lax.axis_index("x")]).astype(jnp.int32)
+    vmem = pl.BlockSpec(memory_space=pltpu.VMEM)
+    return pl.pallas_call(
+        functools.partial(parts_kernel, nc, nx),
+        out_shape=(
+            jax.ShapeDtypeStruct((ny, width, 2 * dim + count), f32),
+            jax.ShapeDtypeStruct((count, dim), bf16),
+            jax.ShapeDtypeStruct((group, count, pool), bf16),
+        ),
+        in_specs=[pl.BlockSpec(memory_space=pltpu.SMEM), vmem, vmem, vmem],
+        out_specs=(vmem, vmem, vmem),
+        scratch_shapes=[
+            pltpu.VMEM((count * max(group, dim // lane), lane), f32),
+            pltpu.VMEM((group, count, pool), f32),
+        ],
+        compiler_params=pltpu.CompilerParams(vmem_limit_bytes=24 * 2**20),
+        cost_estimate=pl.CostEstimate(
+            flops=10 * count * group * pool * dim,
+            bytes_accessed=4 * 2**20,
+            transcendentals=2 * count * group * pool,
+        ),
+    )(place, got, near.reshape(nx * pool, dim), far.reshape(nx * pool, dim))
+
+
 def per_device(queries, passages, teacher):
     own, dim = queries.shape
     pool = passages.shape[0]
@@ -52,46 +141,28 @@
     near = [from_next(passages, "x", k) for k in range(1, nx)]
 
     tiles = teacher.reshape(own, ny, nzl, nc, nx, nzh, pool)
-    tiles = rolled(rolled(tiles, "x", 4), "core", 3).transpose(5, 2, 1, 0, 3, 4, 6)
+    tiles = tiles.transpose(5, 2, 1, 0, 3, 4, 6)
     tiles = tiles.reshape(nz, ny * own * group, pool)
     rows = jnp.broadcast_to(queries.reshape(1, own * fold, lane), (nz, own * fold, lane))
     got = exchange(jnp.concatenate([tiles, rows], axis=1), z_axes)
     got, *near = lax.optimization_barrier((got, *near))
-    near = jnp.stack([passages, *near])
-    far = from_next(near, "core", 1)
     cut = ny * own * group
     tiles = got[:, :cut].reshape(nz, ny, own * group, pool).transpose(1, 0, 2, 3)
     tiles = tiles.reshape(ny, nz * own * group, pool)
     rows = jnp.broadcast_to(got[:, cut:].reshape(1, nz * own * fold, lane), (ny, nz * own * fold, lane))
-    got = exchange(jnp.concatenate([tiles, rows], axis=1), "y")
-    cut = nz * own * group
+    sent = jnp.concatenate([tiles, rows], axis=1)
+    got = exchange(sent, "y")
+    *near, _ = lax.optimization_barrier((*near, sent))
+    near = jnp.stack([passages, *near])
+    far = from_next(near, "core", 1)
     count = ny * nz * own
-    logits = got[:, :cut].reshape(count, group * pool)
-    block = got[:, cut:].reshape(count, dim)
-    shared = jnp.concatenate([near, far]).reshape(group * pool, dim)
-
-    def columns(c, k):
-        return logits[:, (c * nx + k) * pool :][:, :pool]
+    sent, block, logits = local_parts(got, near, far, (ny, nz * own, nc, nx, pool, dim))
 
     rows = [
-        jnp.concatenate([block, columns(0, -k % nx), columns(1, -k % nx)], axis=1) for k in range(nx)
+        jnp.concatenate([block] + [logits[c * nx + -k % nx] for c in range(nc)], axis=1)
+        for k in range(nx)
     ]
     rows = [rows[0]] + [from_next(rows[k], "x", k) for k in range(1, nx)]
-
-    student = logit_scale * lax.dot_general(
-        block, shared, (((1,), (1,)), ((), ())), preferred_element_type=f32
-    )
-
-    def local(values):
-        top = jnp.max(values, axis=1, keepdims=True)
-        lifted = jnp.exp(values - top)
-        part = split_dot(lifted, shared, (((1,), (0,)), ((), ())))
-        return part, top[:, 0], jnp.sum(lifted, axis=1)
-
-    part_s, top_s, sum_s = local(student)
-    part_t, top_t, sum_t = local(logits.astype(f32))
-    parts = jnp.concatenate([part_s, part_t], axis=1)
-    stats = jnp.stack([top_s, sum_s, top_t, sum_t])
 
     def pack(parts, stats, n):
         width = parts.shape[0] // n
@@ -115,7 +186,7 @@
 
     y_at = lax.axis_index("y") * (nz * own)
     z_at = y_at + lax.axis_index(z_axes) * own
-    part_s, part_t, stats = unpack(exchange(pack(parts, stats, ny), "y"), y_at)
+    part_s, part_t, stats = unpack(exchange(sent, "y"), y_at)
     sent = pack(jnp.concatenate([part_s, part_t], axis=1), stats, nz)
     got = exchange(sent, z_axes)
     *rows, _ = lax.optimization_barrier((*rows, sent))
@@ -123,9 +194,6 @@
     away = jnp.stack([jnp.concatenate([r[:, :dim], r[:, dim + pool :]], axis=1) for r in rows])
     every_row = jnp.concatenate([kept, from_next(away, "core", 1)]).reshape(group * count, dim + pool)
     all_rows, own_logits = every_row[:, :dim], every_row[:, dim:]
-    part_s, part_t, stats = unpack(got, z_at)
-    mine = lax.dynamic_slice_in_dim(stats, z_at, own, 1)
-    query_grad = logit_scale * (part_s / mine[1][:, None] - part_t / mine[3][:, None])
 
     def lifted(values):
         top = jnp.max(values, axis=0)
@@ -136,9 +204,13 @@
         * lax.dot_general(passages, all_rows, (((1,), (1,)), ((), ())), preferred_element_type=f32)
     )
     wanted, high_t = lifted(own_logits.T.astype(f32))
-    stats, scores, wanted, high_s, high_t = lax.optimization_barrier(
-        (stats, scores, wanted, high_s, high_t)
+    got, scores, wanted, high_s, high_t = lax.optimization_barrier(
+        (got, scores, wanted, high_s, high_t)
     )
+    part_s, part_t, stats = unpack(got, z_at)
+    mine = lax.dynamic_slice_in_dim(stats, z_at, own, 1)
+    query_grad = logit_scale * (part_s / mine[1][:, None] - part_t / mine[3][:, None])
+
     every = exchange(jnp.broadcast_to(stats[None], (group,) + stats.shape), group_axes)
     every = rolled(rolled(every.reshape(nc, nx, 4, count), "x", 1), "core", 0)
     every = every.transpose(2, 0, 1, 3).reshape(4, group * count)

time: 118 us -> 116 us (0.983)
  waiting for transfers between devices: 18.2 us -> 29.5 us
  starting transfers between devices: 75.6 us -> 70.3 us
  other arithmetic: 8.57 us -> 4.37 us
  local copies, waits for them, and re-layouts: 8.47 us -> 4.53 us
  Pallas kernels: 0 us -> 3.79 us
  matrix products: 4.56 us -> 2.2 us
    all_to_all x5, waiting for transfers between devices: 9.15 us -> 18.8 us  [exchange(): return lax.all_to_all(values, axes, 0, 0, tiled=True)]
    pallas_call x0 -> x1, Pallas kernels: none -> 3.79 us  [local_parts(): pl.pallas_call(functools.partial(parts_kernel, nc, nx), out_shape=(jax.Sh...]
    all_to_all x5, starting transfers between devices: 44.6 us -> 41.9 us  [exchange(): return lax.all_to_all(values, axes, 0, 0, tiled=True)]
    ppermute x8, starting transfers between devices: 31 us -> 28.4 us  [from_next(): return lax.ppermute(values, axis, [(i, (i - step) % n) for i in range(n)])]
    ppermute x8, waiting for transfers between devices: 9.1 us -> 10.7 us  [from_next(): return lax.ppermute(values, axis, [(i, (i - step) % n) for i in range(n)])]
    concatenate x1 -> x0, local copies, waits for them, and re-layouts: 1.19 us -> none  [per_device(): shared = jnp.concatenate([near, far]).reshape(group * pool, dim)]
    concatenate x1, local copies, waits for them, and re-layouts: 1.31 us -> 0.13 us  [per_device(): jnp.concatenate([kept, from_next(away, 'core', 1)])]
  transfers between devices with their start and end apart: 13 -> 13, of which waited for: 5 -> 8; matrix products, arithmetic and copies ran while one was open for 6% -> 4% of each run, Pallas kernels for 0% -> 0%
where the time goes in v5:
time: 116 us
  starting transfers between devices  70.3 us (61%)
  waiting for transfers between devices  29.5 us (25%)
  local copies, waits for them, and re-layouts  4.53 us (4%)
  other arithmetic  4.37 us (4%)
  Pallas kernels  3.79 us (3%)
  matrix products  2.2 us (2%)
    all_to_all x5, starting transfers between devices, exchange(): return lax.all_to_all(values, axes, 0, 0, tiled=True)  41.9 us
    ppermute x8, starting transfers between devices, from_next(): return lax.ppermute(values, axis, [(i, (i - step) % n) for i in range(n)])  28.4 us
    all_to_all x5, waiting for transfers between devices, exchange(): return lax.all_to_all(values, axes, 0, 0, tiled=True)  18.8 us
    ppermute x8, waiting for transfers between devices, from_next(): return lax.ppermute(values, axis, [(i, (i - step) % n) for i in range(n)])  10.7 us
    pallas_call x1, Pallas kernels, local_parts(): pl.pallas_call(functools.partial(parts_kernel, nc, nx), out_shape=(jax.Sh...  3.79 us
  transfers between devices with their start and end apart: 13, of which 8 were waited for; matrix products, arithmetic and copies ran while one was open for 4% of the time, Pallas kernels for 0%

profile of v5, /device:TPU:1, one launch (start us, length us, event | category | flops | bytes accessed | tf_op | source)
XLA Modules:
  0.0 115.8 jit_solution(1968385911917259391)
XLA Ops:
  0.6 0.7 broadcast_in_dim.20
  1.4 1.2 reshape.67
  2.7 0.8 copy.52
  3.5 15.7 %all-to-all-start = ((bf16[16,76,128]{2,1,0:T(8,128)(2,1)}), bf16[16,76,128]{2,1,0:T(8,128)(2,1)S(1)}, u32[]{:S(2)}, u32[]{:S(2)}) async-start(bf16[16,76,128]{2,1,0:T(8,128)(2,1)} %copy.52), calls=%async_computation | async-start | bytes 655360 | tf_op jit(solution)/shard_map/all_to_all | solution.py:22
  19.2 4.4 %collective-permute-start = (bf16[128,768]{1,0:T(8,128)(2,1)S(1)}, bf16[128,768]{1,0:T(8,128)(2,1)S(1)}, u32[]{:S(2)}, u32[]{:S(2)}) collective-permute-start(bf16[128,768]{1,0:T(8,128)(2,1)S(1)} %copy-done), channel_id=1, source_target_pairs={{0,6},{2,0},{4,2},{6,4},{1,7},{3,1},{5,3},{7,5},{8,14},{10,8},{12,... | collective-permute-start | bytes 589832 | tf_op jit(solution)/shard_map/ppermute | solution.py:27
  23.6 2.4 %collective-permute-start.1 = (bf16[128,768]{1,0:T(8,128)(2,1)S(1)}, bf16[128,768]{1,0:T(8,128)(2,1)S(1)}, u32[]{:S(2)}, u32[]{:S(2)}) collective-permute-start(bf16[128,768]{1,0:T(8,128)(2,1)S(1)} %copy-done), channel_id=1, source_target_pairs={{0,4},{2,6},{4,0},{6,2},{1,5},{3,7},{5,1},{7,3},{8,12},{10,14},{12... | collective-permute-start | bytes 589832 | tf_op jit(solution)/shard_map/ppermute | solution.py:27
  26.1 2.5 %collective-permute-start.2 = (bf16[128,768]{1,0:T(8,128)(2,1)S(1)}, bf16[128,768]{1,0:T(8,128)(2,1)S(1)}, u32[]{:S(2)}, u32[]{:S(2)}) collective-permute-start(bf16[128,768]{1,0:T(8,128)(2,1)S(1)} %copy-done), channel_id=1, source_target_pairs={{0,2},{2,4},{4,6},{6,0},{1,3},{3,5},{5,7},{7,1},{8,10},{10,12},{12... | collective-permute-start | bytes 589832 | tf_op jit(solution)/shard_map/ppermute | solution.py:27
  28.6 3.6 %collective-permute-done.1 = bf16[128,768]{1,0:T(8,128)(2,1)S(1)} collective-permute-done((bf16[128,768]{1,0:T(8,128)(2,1)S(1)}, bf16[128,768]{1,0:T(8,128)(2,1)S(1)}, u32[]{:S(2)}, u32[]{:S(2)}) %collective-permute-start.1) | collective-permute-done | bytes 196640 | tf_op jit(solution)/shard_map/ppermute | solution.py:27
  32.2 5.1 %collective-permute-done.2 = bf16[128,768]{1,0:T(8,128)(2,1)S(1)} collective-permute-done((bf16[128,768]{1,0:T(8,128)(2,1)S(1)}, bf16[128,768]{1,0:T(8,128)(2,1)S(1)}, u32[]{:S(2)}, u32[]{:S(2)}) %collective-permute-start.2) | collective-permute-done | bytes 196640 | tf_op jit(solution)/shard_map/ppermute | solution.py:27
  37.4 0.8 pad_maximum_fusion.2
  38.2 0.1 pad_maximum_fusion.1
  38.3 5.6 %collective-permute-start.3 = (bf16[4,128,768]{2,1,0:T(8,128)(2,1)S(1)}, bf16[4,128,768]{2,1,0:T(8,128)(2,1)S(1)}, u32[]{:S(2)}, u32[]{:S(2)}) collective-permute-start(bf16[4,128,768]{2,1,0:T(8,128)(2,1)S(1)} %pad_maximum_fusion.1), channel_id=1, source_target_pairs={{0,8},{8,0},{1,9},{9,1},{2,10},{10,2},{3,11},{11,3},{4,12},{12,4},... | collective-permute-start | bytes 2359304 | tf_op jit(solution)/shard_map/ppermute | solution.py:27
  43.9 4.2 %all-to-all-start.1 = ((bf16[4,448,128]{2,1,0:T(8,128)(2,1)}), bf16[4,448,128]{2,1,0:T(8,128)(2,1)S(1)}, u32[]{:S(2)}, u32[]{:S(2)}) async-start(bf16[4,448,128]{2,1,0:T(8,128)(2,1)} %pad_maximum_fusion.2), calls=%async_computation.1 | async-start | bytes 917504 | tf_op jit(solution)/shard_map/all_to_all | solution.py:22
  48.1 0.1 pad_add_fusion.place
  48.2 8.5 %all-to-all-done.1.got = bf16[4,448,128]{2,1,0:T(8,128)(2,1)S(1)} async-done(((bf16[4,448,128]{2,1,0:T(8,128)(2,1)}), bf16[4,448,128]{2,1,0:T(8,128)(2,1)S(1)}, u32[]{:S(2)}, u32[]{:S(2)}) %all-to-all-start.1) | async-done | bytes 458784 | tf_op jit(solution)/shard_map/all_to_all | solution.py:22
  56.7 3.8 %shard_map.50 = (f32[4,32,1664]{2,1,0:T(8,128)}, bf16[128,768]{1,0:T(8,128)(2,1)S(1)}, bf16[8,128,128]{2,1,0:T(8,128)(2,1)S(1)}) custom-call(s32[2]{0:T(128)S(1)} %pad_add_fusion.place, bf16[4,448,128]{2,1,0:T(8,128)(2,1)S(1)} %all-to-all-done.1.got, bf16[512,768]{1,0:T(8,128)(2,1)S(1)} %bitcast.87, bf16[512,768]{1,0:T(8,128)(2,1)S(1)} %bitcast.88), custom_call_target="tpu_custom_call" | custom-call | flops 1006632960 | bytes 4194304 | tf_op jit(solution)/shard_map/pallas_call | solution.py:112
  60.5 3.5 %all-to-all-start.2 = ((f32[4,32,1664]{2,1,0:T(8,128)}), f32[4,32,1664]{2,1,0:T(8,128)S(1)}, u32[]{:S(2)}, u32[]{:S(2)}) async-start(f32[4,32,1664]{2,1,0:T(8,128)} %get-tuple-element.28), calls=%async_computation.2 | async-start | bytes 1703936 | tf_op jit(solution)/shard_map/all_to_all | solution.py:22
  64.1 0.8 fusion.10
  64.9 4.4 %collective-permute-start.4 = (bf16[128,1024]{1,0:T(8,128)(2,1)}, bf16[128,1024]{1,0:T(8,128)(2,1)S(1)}, u32[]{:S(2)}, u32[]{:S(2)}) collective-permute-start(bf16[128,1024]{1,0:T(8,128)(2,1)} %get-tuple-element.67), channel_id=1, source_target_pairs={{0,6},{2,0},{4,2},{6,4},{1,7},{3,1},{5,3},{7,5},{8,14},{10,8},{12,... | collective-permute-start | bytes 786440 | tf_op jit(solution)/shard_map/ppermute | solution.py:27
  69.3 2.4 %collective-permute-start.5 = (bf16[128,1024]{1,0:T(8,128)(2,1)S(1)}, bf16[128,1024]{1,0:T(8,128)(2,1)S(1)}, u32[]{:S(2)}, u32[]{:S(2)}) collective-permute-start(bf16[128,1024]{1,0:T(8,128)(2,1)S(1)} %get-tuple-element.68), channel_id=1, source_target_pairs={{0,4},{2,6},{4,0},{6,2},{1,5},{3,7},{5,1},{7,3},{8,12},{10,14},{12... | collective-permute-start | bytes 786440 | tf_op jit(solution)/shard_map/ppermute | solution.py:27
  71.7 2.5 %collective-permute-start.6 = (bf16[128,1024]{1,0:T(8,128)(2,1)S(1)}, bf16[128,1024]{1,0:T(8,128)(2,1)S(1)}, u32[]{:S(2)}, u32[]{:S(2)}) collective-permute-start(bf16[128,1024]{1,0:T(8,128)(2,1)S(1)} %get-tuple-element.66), channel_id=1, source_target_pairs={{0,2},{2,4},{4,6},{6,0},{1,3},{3,5},{5,7},{7,1},{8,10},{10,12},{12... | collective-permute-start | bytes 786440 | tf_op jit(solution)/shard_map/ppermute | solution.py:27
  74.2 1.7 %all-to-all-done.2 = f32[4,32,1664]{2,1,0:T(8,128)S(1)} async-done(((f32[4,32,1664]{2,1,0:T(8,128)}), f32[4,32,1664]{2,1,0:T(8,128)S(1)}, u32[]{:S(2)}, u32[]{:S(2)}) %all-to-all-start.2) | async-done | bytes 852000 | tf_op jit(solution)/shard_map/all_to_all | solution.py:22
  76.0 0.1 constant_dynamic-slice_fusion.3
  76.1 0.1 fusion.6
  76.2 0.1 reshape.73
  76.4 0.8 pad_maximum_fusion.8
  77.1 9.1 %all-to-all-start.3 = ((f32[16,2,1792]{2,1,0:T(2,128)}), f32[16,2,1792]{2,1,0:T(2,128)S(1)}, u32[]{:S(2)}, u32[]{:S(2)}) async-start(f32[16,2,1792]{2,1,0:T(2,128)} %pad_maximum_fusion.8), calls=%async_computation.3 | async-start | bytes 458752 | tf_op jit(solution)/shard_map/all_to_all | solution.py:22
  86.2 0.1 collective-permute-done.6
  86.6 0.1 pad_maximum_fusion
  86.8 4.2 %collective-permute-start.7 = (bf16[4,128,896]{2,1,0:T(8,128)(2,1)S(1)}, bf16[4,128,896]{2,1,0:T(8,128)(2,1)S(1)}, u32[]{:S(2)}, u32[]{:S(2)}) collective-permute-start(bf16[4,128,896]{2,1,0:T(8,128)(2,1)S(1)} %pad_maximum_fusion), channel_id=1, source_target_pairs={{0,8},{8,0},{1,9},{9,1},{2,10},{10,2},{3,11},{11,3},{4,12},{12,4},... | collective-permute-start | bytes 2752520 | tf_op jit(solution)/shard_map/ppermute | solution.py:27
  91.1 1.9 %collective-permute-done.7 = bf16[4,128,896]{2,1,0:T(8,128)(2,1)S(1)} collective-permute-done((bf16[4,128,896]{2,1,0:T(8,128)(2,1)S(1)}, bf16[4,128,896]{2,1,0:T(8,128)(2,1)S(1)}, u32[]{:S(2)}, u32[]{:S(2)}) %collective-permute-start.7) | collective-permute-done | bytes 917536 | tf_op jit(solution)/shard_map/ppermute | solution.py:27
  93.0 0.1 constant_dynamic-update-slice_fusion
  93.1 0.2 slice_reduce_fusion
  93.3 0.1 copy.65
  93.5 0.1 exponential_bitcast_fusion
  93.6 0.7 fusion.19
  94.2 0.1 exponential_bitcast_fusion.1
  94.3 4.5 %all-to-all-done.3 = f32[16,2,1792]{2,1,0:T(2,128)S(1)} async-done(((f32[16,2,1792]{2,1,0:T(2,128)}), f32[16,2,1792]{2,1,0:T(2,128)S(1)}, u32[]{:S(2)}, u32[]{:S(2)}) %all-to-all-start.3) | async-done | bytes 229408 | tf_op jit(solution)/shard_map/all_to_all | solution.py:22
  99.0 0.1 constant_dynamic-slice_fusion.2
  99.1 0.1 constant_dynamic-slice_fusion
  99.1 0.1 constant_dynamic-slice_fusion.1
  99.2 0.6 broadcast_in_dim.52
  99.8 9.4 %all-to-all-start.4 = ((f32[8,4,128]{2,1,0:T(4,128)}), f32[8,4,128]{2,1,0:T(4,128)S(1)}, u32[]{:S(2)}, u32[]{:S(2)}) async-start(f32[8,4,128]{2,1,0:T(4,128)} %broadcast_in_dim.52), calls=%async_computation.4 | async-start | bytes 32768 | tf_op jit(solution)/shard_map/all_to_all | solution.py:22
  109.2 0.1 multiply_reduce_fusion.1
  109.4 0.7 fusion.15
  110.1 4.1 %all-to-all-done.4 = f32[8,4,128]{2,1,0:T(4,128)S(1)} async-done(((f32[8,4,128]{2,1,0:T(4,128)}), f32[8,4,128]{2,1,0:T(4,128)S(1)}, u32[]{:S(2)}, u32[]{:S(2)}) %all-to-all-start.4) | async-done | bytes 16416 | tf_op jit(solution)/shard_map/all_to_all | solution.py:22
  114.2 0.4 fusion
  114.6 1.1 convolution_add_fusion
  (58 shorter events, 0.9 us)
Async XLA Ops:
  0.6 18.6 %copy-start = (bf16[128,768]{1,0:T(8,128)(2,1)S(1)}, bf16[128,768]{1,0:T(8,128)(2,1)}, u32[]{:S(2)}) copy-start(bf16[128,768]{1,0:T(8,128)(2,1)} %param.4) | copy-start | bytes 589828
  3.5 33.8 %all-to-all-start = ((bf16[16,76,128]{2,1,0:T(8,128)(2,1)}), bf16[16,76,128]{2,1,0:T(8,128)(2,1)S(1)}, u32[]{:S(2)}, u32[]{:S(2)}) async-start(bf16[16,76,128]{2,1,0:T(8,128)(2,1)} %copy.52), calls=%async_computation | async-start | bytes 655360 | tf_op jit(solution)/shard_map/all_to_all | solution.py:22
  19.2 9.4 %collective-permute-start = (bf16[128,768]{1,0:T(8,128)(2,1)S(1)}, bf16[128,768]{1,0:T(8,128)(2,1)S(1)}, u32[]{:S(2)}, u32[]{:S(2)}) collective-permute-start(bf16[128,768]{1,0:T(8,128)(2,1)S(1)} %copy-done), channel_id=1, source_target_pairs={{0,6},{2,0},{4,2},{6,4},{1,7},{3,1},{5,3},{7,5},{8,14},{10,8},{12,... | collective-permute-start | bytes 589832 | tf_op jit(solution)/shard_map/ppermute | solution.py:27
  23.6 8.6 %collective-permute-start.1 = (bf16[128,768]{1,0:T(8,128)(2,1)S(1)}, bf16[128,768]{1,0:T(8,128)(2,1)S(1)}, u32[]{:S(2)}, u32[]{:S(2)}) collective-permute-start(bf16[128,768]{1,0:T(8,128)(2,1)S(1)} %copy-done), channel_id=1, source_target_pairs={{0,4},{2,6},{4,0},{6,2},{1,5},{3,7},{5,1},{7,3},{8,12},{10,14},{12... | collective-permute-start | bytes 589832 | tf_op jit(solution)/shard_map/ppermute | solution.py:27
  26.1 11.2 %collective-permute-start.2 = (bf16[128,768]{1,0:T(8,128)(2,1)S(1)}, bf16[128,768]{1,0:T(8,128)(2,1)S(1)}, u32[]{:S(2)}, u32[]{:S(2)}) collective-permute-start(bf16[128,768]{1,0:T(8,128)(2,1)S(1)} %copy-done), channel_id=1, source_target_pairs={{0,2},{2,4},{4,6},{6,0},{1,3},{3,5},{5,7},{7,1},{8,10},{10,12},{12... | collective-permute-start | bytes 589832 | tf_op jit(solution)/shard_map/ppermute | solution.py:27
  38.3 18.4 %collective-permute-start.3 = (bf16[4,128,768]{2,1,0:T(8,128)(2,1)S(1)}, bf16[4,128,768]{2,1,0:T(8,128)(2,1)S(1)}, u32[]{:S(2)}, u32[]{:S(2)}) collective-permute-start(bf16[4,128,768]{2,1,0:T(8,128)(2,1)S(1)} %pad_maximum_fusion.1), channel_id=1, source_target_pairs={{0,8},{8,0},{1,9},{9,1},{2,10},{10,2},{3,11},{11,3},{4,12},{12,4},... | collective-permute-start | bytes 2359304 | tf_op jit(solution)/shard_map/ppermute | solution.py:27
  43.9 12.8 %all-to-all-start.1 = ((bf16[4,448,128]{2,1,0:T(8,128)(2,1)}), bf16[4,448,128]{2,1,0:T(8,128)(2,1)S(1)}, u32[]{:S(2)}, u32[]{:S(2)}) async-start(bf16[4,448,128]{2,1,0:T(8,128)(2,1)} %pad_maximum_fusion.2), calls=%async_computation.1 | async-start | bytes 917504 | tf_op jit(solution)/shard_map/all_to_all | solution.py:22
  60.5 15.4 %all-to-all-start.2 = ((f32[4,32,1664]{2,1,0:T(8,128)}), f32[4,32,1664]{2,1,0:T(8,128)S(1)}, u32[]{:S(2)}, u32[]{:S(2)}) async-start(f32[4,32,1664]{2,1,0:T(8,128)} %get-tuple-element.28), calls=%async_computation.2 | async-start | bytes 1703936 | tf_op jit(solution)/shard_map/all_to_all | solution.py:22
  64.9 21.3 %collective-permute-start.4 = (bf16[128,1024]{1,0:T(8,128)(2,1)}, bf16[128,1024]{1,0:T(8,128)(2,1)S(1)}, u32[]{:S(2)}, u32[]{:S(2)}) collective-permute-start(bf16[128,1024]{1,0:T(8,128)(2,1)} %get-tuple-element.67), channel_id=1, source_target_pairs={{0,6},{2,0},{4,2},{6,4},{1,7},{3,1},{5,3},{7,5},{8,14},{10,8},{12,... | collective-permute-start | bytes 786440 | tf_op jit(solution)/shard_map/ppermute | solution.py:27
  69.3 17.0 %collective-permute-start.5 = (bf16[128,1024]{1,0:T(8,128)(2,1)S(1)}, bf16[128,1024]{1,0:T(8,128)(2,1)S(1)}, u32[]{:S(2)}, u32[]{:S(2)}) collective-permute-start(bf16[128,1024]{1,0:T(8,128)(2,1)S(1)} %get-tuple-element.68), channel_id=1, source_target_pairs={{0,4},{2,6},{4,0},{6,2},{1,5},{3,7},{5,1},{7,3},{8,12},{10,14},{12... | collective-permute-start | bytes 786440 | tf_op jit(solution)/shard_map/ppermute | solution.py:27
  71.7 14.6 %collective-permute-start.6 = (bf16[128,1024]{1,0:T(8,128)(2,1)S(1)}, bf16[128,1024]{1,0:T(8,128)(2,1)S(1)}, u32[]{:S(2)}, u32[]{:S(2)}) collective-permute-start(bf16[128,1024]{1,0:T(8,128)(2,1)S(1)} %get-tuple-element.66), channel_id=1, source_target_pairs={{0,2},{2,4},{4,6},{6,0},{1,3},{3,5},{5,7},{7,1},{8,10},{10,12},{12... | collective-permute-start | bytes 786440 | tf_op jit(solution)/shard_map/ppermute | solution.py:27
  77.1 21.7 %all-to-all-start.3 = ((f32[16,2,1792]{2,1,0:T(2,128)}), f32[16,2,1792]{2,1,0:T(2,128)S(1)}, u32[]{:S(2)}, u32[]{:S(2)}) async-start(f32[16,2,1792]{2,1,0:T(2,128)} %pad_maximum_fusion.8), calls=%async_computation.3 | async-start | bytes 458752 | tf_op jit(solution)/shard_map/all_to_all | solution.py:22
  86.8 6.2 %collective-permute-start.7 = (bf16[4,128,896]{2,1,0:T(8,128)(2,1)S(1)}, bf16[4,128,896]{2,1,0:T(8,128)(2,1)S(1)}, u32[]{:S(2)}, u32[]{:S(2)}) collective-permute-start(bf16[4,128,896]{2,1,0:T(8,128)(2,1)S(1)} %pad_maximum_fusion), channel_id=1, source_target_pairs={{0,8},{8,0},{1,9},{9,1},{2,10},{10,2},{3,11},{11,3},{4,12},{12,4},... | collective-permute-start | bytes 2752520 | tf_op jit(solution)/shard_map/ppermute | solution.py:27
  91.1 2.5 %copy-start.1 = (bf16[128,768]{1,0:T(8,128)(2,1)S(1)}, bf16[128,768]{1,0:T(8,128)(2,1)}, u32[]{:S(2)}) copy-start(bf16[128,768]{1,0:T(8,128)(2,1)} %param.4) | copy-start | bytes 589828
  99.8 14.3 %all-to-all-start.4 = ((f32[8,4,128]{2,1,0:T(4,128)}), f32[8,4,128]{2,1,0:T(4,128)S(1)}, u32[]{:S(2)}, u32[]{:S(2)}) async-start(f32[8,4,128]{2,1,0:T(4,128)} %broadcast_in_dim.52), calls=%async_computation.4 | async-start | bytes 32768 | tf_op jit(solution)/shard_map/all_to_all | solution.py:22

commit v6 on v5

--- a/solution.py
+++ b/solution.py
@@ -58,77 +58,111 @@
     return jnp.sum(jnp.where(at_row == at_lane, column, 0.0), axis=0, keepdims=True)
 
 
-def parts_kernel(nc, nx, place, got, near, far, sent, block, logits, wide, columns):
-    ny, width, out = sent.shape
+def layout_kernel(nc, nx, place, got, block, high, low, stats, *rest):
+    *rows, wide, columns = rest
+    ny = got.shape[0]
     count, dim = block.shape
-    pool = logits.shape[2]
     group, fold = nc * nx, dim // lane
+    width = count // ny
     cut = width * group
-    for y in range(ny):
-        wide[y * cut : (y + 1) * cut] = got[y, :cut].astype(f32)
-    for i in range(group):
-        columns[i] = wide[pl.ds(i, count, stride=group), :]
-    for i in range(group):
-        c, k = divmod(i, nx)
-        logits[i] = columns[(place[0] + c) % nc * nx + (place[1] + k) % nx].astype(bf16)
     cut_rows = width * fold
     for y in range(ny):
         wide[y * cut_rows : (y + 1) * cut_rows] = got[y, cut:].astype(f32)
     for i in range(fold):
         block[:, i * lane : (i + 1) * lane] = wide[pl.ds(i, count, stride=fold), :].astype(bf16)
-
+    for y in range(ny):
+        wide[y * cut : (y + 1) * cut] = got[y, :cut].astype(f32)
+    for i in range(group):
+        columns[i] = wide[pl.ds(i, count, stride=group), :]
+    taught = []
+    for i in range(group):
+        c, k = divmod(i, nx)
+        taught.append(columns[(place[0] + c) % nc * nx + (place[1] + k) % nx])
+        at = dim + c * lane
+        rows[-k % nx][:, at : at + lane] = taught[i].astype(bf16)
+    for row in rows:
+        row[:, :dim] = block[...]
+    taught = jnp.concatenate(taught, axis=1)
+    top = jnp.max(taught, axis=1, keepdims=True)
+    lifted = jnp.exp(taught - top)
+    high[...], low[...] = bf16_parts(lifted)
+    stats[...] = jnp.concatenate(
+        [along_lanes(top), along_lanes(jnp.sum(lifted, axis=1, keepdims=True))]
+        + [jnp.zeros((stats.shape[0] - 2, count), f32)],
+        axis=0,
+    )
+
+
+def parts_kernel(block, high, low, taught, near, far, sent):
+    ny, width, _ = sent.shape
+    dim = block.shape[1]
+    half = near.shape[0]
     rows = block[...]
     shared = near[...], far[...]
     student = [
         logit_scale * lax.dot_general(rows, p, (((1,), (1,)), ((), ())), preferred_element_type=f32)
         for p in shared
     ]
-    taught = [
-        jnp.concatenate([logits[c * nx + k].astype(f32) for k in range(nx)], axis=1) for c in range(nc)
-    ]
-    stats = []
-    for at, values in enumerate((student, taught)):
-        top = functools.reduce(jnp.maximum, [jnp.max(v, axis=1, keepdims=True) for v in values])
-        total = jnp.zeros_like(top)
-        part = jnp.zeros((count, dim), f32)
-        for v, p in zip(values, shared):
-            lifted = jnp.exp(v - top)
-            total += jnp.sum(lifted, axis=1, keepdims=True)
-            for piece in bf16_parts(lifted):
-                part += jnp.dot(piece, p, preferred_element_type=f32)
-        for y in range(ny):
-            sent[y, :, at * dim : (at + 1) * dim] = part[y * width : (y + 1) * width]
-        stats += [along_lanes(top), along_lanes(total)]
-    spread = jnp.concatenate(stats + [jnp.zeros((width - 4, count), f32)], axis=0)
+    top = jnp.maximum(*[jnp.max(v, axis=1, keepdims=True) for v in student])
+    total = jnp.zeros_like(top)
+    parts = [jnp.zeros(rows.shape, f32) for _ in range(2)]
+    for i, p in enumerate(shared):
+        lifted = jnp.exp(student[i] - top)
+        total += jnp.sum(lifted, axis=1, keepdims=True)
+        for piece in bf16_parts(lifted):
+            parts[0] += jnp.dot(piece, p, preferred_element_type=f32)
+        for piece in (high, low):
+            piece = piece[:, i * half : (i + 1) * half]
+            parts[1] += jnp.dot(piece, p, preferred_element_type=f32)
+    mine = [along_lanes(top), along_lanes(total)]
+    spread = jnp.concatenate(mine + [taught[: width - 2]], axis=0)
     for y in range(ny):
+        for at in range(2):
+            sent[y, :, at * dim : (at + 1) * dim] = parts[at][y * width : (y + 1) * width]
         sent[y, :, 2 * dim :] = spread
 
 
-def local_parts(got, near, far, sizes):
+vmem = pl.BlockSpec(memory_space=pltpu.VMEM)
+
+
+def laid_out(got, sizes):
     ny, width, nc, nx, pool, dim = sizes
     count, group = ny * width, nc * nx
     place = jnp.stack([lax.axis_index("core"), lax.axis_index("x")]).astype(jnp.int32)
-    vmem = pl.BlockSpec(memory_space=pltpu.VMEM)
+    lifted = jax.ShapeDtypeStruct((count, group * pool), bf16)
+    row = jax.ShapeDtypeStruct((count, dim + nc * pool), bf16)
+    block = jax.ShapeDtypeStruct((count, dim), bf16)
+    stats = jax.ShapeDtypeStruct((width, count), f32)
     return pl.pallas_call(
-        functools.partial(parts_kernel, nc, nx),
-        out_shape=(
-            jax.ShapeDtypeStruct((ny, width, 2 * dim + count), f32),
-            jax.ShapeDtypeStruct((count, dim), bf16),
-            jax.ShapeDtypeStruct((group, count, pool), bf16),
-        ),
-        in_specs=[pl.BlockSpec(memory_space=pltpu.SMEM), vmem, vmem, vmem],
-        out_specs=(vmem, vmem, vmem),
+        functools.partial(layout_kernel, nc, nx),
+        out_shape=(block, lifted, lifted, stats) + (row,) * nx,
+        in_specs=[pl.BlockSpec(memory_space=pltpu.SMEM), vmem],
+        out_specs=(vmem,) * (4 + nx),
         scratch_shapes=[
             pltpu.VMEM((count * max(group, dim // lane), lane), f32),
             pltpu.VMEM((group, count, pool), f32),
         ],
-        compiler_params=pltpu.CompilerParams(vmem_limit_bytes=24 * 2**20),
+        compiler_params=pltpu.CompilerParams(vmem_limit_bytes=16 * 2**20),
         cost_estimate=pl.CostEstimate(
-            flops=10 * count * group * pool * dim,
+            flops=30 * 10**9, bytes_accessed=32 * 2**20, transcendentals=0
+        ),
+    )(place, got)
+
+
+def local_parts(block, high, low, stats, near, far, ny):
+    count, dim = block.shape
+    return pl.pallas_call(
+        parts_kernel,
+        out_shape=jax.ShapeDtypeStruct((ny, count // ny, 2 * dim + count), f32),
+        in_specs=[vmem] * 6,
+        out_specs=vmem,
+        compiler_params=pltpu.CompilerParams(vmem_limit_bytes=16 * 2**20),
+        cost_estimate=pl.CostEstimate(
+            flops=10 * count * high.shape[1] * dim,
             bytes_accessed=4 * 2**20,
-            transcendentals=2 * count * group * pool,
+            transcendentals=count * high.shape[1],
         ),
-    )(place, got, near.reshape(nx * pool, dim), far.reshape(nx * pool, dim))
+    )(block, high, low, stats, near.reshape(-1, dim), far.reshape(-1, dim))
 
 
 def per_device(queries, passages, teacher):
@@ -156,13 +190,11 @@
     near = jnp.stack([passages, *near])
     far = from_next(near, "core", 1)
     count = ny * nz * own
-    sent, block, logits = local_parts(got, near, far, (ny, nz * own, nc, nx, pool, dim))
-
-    rows = [
-        jnp.concatenate([block] + [logits[c * nx + -k % nx] for c in range(nc)], axis=1)
-        for k in range(nx)
-    ]
-    rows = [rows[0]] + [from_next(rows[k], "x", k) for k in range(1, nx)]
+    block, high, low, stats, *rows = laid_out(got, (ny, nz * own, nc, nx, pool, dim))
+    parts = local_parts(block, high, low, stats, near, far, ny)
+
+    for k in range(1, nx - 1):
+        rows[k] = from_next(rows[k], "x", k)
 
     def pack(parts, stats, n):
         width = parts.shape[0] // n
@@ -186,10 +218,11 @@
 
     y_at = lax.axis_index("y") * (nz * own)
     z_at = y_at + lax.axis_index(z_axes) * own
-    part_s, part_t, stats = unpack(exchange(sent, "y"), y_at)
+    part_s, part_t, stats = unpack(exchange(parts, "y"), y_at)
     sent = pack(jnp.concatenate([part_s, part_t], axis=1), stats, nz)
     got = exchange(sent, z_axes)
     *rows, _ = lax.optimization_barrier((*rows, sent))
+    rows[-1] = from_next(rows[-1], "x", nx - 1)
     kept = jnp.stack([r[:, : dim + pool] for r in rows])
     away = jnp.stack([jnp.concatenate([r[:, :dim], r[:, dim + pool :]], axis=1) for r in rows])
     every_row = jnp.concatenate([kept, from_next(away, "core", 1)]).reshape(group * count, dim + pool)

time: 116 us -> 110 us (0.948)
  waiting for transfers between devices: 29.5 us -> 23.5 us
    all_to_all x5, waiting for transfers between devices: 18.8 us -> 6.68 us  [exchange(): return lax.all_to_all(values, axes, 0, 0, tiled=True)]
    ppermute x8, waiting for transfers between devices: 10.7 us -> 16.8 us  [from_next(): return lax.ppermute(values, axis, [(i, (i - step) % n) for i in range(n)])]
    ppermute x8, starting transfers between devices: 28.4 us -> 31.8 us  [from_next(): return lax.ppermute(values, axis, [(i, (i - step) % n) for i in range(n)])]
    all_to_all x5, starting transfers between devices: 41.9 us -> 38.8 us  [exchange(): return lax.all_to_all(values, axes, 0, 0, tiled=True)]
    pallas_call x1 -> x2, Pallas kernels: 3.79 us -> 3.74 us  [the longest x1 2.63 us: local_parts(): pl.pallas_call(parts_kernel, out_shape=jax.ShapeDtypeStruct((ny, count //...]
  transfers between devices with their start and end apart: 13 -> 13, of which waited for: 8 -> 8; matrix products, arithmetic and copies ran while one was open for 4% -> 4% of each run, Pallas kernels for 0% -> 1%
where the time goes in v6:
time: 110 us; the launch traced here: 109 us
  starting transfers between devices  70.6 us (64%)
  waiting for transfers between devices  23.5 us (21%)
  local copies, waits for them, and re-layouts  4.5 us (4%)
  Pallas kernels  3.74 us (3%)
  other arithmetic  3.55 us (3%)
  matrix products  2.21 us (2%)
  between operations  1.13 us (1%)
    all_to_all x5, starting transfers between devices, exchange(): return lax.all_to_all(values, axes, 0, 0, tiled=True)  38.8 us
    ppermute x8, starting transfers between devices, from_next(): return lax.ppermute(values, axis, [(i, (i - step) % n) for i in range(n)])  31.8 us
    ppermute x8, waiting for transfers between devices, from_next(): return lax.ppermute(values, axis, [(i, (i - step) % n) for i in range(n)])  16.8 us
    all_to_all x5, waiting for transfers between devices, exchange(): return lax.all_to_all(values, axes, 0, 0, tiled=True)  6.68 us
    pallas_call x1, Pallas kernels, local_parts(): pl.pallas_call(parts_kernel, out_shape=jax.ShapeDtypeStruct((ny, count //...  2.63 us
  transfers between devices with their start and end apart: 13, of which 8 were waited for; matrix products, arithmetic and copies ran while one was open for 4% of the time, Pallas kernels for 1%

profile of v6, /device:TPU:1, one launch (start us, length us, event | category | flops | bytes accessed | tf_op | source)
XLA Modules:
  0.0 109.3 jit_solution(5493854336643819850)
XLA Ops:
  0.6 0.7 broadcast_in_dim.20
  1.4 1.2 %reshape.67 = bf16[2,4,8,2,4,2,128]{6,5,4,3,2,1,0:T(2,128)(2,1)S(1)} reshape(bf16[2,65536]{1,0:T(2,128)(2,1)} %param.5) | data formatting | bytes 524288 | tf_op jit(solution)/shard_map/reshape | solution.py:177
  2.7 0.8 copy.52
  3.5 15.7 %all-to-all-start = ((bf16[16,76,128]{2,1,0:T(8,128)(2,1)}), bf16[16,76,128]{2,1,0:T(8,128)(2,1)S(1)}, u32[]{:S(2)}, u32[]{:S(2)}) async-start(bf16[16,76,128]{2,1,0:T(8,128)(2,1)} %copy.52), calls=%async_computation | async-start | bytes 655360 | tf_op jit(solution)/shard_map/all_to_all | solution.py:22
  19.2 4.4 %collective-permute-start = (bf16[128,768]{1,0:T(8,128)(2,1)S(1)}, bf16[128,768]{1,0:T(8,128)(2,1)S(1)}, u32[]{:S(2)}, u32[]{:S(2)}) collective-permute-start(bf16[128,768]{1,0:T(8,128)(2,1)S(1)} %copy-done), channel_id=1, source_target_pairs={{0,6},{2,0},{4,2},{6,4},{1,7},{3,1},{5,3},{7,5},{8,14},{10,8},{12,... | collective-permute-start | bytes 589832 | tf_op jit(solution)/shard_map/ppermute | solution.py:27
  23.6 2.4 %collective-permute-start.1 = (bf16[128,768]{1,0:T(8,128)(2,1)S(1)}, bf16[128,768]{1,0:T(8,128)(2,1)S(1)}, u32[]{:S(2)}, u32[]{:S(2)}) collective-permute-start(bf16[128,768]{1,0:T(8,128)(2,1)S(1)} %copy-done), channel_id=1, source_target_pairs={{0,4},{2,6},{4,0},{6,2},{1,5},{3,7},{5,1},{7,3},{8,12},{10,14},{12... | collective-permute-start | bytes 589832 | tf_op jit(solution)/shard_map/ppermute | solution.py:27
  26.1 2.5 %collective-permute-start.2 = (bf16[128,768]{1,0:T(8,128)(2,1)S(1)}, bf16[128,768]{1,0:T(8,128)(2,1)S(1)}, u32[]{:S(2)}, u32[]{:S(2)}) collective-permute-start(bf16[128,768]{1,0:T(8,128)(2,1)S(1)} %copy-done), channel_id=1, source_target_pairs={{0,2},{2,4},{4,6},{6,0},{1,3},{3,5},{5,7},{7,1},{8,10},{10,12},{12... | collective-permute-start | bytes 589832 | tf_op jit(solution)/shard_map/ppermute | solution.py:27
  28.6 3.6 %collective-permute-done.1 = bf16[128,768]{1,0:T(8,128)(2,1)S(1)} collective-permute-done((bf16[128,768]{1,0:T(8,128)(2,1)S(1)}, bf16[128,768]{1,0:T(8,128)(2,1)S(1)}, u32[]{:S(2)}, u32[]{:S(2)}) %collective-permute-start.1) | collective-permute-done | bytes 196640 | tf_op jit(solution)/shard_map/ppermute | solution.py:27
  32.2 5.1 %collective-permute-done.2 = bf16[128,768]{1,0:T(8,128)(2,1)S(1)} collective-permute-done((bf16[128,768]{1,0:T(8,128)(2,1)S(1)}, bf16[128,768]{1,0:T(8,128)(2,1)S(1)}, u32[]{:S(2)}, u32[]{:S(2)}) %collective-permute-start.2) | collective-permute-done | bytes 196640 | tf_op jit(solution)/shard_map/ppermute | solution.py:27
  37.4 0.8 pad_maximum_fusion.2
  38.2 4.2 %all-to-all-start.1 = ((bf16[4,448,128]{2,1,0:T(8,128)(2,1)}), bf16[4,448,128]{2,1,0:T(8,128)(2,1)S(1)}, u32[]{:S(2)}, u32[]{:S(2)}) async-start(bf16[4,448,128]{2,1,0:T(8,128)(2,1)} %pad_maximum_fusion.2), calls=%async_computation.1 | async-start | bytes 917504 | tf_op jit(solution)/shard_map/all_to_all | solution.py:22
  42.4 0.1 pad_add_fusion.place
  42.5 0.1 pad_maximum_fusion.1
  42.6 5.9 %collective-permute-start.3 = (bf16[4,128,768]{2,1,0:T(8,128)(2,1)S(1)}, bf16[4,128,768]{2,1,0:T(8,128)(2,1)S(1)}, u32[]{:S(2)}, u32[]{:S(2)}) collective-permute-start(bf16[4,128,768]{2,1,0:T(8,128)(2,1)S(1)} %pad_maximum_fusion.1), channel_id=1, source_target_pairs={{0,8},{8,0},{1,9},{9,1},{2,10},{10,2},{3,11},{11,3},{4,12},{12,4},... | collective-permute-start | bytes 2359304 | tf_op jit(solution)/shard_map/ppermute | solution.py:27
  48.4 0.5 all-to-all-done.1.got
  49.0 1.1 %shard_map.50 = (bf16[128,768]{1,0:T(8,128)(2,1)S(1)}, bf16[128,1024]{1,0:T(8,128)(2,1)S(1)}, bf16[128,1024]{1,0:T(8,128)(2,1)S(1)}, f32[32,128]{1,0:T(8,128)S(1...) custom-call(s32[2]{0:T(128)S(1)} %pad_add_fusion.place, ...), custom_call_target="tpu_custom_call" | custom-call | flops 30000001024 | bytes 33554432 | tf_op jit(solution)/shard_map/pallas_call | solution.py:136
  50.1 0.2 collective-permute-done.3
  50.3 2.6 %shard_map.51 = f32[4,32,1664]{2,1,0:T(8,128)} custom-call(bf16[128,768]{1,0:T(8,128)(2,1)S(1)} %get-tuple-element.27.block, bf16[128,1024]{1,0:T(8,128)(2,1)S(1)} %get-tuple-element.28.high, bf16[128,1024]{1,0:T(8,128)(2,1)S(1)} %get-tuple-element.29.low, f32[32,128]{1,0:T(8,128)S(1)} %get-tuple-element.30.taught, bf16[512,768]{1,0:T(8,128)(2,1)S(1)} %bitcast.73, ...), custom_call_target="tpu_custom_call" | custom-call | flops 1006632960 | bytes 4194304 | tf_op jit(solution)/shard_map/pallas_call | solution.py:154
  53.0 4.5 %all-to-all-start.2 = ((f32[4,32,1664]{2,1,0:T(8,128)}), f32[4,32,1664]{2,1,0:T(8,128)S(1)}, u32[]{:S(2)}, u32[]{:S(2)}) async-start(f32[4,32,1664]{2,1,0:T(8,128)} %shard_map.51), calls=%async_computation.2 | async-start | bytes 1703936 | tf_op jit(solution)/shard_map/all_to_all | solution.py:22
  57.5 4.4 %collective-permute-start.4 = (bf16[128,1024]{1,0:T(8,128)(2,1)S(1)}, bf16[128,1024]{1,0:T(8,128)(2,1)S(1)}, u32[]{:S(2)}, u32[]{:S(2)}) collective-permute-start(bf16[128,1024]{1,0:T(8,128)(2,1)S(1)} %get-tuple-element.38), channel_id=1, source_target_pairs={{0,6},{2,0},{4,2},{6,4},{1,7},{3,1},{5,3},{7,5},{8,14},{10,8},{12,... | collective-permute-start | bytes 786440 | tf_op jit(solution)/shard_map/ppermute | solution.py:27
  61.9 2.4 %collective-permute-start.5 = (bf16[128,1024]{1,0:T(8,128)(2,1)S(1)}, bf16[128,1024]{1,0:T(8,128)(2,1)S(1)}, u32[]{:S(2)}, u32[]{:S(2)}) collective-permute-start(bf16[128,1024]{1,0:T(8,128)(2,1)S(1)} %get-tuple-element.39), channel_id=1, source_target_pairs={{0,4},{2,6},{4,0},{6,2},{1,5},{3,7},{5,1},{7,3},{8,12},{10,14},{12... | collective-permute-start | bytes 786440 | tf_op jit(solution)/shard_map/ppermute | solution.py:27
  64.3 2.1 %all-to-all-done.2 = f32[4,32,1664]{2,1,0:T(8,128)S(1)} async-done(((f32[4,32,1664]{2,1,0:T(8,128)}), f32[4,32,1664]{2,1,0:T(8,128)S(1)}, u32[]{:S(2)}, u32[]{:S(2)}) %all-to-all-start.2) | async-done | bytes 852000 | tf_op jit(solution)/shard_map/all_to_all | solution.py:22
  66.5 0.1 constant_dynamic-slice_fusion.3
  66.5 0.1 fusion.6
  66.7 0.1 reshape.73
  66.9 0.8 pad_maximum_fusion.4
  67.6 10.7 %all-to-all-start.3 = ((f32[16,2,1792]{2,1,0:T(2,128)}), f32[16,2,1792]{2,1,0:T(2,128)S(1)}, u32[]{:S(2)}, u32[]{:S(2)}) async-start(f32[16,2,1792]{2,1,0:T(2,128)} %pad_maximum_fusion.4), calls=%async_computation.3 | async-start | bytes 458752 | tf_op jit(solution)/shard_map/all_to_all | solution.py:22
  78.5 2.2 %collective-permute-start.6 = (bf16[128,1024]{1,0:T(8,128)(2,1)S(1)}, bf16[128,1024]{1,0:T(8,128)(2,1)S(1)}, u32[]{:S(2)}, u32[]{:S(2)}) collective-permute-start(bf16[128,1024]{1,0:T(8,128)(2,1)S(1)} %get-tuple-element.44), channel_id=1, source_target_pairs={{0,2},{2,4},{4,6},{6,0},{1,3},{3,5},{5,7},{7,1},{8,10},{10,12},{12... | collective-permute-start | bytes 786440 | tf_op jit(solution)/shard_map/ppermute | solution.py:27
  80.8 6.0 %collective-permute-done.6 = bf16[128,1024]{1,0:T(8,128)(2,1)S(1)} collective-permute-done((bf16[128,1024]{1,0:T(8,128)(2,1)S(1)}, bf16[128,1024]{1,0:T(8,128)(2,1)S(1)}, u32[]{:S(2)}, u32[]{:S(2)}) %collective-permute-start.6) | collective-permute-done | bytes 262176 | tf_op jit(solution)/shard_map/ppermute | solution.py:27
  86.9 0.1 pad_maximum_fusion
  87.0 7.6 %collective-permute-start.7 = (bf16[4,128,896]{2,1,0:T(8,128)(2,1)S(1)}, bf16[4,128,896]{2,1,0:T(8,128)(2,1)S(1)}, u32[]{:S(2)}, u32[]{:S(2)}) collective-permute-start(bf16[4,128,896]{2,1,0:T(8,128)(2,1)S(1)} %pad_maximum_fusion), channel_id=1, source_target_pairs={{0,8},{8,0},{1,9},{9,1},{2,10},{10,2},{3,11},{11,3},{4,12},{12,4},... | collective-permute-start | bytes 2752520 | tf_op jit(solution)/shard_map/ppermute | solution.py:27
  94.8 2.0 %collective-permute-done.7 = bf16[4,128,896]{2,1,0:T(8,128)(2,1)S(1)} collective-permute-done((bf16[4,128,896]{2,1,0:T(8,128)(2,1)S(1)}, bf16[4,128,896]{2,1,0:T(8,128)(2,1)S(1)}, u32[]{:S(2)}, u32[]{:S(2)}) %collective-permute-start.7) | collective-permute-done | bytes 917536 | tf_op jit(solution)/shard_map/ppermute | solution.py:27
  96.7 0.1 constant_dynamic-update-slice_fusion
  96.9 0.2 slice_reduce_fusion
  97.0 0.1 copy.65
  97.2 0.1 exponential_bitcast_fusion
  97.3 0.7 fusion.16
  97.9 0.1 exponential_bitcast_fusion.1
  98.2 0.1 constant_dynamic-slice_fusion.2
  98.3 0.1 constant_dynamic-slice_fusion
  98.4 0.1 constant_dynamic-slice_fusion.1
  98.4 0.6 broadcast_in_dim.52
  99.1 3.6 %all-to-all-start.4 = ((f32[8,4,128]{2,1,0:T(4,128)}), f32[8,4,128]{2,1,0:T(4,128)S(1)}, u32[]{:S(2)}, u32[]{:S(2)}) async-start(f32[8,4,128]{2,1,0:T(4,128)} %broadcast_in_dim.52), calls=%async_computation.4 | async-start | bytes 32768 | tf_op jit(solution)/shard_map/all_to_all | solution.py:22
  102.7 0.1 multiply_reduce_fusion.1
  102.9 0.7 fusion.12
  103.5 4.1 %all-to-all-done.4 = f32[8,4,128]{2,1,0:T(4,128)S(1)} async-done(((f32[8,4,128]{2,1,0:T(4,128)}), f32[8,4,128]{2,1,0:T(4,128)S(1)}, u32[]{:S(2)}, u32[]{:S(2)}) %all-to-all-start.4) | async-done | bytes 16416 | tf_op jit(solution)/shard_map/all_to_all | solution.py:22
  107.7 0.4 fusion
  108.1 1.1 %convolution_add_fusion = f32[128,768]{1,0:T(8,128)} fusion(f32[128,768]{1,0:T(8,128)S(1)} %fusion, bf16[1024,896]{1,0:T(8,128)(2,1)S(1)} %bitcast.78, f32[128,1024]{1,0:T(8,128)S(1)} %exponential_bitcast_fusion, f32[128,1024]{1,0:T(8,128)S(1)} %exponential_bitcast_fusion.1, f32[1024]{0:T(1024)S(1)} %multiply_divide_fusion, f32[1024]{0:T(1024)S(1)} %multiply_divide_fusion.1), kind=kOutput, calls=%fused_computation.1 | convolution fusion | flops 202080256 | bytes 3416064 | tf_op jit(solution)/shard_map/dot_general | solution.py:38
  (55 shorter events, 0.9 us)
Async XLA Ops:
  0.6 18.6 %copy-start = (bf16[128,768]{1,0:T(8,128)(2,1)S(1)}, bf16[128,768]{1,0:T(8,128)(2,1)}, u32[]{:S(2)}) copy-start(bf16[128,768]{1,0:T(8,128)(2,1)} %param.4) | copy-start | bytes 589828
  3.5 33.8 %all-to-all-start = ((bf16[16,76,128]{2,1,0:T(8,128)(2,1)}), bf16[16,76,128]{2,1,0:T(8,128)(2,1)S(1)}, u32[]{:S(2)}, u32[]{:S(2)}) async-start(bf16[16,76,128]{2,1,0:T(8,128)(2,1)} %copy.52), calls=%async_computation | async-start | bytes 655360 | tf_op jit(solution)/shard_map/all_to_all | solution.py:22
  19.2 9.4 %collective-permute-start = (bf16[128,768]{1,0:T(8,128)(2,1)S(1)}, bf16[128,768]{1,0:T(8,128)(2,1)S(1)}, u32[]{:S(2)}, u32[]{:S(2)}) collective-permute-start(bf16[128,768]{1,0:T(8,128)(2,1)S(1)} %copy-done), channel_id=1, source_target_pairs={{0,6},{2,0},{4,2},{6,4},{1,7},{3,1},{5,3},{7,5},{8,14},{10,8},{12,... | collective-permute-start | bytes 589832 | tf_op jit(solution)/shard_map/ppermute | solution.py:27
  23.6 8.6 %collective-permute-start.1 = (bf16[128,768]{1,0:T(8,128)(2,1)S(1)}, bf16[128,768]{1,0:T(8,128)(2,1)S(1)}, u32[]{:S(2)}, u32[]{:S(2)}) collective-permute-start(bf16[128,768]{1,0:T(8,128)(2,1)S(1)} %copy-done), channel_id=1, source_target_pairs={{0,4},{2,6},{4,0},{6,2},{1,5},{3,7},{5,1},{7,3},{8,12},{10,14},{12... | collective-permute-start | bytes 589832 | tf_op jit(solution)/shard_map/ppermute | solution.py:27
  26.1 11.2 %collective-permute-start.2 = (bf16[128,768]{1,0:T(8,128)(2,1)S(1)}, bf16[128,768]{1,0:T(8,128)(2,1)S(1)}, u32[]{:S(2)}, u32[]{:S(2)}) collective-permute-start(bf16[128,768]{1,0:T(8,128)(2,1)S(1)} %copy-done), channel_id=1, source_target_pairs={{0,2},{2,4},{4,6},{6,0},{1,3},{3,5},{5,7},{7,1},{8,10},{10,12},{12... | collective-permute-start | bytes 589832 | tf_op jit(solution)/shard_map/ppermute | solution.py:27
  38.2 10.8 %all-to-all-start.1 = ((bf16[4,448,128]{2,1,0:T(8,128)(2,1)}), bf16[4,448,128]{2,1,0:T(8,128)(2,1)S(1)}, u32[]{:S(2)}, u32[]{:S(2)}) async-start(bf16[4,448,128]{2,1,0:T(8,128)(2,1)} %pad_maximum_fusion.2), calls=%async_computation.1 | async-start | bytes 917504 | tf_op jit(solution)/shard_map/all_to_all | solution.py:22
  42.6 7.8 %collective-permute-start.3 = (bf16[4,128,768]{2,1,0:T(8,128)(2,1)S(1)}, bf16[4,128,768]{2,1,0:T(8,128)(2,1)S(1)}, u32[]{:S(2)}, u32[]{:S(2)}) collective-permute-start(bf16[4,128,768]{2,1,0:T(8,128)(2,1)S(1)} %pad_maximum_fusion.1), channel_id=1, source_target_pairs={{0,8},{8,0},{1,9},{9,1},{2,10},{10,2},{3,11},{11,3},{4,12},{12,4},... | collective-permute-start | bytes 2359304 | tf_op jit(solution)/shard_map/ppermute | solution.py:27
  53.0 13.4 %all-to-all-start.2 = ((f32[4,32,1664]{2,1,0:T(8,128)}), f32[4,32,1664]{2,1,0:T(8,128)S(1)}, u32[]{:S(2)}, u32[]{:S(2)}) async-start(f32[4,32,1664]{2,1,0:T(8,128)} %shard_map.51), calls=%async_computation.2 | async-start | bytes 1703936 | tf_op jit(solution)/shard_map/all_to_all | solution.py:22
  57.5 20.9 %collective-permute-start.4 = (bf16[128,1024]{1,0:T(8,128)(2,1)S(1)}, bf16[128,1024]{1,0:T(8,128)(2,1)S(1)}, u32[]{:S(2)}, u32[]{:S(2)}) collective-permute-start(bf16[128,1024]{1,0:T(8,128)(2,1)S(1)} %get-tuple-element.38), channel_id=1, source_target_pairs={{0,6},{2,0},{4,2},{6,4},{1,7},{3,1},{5,3},{7,5},{8,14},{10,8},{12,... | collective-permute-start | bytes 786440 | tf_op jit(solution)/shard_map/ppermute | solution.py:27
  61.9 16.6 %collective-permute-start.5 = (bf16[128,1024]{1,0:T(8,128)(2,1)S(1)}, bf16[128,1024]{1,0:T(8,128)(2,1)S(1)}, u32[]{:S(2)}, u32[]{:S(2)}) collective-permute-start(bf16[128,1024]{1,0:T(8,128)(2,1)S(1)} %get-tuple-element.39), channel_id=1, source_target_pairs={{0,4},{2,6},{4,0},{6,2},{1,5},{3,7},{5,1},{7,3},{8,12},{10,14},{12... | collective-permute-start | bytes 786440 | tf_op jit(solution)/shard_map/ppermute | solution.py:27
  67.6 30.4 %all-to-all-start.3 = ((f32[16,2,1792]{2,1,0:T(2,128)}), f32[16,2,1792]{2,1,0:T(2,128)S(1)}, u32[]{:S(2)}, u32[]{:S(2)}) async-start(f32[16,2,1792]{2,1,0:T(2,128)} %pad_maximum_fusion.4), calls=%async_computation.3 | async-start | bytes 458752 | tf_op jit(solution)/shard_map/all_to_all | solution.py:22
  78.5 8.3 %collective-permute-start.6 = (bf16[128,1024]{1,0:T(8,128)(2,1)S(1)}, bf16[128,1024]{1,0:T(8,128)(2,1)S(1)}, u32[]{:S(2)}, u32[]{:S(2)}) collective-permute-start(bf16[128,1024]{1,0:T(8,128)(2,1)S(1)} %get-tuple-element.44), channel_id=1, source_target_pairs={{0,2},{2,4},{4,6},{6,0},{1,3},{3,5},{5,7},{7,1},{8,10},{10,12},{12... | collective-permute-start | bytes 786440 | tf_op jit(solution)/shard_map/ppermute | solution.py:27
  87.0 9.7 %collective-permute-start.7 = (bf16[4,128,896]{2,1,0:T(8,128)(2,1)S(1)}, bf16[4,128,896]{2,1,0:T(8,128)(2,1)S(1)}, u32[]{:S(2)}, u32[]{:S(2)}) collective-permute-start(bf16[4,128,896]{2,1,0:T(8,128)(2,1)S(1)} %pad_maximum_fusion), channel_id=1, source_target_pairs={{0,8},{8,0},{1,9},{9,1},{2,10},{10,2},{3,11},{11,3},{4,12},{12,4},... | collective-permute-start | bytes 2752520 | tf_op jit(solution)/shard_map/ppermute | solution.py:27
  99.1 8.5 %all-to-all-start.4 = ((f32[8,4,128]{2,1,0:T(4,128)}), f32[8,4,128]{2,1,0:T(4,128)S(1)}, u32[]{:S(2)}, u32[]{:S(2)}) async-start(f32[8,4,128]{2,1,0:T(4,128)} %broadcast_in_dim.52), calls=%async_computation.4 | async-start | bytes 32768 | tf_op jit(solution)/shard_map/all_to_all | solution.py:22

commit v7 on v6

--- a/solution.py
+++ b/solution.py
@@ -58,28 +58,30 @@
     return jnp.sum(jnp.where(at_row == at_lane, column, 0.0), axis=0, keepdims=True)
 
 
-def layout_kernel(nc, nx, place, got, block, high, low, stats, *rest):
-    *rows, wide, columns = rest
-    ny = got.shape[0]
+def first_kernel(sizes, queries, teacher, sent):
+    ny, nzl, group, nzh, pool = sizes
+    for zh in range(nzh):
+        for zl in range(nzl):
+            to = zh * nzl + zl
+            for y in range(ny):
+                for i in range(group):
+                    at = (((y * nzl + zl) * group + i) * nzh + zh) * pool
+                    into = (y * group + i) * pool
+                    sent[to, :, into : into + pool] = teacher[:, at : at + pool]
+            sent[to, :, ny * group * pool :] = queries[...]
+
+
+def layout_kernel(nc, nx, place, got, block, high, low, stats, *rows):
     count, dim = block.shape
-    group, fold = nc * nx, dim // lane
-    width = count // ny
-    cut = width * group
-    cut_rows = width * fold
-    for y in range(ny):
-        wide[y * cut_rows : (y + 1) * cut_rows] = got[y, cut:].astype(f32)
-    for i in range(fold):
-        block[:, i * lane : (i + 1) * lane] = wide[pl.ds(i, count, stride=fold), :].astype(bf16)
-    for y in range(ny):
-        wide[y * cut : (y + 1) * cut] = got[y, :cut].astype(f32)
-    for i in range(group):
-        columns[i] = wide[pl.ds(i, count, stride=group), :]
+    group = nc * nx
+    block[...] = got[:, group * lane :]
     taught = []
     for i in range(group):
         c, k = divmod(i, nx)
-        taught.append(columns[(place[0] + c) % nc * nx + (place[1] + k) % nx])
-        at = dim + c * lane
-        rows[-k % nx][:, at : at + lane] = taught[i].astype(bf16)
+        at = (place[0] + c) % nc * nx + (place[1] + k) % nx
+        column = got[:, pl.ds(pl.multiple_of(at * lane, lane), lane)]
+        rows[-k % nx][:, dim + c * lane : dim + (c + 1) * lane] = column
+        taught.append(column.astype(f32))
     for row in rows:
         row[:, :dim] = block[...]
     taught = jnp.concatenate(taught, axis=1)
@@ -95,7 +97,7 @@
 
 def parts_kernel(block, high, low, taught, near, far, sent):
     ny, width, _ = sent.shape
-    dim = block.shape[1]
+    count, dim = block.shape
     half = near.shape[0]
     rows = block[...]
     shared = near[...], far[...]
@@ -105,15 +107,15 @@
     ]
     top = jnp.maximum(*[jnp.max(v, axis=1, keepdims=True) for v in student])
     total = jnp.zeros_like(top)
-    parts = [jnp.zeros(rows.shape, f32) for _ in range(2)]
+    stacked = jnp.zeros((4 * count, dim), f32)
     for i, p in enumerate(shared):
         lifted = jnp.exp(student[i] - top)
         total += jnp.sum(lifted, axis=1, keepdims=True)
-        for piece in bf16_parts(lifted):
-            parts[0] += jnp.dot(piece, p, preferred_element_type=f32)
-        for piece in (high, low):
-            piece = piece[:, i * half : (i + 1) * half]
-            parts[1] += jnp.dot(piece, p, preferred_element_type=f32)
+        pieces = bf16_parts(lifted) + tuple(v[:, i * half : (i + 1) * half] for v in (high, low))
+        stacked += jnp.dot(jnp.concatenate(pieces, axis=0), p, preferred_element_type=f32)
+    parts = [
+        stacked[at * count : (at + 1) * count] + stacked[(at + 1) * count : (at + 2) * count] for at in (0, 2)
+    ]
     mine = [along_lanes(top), along_lanes(total)]
     spread = jnp.concatenate(mine + [taught[: width - 2]], axis=0)
     for y in range(ny):
@@ -123,6 +125,19 @@
 
 
 vmem = pl.BlockSpec(memory_space=pltpu.VMEM)
+
+
+def first_buffer(queries, teacher, sizes):
+    ny, nzl, group, nzh, pool = sizes
+    own, dim = queries.shape
+    return pl.pallas_call(
+        functools.partial(first_kernel, sizes),
+        out_shape=jax.ShapeDtypeStruct((nzh * nzl, own, ny * group * pool + dim), bf16),
+        in_specs=[vmem] * 2,
+        out_specs=vmem,
+        compiler_params=pltpu.CompilerParams(vmem_limit_bytes=16 * 2**20),
+        cost_estimate=pl.CostEstimate(flops=0, bytes_accessed=2**20, transcendentals=0),
+    )(queries, teacher)
 
 
 def laid_out(got, sizes):
@@ -138,10 +153,6 @@
         out_shape=(block, lifted, lifted, stats) + (row,) * nx,
         in_specs=[pl.BlockSpec(memory_space=pltpu.SMEM), vmem],
         out_specs=(vmem,) * (4 + nx),
-        scratch_shapes=[
-            pltpu.VMEM((count * max(group, dim // lane), lane), f32),
-            pltpu.VMEM((group, count, pool), f32),
-        ],
         compiler_params=pltpu.CompilerParams(vmem_limit_bytes=16 * 2**20),
         cost_estimate=pl.CostEstimate(
             flops=30 * 10**9, bytes_accessed=32 * 2**20, transcendentals=0
@@ -170,27 +181,20 @@
     pool = passages.shape[0]
     ny, nzl, nc, nx, nzh = (lax.axis_size(a) for a in names)
     nz, group = nzh * nzl, nc * nx
-    fold = dim // lane
 
     near = [from_next(passages, "x", k) for k in range(1, nx)]
 
-    tiles = teacher.reshape(own, ny, nzl, nc, nx, nzh, pool)
-    tiles = tiles.transpose(5, 2, 1, 0, 3, 4, 6)
-    tiles = tiles.reshape(nz, ny * own * group, pool)
-    rows = jnp.broadcast_to(queries.reshape(1, own * fold, lane), (nz, own * fold, lane))
-    got = exchange(jnp.concatenate([tiles, rows], axis=1), z_axes)
+    got = exchange(first_buffer(queries, teacher, (ny, nzl, group, nzh, pool)), z_axes)
     got, *near = lax.optimization_barrier((got, *near))
-    cut = ny * own * group
-    tiles = got[:, :cut].reshape(nz, ny, own * group, pool).transpose(1, 0, 2, 3)
-    tiles = tiles.reshape(ny, nz * own * group, pool)
-    rows = jnp.broadcast_to(got[:, cut:].reshape(1, nz * own * fold, lane), (ny, nz * own * fold, lane))
-    sent = jnp.concatenate([tiles, rows], axis=1)
+    width, count = nz * own, ny * nz * own
+    got = got.reshape(width, -1)
+    tiles = [got[:, i * group * pool : (i + 1) * group * pool] for i in range(ny)]
+    sent = jnp.stack([jnp.concatenate([t, got[:, ny * group * pool :]], axis=1) for t in tiles])
     got = exchange(sent, "y")
     *near, _ = lax.optimization_barrier((*near, sent))
     near = jnp.stack([passages, *near])
     far = from_next(near, "core", 1)
-    count = ny * nz * own
-    block, high, low, stats, *rows = laid_out(got, (ny, nz * own, nc, nx, pool, dim))
+    block, high, low, stats, *rows = laid_out(got.reshape(count, -1), (ny, width, nc, nx, pool, dim))
     parts = local_parts(block, high, low, stats, near, far, ny)
 
     for k in range(1, nx - 1):

time: 110 us -> 110 us (level)
  waiting for transfers between devices: 23.5 us -> 25.1 us
  starting transfers between devices: 70.6 us -> 69.4 us
    unnamed x7 -> x11, local copies, waits for them, and re-layouts: 0.25 us -> 1.88 us
    all_to_all x5, waiting for transfers between devices: 6.68 us -> 8 us  [exchange(): return lax.all_to_all(values, axes, 0, 0, tiled=True)]
    ppermute x8, starting transfers between devices: 31.8 us -> 30.5 us  [from_next(): return lax.ppermute(values, axis, [(i, (i - step) % n) for i in range(n)])]
  transfers between devices with their start and end apart: 13 -> 13, of which waited for: 8 -> 7; matrix products, arithmetic and copies ran while one was open for 4% -> 4% of each run, Pallas kernels for 1% -> 1%
where the time goes in v7:
time: 110 us; the launch traced here: 109 us
  starting transfers between devices  69.4 us (63%)
  waiting for transfers between devices  25.1 us (23%)
  Pallas kernels  4.42 us (4%)
  other arithmetic  3.58 us (3%)
  local copies, waits for them, and re-layouts  3.47 us (3%)
  matrix products  2.2 us (2%)
  between operations  1.1 us (1%)
    all_to_all x5, starting transfers between devices, exchange(): return lax.all_to_all(values, axes, 0, 0, tiled=True)  38.8 us
    ppermute x8, starting transfers between devices, from_next(): return lax.ppermute(values, axis, [(i, (i - step) % n) for i in range(n)])  30.5 us
    ppermute x8, waiting for transfers between devices, from_next(): return lax.ppermute(values, axis, [(i, (i - step) % n) for i in range(n)])  17.1 us
    all_to_all x5, waiting for transfers between devices, exchange(): return lax.all_to_all(values, axes, 0, 0, tiled=True)  8 us
    pallas_call x1, Pallas kernels, local_parts(): pl.pallas_call(parts_kernel, out_shape=jax.ShapeDtypeStruct((ny, count //...  2.6 us
  transfers between devices with their start and end apart: 13, of which 7 were waited for; matrix products, arithmetic and copies ran while one was open for 4% of the time, Pallas kernels for 1%

profile of v7, /device:TPU:1, one launch (start us, length us, event | category | flops | bytes accessed | tf_op | source)
XLA Modules:
  0.0 109.2 jit_solution(7426131599511740579)
XLA Ops:
  0.6 0.9 copy-done
  1.6 0.7 copy-done.1
  2.3 0.9 shard_map.50
  3.2 15.7 %all-to-all-start = ((bf16[16,2,4864]{2,1,0:T(2,128)(2,1)}), bf16[16,2,4864]{2,1,0:T(2,128)(2,1)S(1)}, u32[]{:S(2)}, u32[]{:S(2)}) async-start(bf16[16,2,4864]{2,1,0:T(2,128)(2,1)} %shard_map.50), calls=%async_computation | async-start | bytes 622592 | tf_op jit(solution)/shard_map/all_to_all | solution.py:22
  18.9 4.5 %collective-permute-start = (bf16[128,768]{1,0:T(8,128)(2,1)}, bf16[128,768]{1,0:T(8,128)(2,1)S(1)}, u32[]{:S(2)}, u32[]{:S(2)}) collective-permute-start(bf16[128,768]{1,0:T(8,128)(2,1)} %param.4), channel_id=1, source_target_pairs={{0,6},{2,0},{4,2},{6,4},{1,7},{3,1},{5,3},{7,5},{8,14},{10,8},{12,... | collective-permute-start | bytes 589832 | tf_op jit(solution)/shard_map/ppermute | solution.py:27
  23.5 2.4 %collective-permute-start.1 = (bf16[128,768]{1,0:T(8,128)(2,1)}, bf16[128,768]{1,0:T(8,128)(2,1)S(1)}, u32[]{:S(2)}, u32[]{:S(2)}) collective-permute-start(bf16[128,768]{1,0:T(8,128)(2,1)} %param.4), channel_id=1, source_target_pairs={{0,4},{2,6},{4,0},{6,2},{1,5},{3,7},{5,1},{7,3},{8,12},{10,14},{12... | collective-permute-start | bytes 589832 | tf_op jit(solution)/shard_map/ppermute | solution.py:27
  25.9 2.5 %collective-permute-start.2 = (bf16[128,768]{1,0:T(8,128)(2,1)}, bf16[128,768]{1,0:T(8,128)(2,1)S(1)}, u32[]{:S(2)}, u32[]{:S(2)}) collective-permute-start(bf16[128,768]{1,0:T(8,128)(2,1)} %param.4), channel_id=1, source_target_pairs={{0,2},{2,4},{4,6},{6,0},{1,3},{3,5},{5,7},{7,1},{8,10},{10,12},{12... | collective-permute-start | bytes 589832 | tf_op jit(solution)/shard_map/ppermute | solution.py:27
  28.4 3.8 %collective-permute-done.1 = bf16[128,768]{1,0:T(8,128)(2,1)S(1)} collective-permute-done((bf16[128,768]{1,0:T(8,128)(2,1)}, bf16[128,768]{1,0:T(8,128)(2,1)S(1)}, u32[]{:S(2)}, u32[]{:S(2)}) %collective-permute-start.1) | collective-permute-done | bytes 196640 | tf_op jit(solution)/shard_map/ppermute | solution.py:27
  32.2 5.1 %collective-permute-done.2 = bf16[128,768]{1,0:T(8,128)(2,1)S(1)} collective-permute-done((bf16[128,768]{1,0:T(8,128)(2,1)}, bf16[128,768]{1,0:T(8,128)(2,1)S(1)}, u32[]{:S(2)}, u32[]{:S(2)}) %collective-permute-start.2) | collective-permute-done | bytes 196640 | tf_op jit(solution)/shard_map/ppermute | solution.py:27
  37.3 0.1 reshape.57
  37.5 0.8 pad_maximum_fusion.2
  38.3 4.2 %all-to-all-start.1 = ((bf16[4,32,1792]{2,1,0:T(8,128)(2,1)}), bf16[4,32,1792]{2,1,0:T(8,128)(2,1)S(1)}, u32[]{:S(2)}, u32[]{:S(2)}) async-start(bf16[4,32,1792]{2,1,0:T(8,128)(2,1)} %pad_maximum_fusion.2), calls=%async_computation.1 | async-start | bytes 917504 | tf_op jit(solution)/shard_map/all_to_all | solution.py:22
  42.5 0.1 pad_add_fusion.place
  42.6 0.1 pad_maximum_fusion.1
  42.7 4.7 %collective-permute-start.3 = (bf16[4,128,768]{2,1,0:T(8,128)(2,1)S(1)}, bf16[4,128,768]{2,1,0:T(8,128)(2,1)S(1)}, u32[]{:S(2)}, u32[]{:S(2)}) collective-permute-start(bf16[4,128,768]{2,1,0:T(8,128)(2,1)S(1)} %pad_maximum_fusion.1), channel_id=1, source_target_pairs={{0,8},{8,0},{1,9},{9,1},{2,10},{10,2},{3,11},{11,3},{4,12},{12,4},... | collective-permute-start | bytes 2359304 | tf_op jit(solution)/shard_map/ppermute | solution.py:27
  47.4 1.7 %all-to-all-done.1 = bf16[4,32,1792]{2,1,0:T(8,128)(2,1)S(1)} async-done(((bf16[4,32,1792]{2,1,0:T(8,128)(2,1)}), bf16[4,32,1792]{2,1,0:T(8,128)(2,1)S(1)}, u32[]{:S(2)}, u32[]{:S(2)}) %all-to-all-start.1) | async-done | bytes 458784 | tf_op jit(solution)/shard_map/all_to_all | solution.py:22
  49.1 0.9 shard_map.51
  50.0 2.6 %shard_map.52 = f32[4,32,1664]{2,1,0:T(8,128)} custom-call(bf16[128,768]{1,0:T(8,128)(2,1)S(1)} %get-tuple-element.27.block, bf16[128,1024]{1,0:T(8,128)(2,1)S(1)} %get-tuple-element.28.high, bf16[128,1024]{1,0:T(8,128)(2,1)S(1)} %get-tuple-element.29.low, f32[32,128]{1,0:T(8,128)S(1)} %get-tuple-element.30.taught, bf16[512,768]{1,0:T(8,128)(2,1)S(1)} %bitcast.76, ...), custom_call_target="tpu_custom_call" | custom-call | flops 1006632960 | bytes 4194304 | tf_op jit(solution)/shard_map/pallas_call | solution.py:165
  52.6 3.8 %all-to-all-start.2 = ((f32[4,32,1664]{2,1,0:T(8,128)}), f32[4,32,1664]{2,1,0:T(8,128)S(1)}, u32[]{:S(2)}, u32[]{:S(2)}) async-start(f32[4,32,1664]{2,1,0:T(8,128)} %shard_map.52), calls=%async_computation.2 | async-start | bytes 1703936 | tf_op jit(solution)/shard_map/all_to_all | solution.py:22
  56.4 4.4 %collective-permute-start.4 = (bf16[128,1024]{1,0:T(8,128)(2,1)S(1)}, bf16[128,1024]{1,0:T(8,128)(2,1)S(1)}, u32[]{:S(2)}, u32[]{:S(2)}) collective-permute-start(bf16[128,1024]{1,0:T(8,128)(2,1)S(1)} %get-tuple-element.38), channel_id=1, source_target_pairs={{0,6},{2,0},{4,2},{6,4},{1,7},{3,1},{5,3},{7,5},{8,14},{10,8},{12,... | collective-permute-start | bytes 786440 | tf_op jit(solution)/shard_map/ppermute | solution.py:27
  60.8 2.4 %collective-permute-start.5 = (bf16[128,1024]{1,0:T(8,128)(2,1)S(1)}, bf16[128,1024]{1,0:T(8,128)(2,1)S(1)}, u32[]{:S(2)}, u32[]{:S(2)}) collective-permute-start(bf16[128,1024]{1,0:T(8,128)(2,1)S(1)} %get-tuple-element.39), channel_id=1, source_target_pairs={{0,4},{2,6},{4,0},{6,2},{1,5},{3,7},{5,1},{7,3},{8,12},{10,14},{12... | collective-permute-start | bytes 786440 | tf_op jit(solution)/shard_map/ppermute | solution.py:27
  63.3 2.3 %all-to-all-done.2 = f32[4,32,1664]{2,1,0:T(8,128)S(1)} async-done(((f32[4,32,1664]{2,1,0:T(8,128)}), f32[4,32,1664]{2,1,0:T(8,128)S(1)}, u32[]{:S(2)}, u32[]{:S(2)}) %all-to-all-start.2) | async-done | bytes 852000 | tf_op jit(solution)/shard_map/all_to_all | solution.py:22
  65.6 0.1 constant_dynamic-slice_fusion.4
  65.8 0.1 fusion.6
  65.9 0.1 reshape.61
  66.1 0.8 pad_maximum_fusion.3
  66.9 11.5 %all-to-all-start.3 = ((f32[16,2,1792]{2,1,0:T(2,128)}), f32[16,2,1792]{2,1,0:T(2,128)S(1)}, u32[]{:S(2)}, u32[]{:S(2)}) async-start(f32[16,2,1792]{2,1,0:T(2,128)} %pad_maximum_fusion.3), calls=%async_computation.3 | async-start | bytes 458752 | tf_op jit(solution)/shard_map/all_to_all | solution.py:22
  78.4 1.9 %collective-permute-start.6 = (bf16[128,1024]{1,0:T(8,128)(2,1)S(1)}, bf16[128,1024]{1,0:T(8,128)(2,1)S(1)}, u32[]{:S(2)}, u32[]{:S(2)}) collective-permute-start(bf16[128,1024]{1,0:T(8,128)(2,1)S(1)} %get-tuple-element.44), channel_id=1, source_target_pairs={{0,2},{2,4},{4,6},{6,0},{1,3},{3,5},{5,7},{7,1},{8,10},{10,12},{12... | collective-permute-start | bytes 786440 | tf_op jit(solution)/shard_map/ppermute | solution.py:27
  80.5 6.2 %collective-permute-done.6 = bf16[128,1024]{1,0:T(8,128)(2,1)S(1)} collective-permute-done((bf16[128,1024]{1,0:T(8,128)(2,1)S(1)}, bf16[128,1024]{1,0:T(8,128)(2,1)S(1)}, u32[]{:S(2)}, u32[]{:S(2)}) %collective-permute-start.6) | collective-permute-done | bytes 262176 | tf_op jit(solution)/shard_map/ppermute | solution.py:27
  86.8 0.1 pad_maximum_fusion
  87.0 7.6 %collective-permute-start.7 = (bf16[4,128,896]{2,1,0:T(8,128)(2,1)S(1)}, bf16[4,128,896]{2,1,0:T(8,128)(2,1)S(1)}, u32[]{:S(2)}, u32[]{:S(2)}) collective-permute-start(bf16[4,128,896]{2,1,0:T(8,128)(2,1)S(1)} %pad_maximum_fusion), channel_id=1, source_target_pairs={{0,8},{8,0},{1,9},{9,1},{2,10},{10,2},{3,11},{11,3},{4,12},{12,4},... | collective-permute-start | bytes 2752520 | tf_op jit(solution)/shard_map/ppermute | solution.py:27
  94.7 2.0 %collective-permute-done.7 = bf16[4,128,896]{2,1,0:T(8,128)(2,1)S(1)} collective-permute-done((bf16[4,128,896]{2,1,0:T(8,128)(2,1)S(1)}, bf16[4,128,896]{2,1,0:T(8,128)(2,1)S(1)}, u32[]{:S(2)}, u32[]{:S(2)}) %collective-permute-start.7) | collective-permute-done | bytes 917536 | tf_op jit(solution)/shard_map/ppermute | solution.py:27
  96.7 0.1 constant_dynamic-update-slice_fusion
  96.8 0.2 slice_reduce_fusion
  97.0 0.1 copy.28
  97.1 0.1 exponential_bitcast_fusion
  97.2 0.7 fusion.20
  97.9 0.1 exponential_bitcast_fusion.1
  98.2 0.1 constant_dynamic-slice_fusion.2
  98.2 0.1 constant_dynamic-slice_fusion
  98.3 0.1 constant_dynamic-slice_fusion.1
  98.4 0.6 broadcast_in_dim.34
  99.0 3.6 %all-to-all-start.4 = ((f32[8,4,128]{2,1,0:T(4,128)}), f32[8,4,128]{2,1,0:T(4,128)S(1)}, u32[]{:S(2)}, u32[]{:S(2)}) async-start(f32[8,4,128]{2,1,0:T(4,128)} %broadcast_in_dim.34), calls=%async_computation.4 | async-start | bytes 32768 | tf_op jit(solution)/shard_map/all_to_all | solution.py:22
  102.7 0.1 multiply_reduce_fusion.1
  102.8 0.7 fusion.15
  103.5 4.1 %all-to-all-done.4 = f32[8,4,128]{2,1,0:T(4,128)S(1)} async-done(((f32[8,4,128]{2,1,0:T(4,128)}), f32[8,4,128]{2,1,0:T(4,128)S(1)}, u32[]{:S(2)}, u32[]{:S(2)}) %all-to-all-start.4) | async-done | bytes 16416 | tf_op jit(solution)/shard_map/all_to_all | solution.py:22
  107.7 0.4 fusion
  108.1 1.1 %convolution_add_fusion = f32[128,768]{1,0:T(8,128)} fusion(f32[128,768]{1,0:T(8,128)S(1)} %fusion, bf16[1024,896]{1,0:T(8,128)(2,1)S(1)} %bitcast.82, f32[128,1024]{1,0:T(8,128)S(1)} %exponential_bitcast_fusion, f32[128,1024]{1,0:T(8,128)S(1)} %exponential_bitcast_fusion.1, f32[1024]{0:T(1024)S(1)} %multiply_divide_fusion, f32[1024]{0:T(1024)S(1)} %multiply_divide_fusion.1), kind=kOutput, calls=%fused_computation.1 | convolution fusion | flops 202080256 | bytes 3416064 | tf_op jit(solution)/shard_map/dot_general | solution.py:38
  (54 shorter events, 0.8 us)
Async XLA Ops:
  0.6 1.0 copy-start
  1.6 0.7 copy-start.1
  3.2 34.1 %all-to-all-start = ((bf16[16,2,4864]{2,1,0:T(2,128)(2,1)}), bf16[16,2,4864]{2,1,0:T(2,128)(2,1)S(1)}, u32[]{:S(2)}, u32[]{:S(2)}) async-start(bf16[16,2,4864]{2,1,0:T(2,128)(2,1)} %shard_map.50), calls=%async_computation | async-start | bytes 622592 | tf_op jit(solution)/shard_map/all_to_all | solution.py:22
  18.9 23.7 %copy-start.2 = (bf16[128,768]{1,0:T(8,128)(2,1)S(1)}, bf16[128,768]{1,0:T(8,128)(2,1)}, u32[]{:S(2)}) copy-start(bf16[128,768]{1,0:T(8,128)(2,1)} %param.4) | copy-start | bytes 589828
  18.9 9.5 %collective-permute-start = (bf16[128,768]{1,0:T(8,128)(2,1)}, bf16[128,768]{1,0:T(8,128)(2,1)S(1)}, u32[]{:S(2)}, u32[]{:S(2)}) collective-permute-start(bf16[128,768]{1,0:T(8,128)(2,1)} %param.4), channel_id=1, source_target_pairs={{0,6},{2,0},{4,2},{6,4},{1,7},{3,1},{5,3},{7,5},{8,14},{10,8},{12,... | collective-permute-start | bytes 589832 | tf_op jit(solution)/shard_map/ppermute | solution.py:27
  23.5 8.8 %collective-permute-start.1 = (bf16[128,768]{1,0:T(8,128)(2,1)}, bf16[128,768]{1,0:T(8,128)(2,1)S(1)}, u32[]{:S(2)}, u32[]{:S(2)}) collective-permute-start(bf16[128,768]{1,0:T(8,128)(2,1)} %param.4), channel_id=1, source_target_pairs={{0,4},{2,6},{4,0},{6,2},{1,5},{3,7},{5,1},{7,3},{8,12},{10,14},{12... | collective-permute-start | bytes 589832 | tf_op jit(solution)/shard_map/ppermute | solution.py:27
  25.9 11.4 %collective-permute-start.2 = (bf16[128,768]{1,0:T(8,128)(2,1)}, bf16[128,768]{1,0:T(8,128)(2,1)S(1)}, u32[]{:S(2)}, u32[]{:S(2)}) collective-permute-start(bf16[128,768]{1,0:T(8,128)(2,1)} %param.4), channel_id=1, source_target_pairs={{0,2},{2,4},{4,6},{6,0},{1,3},{3,5},{5,7},{7,1},{8,10},{10,12},{12... | collective-permute-start | bytes 589832 | tf_op jit(solution)/shard_map/ppermute | solution.py:27
  38.3 10.8 %all-to-all-start.1 = ((bf16[4,32,1792]{2,1,0:T(8,128)(2,1)}), bf16[4,32,1792]{2,1,0:T(8,128)(2,1)S(1)}, u32[]{:S(2)}, u32[]{:S(2)}) async-start(bf16[4,32,1792]{2,1,0:T(8,128)(2,1)} %pad_maximum_fusion.2), calls=%async_computation.1 | async-start | bytes 917504 | tf_op jit(solution)/shard_map/all_to_all | solution.py:22
  42.7 7.3 %collective-permute-start.3 = (bf16[4,128,768]{2,1,0:T(8,128)(2,1)S(1)}, bf16[4,128,768]{2,1,0:T(8,128)(2,1)S(1)}, u32[]{:S(2)}, u32[]{:S(2)}) collective-permute-start(bf16[4,128,768]{2,1,0:T(8,128)(2,1)S(1)} %pad_maximum_fusion.1), channel_id=1, source_target_pairs={{0,8},{8,0},{1,9},{9,1},{2,10},{10,2},{3,11},{11,3},{4,12},{12,4},... | collective-permute-start | bytes 2359304 | tf_op jit(solution)/shard_map/ppermute | solution.py:27
  52.6 12.9 %all-to-all-start.2 = ((f32[4,32,1664]{2,1,0:T(8,128)}), f32[4,32,1664]{2,1,0:T(8,128)S(1)}, u32[]{:S(2)}, u32[]{:S(2)}) async-start(f32[4,32,1664]{2,1,0:T(8,128)} %shard_map.52), calls=%async_computation.2 | async-start | bytes 1703936 | tf_op jit(solution)/shard_map/all_to_all | solution.py:22
  56.4 21.9 %collective-permute-start.4 = (bf16[128,1024]{1,0:T(8,128)(2,1)S(1)}, bf16[128,1024]{1,0:T(8,128)(2,1)S(1)}, u32[]{:S(2)}, u32[]{:S(2)}) collective-permute-start(bf16[128,1024]{1,0:T(8,128)(2,1)S(1)} %get-tuple-element.38), channel_id=1, source_target_pairs={{0,6},{2,0},{4,2},{6,4},{1,7},{3,1},{5,3},{7,5},{8,14},{10,8},{12,... | collective-permute-start | bytes 786440 | tf_op jit(solution)/shard_map/ppermute | solution.py:27
  60.8 17.6 %collective-permute-start.5 = (bf16[128,1024]{1,0:T(8,128)(2,1)S(1)}, bf16[128,1024]{1,0:T(8,128)(2,1)S(1)}, u32[]{:S(2)}, u32[]{:S(2)}) collective-permute-start(bf16[128,1024]{1,0:T(8,128)(2,1)S(1)} %get-tuple-element.39), channel_id=1, source_target_pairs={{0,4},{2,6},{4,0},{6,2},{1,5},{3,7},{5,1},{7,3},{8,12},{10,14},{12... | collective-permute-start | bytes 786440 | tf_op jit(solution)/shard_map/ppermute | solution.py:27
  66.9 31.1 %all-to-all-start.3 = ((f32[16,2,1792]{2,1,0:T(2,128)}), f32[16,2,1792]{2,1,0:T(2,128)S(1)}, u32[]{:S(2)}, u32[]{:S(2)}) async-start(f32[16,2,1792]{2,1,0:T(2,128)} %pad_maximum_fusion.3), calls=%async_computation.3 | async-start | bytes 458752 | tf_op jit(solution)/shard_map/all_to_all | solution.py:22
  78.4 8.3 %collective-permute-start.6 = (bf16[128,1024]{1,0:T(8,128)(2,1)S(1)}, bf16[128,1024]{1,0:T(8,128)(2,1)S(1)}, u32[]{:S(2)}, u32[]{:S(2)}) collective-permute-start(bf16[128,1024]{1,0:T(8,128)(2,1)S(1)} %get-tuple-element.44), channel_id=1, source_target_pairs={{0,2},{2,4},{4,6},{6,0},{1,3},{3,5},{5,7},{7,1},{8,10},{10,12},{12... | collective-permute-start | bytes 786440 | tf_op jit(solution)/shard_map/ppermute | solution.py:27
  87.0 9.7 %collective-permute-start.7 = (bf16[4,128,896]{2,1,0:T(8,128)(2,1)S(1)}, bf16[4,128,896]{2,1,0:T(8,128)(2,1)S(1)}, u32[]{:S(2)}, u32[]{:S(2)}) collective-permute-start(bf16[4,128,896]{2,1,0:T(8,128)(2,1)S(1)} %pad_maximum_fusion), channel_id=1, source_target_pairs={{0,8},{8,0},{1,9},{9,1},{2,10},{10,2},{3,11},{11,3},{4,12},{12,4},... | collective-permute-start | bytes 2752520 | tf_op jit(solution)/shard_map/ppermute | solution.py:27
  99.0 8.5 %all-to-all-start.4 = ((f32[8,4,128]{2,1,0:T(4,128)}), f32[8,4,128]{2,1,0:T(4,128)S(1)}, u32[]{:S(2)}, u32[]{:S(2)}) async-start(f32[8,4,128]{2,1,0:T(4,128)} %broadcast_in_dim.34), calls=%async_computation.4 | async-start | bytes 32768 | tf_op jit(solution)/shard_map/all_to_all | solution.py:22

commit v8 on v7

--- a/solution.py
+++ b/solution.py
@@ -27,25 +27,6 @@
     return lax.ppermute(values, axis, [(i, (i - step) % n) for i in range(n)])
 
 
-def rolled(values, axis, dim):
-    twice = jnp.concatenate([values, values], axis=dim)
-    return lax.dynamic_slice_in_dim(twice, lax.axis_index(axis), lax.axis_size(axis), dim)
-
-
-def split_dot(weights, exact, dims):
-    high = lax.reduce_precision(weights, 8, 7)
-    low = weights - high
-    return lax.dot_general(
-        high.astype(bf16), exact, dims, preferred_element_type=f32
-    ) + lax.dot_general(low.astype(bf16), exact, dims, preferred_element_type=f32)
-
-
-def combine(top, total, axis):
-    high = jnp.max(top, axis=axis, keepdims=True)
-    weight = jnp.exp(top - high)
-    return weight, jnp.squeeze(high, axis), jnp.sum(weight * total, axis=axis)
-
-
 def bf16_parts(values):
     high = values.astype(bf16)
     return high, (values - high.astype(f32)).astype(bf16)
@@ -58,8 +39,16 @@
     return jnp.sum(jnp.where(at_row == at_lane, column, 0.0), axis=0, keepdims=True)
 
 
-def first_kernel(sizes, queries, teacher, sent):
+def first_kernel(sizes, queries_in, teacher_in, sent, queries, teacher, sems):
     ny, nzl, group, nzh, pool = sizes
+    copies = [
+        pltpu.make_async_copy(teacher_in, teacher, sems.at[0]),
+        pltpu.make_async_copy(queries_in, queries, sems.at[1]),
+    ]
+    for copy in copies:
+        copy.start()
+    for copy in copies:
+        copy.wait()
     for zh in range(nzh):
         for zl in range(nzl):
             to = zh * nzl + zl
@@ -124,6 +113,107 @@
         sent[y, :, 2 * dim :] = spread
 
 
+def merged(pairs):
+    high = functools.reduce(jnp.maximum, [top for top, _ in pairs])
+    weights = [jnp.exp(top - high) for top, _ in pairs]
+    total = functools.reduce(jnp.add, [w * t for w, (_, t) in zip(weights, pairs)])
+    return weights, high, total
+
+
+def stats_place(own, count, i):
+    rows = min(own, 4)
+    row, at = divmod(i, 4 // rows)
+    return row, at * count
+
+
+def middle_kernel(place, got, sent):
+    nz, own, _ = sent.shape
+    ny, width, full = got.shape
+    count = ny * width
+    dim = (full - count) // 2
+    at_lane = lax.broadcasted_iota(jnp.int32, (width, count), 1)
+    at_row = lax.broadcasted_iota(jnp.int32, (width, count), 0)
+    mine = at_lane == at_row + place[0] * width
+    stats = []
+    for at in range(2):
+        pairs = [
+            tuple(got[y, 2 * at + i : 2 * at + i + 1, 2 * dim :] for i in range(2)) for y in range(ny)
+        ]
+        weights, high, total = merged(pairs)
+        stats += [high, total]
+        part = jnp.zeros((width, dim), f32)
+        for y, weight in enumerate(weights):
+            column = jnp.sum(jnp.where(mine, weight, 0.0), axis=1, keepdims=True)
+            part += column * got[y, :, at * dim : (at + 1) * dim]
+        for z in range(nz):
+            sent[z, :, at * dim : (at + 1) * dim] = part[z * own : (z + 1) * own]
+    for i, values in enumerate(stats):
+        row, at = stats_place(own, count, i)
+        for z in range(nz):
+            sent[z, row : row + 1, 2 * dim + at : 2 * dim + at + count] = values
+
+
+def all_pairs(got, dim, count, kind):
+    nz, own, _ = got.shape
+    pairs = []
+    for z in range(nz):
+        pair = []
+        for i in (2 * kind, 2 * kind + 1):
+            row, at = stats_place(own, count, i)
+            pair.append(got[z, row : row + 1, 2 * dim + at : 2 * dim + at + count])
+        pairs.append(pair)
+    return pairs
+
+
+def after_kernel(dim, got, sent):
+    group, _, count = sent.shape
+    stats = [v for kind in range(2) for v in merged(all_pairs(got, dim, count, kind))[1:]]
+    stats = jnp.concatenate(stats, axis=0)
+    for i in range(group):
+        sent[i] = stats
+
+
+def query_kernel(count, place, got, grads):
+    own, dim = grads.shape
+    at_lane = lax.broadcasted_iota(jnp.int32, (own, count), 1)
+    at_row = lax.broadcasted_iota(jnp.int32, (own, count), 0)
+    mine = at_lane == at_row + place[0]
+
+    def column(values):
+        return jnp.sum(jnp.where(mine, values, 0.0), axis=1, keepdims=True)
+
+    parts = []
+    for kind in range(2):
+        weights, _, total = merged(all_pairs(got, dim, count, kind))
+        part = jnp.zeros((own, dim), f32)
+        for z, weight in enumerate(weights):
+            part += column(weight) * got[z, :, kind * dim : (kind + 1) * dim]
+        parts.append(part / column(total))
+    grads[...] = logit_scale * (parts[0] - parts[1])
+
+
+def last_kernel(blocks, nc, nx, place, got, *rest):
+    *sets, grads = rest
+    count = got.shape[2]
+    dim = grads.shape[1]
+    total = jnp.zeros((2 * grads.shape[0], dim), f32)
+    for j, block in enumerate(blocks):
+        scores, wanted, high_s, high_t, rows = sets[5 * j : 5 * j + 5]
+        pieces = []
+        for i, (c, k) in enumerate(block):
+            of = (place[0] + c) % nc * nx + (place[1] + k) % nx
+            at = slice(i * count, (i + 1) * count)
+            stats = got[of]
+            weight_s = logit_scale * jnp.exp(high_s[:, at] - stats[0:1]) / stats[1:2]
+            weight_t = logit_scale * jnp.exp(high_t[:, at] - stats[2:3]) / stats[3:4]
+            grad = weight_s * scores[:, at] - weight_t * wanted[:, at]
+            pieces.append(jnp.concatenate(bf16_parts(grad), axis=0))
+        total += jnp.dot(
+            jnp.concatenate(pieces, axis=1), rows[:, :dim], preferred_element_type=f32
+        )
+    grads[...] = total[: grads.shape[0]] + total[grads.shape[0] :]
+
+
 vmem = pl.BlockSpec(memory_space=pltpu.VMEM)
 
 
@@ -133,17 +223,26 @@
     return pl.pallas_call(
         functools.partial(first_kernel, sizes),
         out_shape=jax.ShapeDtypeStruct((nzh * nzl, own, ny * group * pool + dim), bf16),
-        in_specs=[vmem] * 2,
+        in_specs=[pl.BlockSpec(memory_space=pltpu.HBM)] * 2,
         out_specs=vmem,
-        compiler_params=pltpu.CompilerParams(vmem_limit_bytes=16 * 2**20),
+        scratch_shapes=[
+            pltpu.VMEM(queries.shape, bf16),
+            pltpu.VMEM(teacher.shape, bf16),
+            pltpu.SemaphoreType.DMA((2,)),
+        ],
+        compiler_params=pltpu.CompilerParams(vmem_limit_bytes=60 * 2**20),
         cost_estimate=pl.CostEstimate(flops=0, bytes_accessed=2**20, transcendentals=0),
     )(queries, teacher)
+
+
+def place_of():
+    return jnp.stack([lax.axis_index("core"), lax.axis_index("x")]).astype(jnp.int32)
 
 
 def laid_out(got, sizes):
     ny, width, nc, nx, pool, dim = sizes
     count, group = ny * width, nc * nx
-    place = jnp.stack([lax.axis_index("core"), lax.axis_index("x")]).astype(jnp.int32)
+    place = place_of()
     lifted = jax.ShapeDtypeStruct((count, group * pool), bf16)
     row = jax.ShapeDtypeStruct((count, dim + nc * pool), bf16)
     block = jax.ShapeDtypeStruct((count, dim), bf16)
@@ -176,6 +275,19 @@
     )(block, high, low, stats, near.reshape(-1, dim), far.reshape(-1, dim))
 
 
+def simple_call(kernel, out, scalars, arrays, flops=0):
+    size = sum(v.size * v.dtype.itemsize for v in arrays) + 4 * out.size
+    smem = pl.BlockSpec(memory_space=pltpu.SMEM)
+    return pl.pallas_call(
+        kernel,
+        out_shape=out,
+        in_specs=[smem] * len(scalars) + [vmem] * len(arrays),
+        out_specs=vmem,
+        compiler_params=pltpu.CompilerParams(vmem_limit_bytes=16 * 2**20),
+        cost_estimate=pl.CostEstimate(flops=flops, bytes_accessed=size, transcendentals=0),
+    )(*scalars, *arrays)
+
+
 def per_device(queries, passages, teacher):
     own, dim = queries.shape
     pool = passages.shape[0]
@@ -200,37 +312,23 @@
     for k in range(1, nx - 1):
         rows[k] = from_next(rows[k], "x", k)
 
-    def pack(parts, stats, n):
-        width = parts.shape[0] // n
-        extra = -(-stats.size // width)
-        extra += -extra % lane
-        spread = jnp.pad(stats.reshape(-1, extra), ((0, width - stats.size // extra), (0, 0)))
-        spread = jnp.broadcast_to(spread, (n, width, extra))
-        return jnp.concatenate([parts.reshape(n, width, 2 * dim), spread], axis=2)
-
-    def unpack(got, place):
-        n, width, full = got.shape
-        extra = full - 2 * dim
-        stats = got[:, : 4 * count // extra, 2 * dim :].reshape(n, 4, count)
-        weight_s, top_s, sum_s = combine(stats[:, 0], stats[:, 1], 0)
-        weight_t, top_t, sum_t = combine(stats[:, 2], stats[:, 3], 0)
-        weight_s = lax.dynamic_slice_in_dim(weight_s, place, width, 1)
-        weight_t = lax.dynamic_slice_in_dim(weight_t, place, width, 1)
-        part_s = jnp.sum(weight_s[:, :, None] * got[:, :, :dim], axis=0)
-        part_t = jnp.sum(weight_t[:, :, None] * got[:, :, dim : 2 * dim], axis=0)
-        return part_s, part_t, jnp.stack([top_s, sum_s, top_t, sum_t])
-
-    y_at = lax.axis_index("y") * (nz * own)
-    z_at = y_at + lax.axis_index(z_axes) * own
-    part_s, part_t, stats = unpack(exchange(parts, "y"), y_at)
-    sent = pack(jnp.concatenate([part_s, part_t], axis=1), stats, nz)
+    z_at = lax.axis_index("y") * width + lax.axis_index(z_axes) * own
+    extra = 4 // min(own, 4) * count
+    sent = simple_call(
+        middle_kernel,
+        jax.ShapeDtypeStruct((nz, own, 2 * dim + extra), f32),
+        [lax.axis_index("y").astype(jnp.int32)[None]],
+        [exchange(parts, "y")],
+    )
     got = exchange(sent, z_axes)
     *rows, _ = lax.optimization_barrier((*rows, sent))
     rows[-1] = from_next(rows[-1], "x", nx - 1)
+
     kept = jnp.stack([r[:, : dim + pool] for r in rows])
     away = jnp.stack([jnp.concatenate([r[:, :dim], r[:, dim + pool :]], axis=1) for r in rows])
     every_row = jnp.concatenate([kept, from_next(away, "core", 1)]).reshape(group * count, dim + pool)
-    all_rows, own_logits = every_row[:, :dim], every_row[:, dim:]
+    row_sets = [every_row]
+    blocks = [[(c, k) for c in range(nc) for k in range(nx)]]
 
     def lifted(values):
         top = jnp.max(values, axis=0)
@@ -238,23 +336,33 @@
 
     scores, high_s = lifted(
         logit_scale
-        * lax.dot_general(passages, all_rows, (((1,), (1,)), ((), ())), preferred_element_type=f32)
-    )
-    wanted, high_t = lifted(own_logits.T.astype(f32))
-    got, scores, wanted, high_s, high_t = lax.optimization_barrier(
-        (got, scores, wanted, high_s, high_t)
-    )
-    part_s, part_t, stats = unpack(got, z_at)
-    mine = lax.dynamic_slice_in_dim(stats, z_at, own, 1)
-    query_grad = logit_scale * (part_s / mine[1][:, None] - part_t / mine[3][:, None])
-
-    every = exchange(jnp.broadcast_to(stats[None], (group,) + stats.shape), group_axes)
-    every = rolled(rolled(every.reshape(nc, nx, 4, count), "x", 1), "core", 0)
-    every = every.transpose(2, 0, 1, 3).reshape(4, group * count)
-    grad = (logit_scale * jnp.exp(high_s - every[0]) / every[1]) * scores - (
-        logit_scale * jnp.exp(high_t - every[2]) / every[3]
-    ) * wanted
-    passage_grad = split_dot(grad, all_rows, (((1,), (0,)), ((), ())))
+        * lax.dot_general(
+            passages, every_row[:, :dim], (((1,), (1,)), ((), ())), preferred_element_type=f32
+        )
+    )
+    wanted, high_t = lifted(every_row[:, dim:].T.astype(f32))
+    sets = [scores, wanted, high_s, high_t]
+    got, *sets = lax.optimization_barrier((got, *sets))
+    sets = [*sets[:2], sets[2][None], sets[3][None], every_row]
+    every = simple_call(
+        functools.partial(after_kernel, dim), jax.ShapeDtypeStruct((group, 4, count), f32), [], [got]
+    )
+    got, _ = lax.optimization_barrier((got, every))
+    every = exchange(every, group_axes)
+    query_grad = simple_call(
+        functools.partial(query_kernel, count),
+        jax.ShapeDtypeStruct((own, dim), f32),
+        [z_at.astype(jnp.int32)[None]],
+        [got],
+    )
+
+    passage_grad = simple_call(
+        functools.partial(last_kernel, blocks, nc, nx),
+        jax.ShapeDtypeStruct((pool, dim), f32),
+        [place_of()],
+        [every, *sets],
+        flops=4 * pool * group * count * dim,
+    )
     return query_grad, passage_grad
 
 

time: 110 us -> 109 us (level)
  Pallas kernels: 4.42 us -> 9.54 us
  local copies, waits for them, and re-layouts: 3.47 us -> 1.73 us
  matrix products: 2.2 us -> 0.65 us
  waiting for transfers between devices: 25.1 us -> 23.9 us
    pallas_call x0 -> x4, Pallas kernels: none -> 4.16 us  [simple_call(): pl.pallas_call(kernel, out_shape=out, in_specs=[smem] * len(scalars) + [v...]
    unnamed x11 -> x6, local copies, waits for them, and re-layouts: 1.88 us -> 0.1 us
    dot_general x3 -> x1, matrix products: 2.2 us -> 0.65 us  [per_device(): lax.dot_general(passages, every_row[:, :dim], (((1,), (1,)), ((), ())), p...]
    optimization_barrier x0 -> x1, local copies, waits for them, and re-layouts: none -> 1.24 us  [per_device(): got, *sets = lax.optimization_barrier((got, *sets))]
    all_to_all x5, waiting for transfers between devices: 8 us -> 6.83 us  [exchange(): return lax.all_to_all(values, axes, 0, 0, tiled=True)]
  transfers between devices with their start and end apart: 13 -> 13, of which waited for: 7 -> 7; matrix products, arithmetic and copies ran while one was open for 4% -> 4% of each run, Pallas kernels for 1% -> 2%
where the time goes in v8:
time: 109 us
  starting transfers between devices  69.4 us (64%)
  waiting for transfers between devices  23.9 us (22%)
  Pallas kernels  9.54 us (9%)
  other arithmetic  2.51 us (2%)
  local copies, waits for them, and re-layouts  1.73 us (2%)
    all_to_all x5, starting transfers between devices, exchange(): return lax.all_to_all(values, axes, 0, 0, tiled=True)  38.8 us
    ppermute x8, starting transfers between devices, from_next(): return lax.ppermute(values, axis, [(i, (i - step) % n) for i in range(n)])  30.6 us
    ppermute x8, waiting for transfers between devices, from_next(): return lax.ppermute(values, axis, [(i, (i - step) % n) for i in range(n)])  17.1 us
    all_to_all x5, waiting for transfers between devices, exchange(): return lax.all_to_all(values, axes, 0, 0, tiled=True)  6.83 us
    pallas_call x4, Pallas kernels, simple_call(): pl.pallas_call(kernel, out_shape=out, in_specs=[smem] * len(scalars) + [v...  4.16 us
    pallas_call x1, Pallas kernels, local_parts(): pl.pallas_call(parts_kernel, out_shape=jax.ShapeDtypeStruct((ny, count //...  2.59 us
  transfers between devices with their start and end apart: 13, of which 7 were waited for; matrix products, arithmetic and copies ran while one was open for 4% of the time, Pallas kernels for 2%

profile of v8, /device:TPU:1, one launch (start us, length us, event | category | flops | bytes accessed | tf_op | source)
XLA Modules:
  0.0 108.7 jit_solution(17617368665452383262)
XLA Ops:
  0.6 1.9 %shard_map.50 = bf16[16,2,4864]{2,1,0:T(2,128)(2,1)} custom-call(bf16[2,768]{1,0:T(2,128)(2,1)} %queries_in.1, bf16[2,65536]{1,0:T(2,128)(2,1)} %teacher_in.1), custom_call_target="tpu_custom_call" | custom-call | bytes 1048576 | tf_op jit(solution)/shard_map/pallas_call | solution.py:223
  2.5 15.8 %all-to-all-start = ((bf16[16,2,4864]{2,1,0:T(2,128)(2,1)}), bf16[16,2,4864]{2,1,0:T(2,128)(2,1)S(1)}, u32[]{:S(2)}, u32[]{:S(2)}) async-start(bf16[16,2,4864]{2,1,0:T(2,128)(2,1)} %shard_map.50), calls=%async_computation | async-start | bytes 622592 | tf_op jit(solution)/shard_map/all_to_all | solution.py:22
  18.3 0.0 copy-start
  18.3 4.5 %collective-permute-start = (bf16[128,768]{1,0:T(8,128)(2,1)}, bf16[128,768]{1,0:T(8,128)(2,1)S(1)}, u32[]{:S(2)}, u32[]{:S(2)}) collective-permute-start(bf16[128,768]{1,0:T(8,128)(2,1)} %param.4), channel_id=1, source_target_pairs={{0,6},{2,0},{4,2},{6,4},{1,7},{3,1},{5,3},{7,5},{8,14},{10,8},{12,... | collective-permute-start | bytes 589832 | tf_op jit(solution)/shard_map/ppermute | solution.py:27
  22.8 2.4 %collective-permute-start.1 = (bf16[128,768]{1,0:T(8,128)(2,1)}, bf16[128,768]{1,0:T(8,128)(2,1)S(1)}, u32[]{:S(2)}, u32[]{:S(2)}) collective-permute-start(bf16[128,768]{1,0:T(8,128)(2,1)} %param.4), channel_id=1, source_target_pairs={{0,4},{2,6},{4,0},{6,2},{1,5},{3,7},{5,1},{7,3},{8,12},{10,14},{12... | collective-permute-start | bytes 589832 | tf_op jit(solution)/shard_map/ppermute | solution.py:27
  25.2 2.5 %collective-permute-start.2 = (bf16[128,768]{1,0:T(8,128)(2,1)}, bf16[128,768]{1,0:T(8,128)(2,1)S(1)}, u32[]{:S(2)}, u32[]{:S(2)}) collective-permute-start(bf16[128,768]{1,0:T(8,128)(2,1)} %param.4), channel_id=1, source_target_pairs={{0,2},{2,4},{4,6},{6,0},{1,3},{3,5},{5,7},{7,1},{8,10},{10,12},{12... | collective-permute-start | bytes 589832 | tf_op jit(solution)/shard_map/ppermute | solution.py:27
  27.8 0.0 collective-permute-done
  27.8 3.8 %collective-permute-done.1 = bf16[128,768]{1,0:T(8,128)(2,1)S(1)} collective-permute-done((bf16[128,768]{1,0:T(8,128)(2,1)}, bf16[128,768]{1,0:T(8,128)(2,1)S(1)}, u32[]{:S(2)}, u32[]{:S(2)}) %collective-permute-start.1) | collective-permute-done | bytes 196640 | tf_op jit(solution)/shard_map/ppermute | solution.py:27
  31.6 5.1 %collective-permute-done.2 = bf16[128,768]{1,0:T(8,128)(2,1)S(1)} collective-permute-done((bf16[128,768]{1,0:T(8,128)(2,1)}, bf16[128,768]{1,0:T(8,128)(2,1)S(1)}, u32[]{:S(2)}, u32[]{:S(2)}) %collective-permute-start.2) | collective-permute-done | bytes 196640 | tf_op jit(solution)/shard_map/ppermute | solution.py:27
  36.7 0.0 all-to-all-done
  36.7 0.1 reshape.23
  36.9 0.8 pad_maximum_fusion.2
  37.7 4.2 %all-to-all-start.1 = ((bf16[4,32,1792]{2,1,0:T(8,128)(2,1)}), bf16[4,32,1792]{2,1,0:T(8,128)(2,1)S(1)}, u32[]{:S(2)}, u32[]{:S(2)}) async-start(bf16[4,32,1792]{2,1,0:T(8,128)(2,1)} %pad_maximum_fusion.2), calls=%async_computation.1 | async-start | bytes 917504 | tf_op jit(solution)/shard_map/all_to_all | solution.py:22
  41.9 0.1 pad_add_fusion.place
  42.0 0.0 copy-done
  42.0 0.1 pad_maximum_fusion.1
  42.1 4.7 %collective-permute-start.3 = (bf16[4,128,768]{2,1,0:T(8,128)(2,1)S(1)}, bf16[4,128,768]{2,1,0:T(8,128)(2,1)S(1)}, u32[]{:S(2)}, u32[]{:S(2)}) collective-permute-start(bf16[4,128,768]{2,1,0:T(8,128)(2,1)S(1)} %pad_maximum_fusion.1), channel_id=1, source_target_pairs={{0,8},{8,0},{1,9},{9,1},{2,10},{10,2},{3,11},{11,3},{4,12},{12,4},... | collective-permute-start | bytes 2359304 | tf_op jit(solution)/shard_map/ppermute | solution.py:27
  46.8 1.7 %all-to-all-done.1 = bf16[4,32,1792]{2,1,0:T(8,128)(2,1)S(1)} async-done(((bf16[4,32,1792]{2,1,0:T(8,128)(2,1)}), bf16[4,32,1792]{2,1,0:T(8,128)(2,1)S(1)}, u32[]{:S(2)}, u32[]{:S(2)}) %all-to-all-start.1) | async-done | bytes 458784 | tf_op jit(solution)/shard_map/all_to_all | solution.py:22
  48.5 0.9 shard_map.51
  49.4 0.0 collective-permute-done.3
  49.4 2.6 %shard_map.52 = f32[4,32,1664]{2,1,0:T(8,128)} custom-call(bf16[128,768]{1,0:T(8,128)(2,1)S(1)} %get-tuple-element.28.block, bf16[128,1024]{1,0:T(8,128)(2,1)S(1)} %get-tuple-element.29.high, bf16[128,1024]{1,0:T(8,128)(2,1)S(1)} %get-tuple-element.30.low, f32[32,128]{1,0:T(8,128)S(1)} %get-tuple-element.31.taught, bf16[512,768]{1,0:T(8,128)(2,1)S(1)} %bitcast.49, ...), custom_call_target="tpu_custom_call" | custom-call | flops 1006632960 | bytes 4194304 | tf_op jit(solution)/shard_map/pallas_call | solution.py:264
  52.0 3.8 %all-to-all-start.2 = ((f32[4,32,1664]{2,1,0:T(8,128)}), f32[4,32,1664]{2,1,0:T(8,128)S(1)}, u32[]{:S(2)}, u32[]{:S(2)}) async-start(f32[4,32,1664]{2,1,0:T(8,128)} %shard_map.52), calls=%async_computation.2 | async-start | bytes 1703936 | tf_op jit(solution)/shard_map/all_to_all | solution.py:22
  55.8 4.4 %collective-permute-start.4 = (bf16[128,1024]{1,0:T(8,128)(2,1)S(1)}, bf16[128,1024]{1,0:T(8,128)(2,1)S(1)}, u32[]{:S(2)}, u32[]{:S(2)}) collective-permute-start(bf16[128,1024]{1,0:T(8,128)(2,1)S(1)} %get-tuple-element.39), channel_id=1, source_target_pairs={{0,6},{2,0},{4,2},{6,4},{1,7},{3,1},{5,3},{7,5},{8,14},{10,8},{12,... | collective-permute-start | bytes 786440 | tf_op jit(solution)/shard_map/ppermute | solution.py:27
  60.2 2.4 %collective-permute-start.5 = (bf16[128,1024]{1,0:T(8,128)(2,1)S(1)}, bf16[128,1024]{1,0:T(8,128)(2,1)S(1)}, u32[]{:S(2)}, u32[]{:S(2)}) collective-permute-start(bf16[128,1024]{1,0:T(8,128)(2,1)S(1)} %get-tuple-element.40), channel_id=1, source_target_pairs={{0,4},{2,6},{4,0},{6,2},{1,5},{3,7},{5,1},{7,3},{8,12},{10,14},{12... | collective-permute-start | bytes 786440 | tf_op jit(solution)/shard_map/ppermute | solution.py:27
  62.6 2.3 %all-to-all-done.2.got = f32[4,32,1664]{2,1,0:T(8,128)S(1)} async-done(((f32[4,32,1664]{2,1,0:T(8,128)}), f32[4,32,1664]{2,1,0:T(8,128)S(1)}, u32[]{:S(2)}, u32[]{:S(2)}) %all-to-all-start.2) | async-done | bytes 852000 | tf_op jit(solution)/shard_map/all_to_all | solution.py:22
  64.9 0.9 shard_map.53
  65.7 11.5 %all-to-all-start.3 = ((f32[16,2,1792]{2,1,0:T(2,128)}), f32[16,2,1792]{2,1,0:T(2,128)S(1)}, u32[]{:S(2)}, u32[]{:S(2)}) async-start(f32[16,2,1792]{2,1,0:T(2,128)} %shard_map.53), calls=%async_computation.3 | async-start | bytes 458752 | tf_op jit(solution)/shard_map/all_to_all | solution.py:22
  77.2 0.0 collective-permute-done.4
  77.2 0.0 collective-permute-done.5
  77.3 1.9 %collective-permute-start.6 = (bf16[128,1024]{1,0:T(8,128)(2,1)S(1)}, bf16[128,1024]{1,0:T(8,128)(2,1)S(1)}, u32[]{:S(2)}, u32[]{:S(2)}) collective-permute-start(bf16[128,1024]{1,0:T(8,128)(2,1)S(1)} %get-tuple-element.45), channel_id=1, source_target_pairs={{0,2},{2,4},{4,6},{6,0},{1,3},{3,5},{5,7},{7,1},{8,10},{10,12},{12... | collective-permute-start | bytes 786440 | tf_op jit(solution)/shard_map/ppermute | solution.py:27
  79.4 6.2 %collective-permute-done.6 = bf16[128,1024]{1,0:T(8,128)(2,1)S(1)} collective-permute-done((bf16[128,1024]{1,0:T(8,128)(2,1)S(1)}, bf16[128,1024]{1,0:T(8,128)(2,1)S(1)}, u32[]{:S(2)}, u32[]{:S(2)}) %collective-permute-start.6) | collective-permute-done | bytes 262176 | tf_op jit(solution)/shard_map/ppermute | solution.py:27
  85.7 0.1 pad_maximum_fusion
  85.8 7.6 %collective-permute-start.7 = (bf16[4,128,896]{2,1,0:T(8,128)(2,1)S(1)}, bf16[4,128,896]{2,1,0:T(8,128)(2,1)S(1)}, u32[]{:S(2)}, u32[]{:S(2)}) collective-permute-start(bf16[4,128,896]{2,1,0:T(8,128)(2,1)S(1)} %pad_maximum_fusion), channel_id=1, source_target_pairs={{0,8},{8,0},{1,9},{9,1},{2,10},{10,2},{3,11},{11,3},{4,12},{12,4},... | collective-permute-start | bytes 2752520 | tf_op jit(solution)/shard_map/ppermute | solution.py:27
  93.6 2.0 %collective-permute-done.7 = bf16[4,128,896]{2,1,0:T(8,128)(2,1)S(1)} collective-permute-done((bf16[4,128,896]{2,1,0:T(8,128)(2,1)S(1)}, bf16[4,128,896]{2,1,0:T(8,128)(2,1)S(1)}, u32[]{:S(2)}, u32[]{:S(2)}) %collective-permute-start.7) | collective-permute-done | bytes 917536 | tf_op jit(solution)/shard_map/ppermute | solution.py:27
  95.5 0.1 constant_dynamic-update-slice_fusion
  95.7 0.1 slice_reduce_fusion
  95.8 1.0 exponential_bitcast_fusion
  96.8 0.6 fusion.10
  97.5 0.1 exponential_bitcast_fusion.1.rest_0_
  97.6 0.0 all-to-all-done.3.got
  97.6 0.7 shard_map.54
  98.3 3.6 %all-to-all-start.4 = ((f32[8,4,128]{2,1,0:T(4,128)}), f32[8,4,128]{2,1,0:T(4,128)S(1)}, u32[]{:S(2)}, u32[]{:S(2)}) async-start(f32[8,4,128]{2,1,0:T(4,128)} %shard_map.54), calls=%async_computation.4 | async-start | bytes 32768 | tf_op jit(solution)/shard_map/all_to_all | solution.py:22
  101.9 1.2 %copy.5.rest_1_ = f32[128,1024]{1,0:T(8,128)S(1)} copy(f32[128,1024]{0,1:T(8,128)} %exponential_bitcast_fusion) | data formatting | bytes 1048576 | tf_op jit(solution)/shard_map/optimization_barrier | solution.py:345
  103.1 0.8 shard_map.55
  103.9 2.9 %all-to-all-done.4.got = f32[8,4,128]{2,1,0:T(4,128)S(1)} async-done(((f32[8,4,128]{2,1,0:T(4,128)}), f32[8,4,128]{2,1,0:T(4,128)S(1)}, u32[]{:S(2)}, u32[]{:S(2)}) %all-to-all-start.4) | async-done | bytes 16416 | tf_op jit(solution)/shard_map/all_to_all | solution.py:22
  106.8 1.9 %shard_map.56 = f32[128,768]{1,0:T(8,128)} custom-call(s32[2]{0:T(128)S(1)} %pad_add_fusion.place, f32[8,4,128]{2,1,0:T(4,128)S(1)} %all-to-all-done.4.got, f32[128,1024]{1,0:T(8,128)S(1)} %exponential_bitcast_fusion.1.rest_0_, f32[128,1024]{1,0:T(8,128)S(1)} %copy.5.rest_1_, f32[1,1024]{1,0:T(1,128)S(1)} %bitcast.52, f32[1,1024]{1,0:T(1,128)S(1)} %bitcast.51, ...), custom_call_target="tpu_custom_call" | custom-call | flops 402653184 | bytes 3301376 | tf_op jit(solution)/shard_map/pallas_call | solution.py:281
  (20 shorter events, 0.4 us)
Async XLA Ops:
  2.5 34.2 %all-to-all-start = ((bf16[16,2,4864]{2,1,0:T(2,128)(2,1)}), bf16[16,2,4864]{2,1,0:T(2,128)(2,1)S(1)}, u32[]{:S(2)}, u32[]{:S(2)}) async-start(bf16[16,2,4864]{2,1,0:T(2,128)(2,1)} %shard_map.50), calls=%async_computation | async-start | bytes 622592 | tf_op jit(solution)/shard_map/all_to_all | solution.py:22
  18.3 23.7 %copy-start = (bf16[128,768]{1,0:T(8,128)(2,1)S(1)}, bf16[128,768]{1,0:T(8,128)(2,1)}, u32[]{:S(2)}) copy-start(bf16[128,768]{1,0:T(8,128)(2,1)} %param.4) | copy-start | bytes 589828
  18.3 9.5 %collective-permute-start = (bf16[128,768]{1,0:T(8,128)(2,1)}, bf16[128,768]{1,0:T(8,128)(2,1)S(1)}, u32[]{:S(2)}, u32[]{:S(2)}) collective-permute-start(bf16[128,768]{1,0:T(8,128)(2,1)} %param.4), channel_id=1, source_target_pairs={{0,6},{2,0},{4,2},{6,4},{1,7},{3,1},{5,3},{7,5},{8,14},{10,8},{12,... | collective-permute-start | bytes 589832 | tf_op jit(solution)/shard_map/ppermute | solution.py:27
  22.8 8.8 %collective-permute-start.1 = (bf16[128,768]{1,0:T(8,128)(2,1)}, bf16[128,768]{1,0:T(8,128)(2,1)S(1)}, u32[]{:S(2)}, u32[]{:S(2)}) collective-permute-start(bf16[128,768]{1,0:T(8,128)(2,1)} %param.4), channel_id=1, source_target_pairs={{0,4},{2,6},{4,0},{6,2},{1,5},{3,7},{5,1},{7,3},{8,12},{10,14},{12... | collective-permute-start | bytes 589832 | tf_op jit(solution)/shard_map/ppermute | solution.py:27
  25.2 11.4 %collective-permute-start.2 = (bf16[128,768]{1,0:T(8,128)(2,1)}, bf16[128,768]{1,0:T(8,128)(2,1)S(1)}, u32[]{:S(2)}, u32[]{:S(2)}) collective-permute-start(bf16[128,768]{1,0:T(8,128)(2,1)} %param.4), channel_id=1, source_target_pairs={{0,2},{2,4},{4,6},{6,0},{1,3},{3,5},{5,7},{7,1},{8,10},{10,12},{12... | collective-permute-start | bytes 589832 | tf_op jit(solution)/shard_map/ppermute | solution.py:27
  37.7 10.8 %all-to-all-start.1 = ((bf16[4,32,1792]{2,1,0:T(8,128)(2,1)}), bf16[4,32,1792]{2,1,0:T(8,128)(2,1)S(1)}, u32[]{:S(2)}, u32[]{:S(2)}) async-start(bf16[4,32,1792]{2,1,0:T(8,128)(2,1)} %pad_maximum_fusion.2), calls=%async_computation.1 | async-start | bytes 917504 | tf_op jit(solution)/shard_map/all_to_all | solution.py:22
  42.1 7.3 %collective-permute-start.3 = (bf16[4,128,768]{2,1,0:T(8,128)(2,1)S(1)}, bf16[4,128,768]{2,1,0:T(8,128)(2,1)S(1)}, u32[]{:S(2)}, u32[]{:S(2)}) collective-permute-start(bf16[4,128,768]{2,1,0:T(8,128)(2,1)S(1)} %pad_maximum_fusion.1), channel_id=1, source_target_pairs={{0,8},{8,0},{1,9},{9,1},{2,10},{10,2},{3,11},{11,3},{4,12},{12,4},... | collective-permute-start | bytes 2359304 | tf_op jit(solution)/shard_map/ppermute | solution.py:27
  52.0 12.9 %all-to-all-start.2 = ((f32[4,32,1664]{2,1,0:T(8,128)}), f32[4,32,1664]{2,1,0:T(8,128)S(1)}, u32[]{:S(2)}, u32[]{:S(2)}) async-start(f32[4,32,1664]{2,1,0:T(8,128)} %shard_map.52), calls=%async_computation.2 | async-start | bytes 1703936 | tf_op jit(solution)/shard_map/all_to_all | solution.py:22
  55.8 21.4 %collective-permute-start.4 = (bf16[128,1024]{1,0:T(8,128)(2,1)S(1)}, bf16[128,1024]{1,0:T(8,128)(2,1)S(1)}, u32[]{:S(2)}, u32[]{:S(2)}) collective-permute-start(bf16[128,1024]{1,0:T(8,128)(2,1)S(1)} %get-tuple-element.39), channel_id=1, source_target_pairs={{0,6},{2,0},{4,2},{6,4},{1,7},{3,1},{5,3},{7,5},{8,14},{10,8},{12,... | collective-permute-start | bytes 786440 | tf_op jit(solution)/shard_map/ppermute | solution.py:27
  60.2 17.1 %collective-permute-start.5 = (bf16[128,1024]{1,0:T(8,128)(2,1)S(1)}, bf16[128,1024]{1,0:T(8,128)(2,1)S(1)}, u32[]{:S(2)}, u32[]{:S(2)}) collective-permute-start(bf16[128,1024]{1,0:T(8,128)(2,1)S(1)} %get-tuple-element.40), channel_id=1, source_target_pairs={{0,4},{2,6},{4,0},{6,2},{1,5},{3,7},{5,1},{7,3},{8,12},{10,14},{12... | collective-permute-start | bytes 786440 | tf_op jit(solution)/shard_map/ppermute | solution.py:27
  65.7 31.9 %all-to-all-start.3 = ((f32[16,2,1792]{2,1,0:T(2,128)}), f32[16,2,1792]{2,1,0:T(2,128)S(1)}, u32[]{:S(2)}, u32[]{:S(2)}) async-start(f32[16,2,1792]{2,1,0:T(2,128)} %shard_map.53), calls=%async_computation.3 | async-start | bytes 458752 | tf_op jit(solution)/shard_map/all_to_all | solution.py:22
  77.3 8.3 %collective-permute-start.6 = (bf16[128,1024]{1,0:T(8,128)(2,1)S(1)}, bf16[128,1024]{1,0:T(8,128)(2,1)S(1)}, u32[]{:S(2)}, u32[]{:S(2)}) collective-permute-start(bf16[128,1024]{1,0:T(8,128)(2,1)S(1)} %get-tuple-element.45), channel_id=1, source_target_pairs={{0,2},{2,4},{4,6},{6,0},{1,3},{3,5},{5,7},{7,1},{8,10},{10,12},{12... | collective-permute-start | bytes 786440 | tf_op jit(solution)/shard_map/ppermute | solution.py:27
  85.8 9.7 %collective-permute-start.7 = (bf16[4,128,896]{2,1,0:T(8,128)(2,1)S(1)}, bf16[4,128,896]{2,1,0:T(8,128)(2,1)S(1)}, u32[]{:S(2)}, u32[]{:S(2)}) collective-permute-start(bf16[4,128,896]{2,1,0:T(8,128)(2,1)S(1)} %pad_maximum_fusion), channel_id=1, source_target_pairs={{0,8},{8,0},{1,9},{9,1},{2,10},{10,2},{3,11},{11,3},{4,12},{12,4},... | collective-permute-start | bytes 2752520 | tf_op jit(solution)/shard_map/ppermute | solution.py:27
  98.3 8.5 %all-to-all-start.4 = ((f32[8,4,128]{2,1,0:T(4,128)}), f32[8,4,128]{2,1,0:T(4,128)S(1)}, u32[]{:S(2)}, u32[]{:S(2)}) async-start(f32[8,4,128]{2,1,0:T(4,128)} %shard_map.54), calls=%async_computation.4 | async-start | bytes 32768 | tf_op jit(solution)/shard_map/all_to_all | solution.py:22

commit v9 on v8

--- a/solution.py
+++ b/solution.py
@@ -12,7 +12,6 @@
 names = ("y", "zl", "core", "x", "zh")
 sizes = (4, 8, 2, 4, 2)
 z_axes = ("zh", "zl")
-group_axes = ("core", "x")
 lane = 128
 f32 = jnp.float32
 bf16 = jnp.bfloat16
@@ -192,26 +191,41 @@
     grads[...] = logit_scale * (parts[0] - parts[1])
 
 
-def last_kernel(blocks, nc, nx, place, got, *rest):
-    *sets, grads = rest
+def own_kernel(passages, rows, scores, wanted, tops):
+    pool, dim = passages.shape
+    own = passages[...]
+    for at in range(0, rows.shape[0], 2 * lane):
+        at = slice(at, at + 2 * lane)
+        student = logit_scale * lax.dot_general(
+            own, rows[at, :dim], (((1,), (1,)), ((), ())), preferred_element_type=f32
+        )
+        taught = rows[at, dim : dim + pool].astype(f32).T
+        for values, out, which in ((student, scores, 0), (taught, wanted, 1)):
+            top = jnp.max(values, axis=0, keepdims=True)
+            out[:, at] = jnp.exp(values - top)
+            tops[which : which + 1, at] = top
+
+
+def last_kernel(nc, nx, place, got, scores, wanted, tops, rows, grads):
     count = got.shape[2]
-    dim = grads.shape[1]
-    total = jnp.zeros((2 * grads.shape[0], dim), f32)
-    for j, block in enumerate(blocks):
-        scores, wanted, high_s, high_t, rows = sets[5 * j : 5 * j + 5]
+    pool, dim = grads.shape
+    total = jnp.zeros((2 * pool, dim), f32)
+    for i in range(0, nc * nx, 2):
         pieces = []
-        for i, (c, k) in enumerate(block):
-            of = (place[0] + c) % nc * nx + (place[1] + k) % nx
-            at = slice(i * count, (i + 1) * count)
-            stats = got[of]
-            weight_s = logit_scale * jnp.exp(high_s[:, at] - stats[0:1]) / stats[1:2]
-            weight_t = logit_scale * jnp.exp(high_t[:, at] - stats[2:3]) / stats[3:4]
+        for j in (i, i + 1):
+            c, k = divmod(j, nx)
+            at = slice(j * count, (j + 1) * count)
+            stats = got[(place[1] + k) % nx * nc + (place[0] + c) % nc]
+            weight_s = logit_scale * jnp.exp(tops[0:1, at] - stats[0:1]) / stats[1:2]
+            weight_t = logit_scale * jnp.exp(tops[1:2, at] - stats[2:3]) / stats[3:4]
             grad = weight_s * scores[:, at] - weight_t * wanted[:, at]
             pieces.append(jnp.concatenate(bf16_parts(grad), axis=0))
         total += jnp.dot(
-            jnp.concatenate(pieces, axis=1), rows[:, :dim], preferred_element_type=f32
+            jnp.concatenate(pieces, axis=1),
+            rows[i * count : (i + 2) * count, :dim],
+            preferred_element_type=f32,
         )
-    grads[...] = total[: grads.shape[0]] + total[grads.shape[0] :]
+    grads[...] = total[:pool] + total[pool:]
 
 
 vmem = pl.BlockSpec(memory_space=pltpu.VMEM)
@@ -276,15 +290,14 @@
 
 
 def simple_call(kernel, out, scalars, arrays, flops=0):
-    size = sum(v.size * v.dtype.itemsize for v in arrays) + 4 * out.size
     smem = pl.BlockSpec(memory_space=pltpu.SMEM)
     return pl.pallas_call(
         kernel,
         out_shape=out,
         in_specs=[smem] * len(scalars) + [vmem] * len(arrays),
-        out_specs=vmem,
+        out_specs=(vmem,) * len(out) if isinstance(out, tuple) else vmem,
         compiler_params=pltpu.CompilerParams(vmem_limit_bytes=16 * 2**20),
-        cost_estimate=pl.CostEstimate(flops=flops, bytes_accessed=size, transcendentals=0),
+        cost_estimate=pl.CostEstimate(flops=flops, bytes_accessed=2**16, transcendentals=0),
     )(*scalars, *arrays)
 
 
@@ -327,28 +340,16 @@
     kept = jnp.stack([r[:, : dim + pool] for r in rows])
     away = jnp.stack([jnp.concatenate([r[:, :dim], r[:, dim + pool :]], axis=1) for r in rows])
     every_row = jnp.concatenate([kept, from_next(away, "core", 1)]).reshape(group * count, dim + pool)
-    row_sets = [every_row]
-    blocks = [[(c, k) for c in range(nc) for k in range(nx)]]
-
-    def lifted(values):
-        top = jnp.max(values, axis=0)
-        return jnp.exp(values - top), top
-
-    scores, high_s = lifted(
-        logit_scale
-        * lax.dot_general(
-            passages, every_row[:, :dim], (((1,), (1,)), ((), ())), preferred_element_type=f32
-        )
-    )
-    wanted, high_t = lifted(every_row[:, dim:].T.astype(f32))
-    sets = [scores, wanted, high_s, high_t]
+
+    lifted = jax.ShapeDtypeStruct((pool, group * count), f32)
+    tops = jax.ShapeDtypeStruct((2, group * count), f32)
+    sets = simple_call(own_kernel, (lifted, lifted, tops), [], [passages, every_row], flops=2 * pool * group * count * dim)
     got, *sets = lax.optimization_barrier((got, *sets))
-    sets = [*sets[:2], sets[2][None], sets[3][None], every_row]
     every = simple_call(
         functools.partial(after_kernel, dim), jax.ShapeDtypeStruct((group, 4, count), f32), [], [got]
     )
     got, _ = lax.optimization_barrier((got, every))
-    every = exchange(every, group_axes)
+    every = exchange(every, ("x", "core"))
     query_grad = simple_call(
         functools.partial(query_kernel, count),
         jax.ShapeDtypeStruct((own, dim), f32),
@@ -357,11 +358,10 @@
     )
 
     passage_grad = simple_call(
-        functools.partial(last_kernel, blocks, nc, nx),
+        functools.partial(last_kernel, nc, nx),
         jax.ShapeDtypeStruct((pool, dim), f32),
         [place_of()],
-        [every, *sets],
-        flops=4 * pool * group * count * dim,
+        [every, *sets, every_row],
     )
     return query_grad, passage_grad
 

time: 109 us -> 110 us (level)
  other arithmetic: 2.51 us -> 1.27 us
    unnamed x6 -> x10, local copies, waits for them, and re-layouts: 0.1 us -> 1.95 us
    optimization_barrier x1 -> x0, local copies, waits for them, and re-layouts: 1.24 us -> none  [per_device(): got, *sets = lax.optimization_barrier((got, *sets))]
    pallas_call x4 -> x5, Pallas kernels: 4.16 us -> 4.9 us  [simple_call(): pl.pallas_call(kernel, out_shape=out, in_specs=[smem] * len(scalars) + [v...]
  transfers between devices with their start and end apart: 13 -> 13, of which waited for: 7 -> 7; matrix products, arithmetic and copies ran while one was open for 4% -> 1% of each run, Pallas kernels for 2% -> 3%
where the time goes in v9:
time: 110 us; the launch traced here: 109 us
  starting transfers between devices  69.4 us (63%)
  waiting for transfers between devices  24.9 us (23%)
  Pallas kernels  10.3 us (9%)
  local copies, waits for them, and re-layouts  2.34 us (2%)
  other arithmetic  1.27 us (1%)
    all_to_all x5, starting transfers between devices, exchange(): return lax.all_to_all(values, axes, 0, 0, tiled=True)  38.8 us
    ppermute x8, starting transfers between devices, from_next(): return lax.ppermute(values, axis, [(i, (i - step) % n) for i in range(n)])  30.5 us
    ppermute x8, waiting for transfers between devices, from_next(): return lax.ppermute(values, axis, [(i, (i - step) % n) for i in range(n)])  17.1 us
    all_to_all x5, waiting for transfers between devices, exchange(): return lax.all_to_all(values, axes, 0, 0, tiled=True)  7.87 us
    pallas_call x5, Pallas kernels, simple_call(): pl.pallas_call(kernel, out_shape=out, in_specs=[smem] * len(scalars) + [v...  4.9 us
    pallas_call x1, Pallas kernels, local_parts(): pl.pallas_call(parts_kernel, out_shape=jax.ShapeDtypeStruct((ny, count //...  2.61 us
  transfers between devices with their start and end apart: 13, of which 7 were waited for; matrix products, arithmetic and copies ran while one was open for 1% of the time, Pallas kernels for 3%

profile of v9, /device:TPU:1, one launch (start us, length us, event | category | flops | bytes accessed | tf_op | source)
XLA Modules:
  0.0 109.1 jit_solution(15752561763262919136)
XLA Ops:
  0.6 1.9 %shard_map.50 = bf16[16,2,4864]{2,1,0:T(2,128)(2,1)} custom-call(bf16[2,768]{1,0:T(2,128)(2,1)} %queries_in.1, bf16[2,65536]{1,0:T(2,128)(2,1)} %teacher_in.1), custom_call_target="tpu_custom_call" | custom-call | bytes 1048576 | tf_op jit(solution)/shard_map/pallas_call | solution.py:237
  2.5 15.8 %all-to-all-start = ((bf16[16,2,4864]{2,1,0:T(2,128)(2,1)}), bf16[16,2,4864]{2,1,0:T(2,128)(2,1)S(1)}, u32[]{:S(2)}, u32[]{:S(2)}) async-start(bf16[16,2,4864]{2,1,0:T(2,128)(2,1)} %shard_map.50), calls=%async_computation | async-start | bytes 622592 | tf_op jit(solution)/shard_map/all_to_all | solution.py:21
  18.3 0.0 copy-start
  18.3 4.5 %collective-permute-start = (bf16[128,768]{1,0:T(8,128)(2,1)}, bf16[128,768]{1,0:T(8,128)(2,1)S(1)}, u32[]{:S(2)}, u32[]{:S(2)}) collective-permute-start(bf16[128,768]{1,0:T(8,128)(2,1)} %passages.1), channel_id=1, source_target_pairs={{0,6},{2,0},{4,2},{6,4},{1,7},{3,1},{5,3},{7,5},{8,14},{10,8},{12,... | collective-permute-start | bytes 589832 | tf_op jit(solution)/shard_map/ppermute | solution.py:26
  22.8 2.4 %collective-permute-start.1 = (bf16[128,768]{1,0:T(8,128)(2,1)}, bf16[128,768]{1,0:T(8,128)(2,1)S(1)}, u32[]{:S(2)}, u32[]{:S(2)}) collective-permute-start(bf16[128,768]{1,0:T(8,128)(2,1)} %passages.1), channel_id=1, source_target_pairs={{0,4},{2,6},{4,0},{6,2},{1,5},{3,7},{5,1},{7,3},{8,12},{10,14},{12... | collective-permute-start | bytes 589832 | tf_op jit(solution)/shard_map/ppermute | solution.py:26
  25.2 2.5 %collective-permute-start.2 = (bf16[128,768]{1,0:T(8,128)(2,1)}, bf16[128,768]{1,0:T(8,128)(2,1)S(1)}, u32[]{:S(2)}, u32[]{:S(2)}) collective-permute-start(bf16[128,768]{1,0:T(8,128)(2,1)} %passages.1), channel_id=1, source_target_pairs={{0,2},{2,4},{4,6},{6,0},{1,3},{3,5},{5,7},{7,1},{8,10},{10,12},{12... | collective-permute-start | bytes 589832 | tf_op jit(solution)/shard_map/ppermute | solution.py:26
  27.8 0.0 collective-permute-done
  27.8 3.8 %collective-permute-done.1 = bf16[128,768]{1,0:T(8,128)(2,1)S(1)} collective-permute-done((bf16[128,768]{1,0:T(8,128)(2,1)}, bf16[128,768]{1,0:T(8,128)(2,1)S(1)}, u32[]{:S(2)}, u32[]{:S(2)}) %collective-permute-start.1) | collective-permute-done | bytes 196640 | tf_op jit(solution)/shard_map/ppermute | solution.py:26
  31.6 5.1 %collective-permute-done.2 = bf16[128,768]{1,0:T(8,128)(2,1)S(1)} collective-permute-done((bf16[128,768]{1,0:T(8,128)(2,1)}, bf16[128,768]{1,0:T(8,128)(2,1)S(1)}, u32[]{:S(2)}, u32[]{:S(2)}) %collective-permute-start.2) | collective-permute-done | bytes 196640 | tf_op jit(solution)/shard_map/ppermute | solution.py:26
  36.7 0.0 all-to-all-done
  36.7 0.1 reshape.19
  36.9 0.8 pad_maximum_fusion.2
  37.7 4.2 %all-to-all-start.1 = ((bf16[4,32,1792]{2,1,0:T(8,128)(2,1)}), bf16[4,32,1792]{2,1,0:T(8,128)(2,1)S(1)}, u32[]{:S(2)}, u32[]{:S(2)}) async-start(bf16[4,32,1792]{2,1,0:T(8,128)(2,1)} %pad_maximum_fusion.2), calls=%async_computation.1 | async-start | bytes 917504 | tf_op jit(solution)/shard_map/all_to_all | solution.py:21
  41.9 0.1 pad_add_fusion.place
  42.0 0.0 copy-done
  42.0 0.1 pad_maximum_fusion.1
  42.1 4.7 %collective-permute-start.3 = (bf16[4,128,768]{2,1,0:T(8,128)(2,1)S(1)}, bf16[4,128,768]{2,1,0:T(8,128)(2,1)S(1)}, u32[]{:S(2)}, u32[]{:S(2)}) collective-permute-start(bf16[4,128,768]{2,1,0:T(8,128)(2,1)S(1)} %pad_maximum_fusion.1), channel_id=1, source_target_pairs={{0,8},{8,0},{1,9},{9,1},{2,10},{10,2},{3,11},{11,3},{4,12},{12,4},... | collective-permute-start | bytes 2359304 | tf_op jit(solution)/shard_map/ppermute | solution.py:26
  46.8 1.7 %all-to-all-done.1 = bf16[4,32,1792]{2,1,0:T(8,128)(2,1)S(1)} async-done(((bf16[4,32,1792]{2,1,0:T(8,128)(2,1)}), bf16[4,32,1792]{2,1,0:T(8,128)(2,1)S(1)}, u32[]{:S(2)}, u32[]{:S(2)}) %all-to-all-start.1) | async-done | bytes 458784 | tf_op jit(solution)/shard_map/all_to_all | solution.py:21
  48.5 0.9 shard_map.51
  49.4 0.0 collective-permute-done.3
  49.4 2.6 %shard_map.52 = f32[4,32,1664]{2,1,0:T(8,128)} custom-call(bf16[128,768]{1,0:T(8,128)(2,1)S(1)} %get-tuple-element.30.block, bf16[128,1024]{1,0:T(8,128)(2,1)S(1)} %get-tuple-element.31.high, bf16[128,1024]{1,0:T(8,128)(2,1)S(1)} %get-tuple-element.32.low, f32[32,128]{1,0:T(8,128)S(1)} %get-tuple-element.33.taught, bf16[512,768]{1,0:T(8,128)(2,1)S(1)} %bitcast.40, ...), custom_call_target="tpu_custom_call" | custom-call | flops 1006632960 | bytes 4194304 | tf_op jit(solution)/shard_map/pallas_call | solution.py:278
  52.0 3.8 %all-to-all-start.2 = ((f32[4,32,1664]{2,1,0:T(8,128)}), f32[4,32,1664]{2,1,0:T(8,128)S(1)}, u32[]{:S(2)}, u32[]{:S(2)}) async-start(f32[4,32,1664]{2,1,0:T(8,128)} %shard_map.52), calls=%async_computation.2 | async-start | bytes 1703936 | tf_op jit(solution)/shard_map/all_to_all | solution.py:21
  55.8 4.4 %collective-permute-start.4 = (bf16[128,1024]{1,0:T(8,128)(2,1)S(1)}, bf16[128,1024]{1,0:T(8,128)(2,1)S(1)}, u32[]{:S(2)}, u32[]{:S(2)}) collective-permute-start(bf16[128,1024]{1,0:T(8,128)(2,1)S(1)} %get-tuple-element.41), channel_id=1, source_target_pairs={{0,6},{2,0},{4,2},{6,4},{1,7},{3,1},{5,3},{7,5},{8,14},{10,8},{12,... | collective-permute-start | bytes 786440 | tf_op jit(solution)/shard_map/ppermute | solution.py:26
  60.2 2.4 %collective-permute-start.5 = (bf16[128,1024]{1,0:T(8,128)(2,1)S(1)}, bf16[128,1024]{1,0:T(8,128)(2,1)S(1)}, u32[]{:S(2)}, u32[]{:S(2)}) collective-permute-start(bf16[128,1024]{1,0:T(8,128)(2,1)S(1)} %get-tuple-element.42), channel_id=1, source_target_pairs={{0,4},{2,6},{4,0},{6,2},{1,5},{3,7},{5,1},{7,3},{8,12},{10,14},{12... | collective-permute-start | bytes 786440 | tf_op jit(solution)/shard_map/ppermute | solution.py:26
  62.6 2.3 %all-to-all-done.2.got = f32[4,32,1664]{2,1,0:T(8,128)S(1)} async-done(((f32[4,32,1664]{2,1,0:T(8,128)}), f32[4,32,1664]{2,1,0:T(8,128)S(1)}, u32[]{:S(2)}, u32[]{:S(2)}) %all-to-all-start.2) | async-done | bytes 852000 | tf_op jit(solution)/shard_map/all_to_all | solution.py:21
  64.9 0.9 shard_map.53
  65.8 11.5 %all-to-all-start.3 = ((f32[16,2,1792]{2,1,0:T(2,128)}), f32[16,2,1792]{2,1,0:T(2,128)S(1)}, u32[]{:S(2)}, u32[]{:S(2)}) async-start(f32[16,2,1792]{2,1,0:T(2,128)} %shard_map.53), calls=%async_computation.3 | async-start | bytes 458752 | tf_op jit(solution)/shard_map/all_to_all | solution.py:21
  77.2 0.0 collective-permute-done.4
  77.3 0.0 collective-permute-done.5
  77.3 1.9 %collective-permute-start.6 = (bf16[128,1024]{1,0:T(8,128)(2,1)S(1)}, bf16[128,1024]{1,0:T(8,128)(2,1)S(1)}, u32[]{:S(2)}, u32[]{:S(2)}) collective-permute-start(bf16[128,1024]{1,0:T(8,128)(2,1)S(1)} %get-tuple-element.47), channel_id=1, source_target_pairs={{0,2},{2,4},{4,6},{6,0},{1,3},{3,5},{5,7},{7,1},{8,10},{10,12},{12... | collective-permute-start | bytes 786440 | tf_op jit(solution)/shard_map/ppermute | solution.py:26
  79.4 6.2 %collective-permute-done.6 = bf16[128,1024]{1,0:T(8,128)(2,1)S(1)} collective-permute-done((bf16[128,1024]{1,0:T(8,128)(2,1)S(1)}, bf16[128,1024]{1,0:T(8,128)(2,1)S(1)}, u32[]{:S(2)}, u32[]{:S(2)}) %collective-permute-start.6) | collective-permute-done | bytes 262176 | tf_op jit(solution)/shard_map/ppermute | solution.py:26
  85.7 0.1 pad_maximum_fusion
  85.8 7.6 %collective-permute-start.7 = (bf16[4,128,896]{2,1,0:T(8,128)(2,1)S(1)}, bf16[4,128,896]{2,1,0:T(8,128)(2,1)S(1)}, u32[]{:S(2)}, u32[]{:S(2)}) collective-permute-start(bf16[4,128,896]{2,1,0:T(8,128)(2,1)S(1)} %pad_maximum_fusion), channel_id=1, source_target_pairs={{0,8},{8,0},{1,9},{9,1},{2,10},{10,2},{3,11},{11,3},{4,12},{12,4},... | collective-permute-start | bytes 2752520 | tf_op jit(solution)/shard_map/ppermute | solution.py:26
  93.6 2.0 %collective-permute-done.7 = bf16[4,128,896]{2,1,0:T(8,128)(2,1)S(1)} collective-permute-done((bf16[4,128,896]{2,1,0:T(8,128)(2,1)S(1)}, bf16[4,128,896]{2,1,0:T(8,128)(2,1)S(1)}, u32[]{:S(2)}, u32[]{:S(2)}) %collective-permute-start.7) | collective-permute-done | bytes 917536 | tf_op jit(solution)/shard_map/ppermute | solution.py:26
  95.6 0.1 constant_dynamic-update-slice_fusion
  95.7 0.8 shard_map.54
  96.5 0.0 copy-start.1
  96.5 0.8 copy-done.1
  97.3 0.0 all-to-all-done.3.got
  97.3 0.7 shard_map.55
  97.9 3.6 %all-to-all-start.4 = ((f32[8,4,128]{2,1,0:T(4,128)}), f32[8,4,128]{2,1,0:T(4,128)S(1)}, u32[]{:S(2)}, u32[]{:S(2)}) async-start(f32[8,4,128]{2,1,0:T(4,128)} %shard_map.55), calls=%async_computation.4 | async-start | bytes 32768 | tf_op jit(solution)/shard_map/all_to_all | solution.py:21
  101.5 0.8 shard_map.56
  102.3 3.9 %all-to-all-done.4.got = f32[8,4,128]{2,1,0:T(4,128)S(1)} async-done(((f32[8,4,128]{2,1,0:T(4,128)}), f32[8,4,128]{2,1,0:T(4,128)S(1)}, u32[]{:S(2)}, u32[]{:S(2)}) %all-to-all-start.4) | async-done | bytes 16416 | tf_op jit(solution)/shard_map/all_to_all | solution.py:21
  106.2 0.0 copy-start.2
  106.2 1.0 copy-done.2
  107.3 1.9 %shard_map.57 = f32[128,768]{1,0:T(8,128)} custom-call(s32[2]{0:T(128)S(1)} %pad_add_fusion.place, f32[8,4,128]{2,1,0:T(4,128)S(1)} %all-to-all-done.4.got, f32[128,1024]{1,0:T(8,128)S(1)} %get-tuple-element.53.scores, f32[128,1024]{1,0:T(8,128)S(1)} %copy-done.2, f32[2,1024]{1,0:T(2,128)S(1)} %get-tuple-element.55.tops, bf16[1024,896]{1,0:T(8,128)(2,1)S(1)} %bitcast.39), custom_call_target="tpu_custom_call" | custom-call | bytes 65536 | tf_op jit(solution)/shard_map/pallas_call | solution.py:294
  (19 shorter events, 0.4 us)
Async XLA Ops:
  2.5 34.2 %all-to-all-start = ((bf16[16,2,4864]{2,1,0:T(2,128)(2,1)}), bf16[16,2,4864]{2,1,0:T(2,128)(2,1)S(1)}, u32[]{:S(2)}, u32[]{:S(2)}) async-start(bf16[16,2,4864]{2,1,0:T(2,128)(2,1)} %shard_map.50), calls=%async_computation | async-start | bytes 622592 | tf_op jit(solution)/shard_map/all_to_all | solution.py:21
  18.3 23.7 %copy-start = (bf16[128,768]{1,0:T(8,128)(2,1)S(1)}, bf16[128,768]{1,0:T(8,128)(2,1)}, u32[]{:S(2)}) copy-start(bf16[128,768]{1,0:T(8,128)(2,1)} %passages.1) | copy-start | bytes 589828
  18.3 9.5 %collective-permute-start = (bf16[128,768]{1,0:T(8,128)(2,1)}, bf16[128,768]{1,0:T(8,128)(2,1)S(1)}, u32[]{:S(2)}, u32[]{:S(2)}) collective-permute-start(bf16[128,768]{1,0:T(8,128)(2,1)} %passages.1), channel_id=1, source_target_pairs={{0,6},{2,0},{4,2},{6,4},{1,7},{3,1},{5,3},{7,5},{8,14},{10,8},{12,... | collective-permute-start | bytes 589832 | tf_op jit(solution)/shard_map/ppermute | solution.py:26
  22.8 8.8 %collective-permute-start.1 = (bf16[128,768]{1,0:T(8,128)(2,1)}, bf16[128,768]{1,0:T(8,128)(2,1)S(1)}, u32[]{:S(2)}, u32[]{:S(2)}) collective-permute-start(bf16[128,768]{1,0:T(8,128)(2,1)} %passages.1), channel_id=1, source_target_pairs={{0,4},{2,6},{4,0},{6,2},{1,5},{3,7},{5,1},{7,3},{8,12},{10,14},{12... | collective-permute-start | bytes 589832 | tf_op jit(solution)/shard_map/ppermute | solution.py:26
  25.2 11.4 %collective-permute-start.2 = (bf16[128,768]{1,0:T(8,128)(2,1)}, bf16[128,768]{1,0:T(8,128)(2,1)S(1)}, u32[]{:S(2)}, u32[]{:S(2)}) collective-permute-start(bf16[128,768]{1,0:T(8,128)(2,1)} %passages.1), channel_id=1, source_target_pairs={{0,2},{2,4},{4,6},{6,0},{1,3},{3,5},{5,7},{7,1},{8,10},{10,12},{12... | collective-permute-start | bytes 589832 | tf_op jit(solution)/shard_map/ppermute | solution.py:26
  37.7 10.8 %all-to-all-start.1 = ((bf16[4,32,1792]{2,1,0:T(8,128)(2,1)}), bf16[4,32,1792]{2,1,0:T(8,128)(2,1)S(1)}, u32[]{:S(2)}, u32[]{:S(2)}) async-start(bf16[4,32,1792]{2,1,0:T(8,128)(2,1)} %pad_maximum_fusion.2), calls=%async_computation.1 | async-start | bytes 917504 | tf_op jit(solution)/shard_map/all_to_all | solution.py:21
  42.1 7.3 %collective-permute-start.3 = (bf16[4,128,768]{2,1,0:T(8,128)(2,1)S(1)}, bf16[4,128,768]{2,1,0:T(8,128)(2,1)S(1)}, u32[]{:S(2)}, u32[]{:S(2)}) collective-permute-start(bf16[4,128,768]{2,1,0:T(8,128)(2,1)S(1)} %pad_maximum_fusion.1), channel_id=1, source_target_pairs={{0,8},{8,0},{1,9},{9,1},{2,10},{10,2},{3,11},{11,3},{4,12},{12,4},... | collective-permute-start | bytes 2359304 | tf_op jit(solution)/shard_map/ppermute | solution.py:26
  52.0 12.9 %all-to-all-start.2 = ((f32[4,32,1664]{2,1,0:T(8,128)}), f32[4,32,1664]{2,1,0:T(8,128)S(1)}, u32[]{:S(2)}, u32[]{:S(2)}) async-start(f32[4,32,1664]{2,1,0:T(8,128)} %shard_map.52), calls=%async_computation.2 | async-start | bytes 1703936 | tf_op jit(solution)/shard_map/all_to_all | solution.py:21
  55.8 21.4 %collective-permute-start.4 = (bf16[128,1024]{1,0:T(8,128)(2,1)S(1)}, bf16[128,1024]{1,0:T(8,128)(2,1)S(1)}, u32[]{:S(2)}, u32[]{:S(2)}) collective-permute-start(bf16[128,1024]{1,0:T(8,128)(2,1)S(1)} %get-tuple-element.41), channel_id=1, source_target_pairs={{0,6},{2,0},{4,2},{6,4},{1,7},{3,1},{5,3},{7,5},{8,14},{10,8},{12,... | collective-permute-start | bytes 786440 | tf_op jit(solution)/shard_map/ppermute | solution.py:26
  60.2 17.1 %collective-permute-start.5 = (bf16[128,1024]{1,0:T(8,128)(2,1)S(1)}, bf16[128,1024]{1,0:T(8,128)(2,1)S(1)}, u32[]{:S(2)}, u32[]{:S(2)}) collective-permute-start(bf16[128,1024]{1,0:T(8,128)(2,1)S(1)} %get-tuple-element.42), channel_id=1, source_target_pairs={{0,4},{2,6},{4,0},{6,2},{1,5},{3,7},{5,1},{7,3},{8,12},{10,14},{12... | collective-permute-start | bytes 786440 | tf_op jit(solution)/shard_map/ppermute | solution.py:26
  65.8 31.5 %all-to-all-start.3 = ((f32[16,2,1792]{2,1,0:T(2,128)}), f32[16,2,1792]{2,1,0:T(2,128)S(1)}, u32[]{:S(2)}, u32[]{:S(2)}) async-start(f32[16,2,1792]{2,1,0:T(2,128)} %shard_map.53), calls=%async_computation.3 | async-start | bytes 458752 | tf_op jit(solution)/shard_map/all_to_all | solution.py:21
  77.3 8.3 %collective-permute-start.6 = (bf16[128,1024]{1,0:T(8,128)(2,1)S(1)}, bf16[128,1024]{1,0:T(8,128)(2,1)S(1)}, u32[]{:S(2)}, u32[]{:S(2)}) collective-permute-start(bf16[128,1024]{1,0:T(8,128)(2,1)S(1)} %get-tuple-element.47), channel_id=1, source_target_pairs={{0,2},{2,4},{4,6},{6,0},{1,3},{3,5},{5,7},{7,1},{8,10},{10,12},{12... | collective-permute-start | bytes 786440 | tf_op jit(solution)/shard_map/ppermute | solution.py:26
  85.8 9.7 %collective-permute-start.7 = (bf16[4,128,896]{2,1,0:T(8,128)(2,1)S(1)}, bf16[4,128,896]{2,1,0:T(8,128)(2,1)S(1)}, u32[]{:S(2)}, u32[]{:S(2)}) collective-permute-start(bf16[4,128,896]{2,1,0:T(8,128)(2,1)S(1)} %pad_maximum_fusion), channel_id=1, source_target_pairs={{0,8},{8,0},{1,9},{9,1},{2,10},{10,2},{3,11},{11,3},{4,12},{12,4},... | collective-permute-start | bytes 2752520 | tf_op jit(solution)/shard_map/ppermute | solution.py:26
  96.5 0.8 copy-start.1
  97.9 8.3 %all-to-all-start.4 = ((f32[8,4,128]{2,1,0:T(4,128)}), f32[8,4,128]{2,1,0:T(4,128)S(1)}, u32[]{:S(2)}, u32[]{:S(2)}) async-start(f32[8,4,128]{2,1,0:T(4,128)} %shard_map.55), calls=%async_computation.4 | async-start | bytes 32768 | tf_op jit(solution)/shard_map/all_to_all | solution.py:21
  106.2 1.0 copy-start.2

commit v10 on v9

--- a/solution.py
+++ b/solution.py
@@ -191,7 +191,7 @@
     grads[...] = logit_scale * (parts[0] - parts[1])
 
 
-def own_kernel(passages, rows, scores, wanted, tops):
+def own_kernel(passages, rows, lifted, tops):
     pool, dim = passages.shape
     own = passages[...]
     for at in range(0, rows.shape[0], 2 * lane):
@@ -200,13 +200,13 @@
             own, rows[at, :dim], (((1,), (1,)), ((), ())), preferred_element_type=f32
         )
         taught = rows[at, dim : dim + pool].astype(f32).T
-        for values, out, which in ((student, scores, 0), (taught, wanted, 1)):
+        for which, values in enumerate((student, taught)):
             top = jnp.max(values, axis=0, keepdims=True)
-            out[:, at] = jnp.exp(values - top)
+            lifted[which, :, at] = jnp.exp(values - top)
             tops[which : which + 1, at] = top
 
 
-def last_kernel(nc, nx, place, got, scores, wanted, tops, rows, grads):
+def last_kernel(nc, nx, place, got, lifted, tops, rows, grads):
     count = got.shape[2]
     pool, dim = grads.shape
     total = jnp.zeros((2 * pool, dim), f32)
@@ -218,7 +218,7 @@
             stats = got[(place[1] + k) % nx * nc + (place[0] + c) % nc]
             weight_s = logit_scale * jnp.exp(tops[0:1, at] - stats[0:1]) / stats[1:2]
             weight_t = logit_scale * jnp.exp(tops[1:2, at] - stats[2:3]) / stats[3:4]
-            grad = weight_s * scores[:, at] - weight_t * wanted[:, at]
+            grad = weight_s * lifted[0, :, at] - weight_t * lifted[1, :, at]
             pieces.append(jnp.concatenate(bf16_parts(grad), axis=0))
         total += jnp.dot(
             jnp.concatenate(pieces, axis=1),
@@ -341,10 +341,9 @@
     away = jnp.stack([jnp.concatenate([r[:, :dim], r[:, dim + pool :]], axis=1) for r in rows])
     every_row = jnp.concatenate([kept, from_next(away, "core", 1)]).reshape(group * count, dim + pool)
 
-    lifted = jax.ShapeDtypeStruct((pool, group * count), f32)
+    lifted = jax.ShapeDtypeStruct((2, pool, group * count), f32)
     tops = jax.ShapeDtypeStruct((2, group * count), f32)
-    sets = simple_call(own_kernel, (lifted, lifted, tops), [], [passages, every_row], flops=2 * pool * group * count * dim)
-    got, *sets = lax.optimization_barrier((got, *sets))
+    sets = simple_call(own_kernel, (lifted, tops), [], [passages, every_row], flops=2 * pool * group * count * dim)
     every = simple_call(
         functools.partial(after_kernel, dim), jax.ShapeDtypeStruct((group, 4, count), f32), [], [got]
     )

time: 110 us -> 109 us (level)
  waiting for transfers between devices: 24.9 us -> 20.9 us
    all_to_all x5, waiting for transfers between devices: 7.87 us -> 5.82 us  [exchange(): return lax.all_to_all(values, axes, 0, 0, tiled=True)]
    ppermute x8, waiting for transfers between devices: 17.1 us -> 15.1 us  [from_next(): return lax.ppermute(values, axis, [(i, (i - step) % n) for i in range(n)])]
    all_to_all x5, starting transfers between devices: 38.8 us -> 40.2 us  [exchange(): return lax.all_to_all(values, axes, 0, 0, tiled=True)]
    concatenate x1, local copies, waits for them, and re-layouts: 0.13 us -> 1.31 us  [per_device(): jnp.concatenate([kept, from_next(away, 'core', 1)])]
  transfers between devices with their start and end apart: 13 -> 13, of which waited for: 7 -> 6; matrix products, arithmetic and copies ran while one was open for 1% -> 4% of each run, Pallas kernels for 3% -> 4%
where the time goes in v10:
time: 109 us; the launch traced here: 108 us
  starting transfers between devices  70.3 us (64%)
  waiting for transfers between devices  20.9 us (19%)
  Pallas kernels  10.3 us (9%)
  local copies, waits for them, and re-layouts  3.33 us (3%)
  other arithmetic  2.22 us (2%)
    all_to_all x5, starting transfers between devices, exchange(): return lax.all_to_all(values, axes, 0, 0, tiled=True)  40.2 us
    ppermute x8, starting transfers between devices, from_next(): return lax.ppermute(values, axis, [(i, (i - step) % n) for i in range(n)])  30.1 us
    ppermute x8, waiting for transfers between devices, from_next(): return lax.ppermute(values, axis, [(i, (i - step) % n) for i in range(n)])  15.1 us
    all_to_all x5, waiting for transfers between devices, exchange(): return lax.all_to_all(values, axes, 0, 0, tiled=True)  5.82 us
    pallas_call x5, Pallas kernels, simple_call(): pl.pallas_call(kernel, out_shape=out, in_specs=[smem] * len(scalars) + [v...  4.88 us
    pallas_call x1, Pallas kernels, local_parts(): pl.pallas_call(parts_kernel, out_shape=jax.ShapeDtypeStruct((ny, count //...  2.62 us
  transfers between devices with their start and end apart: 13, of which 6 were waited for; matrix products, arithmetic and copies ran while one was open for 4% of the time, Pallas kernels for 4%

profile of v10, /device:TPU:1, one launch (start us, length us, event | category | flops | bytes accessed | tf_op | source)
XLA Modules:
  0.0 108.0 jit_solution(4796786940634447198)
XLA Ops:
  0.6 1.9 %shard_map.50 = bf16[16,2,4864]{2,1,0:T(2,128)(2,1)} custom-call(bf16[2,768]{1,0:T(2,128)(2,1)} %queries_in.1, bf16[2,65536]{1,0:T(2,128)(2,1)} %teacher_in.1), custom_call_target="tpu_custom_call" | custom-call | bytes 1048576 | tf_op jit(solution)/shard_map/pallas_call | solution.py:237
  2.5 15.8 %all-to-all-start = ((bf16[16,2,4864]{2,1,0:T(2,128)(2,1)}), bf16[16,2,4864]{2,1,0:T(2,128)(2,1)S(1)}, u32[]{:S(2)}, u32[]{:S(2)}) async-start(bf16[16,2,4864]{2,1,0:T(2,128)(2,1)} %shard_map.50), calls=%async_computation | async-start | bytes 622592 | tf_op jit(solution)/shard_map/all_to_all | solution.py:21
  18.3 0.0 copy-start
  18.3 4.5 %collective-permute-start = (bf16[128,768]{1,0:T(8,128)(2,1)}, bf16[128,768]{1,0:T(8,128)(2,1)S(1)}, u32[]{:S(2)}, u32[]{:S(2)}) collective-permute-start(bf16[128,768]{1,0:T(8,128)(2,1)} %passages.1), channel_id=1, source_target_pairs={{0,6},{2,0},{4,2},{6,4},{1,7},{3,1},{5,3},{7,5},{8,14},{10,8},{12,... | collective-permute-start | bytes 589832 | tf_op jit(solution)/shard_map/ppermute | solution.py:26
  22.8 2.4 %collective-permute-start.1 = (bf16[128,768]{1,0:T(8,128)(2,1)}, bf16[128,768]{1,0:T(8,128)(2,1)S(1)}, u32[]{:S(2)}, u32[]{:S(2)}) collective-permute-start(bf16[128,768]{1,0:T(8,128)(2,1)} %passages.1), channel_id=1, source_target_pairs={{0,4},{2,6},{4,0},{6,2},{1,5},{3,7},{5,1},{7,3},{8,12},{10,14},{12... | collective-permute-start | bytes 589832 | tf_op jit(solution)/shard_map/ppermute | solution.py:26
  25.2 2.5 %collective-permute-start.2 = (bf16[128,768]{1,0:T(8,128)(2,1)}, bf16[128,768]{1,0:T(8,128)(2,1)S(1)}, u32[]{:S(2)}, u32[]{:S(2)}) collective-permute-start(bf16[128,768]{1,0:T(8,128)(2,1)} %passages.1), channel_id=1, source_target_pairs={{0,2},{2,4},{4,6},{6,0},{1,3},{3,5},{5,7},{7,1},{8,10},{10,12},{12... | collective-permute-start | bytes 589832 | tf_op jit(solution)/shard_map/ppermute | solution.py:26
  27.8 0.0 collective-permute-done
  27.8 3.8 %collective-permute-done.1 = bf16[128,768]{1,0:T(8,128)(2,1)S(1)} collective-permute-done((bf16[128,768]{1,0:T(8,128)(2,1)}, bf16[128,768]{1,0:T(8,128)(2,1)S(1)}, u32[]{:S(2)}, u32[]{:S(2)}) %collective-permute-start.1) | collective-permute-done | bytes 196640 | tf_op jit(solution)/shard_map/ppermute | solution.py:26
  31.6 5.1 %collective-permute-done.2 = bf16[128,768]{1,0:T(8,128)(2,1)S(1)} collective-permute-done((bf16[128,768]{1,0:T(8,128)(2,1)}, bf16[128,768]{1,0:T(8,128)(2,1)S(1)}, u32[]{:S(2)}, u32[]{:S(2)}) %collective-permute-start.2) | collective-permute-done | bytes 196640 | tf_op jit(solution)/shard_map/ppermute | solution.py:26
  36.7 0.0 all-to-all-done
  36.7 0.1 reshape.19
  36.9 0.8 pad_maximum_fusion.2
  37.7 4.2 %all-to-all-start.1 = ((bf16[4,32,1792]{2,1,0:T(8,128)(2,1)}), bf16[4,32,1792]{2,1,0:T(8,128)(2,1)S(1)}, u32[]{:S(2)}, u32[]{:S(2)}) async-start(bf16[4,32,1792]{2,1,0:T(8,128)(2,1)} %pad_maximum_fusion.2), calls=%async_computation.1 | async-start | bytes 917504 | tf_op jit(solution)/shard_map/all_to_all | solution.py:21
  41.9 0.1 pad_add_fusion.place
  42.0 0.1 pad_maximum_fusion.1
  42.1 4.7 %collective-permute-start.3 = (bf16[4,128,768]{2,1,0:T(8,128)(2,1)S(1)}, bf16[4,128,768]{2,1,0:T(8,128)(2,1)S(1)}, u32[]{:S(2)}, u32[]{:S(2)}) collective-permute-start(bf16[4,128,768]{2,1,0:T(8,128)(2,1)S(1)} %pad_maximum_fusion.1), channel_id=1, source_target_pairs={{0,8},{8,0},{1,9},{9,1},{2,10},{10,2},{3,11},{11,3},{4,12},{12,4},... | collective-permute-start | bytes 2359304 | tf_op jit(solution)/shard_map/ppermute | solution.py:26
  46.8 1.7 %all-to-all-done.1 = bf16[4,32,1792]{2,1,0:T(8,128)(2,1)S(1)} async-done(((bf16[4,32,1792]{2,1,0:T(8,128)(2,1)}), bf16[4,32,1792]{2,1,0:T(8,128)(2,1)S(1)}, u32[]{:S(2)}, u32[]{:S(2)}) %all-to-all-start.1) | async-done | bytes 458784 | tf_op jit(solution)/shard_map/all_to_all | solution.py:21
  48.5 0.9 shard_map.51
  49.4 0.0 copy-start.1
  49.4 0.7 copy-done.1
  50.1 0.0 collective-permute-done.3
  50.1 2.6 %shard_map.52 = f32[4,32,1664]{2,1,0:T(8,128)} custom-call(bf16[128,768]{1,0:T(8,128)(2,1)S(1)} %get-tuple-element.25.block, bf16[128,1024]{1,0:T(8,128)(2,1)S(1)} %get-tuple-element.26.high, bf16[128,1024]{1,0:T(8,128)(2,1)S(1)} %get-tuple-element.27.low, f32[32,128]{1,0:T(8,128)S(1)} %get-tuple-element.28.taught, bf16[512,768]{1,0:T(8,128)(2,1)S(1)} %bitcast.40, ...), custom_call_target="tpu_custom_call" | custom-call | flops 1006632960 | bytes 4194304 | tf_op jit(solution)/shard_map/pallas_call | solution.py:278
  52.7 3.5 %all-to-all-start.2 = ((f32[4,32,1664]{2,1,0:T(8,128)}), f32[4,32,1664]{2,1,0:T(8,128)S(1)}, u32[]{:S(2)}, u32[]{:S(2)}) async-start(f32[4,32,1664]{2,1,0:T(8,128)} %shard_map.52), calls=%async_computation.2 | async-start | bytes 1703936 | tf_op jit(solution)/shard_map/all_to_all | solution.py:21
  56.2 4.0 %collective-permute-start.4 = (bf16[128,1024]{1,0:T(8,128)(2,1)S(1)}, bf16[128,1024]{1,0:T(8,128)(2,1)S(1)}, u32[]{:S(2)}, u32[]{:S(2)}) collective-permute-start(bf16[128,1024]{1,0:T(8,128)(2,1)S(1)} %copy-done.2), channel_id=1, source_target_pairs={{0,6},{2,0},{4,2},{6,4},{1,7},{3,1},{5,3},{7,5},{8,14},{10,8},{12,... | collective-permute-start | bytes 786440 | tf_op jit(solution)/shard_map/ppermute | solution.py:26
  60.2 2.4 %collective-permute-start.5 = (bf16[128,1024]{1,0:T(8,128)(2,1)S(1)}, bf16[128,1024]{1,0:T(8,128)(2,1)S(1)}, u32[]{:S(2)}, u32[]{:S(2)}) collective-permute-start(bf16[128,1024]{1,0:T(8,128)(2,1)S(1)} %get-tuple-element.38), channel_id=1, source_target_pairs={{0,4},{2,6},{4,0},{6,2},{1,5},{3,7},{5,1},{7,3},{8,12},{10,14},{12... | collective-permute-start | bytes 786440 | tf_op jit(solution)/shard_map/ppermute | solution.py:26
  62.7 2.3 %all-to-all-done.2.got = f32[4,32,1664]{2,1,0:T(8,128)S(1)} async-done(((f32[4,32,1664]{2,1,0:T(8,128)}), f32[4,32,1664]{2,1,0:T(8,128)S(1)}, u32[]{:S(2)}, u32[]{:S(2)}) %all-to-all-start.2) | async-done | bytes 852000 | tf_op jit(solution)/shard_map/all_to_all | solution.py:21
  65.0 0.8 shard_map.53
  65.8 12.1 %all-to-all-start.3 = ((f32[16,2,1792]{2,1,0:T(2,128)}), f32[16,2,1792]{2,1,0:T(2,128)S(1)}, u32[]{:S(2)}, u32[]{:S(2)}) async-start(f32[16,2,1792]{2,1,0:T(2,128)} %shard_map.53), calls=%async_computation.3 | async-start | bytes 458752 | tf_op jit(solution)/shard_map/all_to_all | solution.py:21
  77.9 0.0 collective-permute-done.4
  77.9 0.0 copy-start.3
  78.0 0.0 collective-permute-done.5
  78.0 1.9 %collective-permute-start.6 = (bf16[128,1024]{1,0:T(8,128)(2,1)S(1)}, bf16[128,1024]{1,0:T(8,128)(2,1)S(1)}, u32[]{:S(2)}, u32[]{:S(2)}) collective-permute-start(bf16[128,1024]{1,0:T(8,128)(2,1)S(1)} %get-tuple-element.43), channel_id=1, source_target_pairs={{0,2},{2,4},{4,6},{6,0},{1,3},{3,5},{5,7},{7,1},{8,10},{10,12},{12... | collective-permute-start | bytes 786440 | tf_op jit(solution)/shard_map/ppermute | solution.py:26
  80.0 0.0 copy-done.3
  80.1 0.0 copy-start.4
  80.2 6.2 %collective-permute-done.6 = bf16[128,1024]{1,0:T(8,128)(2,1)S(1)} collective-permute-done((bf16[128,1024]{1,0:T(8,128)(2,1)S(1)}, bf16[128,1024]{1,0:T(8,128)(2,1)S(1)}, u32[]{:S(2)}, u32[]{:S(2)}) %collective-permute-start.6) | collective-permute-done | bytes 262176 | tf_op jit(solution)/shard_map/ppermute | solution.py:26
  86.4 0.0 copy-done.5
  86.4 1.1 pad_maximum_fusion
  87.5 7.6 %collective-permute-start.7 = (bf16[4,128,896]{2,1,0:T(8,128)(2,1)}, bf16[4,128,896]{2,1,0:T(8,128)(2,1)}, u32[]{:S(2)}, u32[]{:S(2)}) collective-permute-start(bf16[4,128,896]{2,1,0:T(8,128)(2,1)} %pad_maximum_fusion), channel_id=1, source_target_pairs={{0,8},{8,0},{1,9},{9,1},{2,10},{10,2},{3,11},{11,3},{4,12},{12,4},... | collective-permute-start | bytes 2752520 | tf_op jit(solution)/shard_map/ppermute | solution.py:26
  95.2 1.0 bitcast_dynamic-update-slice_fusion
  96.2 0.0 all-to-all-done.3.got
  96.2 0.7 shard_map.54
  96.9 4.6 %all-to-all-start.4 = ((f32[8,4,128]{2,1,0:T(4,128)}), f32[8,4,128]{2,1,0:T(4,128)S(1)}, u32[]{:S(2)}, u32[]{:S(2)}) async-start(f32[8,4,128]{2,1,0:T(4,128)} %shard_map.54), calls=%async_computation.4 | async-start | bytes 32768 | tf_op jit(solution)/shard_map/all_to_all | solution.py:21
  101.5 0.8 shard_map.55
  102.3 0.0 collective-permute-done.7
  102.3 1.3 %constant_dynamic-update-slice_fusion = bf16[8,128,896]{2,1,0:T(8,128)(2,1)S(1)} fusion(bf16[8,128,896]{2,1,0:T(8,128)(2,1)S(1)} %fusion, bf16[4,128,896]{2,1,0:T(8,128)(2,1)} %collective-permute-done.7), kind=kLoop, calls=%fused_computation.19 | loop fusion | bytes 1835008 | tf_op jit(solution)/shard_map/concatenate | solution.py:342
  103.6 0.7 shard_map.56
  104.3 1.8 %all-to-all-done.4.got = f32[8,4,128]{2,1,0:T(4,128)S(1)} async-done(((f32[8,4,128]{2,1,0:T(4,128)}), f32[8,4,128]{2,1,0:T(4,128)S(1)}, u32[]{:S(2)}, u32[]{:S(2)}) %all-to-all-start.4) | async-done | bytes 16416 | tf_op jit(solution)/shard_map/all_to_all | solution.py:21
  106.2 1.9 %shard_map.57 = f32[128,768]{1,0:T(8,128)} custom-call(s32[2]{0:T(128)S(1)} %pad_add_fusion.place, f32[8,4,128]{2,1,0:T(4,128)S(1)} %all-to-all-done.4.got, f32[2,128,1024]{2,1,0:T(8,128)S(1)} %get-tuple-element.44.lifted, f32[2,1024]{1,0:T(2,128)S(1)} %get-tuple-element.45.tops, bf16[1024,896]{1,0:T(8,128)(2,1)S(1)} %bitcast.39), custom_call_target="tpu_custom_call" | custom-call | bytes 65536 | tf_op jit(solution)/shard_map/pallas_call | solution.py:294
  (23 shorter events, 0.3 us)
Async XLA Ops:
  2.5 34.2 %all-to-all-start = ((bf16[16,2,4864]{2,1,0:T(2,128)(2,1)}), bf16[16,2,4864]{2,1,0:T(2,128)(2,1)S(1)}, u32[]{:S(2)}, u32[]{:S(2)}) async-start(bf16[16,2,4864]{2,1,0:T(2,128)(2,1)} %shard_map.50), calls=%async_computation | async-start | bytes 622592 | tf_op jit(solution)/shard_map/all_to_all | solution.py:21
  18.3 23.7 %copy-start = (bf16[128,768]{1,0:T(8,128)(2,1)S(1)}, bf16[128,768]{1,0:T(8,128)(2,1)}, u32[]{:S(2)}) copy-start(bf16[128,768]{1,0:T(8,128)(2,1)} %passages.1) | copy-start | bytes 589828
  18.3 9.5 %collective-permute-start = (bf16[128,768]{1,0:T(8,128)(2,1)}, bf16[128,768]{1,0:T(8,128)(2,1)S(1)}, u32[]{:S(2)}, u32[]{:S(2)}) collective-permute-start(bf16[128,768]{1,0:T(8,128)(2,1)} %passages.1), channel_id=1, source_target_pairs={{0,6},{2,0},{4,2},{6,4},{1,7},{3,1},{5,3},{7,5},{8,14},{10,8},{12,... | collective-permute-start | bytes 589832 | tf_op jit(solution)/shard_map/ppermute | solution.py:26
  22.8 8.8 %collective-permute-start.1 = (bf16[128,768]{1,0:T(8,128)(2,1)}, bf16[128,768]{1,0:T(8,128)(2,1)S(1)}, u32[]{:S(2)}, u32[]{:S(2)}) collective-permute-start(bf16[128,768]{1,0:T(8,128)(2,1)} %passages.1), channel_id=1, source_target_pairs={{0,4},{2,6},{4,0},{6,2},{1,5},{3,7},{5,1},{7,3},{8,12},{10,14},{12... | collective-permute-start | bytes 589832 | tf_op jit(solution)/shard_map/ppermute | solution.py:26
  25.2 11.4 %collective-permute-start.2 = (bf16[128,768]{1,0:T(8,128)(2,1)}, bf16[128,768]{1,0:T(8,128)(2,1)S(1)}, u32[]{:S(2)}, u32[]{:S(2)}) collective-permute-start(bf16[128,768]{1,0:T(8,128)(2,1)} %passages.1), channel_id=1, source_target_pairs={{0,2},{2,4},{4,6},{6,0},{1,3},{3,5},{5,7},{7,1},{8,10},{10,12},{12... | collective-permute-start | bytes 589832 | tf_op jit(solution)/shard_map/ppermute | solution.py:26
  37.7 10.8 %all-to-all-start.1 = ((bf16[4,32,1792]{2,1,0:T(8,128)(2,1)}), bf16[4,32,1792]{2,1,0:T(8,128)(2,1)S(1)}, u32[]{:S(2)}, u32[]{:S(2)}) async-start(bf16[4,32,1792]{2,1,0:T(8,128)(2,1)} %pad_maximum_fusion.2), calls=%async_computation.1 | async-start | bytes 917504 | tf_op jit(solution)/shard_map/all_to_all | solution.py:21
  42.1 8.0 %collective-permute-start.3 = (bf16[4,128,768]{2,1,0:T(8,128)(2,1)S(1)}, bf16[4,128,768]{2,1,0:T(8,128)(2,1)S(1)}, u32[]{:S(2)}, u32[]{:S(2)}) collective-permute-start(bf16[4,128,768]{2,1,0:T(8,128)(2,1)S(1)} %pad_maximum_fusion.1), channel_id=1, source_target_pairs={{0,8},{8,0},{1,9},{9,1},{2,10},{10,2},{3,11},{11,3},{4,12},{12,4},... | collective-permute-start | bytes 2359304 | tf_op jit(solution)/shard_map/ppermute | solution.py:26
  49.4 0.7 copy-start.1
  50.1 6.1 %copy-start.2 = (bf16[128,1024]{1,0:T(8,128)(2,1)S(1)}, bf16[128,1024]{1,0:T(8,128)(2,1)}, u32[]{:S(2)}) copy-start(bf16[128,1024]{1,0:T(8,128)(2,1)} %copy-done.1) | copy-start | bytes 786436
  52.7 12.2 %all-to-all-start.2 = ((f32[4,32,1664]{2,1,0:T(8,128)}), f32[4,32,1664]{2,1,0:T(8,128)S(1)}, u32[]{:S(2)}, u32[]{:S(2)}) async-start(f32[4,32,1664]{2,1,0:T(8,128)} %shard_map.52), calls=%async_computation.2 | async-start | bytes 1703936 | tf_op jit(solution)/shard_map/all_to_all | solution.py:21
  56.2 21.7 %collective-permute-start.4 = (bf16[128,1024]{1,0:T(8,128)(2,1)S(1)}, bf16[128,1024]{1,0:T(8,128)(2,1)S(1)}, u32[]{:S(2)}, u32[]{:S(2)}) collective-permute-start(bf16[128,1024]{1,0:T(8,128)(2,1)S(1)} %copy-done.2), channel_id=1, source_target_pairs={{0,6},{2,0},{4,2},{6,4},{1,7},{3,1},{5,3},{7,5},{8,14},{10,8},{12,... | collective-permute-start | bytes 786440 | tf_op jit(solution)/shard_map/ppermute | solution.py:26
  60.2 17.8 %collective-permute-start.5 = (bf16[128,1024]{1,0:T(8,128)(2,1)S(1)}, bf16[128,1024]{1,0:T(8,128)(2,1)S(1)}, u32[]{:S(2)}, u32[]{:S(2)}) collective-permute-start(bf16[128,1024]{1,0:T(8,128)(2,1)S(1)} %get-tuple-element.38), channel_id=1, source_target_pairs={{0,4},{2,6},{4,0},{6,2},{1,5},{3,7},{5,1},{7,3},{8,12},{10,14},{12... | collective-permute-start | bytes 786440 | tf_op jit(solution)/shard_map/ppermute | solution.py:26
  65.8 30.4 %all-to-all-start.3 = ((f32[16,2,1792]{2,1,0:T(2,128)}), f32[16,2,1792]{2,1,0:T(2,128)S(1)}, u32[]{:S(2)}, u32[]{:S(2)}) async-start(f32[16,2,1792]{2,1,0:T(2,128)} %shard_map.53), calls=%async_computation.3 | async-start | bytes 458752 | tf_op jit(solution)/shard_map/all_to_all | solution.py:21
  77.9 2.1 %copy-start.3 = (bf16[128,1024]{1,0:T(8,128)(2,1)}, bf16[128,1024]{1,0:T(8,128)(2,1)S(1)}, u32[]{:S(2)}) copy-start(bf16[128,1024]{1,0:T(8,128)(2,1)S(1)} %collective-permute-done.4) | copy-start | bytes 786436
  78.0 8.5 %copy-start.5 = (bf16[128,1024]{1,0:T(8,128)(2,1)}, bf16[128,1024]{1,0:T(8,128)(2,1)S(1)}, u32[]{:S(2)}) copy-start(bf16[128,1024]{1,0:T(8,128)(2,1)S(1)} %collective-permute-done.5) | copy-start | bytes 786436
  78.0 8.3 %collective-permute-start.6 = (bf16[128,1024]{1,0:T(8,128)(2,1)S(1)}, bf16[128,1024]{1,0:T(8,128)(2,1)S(1)}, u32[]{:S(2)}, u32[]{:S(2)}) collective-permute-start(bf16[128,1024]{1,0:T(8,128)(2,1)S(1)} %get-tuple-element.43), channel_id=1, source_target_pairs={{0,2},{2,4},{4,6},{6,0},{1,3},{3,5},{5,7},{7,1},{8,10},{10,12},{12... | collective-permute-start | bytes 786440 | tf_op jit(solution)/shard_map/ppermute | solution.py:26
  80.1 15.1 %copy-start.4 = (bf16[128,1024]{1,0:T(8,128)(2,1)S(1)}, bf16[128,1024]{1,0:T(8,128)(2,1)}, u32[]{:S(2)}) copy-start(bf16[128,1024]{1,0:T(8,128)(2,1)} %copy-done.3) | copy-start | bytes 786436
  87.5 14.7 %collective-permute-start.7 = (bf16[4,128,896]{2,1,0:T(8,128)(2,1)}, bf16[4,128,896]{2,1,0:T(8,128)(2,1)}, u32[]{:S(2)}, u32[]{:S(2)}) collective-permute-start(bf16[4,128,896]{2,1,0:T(8,128)(2,1)} %pad_maximum_fusion), channel_id=1, source_target_pairs={{0,8},{8,0},{1,9},{9,1},{2,10},{10,2},{3,11},{11,3},{4,12},{12,4},... | collective-permute-start | bytes 2752520 | tf_op jit(solution)/shard_map/ppermute | solution.py:26
  96.9 9.3 %all-to-all-start.4 = ((f32[8,4,128]{2,1,0:T(4,128)}), f32[8,4,128]{2,1,0:T(4,128)S(1)}, u32[]{:S(2)}, u32[]{:S(2)}) async-start(f32[8,4,128]{2,1,0:T(4,128)} %shard_map.54), calls=%async_computation.4 | async-start | bytes 32768 | tf_op jit(solution)/shard_map/all_to_all | solution.py:21

commit v11 on v10

--- a/solution.py
+++ b/solution.py
@@ -68,9 +68,11 @@
         c, k = divmod(i, nx)
         at = (place[0] + c) % nc * nx + (place[1] + k) % nx
         column = got[:, pl.ds(pl.multiple_of(at * lane, lane), lane)]
-        rows[-k % nx][:, dim + c * lane : dim + (c + 1) * lane] = column
+        to = rows[-k % nx]
+        at = to.shape[1] - (nc - c) * lane
+        to[:, at : at + lane] = column
         taught.append(column.astype(f32))
-    for row in rows:
+    for row in rows[1:]:
         row[:, :dim] = block[...]
     taught = jnp.concatenate(taught, axis=1)
     top = jnp.max(taught, axis=1, keepdims=True)
@@ -95,12 +97,13 @@
     ]
     top = jnp.maximum(*[jnp.max(v, axis=1, keepdims=True) for v in student])
     total = jnp.zeros_like(top)
-    stacked = jnp.zeros((4 * count, dim), f32)
+    products = []
     for i, p in enumerate(shared):
         lifted = jnp.exp(student[i] - top)
         total += jnp.sum(lifted, axis=1, keepdims=True)
         pieces = bf16_parts(lifted) + tuple(v[:, i * half : (i + 1) * half] for v in (high, low))
-        stacked += jnp.dot(jnp.concatenate(pieces, axis=0), p, preferred_element_type=f32)
+        products.append(jnp.dot(jnp.concatenate(pieces, axis=0), p, preferred_element_type=f32))
+    stacked = products[0] + products[1]
     parts = [
         stacked[at * count : (at + 1) * count] + stacked[(at + 1) * count : (at + 2) * count] for at in (0, 2)
     ]
@@ -209,22 +212,18 @@
 def last_kernel(nc, nx, place, got, lifted, tops, rows, grads):
     count = got.shape[2]
     pool, dim = grads.shape
-    total = jnp.zeros((2 * pool, dim), f32)
-    for i in range(0, nc * nx, 2):
-        pieces = []
-        for j in (i, i + 1):
-            c, k = divmod(j, nx)
-            at = slice(j * count, (j + 1) * count)
-            stats = got[(place[1] + k) % nx * nc + (place[0] + c) % nc]
-            weight_s = logit_scale * jnp.exp(tops[0:1, at] - stats[0:1]) / stats[1:2]
-            weight_t = logit_scale * jnp.exp(tops[1:2, at] - stats[2:3]) / stats[3:4]
-            grad = weight_s * lifted[0, :, at] - weight_t * lifted[1, :, at]
-            pieces.append(jnp.concatenate(bf16_parts(grad), axis=0))
-        total += jnp.dot(
-            jnp.concatenate(pieces, axis=1),
-            rows[i * count : (i + 2) * count, :dim],
-            preferred_element_type=f32,
-        )
+    pieces = []
+    for i in range(nc * nx):
+        c, k = divmod(i, nx)
+        at = slice(i * count, (i + 1) * count)
+        stats = got[(place[1] + k) % nx * nc + (place[0] + c) % nc]
+        weight_s = logit_scale * jnp.exp(tops[0:1, at] - stats[0:1]) / stats[1:2]
+        weight_t = logit_scale * jnp.exp(tops[1:2, at] - stats[2:3]) / stats[3:4]
+        grad = weight_s * lifted[0, :, at] - weight_t * lifted[1, :, at]
+        pieces.append(jnp.concatenate(bf16_parts(grad), axis=0))
+    total = jnp.dot(
+        jnp.concatenate(pieces, axis=1), rows[:, :dim], preferred_element_type=f32
+    )
     grads[...] = total[:pool] + total[pool:]
 
 
@@ -259,11 +258,12 @@
     place = place_of()
     lifted = jax.ShapeDtypeStruct((count, group * pool), bf16)
     row = jax.ShapeDtypeStruct((count, dim + nc * pool), bf16)
+    mine = jax.ShapeDtypeStruct((count, nc * pool), bf16)
     block = jax.ShapeDtypeStruct((count, dim), bf16)
     stats = jax.ShapeDtypeStruct((width, count), f32)
     return pl.pallas_call(
         functools.partial(layout_kernel, nc, nx),
-        out_shape=(block, lifted, lifted, stats) + (row,) * nx,
+        out_shape=(block, lifted, lifted, stats, mine) + (row,) * (nx - 1),
         in_specs=[pl.BlockSpec(memory_space=pltpu.SMEM), vmem],
         out_specs=(vmem,) * (4 + nx),
         compiler_params=pltpu.CompilerParams(vmem_limit_bytes=16 * 2**20),
@@ -334,6 +334,7 @@
         [exchange(parts, "y")],
     )
     got = exchange(sent, z_axes)
+    rows[0] = jnp.concatenate([block, rows[0]], axis=1)
     *rows, _ = lax.optimization_barrier((*rows, sent))
     rows[-1] = from_next(rows[-1], "x", nx - 1)
 

time: 109 us -> 110 us (level)
  local copies, waits for them, and re-layouts: 3.33 us -> 5.29 us
  starting transfers between devices: 70.3 us -> 69 us
    all_to_all x5, starting transfers between devices: 40.2 us -> 38.5 us  [exchange(): return lax.all_to_all(values, axes, 0, 0, tiled=True)]
  transfers between devices with their start and end apart: 13 -> 13, of which waited for: 6 -> 6; matrix products, arithmetic and copies ran while one was open for 4% -> 6% of each run, Pallas kernels for 4% -> 4%
where the time goes in v11:
time: 110 us; the launch traced here: 109 us
  starting transfers between devices  69 us (63%)
  waiting for transfers between devices  20.8 us (19%)
  Pallas kernels  10.3 us (9%)
  local copies, waits for them, and re-layouts  5.29 us (5%)
  other arithmetic  2.23 us (2%)
    all_to_all x5, starting transfers between devices, exchange(): return lax.all_to_all(values, axes, 0, 0, tiled=True)  38.5 us
    ppermute x8, starting transfers between devices, from_next(): return lax.ppermute(values, axis, [(i, (i - step) % n) for i in range(n)])  30.5 us
    ppermute x8, waiting for transfers between devices, from_next(): return lax.ppermute(values, axis, [(i, (i - step) % n) for i in range(n)])  15.1 us
    all_to_all x5, waiting for transfers between devices, exchange(): return lax.all_to_all(values, axes, 0, 0, tiled=True)  5.72 us
    pallas_call x5, Pallas kernels, simple_call(): pl.pallas_call(kernel, out_shape=out, in_specs=[smem] * len(scalars) + [v...  4.9 us
    pallas_call x1, Pallas kernels, local_parts(): pl.pallas_call(parts_kernel, out_shape=jax.ShapeDtypeStruct((ny, count //...  2.6 us
  transfers between devices with their start and end apart: 13, of which 6 were waited for; matrix products, arithmetic and copies ran while one was open for 6% of the time, Pallas kernels for 4%

profile of v11, /device:TPU:1, one launch (start us, length us, event | category | flops | bytes accessed | tf_op | source)
XLA Modules:
  0.0 108.6 jit_solution(13279823063901904827)
XLA Ops:
  0.6 1.9 %shard_map.50 = bf16[16,2,4864]{2,1,0:T(2,128)(2,1)} custom-call(bf16[2,768]{1,0:T(2,128)(2,1)} %queries_in.1, bf16[2,65536]{1,0:T(2,128)(2,1)} %teacher_in.1), custom_call_target="tpu_custom_call" | custom-call | bytes 1048576 | tf_op jit(solution)/shard_map/pallas_call | solution.py:236
  2.5 15.8 %all-to-all-start = ((bf16[16,2,4864]{2,1,0:T(2,128)(2,1)}), bf16[16,2,4864]{2,1,0:T(2,128)(2,1)S(1)}, u32[]{:S(2)}, u32[]{:S(2)}) async-start(bf16[16,2,4864]{2,1,0:T(2,128)(2,1)} %shard_map.50), calls=%async_computation | async-start | bytes 622592 | tf_op jit(solution)/shard_map/all_to_all | solution.py:21
  18.3 0.0 copy-start
  18.3 4.5 %collective-permute-start = (bf16[128,768]{1,0:T(8,128)(2,1)}, bf16[128,768]{1,0:T(8,128)(2,1)S(1)}, u32[]{:S(2)}, u32[]{:S(2)}) collective-permute-start(bf16[128,768]{1,0:T(8,128)(2,1)} %passages.1), channel_id=1, source_target_pairs={{0,6},{2,0},{4,2},{6,4},{1,7},{3,1},{5,3},{7,5},{8,14},{10,8},{12,... | collective-permute-start | bytes 589832 | tf_op jit(solution)/shard_map/ppermute | solution.py:26
  22.8 2.4 %collective-permute-start.1 = (bf16[128,768]{1,0:T(8,128)(2,1)}, bf16[128,768]{1,0:T(8,128)(2,1)S(1)}, u32[]{:S(2)}, u32[]{:S(2)}) collective-permute-start(bf16[128,768]{1,0:T(8,128)(2,1)} %passages.1), channel_id=1, source_target_pairs={{0,4},{2,6},{4,0},{6,2},{1,5},{3,7},{5,1},{7,3},{8,12},{10,14},{12... | collective-permute-start | bytes 589832 | tf_op jit(solution)/shard_map/ppermute | solution.py:26
  25.2 2.5 %collective-permute-start.2 = (bf16[128,768]{1,0:T(8,128)(2,1)}, bf16[128,768]{1,0:T(8,128)(2,1)S(1)}, u32[]{:S(2)}, u32[]{:S(2)}) collective-permute-start(bf16[128,768]{1,0:T(8,128)(2,1)} %passages.1), channel_id=1, source_target_pairs={{0,2},{2,4},{4,6},{6,0},{1,3},{3,5},{5,7},{7,1},{8,10},{10,12},{12... | collective-permute-start | bytes 589832 | tf_op jit(solution)/shard_map/ppermute | solution.py:26
  27.8 0.0 collective-permute-done
  27.8 3.8 %collective-permute-done.1 = bf16[128,768]{1,0:T(8,128)(2,1)S(1)} collective-permute-done((bf16[128,768]{1,0:T(8,128)(2,1)}, bf16[128,768]{1,0:T(8,128)(2,1)S(1)}, u32[]{:S(2)}, u32[]{:S(2)}) %collective-permute-start.1) | collective-permute-done | bytes 196640 | tf_op jit(solution)/shard_map/ppermute | solution.py:26
  31.6 5.1 %collective-permute-done.2 = bf16[128,768]{1,0:T(8,128)(2,1)S(1)} collective-permute-done((bf16[128,768]{1,0:T(8,128)(2,1)}, bf16[128,768]{1,0:T(8,128)(2,1)S(1)}, u32[]{:S(2)}, u32[]{:S(2)}) %collective-permute-start.2) | collective-permute-done | bytes 196640 | tf_op jit(solution)/shard_map/ppermute | solution.py:26
  36.7 0.0 all-to-all-done
  36.7 0.1 reshape.19
  36.9 0.8 pad_maximum_fusion.2
  37.7 4.2 %all-to-all-start.1 = ((bf16[4,32,1792]{2,1,0:T(8,128)(2,1)}), bf16[4,32,1792]{2,1,0:T(8,128)(2,1)S(1)}, u32[]{:S(2)}, u32[]{:S(2)}) async-start(bf16[4,32,1792]{2,1,0:T(8,128)(2,1)} %pad_maximum_fusion.2), calls=%async_computation.1 | async-start | bytes 917504 | tf_op jit(solution)/shard_map/all_to_all | solution.py:21
  41.9 0.1 pad_add_fusion.place
  42.0 0.0 copy-done
  42.0 0.1 pad_maximum_fusion.1
  42.1 4.7 %collective-permute-start.3 = (bf16[4,128,768]{2,1,0:T(8,128)(2,1)S(1)}, bf16[4,128,768]{2,1,0:T(8,128)(2,1)S(1)}, u32[]{:S(2)}, u32[]{:S(2)}) collective-permute-start(bf16[4,128,768]{2,1,0:T(8,128)(2,1)S(1)} %pad_maximum_fusion.1), channel_id=1, source_target_pairs={{0,8},{8,0},{1,9},{9,1},{2,10},{10,2},{3,11},{11,3},{4,12},{12,4},... | collective-permute-start | bytes 2359304 | tf_op jit(solution)/shard_map/ppermute | solution.py:26
  46.8 1.7 %all-to-all-done.1 = bf16[4,32,1792]{2,1,0:T(8,128)(2,1)S(1)} async-done(((bf16[4,32,1792]{2,1,0:T(8,128)(2,1)}), bf16[4,32,1792]{2,1,0:T(8,128)(2,1)S(1)}, u32[]{:S(2)}, u32[]{:S(2)}) %all-to-all-start.1) | async-done | bytes 458784 | tf_op jit(solution)/shard_map/all_to_all | solution.py:21
  48.5 0.9 shard_map.51
  49.4 0.0 collective-permute-done.3
  49.4 2.6 %shard_map.52 = f32[4,32,1664]{2,1,0:T(8,128)} custom-call(bf16[128,768]{1,0:T(8,128)(2,1)S(1)} %get-tuple-element.25.block, bf16[128,1024]{1,0:T(8,128)(2,1)S(1)} %get-tuple-element.26.high, bf16[128,1024]{1,0:T(8,128)(2,1)S(1)} %get-tuple-element.27.low, f32[32,128]{1,0:T(8,128)S(1)} %get-tuple-element.28.taught, bf16[512,768]{1,0:T(8,128)(2,1)S(1)} %bitcast.40, ...), custom_call_target="tpu_custom_call" | custom-call | flops 1006632960 | bytes 4194304 | tf_op jit(solution)/shard_map/pallas_call | solution.py:278
  52.0 3.8 %all-to-all-start.2 = ((f32[4,32,1664]{2,1,0:T(8,128)}), f32[4,32,1664]{2,1,0:T(8,128)S(1)}, u32[]{:S(2)}, u32[]{:S(2)}) async-start(f32[4,32,1664]{2,1,0:T(8,128)} %shard_map.52), calls=%async_computation.2 | async-start | bytes 1703936 | tf_op jit(solution)/shard_map/all_to_all | solution.py:21
  55.8 4.4 %collective-permute-start.4 = (bf16[128,1024]{1,0:T(8,128)(2,1)S(1)}, bf16[128,1024]{1,0:T(8,128)(2,1)S(1)}, u32[]{:S(2)}, u32[]{:S(2)}) collective-permute-start(bf16[128,1024]{1,0:T(8,128)(2,1)S(1)} %get-tuple-element.37), channel_id=1, source_target_pairs={{0,6},{2,0},{4,2},{6,4},{1,7},{3,1},{5,3},{7,5},{8,14},{10,8},{12,... | collective-permute-start | bytes 786440 | tf_op jit(solution)/shard_map/ppermute | solution.py:26
  60.2 2.4 %collective-permute-start.5 = (bf16[128,1024]{1,0:T(8,128)(2,1)S(1)}, bf16[128,1024]{1,0:T(8,128)(2,1)}, u32[]{:S(2)}, u32[]{:S(2)}) collective-permute-start(bf16[128,1024]{1,0:T(8,128)(2,1)S(1)} %get-tuple-element.38), channel_id=1, source_target_pairs={{0,4},{2,6},{4,0},{6,2},{1,5},{3,7},{5,1},{7,3},{8,12},{10,14},{12... | collective-permute-start | bytes 786440 | tf_op jit(solution)/shard_map/ppermute | solution.py:26
  62.6 0.0 copy-start.1
  62.7 2.2 %all-to-all-done.2.got = f32[4,32,1664]{2,1,0:T(8,128)S(1)} async-done(((f32[4,32,1664]{2,1,0:T(8,128)}), f32[4,32,1664]{2,1,0:T(8,128)S(1)}, u32[]{:S(2)}, u32[]{:S(2)}) %all-to-all-start.2) | async-done | bytes 852000 | tf_op jit(solution)/shard_map/all_to_all | solution.py:21
  64.9 0.8 shard_map.53
  65.8 11.4 %all-to-all-start.3 = ((f32[16,2,1792]{2,1,0:T(2,128)}), f32[16,2,1792]{2,1,0:T(2,128)S(1)}, u32[]{:S(2)}, u32[]{:S(2)}) async-start(f32[16,2,1792]{2,1,0:T(2,128)} %shard_map.53), calls=%async_computation.3 | async-start | bytes 458752 | tf_op jit(solution)/shard_map/all_to_all | solution.py:21
  77.2 0.0 collective-permute-done.4
  77.2 0.0 collective-permute-done.5
  77.2 0.8 slice.66
  78.0 0.9 slice.65
  79.0 1.9 %collective-permute-start.6 = (bf16[128,1024]{1,0:T(8,128)(2,1)S(1)}, bf16[128,1024]{1,0:T(8,128)(2,1)S(1)}, u32[]{:S(2)}, u32[]{:S(2)}) collective-permute-start(bf16[128,1024]{1,0:T(8,128)(2,1)S(1)} %get-tuple-element.43), channel_id=1, source_target_pairs={{0,2},{2,4},{4,6},{6,0},{1,3},{3,5},{5,7},{7,1},{8,10},{10,12},{12... | collective-permute-start | bytes 786440 | tf_op jit(solution)/shard_map/ppermute | solution.py:26
  81.1 0.0 copy-start.2
  81.1 6.2 %collective-permute-done.6 = bf16[128,1024]{1,0:T(8,128)(2,1)S(1)} collective-permute-done((bf16[128,1024]{1,0:T(8,128)(2,1)S(1)}, bf16[128,1024]{1,0:T(8,128)(2,1)S(1)}, u32[]{:S(2)}, u32[]{:S(2)}) %collective-permute-start.6) | collective-permute-done | bytes 262176 | tf_op jit(solution)/shard_map/ppermute | solution.py:26
  87.4 1.1 %pad_maximum_fusion = bf16[4,128,896]{2,1,0:T(8,128)(2,1)} fusion(bf16[1,128,896]{2,1,0:T(8,128)(2,1)S(1)} %maximum_bitcast_fusion.3, bf16[1,128,896]{2,1,0:T(8,128)(2,1)S(1)} %maximum_bitcast_fusion.2, bf16[1,128,896]{2,1,0:T(8,128)(2,1)S(1)} %maximum_bitcast_fusion.1, bf16[1,128,896]{2,1,0:T(8,128)(2,1)S(1)} %maximum_bitcast_fusion), kind=kLoop, calls=%fused_computation | loop fusion | flops 1376256 | bytes 1835008 | tf_op jit(solution)/shard_map/stack | solution.py:342
  88.5 7.6 %collective-permute-start.7 = (bf16[4,128,896]{2,1,0:T(8,128)(2,1)}, bf16[4,128,896]{2,1,0:T(8,128)(2,1)}, u32[]{:S(2)}, u32[]{:S(2)}) collective-permute-start(bf16[4,128,896]{2,1,0:T(8,128)(2,1)} %pad_maximum_fusion), channel_id=1, source_target_pairs={{0,8},{8,0},{1,9},{9,1},{2,10},{10,2},{3,11},{11,3},{4,12},{12,4},... | collective-permute-start | bytes 2752520 | tf_op jit(solution)/shard_map/ppermute | solution.py:26
  96.1 1.0 bitcast_dynamic-update-slice_fusion.1
  97.1 1.0 bitcast_dynamic-update-slice_fusion
  98.1 0.0 all-to-all-done.3.got
  98.1 0.7 shard_map.54
  98.8 3.3 %all-to-all-start.4 = ((f32[8,4,128]{2,1,0:T(4,128)}), f32[8,4,128]{2,1,0:T(4,128)S(1)}, u32[]{:S(2)}, u32[]{:S(2)}) async-start(f32[8,4,128]{2,1,0:T(4,128)} %shard_map.54), calls=%async_computation.4 | async-start | bytes 32768 | tf_op jit(solution)/shard_map/all_to_all | solution.py:21
  102.1 0.8 shard_map.55
  102.8 0.0 collective-permute-done.7
  102.8 1.3 %constant_dynamic-update-slice_fusion = bf16[8,128,896]{2,1,0:T(8,128)(2,1)S(1)} fusion(bf16[8,128,896]{2,1,0:T(8,128)(2,1)S(1)} %fusion, bf16[4,128,896]{2,1,0:T(8,128)(2,1)} %collective-permute-done.7), kind=kLoop, calls=%fused_computation.20 | loop fusion | bytes 1835008 | tf_op jit(solution)/shard_map/concatenate | solution.py:343
  104.2 0.7 shard_map.56
  104.9 1.8 %all-to-all-done.4.got = f32[8,4,128]{2,1,0:T(4,128)S(1)} async-done(((f32[8,4,128]{2,1,0:T(4,128)}), f32[8,4,128]{2,1,0:T(4,128)S(1)}, u32[]{:S(2)}, u32[]{:S(2)}) %all-to-all-start.4) | async-done | bytes 16416 | tf_op jit(solution)/shard_map/all_to_all | solution.py:21
  106.7 1.9 %shard_map.57 = f32[128,768]{1,0:T(8,128)} custom-call(s32[2]{0:T(128)S(1)} %pad_add_fusion.place, f32[8,4,128]{2,1,0:T(4,128)S(1)} %all-to-all-done.4.got, f32[2,128,1024]{2,1,0:T(8,128)S(1)} %get-tuple-element.44.lifted, f32[2,1024]{1,0:T(2,128)S(1)} %get-tuple-element.45.tops, bf16[1024,896]{1,0:T(8,128)(2,1)S(1)} %bitcast.39), custom_call_target="tpu_custom_call" | custom-call | bytes 65536 | tf_op jit(solution)/shard_map/pallas_call | solution.py:294
  (20 shorter events, 0.3 us)
Async XLA Ops:
  2.5 34.2 %all-to-all-start = ((bf16[16,2,4864]{2,1,0:T(2,128)(2,1)}), bf16[16,2,4864]{2,1,0:T(2,128)(2,1)S(1)}, u32[]{:S(2)}, u32[]{:S(2)}) async-start(bf16[16,2,4864]{2,1,0:T(2,128)(2,1)} %shard_map.50), calls=%async_computation | async-start | bytes 622592 | tf_op jit(solution)/shard_map/all_to_all | solution.py:21
  18.3 23.7 %copy-start = (bf16[128,768]{1,0:T(8,128)(2,1)S(1)}, bf16[128,768]{1,0:T(8,128)(2,1)}, u32[]{:S(2)}) copy-start(bf16[128,768]{1,0:T(8,128)(2,1)} %passages.1) | copy-start | bytes 589828
  18.3 9.5 %collective-permute-start = (bf16[128,768]{1,0:T(8,128)(2,1)}, bf16[128,768]{1,0:T(8,128)(2,1)S(1)}, u32[]{:S(2)}, u32[]{:S(2)}) collective-permute-start(bf16[128,768]{1,0:T(8,128)(2,1)} %passages.1), channel_id=1, source_target_pairs={{0,6},{2,0},{4,2},{6,4},{1,7},{3,1},{5,3},{7,5},{8,14},{10,8},{12,... | collective-permute-start | bytes 589832 | tf_op jit(solution)/shard_map/ppermute | solution.py:26
  22.8 8.8 %collective-permute-start.1 = (bf16[128,768]{1,0:T(8,128)(2,1)}, bf16[128,768]{1,0:T(8,128)(2,1)S(1)}, u32[]{:S(2)}, u32[]{:S(2)}) collective-permute-start(bf16[128,768]{1,0:T(8,128)(2,1)} %passages.1), channel_id=1, source_target_pairs={{0,4},{2,6},{4,0},{6,2},{1,5},{3,7},{5,1},{7,3},{8,12},{10,14},{12... | collective-permute-start | bytes 589832 | tf_op jit(solution)/shard_map/ppermute | solution.py:26
  25.2 11.4 %collective-permute-start.2 = (bf16[128,768]{1,0:T(8,128)(2,1)}, bf16[128,768]{1,0:T(8,128)(2,1)S(1)}, u32[]{:S(2)}, u32[]{:S(2)}) collective-permute-start(bf16[128,768]{1,0:T(8,128)(2,1)} %passages.1), channel_id=1, source_target_pairs={{0,2},{2,4},{4,6},{6,0},{1,3},{3,5},{5,7},{7,1},{8,10},{10,12},{12... | collective-permute-start | bytes 589832 | tf_op jit(solution)/shard_map/ppermute | solution.py:26
  37.7 10.8 %all-to-all-start.1 = ((bf16[4,32,1792]{2,1,0:T(8,128)(2,1)}), bf16[4,32,1792]{2,1,0:T(8,128)(2,1)S(1)}, u32[]{:S(2)}, u32[]{:S(2)}) async-start(bf16[4,32,1792]{2,1,0:T(8,128)(2,1)} %pad_maximum_fusion.2), calls=%async_computation.1 | async-start | bytes 917504 | tf_op jit(solution)/shard_map/all_to_all | solution.py:21
  42.1 7.3 %collective-permute-start.3 = (bf16[4,128,768]{2,1,0:T(8,128)(2,1)S(1)}, bf16[4,128,768]{2,1,0:T(8,128)(2,1)S(1)}, u32[]{:S(2)}, u32[]{:S(2)}) collective-permute-start(bf16[4,128,768]{2,1,0:T(8,128)(2,1)S(1)} %pad_maximum_fusion.1), channel_id=1, source_target_pairs={{0,8},{8,0},{1,9},{9,1},{2,10},{10,2},{3,11},{11,3},{4,12},{12,4},... | collective-permute-start | bytes 2359304 | tf_op jit(solution)/shard_map/ppermute | solution.py:26
  52.0 12.9 %all-to-all-start.2 = ((f32[4,32,1664]{2,1,0:T(8,128)}), f32[4,32,1664]{2,1,0:T(8,128)S(1)}, u32[]{:S(2)}, u32[]{:S(2)}) async-start(f32[4,32,1664]{2,1,0:T(8,128)} %shard_map.52), calls=%async_computation.2 | async-start | bytes 1703936 | tf_op jit(solution)/shard_map/all_to_all | solution.py:21
  55.8 21.4 %collective-permute-start.4 = (bf16[128,1024]{1,0:T(8,128)(2,1)S(1)}, bf16[128,1024]{1,0:T(8,128)(2,1)S(1)}, u32[]{:S(2)}, u32[]{:S(2)}) collective-permute-start(bf16[128,1024]{1,0:T(8,128)(2,1)S(1)} %get-tuple-element.37), channel_id=1, source_target_pairs={{0,6},{2,0},{4,2},{6,4},{1,7},{3,1},{5,3},{7,5},{8,14},{10,8},{12,... | collective-permute-start | bytes 786440 | tf_op jit(solution)/shard_map/ppermute | solution.py:26
  60.2 17.1 %collective-permute-start.5 = (bf16[128,1024]{1,0:T(8,128)(2,1)S(1)}, bf16[128,1024]{1,0:T(8,128)(2,1)}, u32[]{:S(2)}, u32[]{:S(2)}) collective-permute-start(bf16[128,1024]{1,0:T(8,128)(2,1)S(1)} %get-tuple-element.38), channel_id=1, source_target_pairs={{0,4},{2,6},{4,0},{6,2},{1,5},{3,7},{5,1},{7,3},{8,12},{10,14},{12... | collective-permute-start | bytes 786440 | tf_op jit(solution)/shard_map/ppermute | solution.py:26
  62.6 18.4 %copy-start.1 = (bf16[128,1024]{1,0:T(8,128)(2,1)}, bf16[128,1024]{1,0:T(8,128)(2,1)S(1)}, u32[]{:S(2)}) copy-start(bf16[128,1024]{1,0:T(8,128)(2,1)S(1)} %pad_maximum_fusion.3) | copy-start | bytes 786436
  65.8 32.4 %all-to-all-start.3 = ((f32[16,2,1792]{2,1,0:T(2,128)}), f32[16,2,1792]{2,1,0:T(2,128)S(1)}, u32[]{:S(2)}, u32[]{:S(2)}) async-start(f32[16,2,1792]{2,1,0:T(2,128)} %shard_map.53), calls=%async_computation.3 | async-start | bytes 458752 | tf_op jit(solution)/shard_map/all_to_all | solution.py:21
  77.2 11.3 %copy-start.3 = (bf16[128,1024]{1,0:T(8,128)(2,1)}, bf16[128,1024]{1,0:T(8,128)(2,1)S(1)}, u32[]{:S(2)}) copy-start(bf16[128,1024]{1,0:T(8,128)(2,1)S(1)} %collective-permute-done.4) | copy-start | bytes 786436
  79.0 8.3 %collective-permute-start.6 = (bf16[128,1024]{1,0:T(8,128)(2,1)S(1)}, bf16[128,1024]{1,0:T(8,128)(2,1)S(1)}, u32[]{:S(2)}, u32[]{:S(2)}) collective-permute-start(bf16[128,1024]{1,0:T(8,128)(2,1)S(1)} %get-tuple-element.43), channel_id=1, source_target_pairs={{0,2},{2,4},{4,6},{6,0},{1,3},{3,5},{5,7},{7,1},{8,10},{10,12},{12... | collective-permute-start | bytes 786440 | tf_op jit(solution)/shard_map/ppermute | solution.py:26
  81.1 15.0 %copy-start.2 = (bf16[128,1024]{1,0:T(8,128)(2,1)S(1)}, bf16[128,1024]{1,0:T(8,128)(2,1)}, u32[]{:S(2)}) copy-start(bf16[128,1024]{1,0:T(8,128)(2,1)} %copy-done.1) | copy-start | bytes 786436
  88.5 14.4 %collective-permute-start.7 = (bf16[4,128,896]{2,1,0:T(8,128)(2,1)}, bf16[4,128,896]{2,1,0:T(8,128)(2,1)}, u32[]{:S(2)}, u32[]{:S(2)}) collective-permute-start(bf16[4,128,896]{2,1,0:T(8,128)(2,1)} %pad_maximum_fusion), channel_id=1, source_target_pairs={{0,8},{8,0},{1,9},{9,1},{2,10},{10,2},{3,11},{11,3},{4,12},{12,4},... | collective-permute-start | bytes 2752520 | tf_op jit(solution)/shard_map/ppermute | solution.py:26
  98.8 7.9 %all-to-all-start.4 = ((f32[8,4,128]{2,1,0:T(4,128)}), f32[8,4,128]{2,1,0:T(4,128)S(1)}, u32[]{:S(2)}, u32[]{:S(2)}) async-start(f32[8,4,128]{2,1,0:T(4,128)} %shard_map.54), calls=%async_computation.4 | async-start | bytes 32768 | tf_op jit(solution)/shard_map/all_to_all | solution.py:21

commit v12 on v11

--- a/solution.py
+++ b/solution.py
@@ -345,6 +345,7 @@
     lifted = jax.ShapeDtypeStruct((2, pool, group * count), f32)
     tops = jax.ShapeDtypeStruct((2, group * count), f32)
     sets = simple_call(own_kernel, (lifted, tops), [], [passages, every_row], flops=2 * pool * group * count * dim)
+    got, *sets = lax.optimization_barrier((got, *sets))
     every = simple_call(
         functools.partial(after_kernel, dim), jax.ShapeDtypeStruct((group, 4, count), f32), [], [got]
     )

time: 110 us -> 108 us (0.982)
  local copies, waits for them, and re-layouts: 5.29 us -> 0.51 us
  waiting for transfers between devices: 20.8 us -> 24.9 us
    all_to_all x5, waiting for transfers between devices: 5.72 us -> 7.83 us  [exchange(): return lax.all_to_all(values, axes, 0, 0, tiled=True)]
    ppermute x8, waiting for transfers between devices: 15.1 us -> 17 us  [from_next(): return lax.ppermute(values, axis, [(i, (i - step) % n) for i in range(n)])]
    unnamed x12 -> x10, local copies, waits for them, and re-layouts: 2 us -> 0.12 us
    concatenate x1, local copies, waits for them, and re-layouts: 1.31 us -> 0.13 us  [per_device(): jnp.concatenate([kept, from_next(away, 'core', 1)])]
  transfers between devices with their start and end apart: 13 -> 13, of which waited for: 6 -> 7; matrix products, arithmetic and copies ran while one was open for 6% -> 1% of each run, Pallas kernels for 4% -> 3%
where the time goes in v12:
time: 108 us; the launch traced here: 107 us
  starting transfers between devices  69.4 us (64%)
  waiting for transfers between devices  24.9 us (23%)
  Pallas kernels  10.3 us (10%)
  other arithmetic  1.29 us (1%)
    all_to_all x5, starting transfers between devices, exchange(): return lax.all_to_all(values, axes, 0, 0, tiled=True)  38.9 us
    ppermute x8, starting transfers between devices, from_next(): return lax.ppermute(values, axis, [(i, (i - step) % n) for i in range(n)])  30.5 us
    ppermute x8, waiting for transfers between devices, from_next(): return lax.ppermute(values, axis, [(i, (i - step) % n) for i in range(n)])  17 us
    all_to_all x5, waiting for transfers between devices, exchange(): return lax.all_to_all(values, axes, 0, 0, tiled=True)  7.83 us
    pallas_call x5, Pallas kernels, simple_call(): pl.pallas_call(kernel, out_shape=out, in_specs=[smem] * len(scalars) + [v...  4.91 us
    pallas_call x1, Pallas kernels, local_parts(): pl.pallas_call(parts_kernel, out_shape=jax.ShapeDtypeStruct((ny, count //...  2.61 us
  transfers between devices with their start and end apart: 13, of which 7 were waited for; matrix products, arithmetic and copies ran while one was open for 1% of the time, Pallas kernels for 3%

profile of v12, /device:TPU:1, one launch (start us, length us, event | category | flops | bytes accessed | tf_op | source)
XLA Modules:
  0.0 107.3 jit_solution(3192351082831289800)
XLA Ops:
  0.6 1.9 %shard_map.50 = bf16[16,2,4864]{2,1,0:T(2,128)(2,1)} custom-call(bf16[2,768]{1,0:T(2,128)(2,1)} %queries_in.1, bf16[2,65536]{1,0:T(2,128)(2,1)} %teacher_in.1), custom_call_target="tpu_custom_call" | custom-call | bytes 1048576 | tf_op jit(solution)/shard_map/pallas_call | solution.py:236
  2.5 15.8 %all-to-all-start = ((bf16[16,2,4864]{2,1,0:T(2,128)(2,1)}), bf16[16,2,4864]{2,1,0:T(2,128)(2,1)S(1)}, u32[]{:S(2)}, u32[]{:S(2)}) async-start(bf16[16,2,4864]{2,1,0:T(2,128)(2,1)} %shard_map.50), calls=%async_computation | async-start | bytes 622592 | tf_op jit(solution)/shard_map/all_to_all | solution.py:21
  18.3 0.0 copy-start
  18.3 4.5 %collective-permute-start = (bf16[128,768]{1,0:T(8,128)(2,1)}, bf16[128,768]{1,0:T(8,128)(2,1)S(1)}, u32[]{:S(2)}, u32[]{:S(2)}) collective-permute-start(bf16[128,768]{1,0:T(8,128)(2,1)} %passages.1), channel_id=1, source_target_pairs={{0,6},{2,0},{4,2},{6,4},{1,7},{3,1},{5,3},{7,5},{8,14},{10,8},{12,... | collective-permute-start | bytes 589832 | tf_op jit(solution)/shard_map/ppermute | solution.py:26
  22.8 2.4 %collective-permute-start.1 = (bf16[128,768]{1,0:T(8,128)(2,1)}, bf16[128,768]{1,0:T(8,128)(2,1)S(1)}, u32[]{:S(2)}, u32[]{:S(2)}) collective-permute-start(bf16[128,768]{1,0:T(8,128)(2,1)} %passages.1), channel_id=1, source_target_pairs={{0,4},{2,6},{4,0},{6,2},{1,5},{3,7},{5,1},{7,3},{8,12},{10,14},{12... | collective-permute-start | bytes 589832 | tf_op jit(solution)/shard_map/ppermute | solution.py:26
  25.2 2.5 %collective-permute-start.2 = (bf16[128,768]{1,0:T(8,128)(2,1)}, bf16[128,768]{1,0:T(8,128)(2,1)S(1)}, u32[]{:S(2)}, u32[]{:S(2)}) collective-permute-start(bf16[128,768]{1,0:T(8,128)(2,1)} %passages.1), channel_id=1, source_target_pairs={{0,2},{2,4},{4,6},{6,0},{1,3},{3,5},{5,7},{7,1},{8,10},{10,12},{12... | collective-permute-start | bytes 589832 | tf_op jit(solution)/shard_map/ppermute | solution.py:26
  27.8 0.0 collective-permute-done
  27.8 3.8 %collective-permute-done.1 = bf16[128,768]{1,0:T(8,128)(2,1)S(1)} collective-permute-done((bf16[128,768]{1,0:T(8,128)(2,1)}, bf16[128,768]{1,0:T(8,128)(2,1)S(1)}, u32[]{:S(2)}, u32[]{:S(2)}) %collective-permute-start.1) | collective-permute-done | bytes 196640 | tf_op jit(solution)/shard_map/ppermute | solution.py:26
  31.6 5.1 %collective-permute-done.2 = bf16[128,768]{1,0:T(8,128)(2,1)S(1)} collective-permute-done((bf16[128,768]{1,0:T(8,128)(2,1)}, bf16[128,768]{1,0:T(8,128)(2,1)S(1)}, u32[]{:S(2)}, u32[]{:S(2)}) %collective-permute-start.2) | collective-permute-done | bytes 196640 | tf_op jit(solution)/shard_map/ppermute | solution.py:26
  36.7 0.0 all-to-all-done
  36.7 0.1 reshape.19
  36.9 0.8 pad_maximum_fusion.2
  37.7 4.2 %all-to-all-start.1 = ((bf16[4,32,1792]{2,1,0:T(8,128)(2,1)}), bf16[4,32,1792]{2,1,0:T(8,128)(2,1)S(1)}, u32[]{:S(2)}, u32[]{:S(2)}) async-start(bf16[4,32,1792]{2,1,0:T(8,128)(2,1)} %pad_maximum_fusion.2), calls=%async_computation.1 | async-start | bytes 917504 | tf_op jit(solution)/shard_map/all_to_all | solution.py:21
  41.9 0.1 pad_add_fusion.place
  42.0 0.0 copy-done
  42.0 0.1 pad_maximum_fusion.1
  42.1 4.7 %collective-permute-start.3 = (bf16[4,128,768]{2,1,0:T(8,128)(2,1)S(1)}, bf16[4,128,768]{2,1,0:T(8,128)(2,1)S(1)}, u32[]{:S(2)}, u32[]{:S(2)}) collective-permute-start(bf16[4,128,768]{2,1,0:T(8,128)(2,1)S(1)} %pad_maximum_fusion.1), channel_id=1, source_target_pairs={{0,8},{8,0},{1,9},{9,1},{2,10},{10,2},{3,11},{11,3},{4,12},{12,4},... | collective-permute-start | bytes 2359304 | tf_op jit(solution)/shard_map/ppermute | solution.py:26
  46.8 1.7 %all-to-all-done.1 = bf16[4,32,1792]{2,1,0:T(8,128)(2,1)S(1)} async-done(((bf16[4,32,1792]{2,1,0:T(8,128)(2,1)}), bf16[4,32,1792]{2,1,0:T(8,128)(2,1)S(1)}, u32[]{:S(2)}, u32[]{:S(2)}) %all-to-all-start.1) | async-done | bytes 458784 | tf_op jit(solution)/shard_map/all_to_all | solution.py:21
  48.5 0.9 shard_map.51
  49.4 0.0 collective-permute-done.3
  49.4 2.6 %shard_map.52 = f32[4,32,1664]{2,1,0:T(8,128)} custom-call(bf16[128,768]{1,0:T(8,128)(2,1)S(1)} %get-tuple-element.28.block, bf16[128,1024]{1,0:T(8,128)(2,1)S(1)} %get-tuple-element.29.high, bf16[128,1024]{1,0:T(8,128)(2,1)S(1)} %get-tuple-element.30.low, f32[32,128]{1,0:T(8,128)S(1)} %get-tuple-element.31.taught, bf16[512,768]{1,0:T(8,128)(2,1)S(1)} %bitcast.40, ...), custom_call_target="tpu_custom_call" | custom-call | flops 1006632960 | bytes 4194304 | tf_op jit(solution)/shard_map/pallas_call | solution.py:278
  52.0 3.8 %all-to-all-start.2 = ((f32[4,32,1664]{2,1,0:T(8,128)}), f32[4,32,1664]{2,1,0:T(8,128)S(1)}, u32[]{:S(2)}, u32[]{:S(2)}) async-start(f32[4,32,1664]{2,1,0:T(8,128)} %shard_map.52), calls=%async_computation.2 | async-start | bytes 1703936 | tf_op jit(solution)/shard_map/all_to_all | solution.py:21
  55.8 4.4 %collective-permute-start.4 = (bf16[128,1024]{1,0:T(8,128)(2,1)S(1)}, bf16[128,1024]{1,0:T(8,128)(2,1)S(1)}, u32[]{:S(2)}, u32[]{:S(2)}) collective-permute-start(bf16[128,1024]{1,0:T(8,128)(2,1)S(1)} %get-tuple-element.39), channel_id=1, source_target_pairs={{0,6},{2,0},{4,2},{6,4},{1,7},{3,1},{5,3},{7,5},{8,14},{10,8},{12,... | collective-permute-start | bytes 786440 | tf_op jit(solution)/shard_map/ppermute | solution.py:26
  60.2 2.4 %collective-permute-start.5 = (bf16[128,1024]{1,0:T(8,128)(2,1)S(1)}, bf16[128,1024]{1,0:T(8,128)(2,1)S(1)}, u32[]{:S(2)}, u32[]{:S(2)}) collective-permute-start(bf16[128,1024]{1,0:T(8,128)(2,1)S(1)} %get-tuple-element.40), channel_id=1, source_target_pairs={{0,4},{2,6},{4,0},{6,2},{1,5},{3,7},{5,1},{7,3},{8,12},{10,14},{12... | collective-permute-start | bytes 786440 | tf_op jit(solution)/shard_map/ppermute | solution.py:26
  62.7 0.0 copy-start.1
  62.7 2.2 %all-to-all-done.2.got = f32[4,32,1664]{2,1,0:T(8,128)S(1)} async-done(((f32[4,32,1664]{2,1,0:T(8,128)}), f32[4,32,1664]{2,1,0:T(8,128)S(1)}, u32[]{:S(2)}, u32[]{:S(2)}) %all-to-all-start.2) | async-done | bytes 852000 | tf_op jit(solution)/shard_map/all_to_all | solution.py:21
  64.9 0.9 shard_map.53
  65.8 11.5 %all-to-all-start.3 = ((f32[16,2,1792]{2,1,0:T(2,128)}), f32[16,2,1792]{2,1,0:T(2,128)S(1)}, u32[]{:S(2)}, u32[]{:S(2)}) async-start(f32[16,2,1792]{2,1,0:T(2,128)} %shard_map.53), calls=%async_computation.3 | async-start | bytes 458752 | tf_op jit(solution)/shard_map/all_to_all | solution.py:21
  77.2 0.0 collective-permute-done.4
  77.2 0.0 collective-permute-done.5
  77.3 1.9 %collective-permute-start.6 = (bf16[128,1024]{1,0:T(8,128)(2,1)S(1)}, bf16[128,1024]{1,0:T(8,128)(2,1)S(1)}, u32[]{:S(2)}, u32[]{:S(2)}) collective-permute-start(bf16[128,1024]{1,0:T(8,128)(2,1)S(1)} %get-tuple-element.45), channel_id=1, source_target_pairs={{0,2},{2,4},{4,6},{6,0},{1,3},{3,5},{5,7},{7,1},{8,10},{10,12},{12... | collective-permute-start | bytes 786440 | tf_op jit(solution)/shard_map/ppermute | solution.py:26
  79.4 0.0 copy-done.1
  79.4 0.0 copy-start.2
  79.4 6.2 %collective-permute-done.6 = bf16[128,1024]{1,0:T(8,128)(2,1)S(1)} collective-permute-done((bf16[128,1024]{1,0:T(8,128)(2,1)S(1)}, bf16[128,1024]{1,0:T(8,128)(2,1)S(1)}, u32[]{:S(2)}, u32[]{:S(2)}) %collective-permute-start.6) | collective-permute-done | bytes 262176 | tf_op jit(solution)/shard_map/ppermute | solution.py:26
  85.7 0.1 pad_maximum_fusion
  85.8 7.6 %collective-permute-start.7 = (bf16[4,128,896]{2,1,0:T(8,128)(2,1)S(1)}, bf16[4,128,896]{2,1,0:T(8,128)(2,1)S(1)}, u32[]{:S(2)}, u32[]{:S(2)}) collective-permute-start(bf16[4,128,896]{2,1,0:T(8,128)(2,1)S(1)} %pad_maximum_fusion), channel_id=1, source_target_pairs={{0,8},{8,0},{1,9},{9,1},{2,10},{10,2},{3,11},{11,3},{4,12},{12,4},... | collective-permute-start | bytes 2752520 | tf_op jit(solution)/shard_map/ppermute | solution.py:26
  93.5 0.0 copy-done.2
  93.6 1.9 %collective-permute-done.7 = bf16[4,128,896]{2,1,0:T(8,128)(2,1)S(1)} collective-permute-done((bf16[4,128,896]{2,1,0:T(8,128)(2,1)S(1)}, bf16[4,128,896]{2,1,0:T(8,128)(2,1)S(1)}, u32[]{:S(2)}, u32[]{:S(2)}) %collective-permute-start.7) | collective-permute-done | bytes 917536 | tf_op jit(solution)/shard_map/ppermute | solution.py:26
  95.6 0.1 constant_dynamic-update-slice_fusion
  95.7 0.8 shard_map.54
  96.5 0.0 all-to-all-done.3.got
  96.5 0.7 shard_map.55
  97.1 3.6 %all-to-all-start.4 = ((f32[8,4,128]{2,1,0:T(4,128)}), f32[8,4,128]{2,1,0:T(4,128)S(1)}, u32[]{:S(2)}, u32[]{:S(2)}) async-start(f32[8,4,128]{2,1,0:T(4,128)} %shard_map.55), calls=%async_computation.4 | async-start | bytes 32768 | tf_op jit(solution)/shard_map/all_to_all | solution.py:21
  100.8 0.8 shard_map.56
  101.5 3.9 %all-to-all-done.4.got = f32[8,4,128]{2,1,0:T(4,128)S(1)} async-done(((f32[8,4,128]{2,1,0:T(4,128)}), f32[8,4,128]{2,1,0:T(4,128)S(1)}, u32[]{:S(2)}, u32[]{:S(2)}) %all-to-all-start.4) | async-done | bytes 16416 | tf_op jit(solution)/shard_map/all_to_all | solution.py:21
  105.4 1.9 %shard_map.57 = f32[128,768]{1,0:T(8,128)} custom-call(s32[2]{0:T(128)S(1)} %pad_add_fusion.place, f32[8,4,128]{2,1,0:T(4,128)S(1)} %all-to-all-done.4.got, f32[2,128,1024]{2,1,0:T(8,128)S(1)} %get-tuple-element.50.lifted, f32[2,1024]{1,0:T(2,128)S(1)} %get-tuple-element.51.tops, bf16[1024,896]{1,0:T(8,128)(2,1)S(1)} %bitcast.39), custom_call_target="tpu_custom_call" | custom-call | bytes 65536 | tf_op jit(solution)/shard_map/pallas_call | solution.py:294
  (20 shorter events, 0.4 us)
Async XLA Ops:
  2.5 34.2 %all-to-all-start = ((bf16[16,2,4864]{2,1,0:T(2,128)(2,1)}), bf16[16,2,4864]{2,1,0:T(2,128)(2,1)S(1)}, u32[]{:S(2)}, u32[]{:S(2)}) async-start(bf16[16,2,4864]{2,1,0:T(2,128)(2,1)} %shard_map.50), calls=%async_computation | async-start | bytes 622592 | tf_op jit(solution)/shard_map/all_to_all | solution.py:21
  18.3 23.7 %copy-start = (bf16[128,768]{1,0:T(8,128)(2,1)S(1)}, bf16[128,768]{1,0:T(8,128)(2,1)}, u32[]{:S(2)}) copy-start(bf16[128,768]{1,0:T(8,128)(2,1)} %passages.1) | copy-start | bytes 589828
  18.3 9.5 %collective-permute-start = (bf16[128,768]{1,0:T(8,128)(2,1)}, bf16[128,768]{1,0:T(8,128)(2,1)S(1)}, u32[]{:S(2)}, u32[]{:S(2)}) collective-permute-start(bf16[128,768]{1,0:T(8,128)(2,1)} %passages.1), channel_id=1, source_target_pairs={{0,6},{2,0},{4,2},{6,4},{1,7},{3,1},{5,3},{7,5},{8,14},{10,8},{12,... | collective-permute-start | bytes 589832 | tf_op jit(solution)/shard_map/ppermute | solution.py:26
  22.8 8.8 %collective-permute-start.1 = (bf16[128,768]{1,0:T(8,128)(2,1)}, bf16[128,768]{1,0:T(8,128)(2,1)S(1)}, u32[]{:S(2)}, u32[]{:S(2)}) collective-permute-start(bf16[128,768]{1,0:T(8,128)(2,1)} %passages.1), channel_id=1, source_target_pairs={{0,4},{2,6},{4,0},{6,2},{1,5},{3,7},{5,1},{7,3},{8,12},{10,14},{12... | collective-permute-start | bytes 589832 | tf_op jit(solution)/shard_map/ppermute | solution.py:26
  25.2 11.4 %collective-permute-start.2 = (bf16[128,768]{1,0:T(8,128)(2,1)}, bf16[128,768]{1,0:T(8,128)(2,1)S(1)}, u32[]{:S(2)}, u32[]{:S(2)}) collective-permute-start(bf16[128,768]{1,0:T(8,128)(2,1)} %passages.1), channel_id=1, source_target_pairs={{0,2},{2,4},{4,6},{6,0},{1,3},{3,5},{5,7},{7,1},{8,10},{10,12},{12... | collective-permute-start | bytes 589832 | tf_op jit(solution)/shard_map/ppermute | solution.py:26
  37.7 10.8 %all-to-all-start.1 = ((bf16[4,32,1792]{2,1,0:T(8,128)(2,1)}), bf16[4,32,1792]{2,1,0:T(8,128)(2,1)S(1)}, u32[]{:S(2)}, u32[]{:S(2)}) async-start(bf16[4,32,1792]{2,1,0:T(8,128)(2,1)} %pad_maximum_fusion.2), calls=%async_computation.1 | async-start | bytes 917504 | tf_op jit(solution)/shard_map/all_to_all | solution.py:21
  42.1 7.3 %collective-permute-start.3 = (bf16[4,128,768]{2,1,0:T(8,128)(2,1)S(1)}, bf16[4,128,768]{2,1,0:T(8,128)(2,1)S(1)}, u32[]{:S(2)}, u32[]{:S(2)}) collective-permute-start(bf16[4,128,768]{2,1,0:T(8,128)(2,1)S(1)} %pad_maximum_fusion.1), channel_id=1, source_target_pairs={{0,8},{8,0},{1,9},{9,1},{2,10},{10,2},{3,11},{11,3},{4,12},{12,4},... | collective-permute-start | bytes 2359304 | tf_op jit(solution)/shard_map/ppermute | solution.py:26
  52.0 12.9 %all-to-all-start.2 = ((f32[4,32,1664]{2,1,0:T(8,128)}), f32[4,32,1664]{2,1,0:T(8,128)S(1)}, u32[]{:S(2)}, u32[]{:S(2)}) async-start(f32[4,32,1664]{2,1,0:T(8,128)} %shard_map.52), calls=%async_computation.2 | async-start | bytes 1703936 | tf_op jit(solution)/shard_map/all_to_all | solution.py:21
  55.8 21.4 %collective-permute-start.4 = (bf16[128,1024]{1,0:T(8,128)(2,1)S(1)}, bf16[128,1024]{1,0:T(8,128)(2,1)S(1)}, u32[]{:S(2)}, u32[]{:S(2)}) collective-permute-start(bf16[128,1024]{1,0:T(8,128)(2,1)S(1)} %get-tuple-element.39), channel_id=1, source_target_pairs={{0,6},{2,0},{4,2},{6,4},{1,7},{3,1},{5,3},{7,5},{8,14},{10,8},{12,... | collective-permute-start | bytes 786440 | tf_op jit(solution)/shard_map/ppermute | solution.py:26
  60.2 17.1 %collective-permute-start.5 = (bf16[128,1024]{1,0:T(8,128)(2,1)S(1)}, bf16[128,1024]{1,0:T(8,128)(2,1)S(1)}, u32[]{:S(2)}, u32[]{:S(2)}) collective-permute-start(bf16[128,1024]{1,0:T(8,128)(2,1)S(1)} %get-tuple-element.40), channel_id=1, source_target_pairs={{0,4},{2,6},{4,0},{6,2},{1,5},{3,7},{5,1},{7,3},{8,12},{10,14},{12... | collective-permute-start | bytes 786440 | tf_op jit(solution)/shard_map/ppermute | solution.py:26
  62.7 16.7 %copy-start.1 = (bf16[128,1024]{1,0:T(8,128)(2,1)}, bf16[128,1024]{1,0:T(8,128)(2,1)S(1)}, u32[]{:S(2)}) copy-start(bf16[128,1024]{1,0:T(8,128)(2,1)S(1)} %pad_maximum_fusion.3) | copy-start | bytes 786436
  65.8 30.7 %all-to-all-start.3 = ((f32[16,2,1792]{2,1,0:T(2,128)}), f32[16,2,1792]{2,1,0:T(2,128)S(1)}, u32[]{:S(2)}, u32[]{:S(2)}) async-start(f32[16,2,1792]{2,1,0:T(2,128)} %shard_map.53), calls=%async_computation.3 | async-start | bytes 458752 | tf_op jit(solution)/shard_map/all_to_all | solution.py:21
  77.3 8.3 %collective-permute-start.6 = (bf16[128,1024]{1,0:T(8,128)(2,1)S(1)}, bf16[128,1024]{1,0:T(8,128)(2,1)S(1)}, u32[]{:S(2)}, u32[]{:S(2)}) collective-permute-start(bf16[128,1024]{1,0:T(8,128)(2,1)S(1)} %get-tuple-element.45), channel_id=1, source_target_pairs={{0,2},{2,4},{4,6},{6,0},{1,3},{3,5},{5,7},{7,1},{8,10},{10,12},{12... | collective-permute-start | bytes 786440 | tf_op jit(solution)/shard_map/ppermute | solution.py:26
  79.4 14.1 %copy-start.2 = (bf16[128,1024]{1,0:T(8,128)(2,1)S(1)}, bf16[128,1024]{1,0:T(8,128)(2,1)}, u32[]{:S(2)}) copy-start(bf16[128,1024]{1,0:T(8,128)(2,1)} %copy-done.1) | copy-start | bytes 786436
  85.8 9.7 %collective-permute-start.7 = (bf16[4,128,896]{2,1,0:T(8,128)(2,1)S(1)}, bf16[4,128,896]{2,1,0:T(8,128)(2,1)S(1)}, u32[]{:S(2)}, u32[]{:S(2)}) collective-permute-start(bf16[4,128,896]{2,1,0:T(8,128)(2,1)S(1)} %pad_maximum_fusion), channel_id=1, source_target_pairs={{0,8},{8,0},{1,9},{9,1},{2,10},{10,2},{3,11},{11,3},{4,12},{12,4},... | collective-permute-start | bytes 2752520 | tf_op jit(solution)/shard_map/ppermute | solution.py:26
  97.1 8.3 %all-to-all-start.4 = ((f32[8,4,128]{2,1,0:T(4,128)}), f32[8,4,128]{2,1,0:T(4,128)S(1)}, u32[]{:S(2)}, u32[]{:S(2)}) async-start(f32[8,4,128]{2,1,0:T(4,128)} %shard_map.55), calls=%async_computation.4 | async-start | bytes 32768 | tf_op jit(solution)/shard_map/all_to_all | solution.py:21

commit v13 on v12

--- a/solution.py
+++ b/solution.py
@@ -40,23 +40,25 @@
 
 def first_kernel(sizes, queries_in, teacher_in, sent, queries, teacher, sems):
     ny, nzl, group, nzh, pool = sizes
-    copies = [
-        pltpu.make_async_copy(teacher_in, teacher, sems.at[0]),
-        pltpu.make_async_copy(queries_in, queries, sems.at[1]),
-    ]
+    chunk = nzl * group * nzh * pool
+    copies = []
+    for y in range(ny):
+        at = pl.ds(y * chunk, chunk)
+        copies.append(pltpu.make_async_copy(teacher_in.at[:, at], teacher.at[:, at], sems.at[y]))
+    copies.append(pltpu.make_async_copy(queries_in, queries, sems.at[ny]))
     for copy in copies:
         copy.start()
-    for copy in copies:
-        copy.wait()
-    for zh in range(nzh):
-        for zl in range(nzl):
-            to = zh * nzl + zl
-            for y in range(ny):
+    for y in range(ny):
+        copies[y].wait()
+        for zh in range(nzh):
+            for zl in range(nzl):
                 for i in range(group):
                     at = (((y * nzl + zl) * group + i) * nzh + zh) * pool
                     into = (y * group + i) * pool
-                    sent[to, :, into : into + pool] = teacher[:, at : at + pool]
-            sent[to, :, ny * group * pool :] = queries[...]
+                    sent[zh * nzl + zl, :, into : into + pool] = teacher[:, at : at + pool]
+    copies[ny].wait()
+    for z in range(nzh * nzl):
+        sent[z, :, ny * group * pool :] = queries[...]
 
 
 def layout_kernel(nc, nx, place, got, block, high, low, stats, *rows):
@@ -241,7 +243,7 @@
         scratch_shapes=[
             pltpu.VMEM(queries.shape, bf16),
             pltpu.VMEM(teacher.shape, bf16),
-            pltpu.SemaphoreType.DMA((2,)),
+            pltpu.SemaphoreType.DMA((ny + 1,)),
         ],
         compiler_params=pltpu.CompilerParams(vmem_limit_bytes=60 * 2**20),
         cost_estimate=pl.CostEstimate(flops=0, bytes_accessed=2**20, transcendentals=0),

time: 108 us -> 108 us (level)
  no operation moved by 1% of the time
where the time goes in v13:
time: 108 us; the launch traced here: 107 us
  starting transfers between devices  69.4 us (64%)
  waiting for transfers between devices  24.8 us (23%)
  Pallas kernels  10.2 us (9%)
  other arithmetic  1.29 us (1%)
    all_to_all x5, starting transfers between devices, exchange(): return lax.all_to_all(values, axes, 0, 0, tiled=True)  38.9 us
    ppermute x8, starting transfers between devices, from_next(): return lax.ppermute(values, axis, [(i, (i - step) % n) for i in range(n)])  30.6 us
    ppermute x8, waiting for transfers between devices, from_next(): return lax.ppermute(values, axis, [(i, (i - step) % n) for i in range(n)])  17 us
    all_to_all x5, waiting for transfers between devices, exchange(): return lax.all_to_all(values, axes, 0, 0, tiled=True)  7.82 us
    pallas_call x5, Pallas kernels, simple_call(): pl.pallas_call(kernel, out_shape=out, in_specs=[smem] * len(scalars) + [v...  4.91 us
    pallas_call x1, Pallas kernels, local_parts(): pl.pallas_call(parts_kernel, out_shape=jax.ShapeDtypeStruct((ny, count //...  2.62 us
  transfers between devices with their start and end apart: 13, of which 7 were waited for; matrix products, arithmetic and copies ran while one was open for 1% of the time, Pallas kernels for 3%

profile of v13, /device:TPU:1, one launch (start us, length us, event | category | flops | bytes accessed | tf_op | source)
XLA Modules:
  0.0 107.3 jit_solution(9586327163085776766)
XLA Ops:
  0.6 1.8 %shard_map.50 = bf16[16,2,4864]{2,1,0:T(2,128)(2,1)} custom-call(bf16[2,768]{1,0:T(2,128)(2,1)} %queries_in.1, bf16[2,65536]{1,0:T(2,128)(2,1)} %teacher_in.1), custom_call_target="tpu_custom_call" | custom-call | bytes 1048576 | tf_op jit(solution)/shard_map/pallas_call | solution.py:238
  2.4 15.8 %all-to-all-start = ((bf16[16,2,4864]{2,1,0:T(2,128)(2,1)}), bf16[16,2,4864]{2,1,0:T(2,128)(2,1)S(1)}, u32[]{:S(2)}, u32[]{:S(2)}) async-start(bf16[16,2,4864]{2,1,0:T(2,128)(2,1)} %shard_map.50), calls=%async_computation | async-start | bytes 622592 | tf_op jit(solution)/shard_map/all_to_all | solution.py:21
  18.2 0.0 copy-start
  18.2 4.5 %collective-permute-start = (bf16[128,768]{1,0:T(8,128)(2,1)}, bf16[128,768]{1,0:T(8,128)(2,1)S(1)}, u32[]{:S(2)}, u32[]{:S(2)}) collective-permute-start(bf16[128,768]{1,0:T(8,128)(2,1)} %passages.1), channel_id=1, source_target_pairs={{0,6},{2,0},{4,2},{6,4},{1,7},{3,1},{5,3},{7,5},{8,14},{10,8},{12,... | collective-permute-start | bytes 589832 | tf_op jit(solution)/shard_map/ppermute | solution.py:26
  22.7 2.4 %collective-permute-start.1 = (bf16[128,768]{1,0:T(8,128)(2,1)}, bf16[128,768]{1,0:T(8,128)(2,1)S(1)}, u32[]{:S(2)}, u32[]{:S(2)}) collective-permute-start(bf16[128,768]{1,0:T(8,128)(2,1)} %passages.1), channel_id=1, source_target_pairs={{0,4},{2,6},{4,0},{6,2},{1,5},{3,7},{5,1},{7,3},{8,12},{10,14},{12... | collective-permute-start | bytes 589832 | tf_op jit(solution)/shard_map/ppermute | solution.py:26
  25.2 2.5 %collective-permute-start.2 = (bf16[128,768]{1,0:T(8,128)(2,1)}, bf16[128,768]{1,0:T(8,128)(2,1)S(1)}, u32[]{:S(2)}, u32[]{:S(2)}) collective-permute-start(bf16[128,768]{1,0:T(8,128)(2,1)} %passages.1), channel_id=1, source_target_pairs={{0,2},{2,4},{4,6},{6,0},{1,3},{3,5},{5,7},{7,1},{8,10},{10,12},{12... | collective-permute-start | bytes 589832 | tf_op jit(solution)/shard_map/ppermute | solution.py:26
  27.7 0.0 collective-permute-done
  27.7 3.8 %collective-permute-done.1 = bf16[128,768]{1,0:T(8,128)(2,1)S(1)} collective-permute-done((bf16[128,768]{1,0:T(8,128)(2,1)}, bf16[128,768]{1,0:T(8,128)(2,1)S(1)}, u32[]{:S(2)}, u32[]{:S(2)}) %collective-permute-start.1) | collective-permute-done | bytes 196640 | tf_op jit(solution)/shard_map/ppermute | solution.py:26
  31.5 5.1 %collective-permute-done.2 = bf16[128,768]{1,0:T(8,128)(2,1)S(1)} collective-permute-done((bf16[128,768]{1,0:T(8,128)(2,1)}, bf16[128,768]{1,0:T(8,128)(2,1)S(1)}, u32[]{:S(2)}, u32[]{:S(2)}) %collective-permute-start.2) | collective-permute-done | bytes 196640 | tf_op jit(solution)/shard_map/ppermute | solution.py:26
  36.6 0.0 all-to-all-done
  36.6 0.1 reshape.19
  36.8 0.8 pad_maximum_fusion.2
  37.6 4.2 %all-to-all-start.1 = ((bf16[4,32,1792]{2,1,0:T(8,128)(2,1)}), bf16[4,32,1792]{2,1,0:T(8,128)(2,1)S(1)}, u32[]{:S(2)}, u32[]{:S(2)}) async-start(bf16[4,32,1792]{2,1,0:T(8,128)(2,1)} %pad_maximum_fusion.2), calls=%async_computation.1 | async-start | bytes 917504 | tf_op jit(solution)/shard_map/all_to_all | solution.py:21
  41.8 0.1 pad_add_fusion.place
  41.9 0.0 copy-done
  41.9 0.1 pad_maximum_fusion.1
  42.0 4.7 %collective-permute-start.3 = (bf16[4,128,768]{2,1,0:T(8,128)(2,1)S(1)}, bf16[4,128,768]{2,1,0:T(8,128)(2,1)S(1)}, u32[]{:S(2)}, u32[]{:S(2)}) collective-permute-start(bf16[4,128,768]{2,1,0:T(8,128)(2,1)S(1)} %pad_maximum_fusion.1), channel_id=1, source_target_pairs={{0,8},{8,0},{1,9},{9,1},{2,10},{10,2},{3,11},{11,3},{4,12},{12,4},... | collective-permute-start | bytes 2359304 | tf_op jit(solution)/shard_map/ppermute | solution.py:26
  46.7 1.7 %all-to-all-done.1 = bf16[4,32,1792]{2,1,0:T(8,128)(2,1)S(1)} async-done(((bf16[4,32,1792]{2,1,0:T(8,128)(2,1)}), bf16[4,32,1792]{2,1,0:T(8,128)(2,1)S(1)}, u32[]{:S(2)}, u32[]{:S(2)}) %all-to-all-start.1) | async-done | bytes 458784 | tf_op jit(solution)/shard_map/all_to_all | solution.py:21
  48.4 0.9 shard_map.51
  49.3 0.0 collective-permute-done.3
  49.3 2.6 %shard_map.52 = f32[4,32,1664]{2,1,0:T(8,128)} custom-call(bf16[128,768]{1,0:T(8,128)(2,1)S(1)} %get-tuple-element.28.block, bf16[128,1024]{1,0:T(8,128)(2,1)S(1)} %get-tuple-element.29.high, bf16[128,1024]{1,0:T(8,128)(2,1)S(1)} %get-tuple-element.30.low, f32[32,128]{1,0:T(8,128)S(1)} %get-tuple-element.31.taught, bf16[512,768]{1,0:T(8,128)(2,1)S(1)} %bitcast.40, ...), custom_call_target="tpu_custom_call" | custom-call | flops 1006632960 | bytes 4194304 | tf_op jit(solution)/shard_map/pallas_call | solution.py:280
  51.9 3.8 %all-to-all-start.2 = ((f32[4,32,1664]{2,1,0:T(8,128)}), f32[4,32,1664]{2,1,0:T(8,128)S(1)}, u32[]{:S(2)}, u32[]{:S(2)}) async-start(f32[4,32,1664]{2,1,0:T(8,128)} %shard_map.52), calls=%async_computation.2 | async-start | bytes 1703936 | tf_op jit(solution)/shard_map/all_to_all | solution.py:21
  55.7 4.4 %collective-permute-start.4 = (bf16[128,1024]{1,0:T(8,128)(2,1)S(1)}, bf16[128,1024]{1,0:T(8,128)(2,1)S(1)}, u32[]{:S(2)}, u32[]{:S(2)}) collective-permute-start(bf16[128,1024]{1,0:T(8,128)(2,1)S(1)} %get-tuple-element.39), channel_id=1, source_target_pairs={{0,6},{2,0},{4,2},{6,4},{1,7},{3,1},{5,3},{7,5},{8,14},{10,8},{12,... | collective-permute-start | bytes 786440 | tf_op jit(solution)/shard_map/ppermute | solution.py:26
  60.1 2.4 %collective-permute-start.5 = (bf16[128,1024]{1,0:T(8,128)(2,1)S(1)}, bf16[128,1024]{1,0:T(8,128)(2,1)S(1)}, u32[]{:S(2)}, u32[]{:S(2)}) collective-permute-start(bf16[128,1024]{1,0:T(8,128)(2,1)S(1)} %get-tuple-element.40), channel_id=1, source_target_pairs={{0,4},{2,6},{4,0},{6,2},{1,5},{3,7},{5,1},{7,3},{8,12},{10,14},{12... | collective-permute-start | bytes 786440 | tf_op jit(solution)/shard_map/ppermute | solution.py:26
  62.6 0.0 copy-start.1
  62.6 2.2 %all-to-all-done.2.got = f32[4,32,1664]{2,1,0:T(8,128)S(1)} async-done(((f32[4,32,1664]{2,1,0:T(8,128)}), f32[4,32,1664]{2,1,0:T(8,128)S(1)}, u32[]{:S(2)}, u32[]{:S(2)}) %all-to-all-start.2) | async-done | bytes 852000 | tf_op jit(solution)/shard_map/all_to_all | solution.py:21
  64.8 0.9 shard_map.53
  65.7 11.5 %all-to-all-start.3 = ((f32[16,2,1792]{2,1,0:T(2,128)}), f32[16,2,1792]{2,1,0:T(2,128)S(1)}, u32[]{:S(2)}, u32[]{:S(2)}) async-start(f32[16,2,1792]{2,1,0:T(2,128)} %shard_map.53), calls=%async_computation.3 | async-start | bytes 458752 | tf_op jit(solution)/shard_map/all_to_all | solution.py:21
  77.2 0.0 collective-permute-done.4
  77.2 0.0 collective-permute-done.5
  77.2 1.9 %collective-permute-start.6 = (bf16[128,1024]{1,0:T(8,128)(2,1)S(1)}, bf16[128,1024]{1,0:T(8,128)(2,1)S(1)}, u32[]{:S(2)}, u32[]{:S(2)}) collective-permute-start(bf16[128,1024]{1,0:T(8,128)(2,1)S(1)} %get-tuple-element.45), channel_id=1, source_target_pairs={{0,2},{2,4},{4,6},{6,0},{1,3},{3,5},{5,7},{7,1},{8,10},{10,12},{12... | collective-permute-start | bytes 786440 | tf_op jit(solution)/shard_map/ppermute | solution.py:26
  79.3 0.0 copy-done.1
  79.3 0.0 copy-start.2
  79.3 6.2 %collective-permute-done.6 = bf16[128,1024]{1,0:T(8,128)(2,1)S(1)} collective-permute-done((bf16[128,1024]{1,0:T(8,128)(2,1)S(1)}, bf16[128,1024]{1,0:T(8,128)(2,1)S(1)}, u32[]{:S(2)}, u32[]{:S(2)}) %collective-permute-start.6) | collective-permute-done | bytes 262176 | tf_op jit(solution)/shard_map/ppermute | solution.py:26
  85.6 0.1 pad_maximum_fusion
  85.8 7.6 %collective-permute-start.7 = (bf16[4,128,896]{2,1,0:T(8,128)(2,1)S(1)}, bf16[4,128,896]{2,1,0:T(8,128)(2,1)S(1)}, u32[]{:S(2)}, u32[]{:S(2)}) collective-permute-start(bf16[4,128,896]{2,1,0:T(8,128)(2,1)S(1)} %pad_maximum_fusion), channel_id=1, source_target_pairs={{0,8},{8,0},{1,9},{9,1},{2,10},{10,2},{3,11},{11,3},{4,12},{12,4},... | collective-permute-start | bytes 2752520 | tf_op jit(solution)/shard_map/ppermute | solution.py:26
  93.4 0.0 copy-done.2
  93.5 1.9 %collective-permute-done.7 = bf16[4,128,896]{2,1,0:T(8,128)(2,1)S(1)} collective-permute-done((bf16[4,128,896]{2,1,0:T(8,128)(2,1)S(1)}, bf16[4,128,896]{2,1,0:T(8,128)(2,1)S(1)}, u32[]{:S(2)}, u32[]{:S(2)}) %collective-permute-start.7) | collective-permute-done | bytes 917536 | tf_op jit(solution)/shard_map/ppermute | solution.py:26
  95.5 0.1 constant_dynamic-update-slice_fusion
  95.6 0.8 shard_map.54
  96.4 0.0 all-to-all-done.3.got
  96.4 0.7 shard_map.55
  97.1 3.6 %all-to-all-start.4 = ((f32[8,4,128]{2,1,0:T(4,128)}), f32[8,4,128]{2,1,0:T(4,128)S(1)}, u32[]{:S(2)}, u32[]{:S(2)}) async-start(f32[8,4,128]{2,1,0:T(4,128)} %shard_map.55), calls=%async_computation.4 | async-start | bytes 32768 | tf_op jit(solution)/shard_map/all_to_all | solution.py:21
  100.7 0.8 shard_map.56
  101.5 3.9 %all-to-all-done.4.got = f32[8,4,128]{2,1,0:T(4,128)S(1)} async-done(((f32[8,4,128]{2,1,0:T(4,128)}), f32[8,4,128]{2,1,0:T(4,128)S(1)}, u32[]{:S(2)}, u32[]{:S(2)}) %all-to-all-start.4) | async-done | bytes 16416 | tf_op jit(solution)/shard_map/all_to_all | solution.py:21
  105.4 1.9 %shard_map.57 = f32[128,768]{1,0:T(8,128)} custom-call(s32[2]{0:T(128)S(1)} %pad_add_fusion.place, f32[8,4,128]{2,1,0:T(4,128)S(1)} %all-to-all-done.4.got, f32[2,128,1024]{2,1,0:T(8,128)S(1)} %get-tuple-element.50.lifted, f32[2,1024]{1,0:T(2,128)S(1)} %get-tuple-element.51.tops, bf16[1024,896]{1,0:T(8,128)(2,1)S(1)} %bitcast.39), custom_call_target="tpu_custom_call" | custom-call | bytes 65536 | tf_op jit(solution)/shard_map/pallas_call | solution.py:296
  (20 shorter events, 0.4 us)
Async XLA Ops:
  2.4 34.2 %all-to-all-start = ((bf16[16,2,4864]{2,1,0:T(2,128)(2,1)}), bf16[16,2,4864]{2,1,0:T(2,128)(2,1)S(1)}, u32[]{:S(2)}, u32[]{:S(2)}) async-start(bf16[16,2,4864]{2,1,0:T(2,128)(2,1)} %shard_map.50), calls=%async_computation | async-start | bytes 622592 | tf_op jit(solution)/shard_map/all_to_all | solution.py:21
  18.2 23.7 %copy-start = (bf16[128,768]{1,0:T(8,128)(2,1)S(1)}, bf16[128,768]{1,0:T(8,128)(2,1)}, u32[]{:S(2)}) copy-start(bf16[128,768]{1,0:T(8,128)(2,1)} %passages.1) | copy-start | bytes 589828
  18.2 9.5 %collective-permute-start = (bf16[128,768]{1,0:T(8,128)(2,1)}, bf16[128,768]{1,0:T(8,128)(2,1)S(1)}, u32[]{:S(2)}, u32[]{:S(2)}) collective-permute-start(bf16[128,768]{1,0:T(8,128)(2,1)} %passages.1), channel_id=1, source_target_pairs={{0,6},{2,0},{4,2},{6,4},{1,7},{3,1},{5,3},{7,5},{8,14},{10,8},{12,... | collective-permute-start | bytes 589832 | tf_op jit(solution)/shard_map/ppermute | solution.py:26
  22.7 8.8 %collective-permute-start.1 = (bf16[128,768]{1,0:T(8,128)(2,1)}, bf16[128,768]{1,0:T(8,128)(2,1)S(1)}, u32[]{:S(2)}, u32[]{:S(2)}) collective-permute-start(bf16[128,768]{1,0:T(8,128)(2,1)} %passages.1), channel_id=1, source_target_pairs={{0,4},{2,6},{4,0},{6,2},{1,5},{3,7},{5,1},{7,3},{8,12},{10,14},{12... | collective-permute-start | bytes 589832 | tf_op jit(solution)/shard_map/ppermute | solution.py:26
  25.2 11.4 %collective-permute-start.2 = (bf16[128,768]{1,0:T(8,128)(2,1)}, bf16[128,768]{1,0:T(8,128)(2,1)S(1)}, u32[]{:S(2)}, u32[]{:S(2)}) collective-permute-start(bf16[128,768]{1,0:T(8,128)(2,1)} %passages.1), channel_id=1, source_target_pairs={{0,2},{2,4},{4,6},{6,0},{1,3},{3,5},{5,7},{7,1},{8,10},{10,12},{12... | collective-permute-start | bytes 589832 | tf_op jit(solution)/shard_map/ppermute | solution.py:26
  37.6 10.8 %all-to-all-start.1 = ((bf16[4,32,1792]{2,1,0:T(8,128)(2,1)}), bf16[4,32,1792]{2,1,0:T(8,128)(2,1)S(1)}, u32[]{:S(2)}, u32[]{:S(2)}) async-start(bf16[4,32,1792]{2,1,0:T(8,128)(2,1)} %pad_maximum_fusion.2), calls=%async_computation.1 | async-start | bytes 917504 | tf_op jit(solution)/shard_map/all_to_all | solution.py:21
  42.0 7.3 %collective-permute-start.3 = (bf16[4,128,768]{2,1,0:T(8,128)(2,1)S(1)}, bf16[4,128,768]{2,1,0:T(8,128)(2,1)S(1)}, u32[]{:S(2)}, u32[]{:S(2)}) collective-permute-start(bf16[4,128,768]{2,1,0:T(8,128)(2,1)S(1)} %pad_maximum_fusion.1), channel_id=1, source_target_pairs={{0,8},{8,0},{1,9},{9,1},{2,10},{10,2},{3,11},{11,3},{4,12},{12,4},... | collective-permute-start | bytes 2359304 | tf_op jit(solution)/shard_map/ppermute | solution.py:26
  51.9 12.9 %all-to-all-start.2 = ((f32[4,32,1664]{2,1,0:T(8,128)}), f32[4,32,1664]{2,1,0:T(8,128)S(1)}, u32[]{:S(2)}, u32[]{:S(2)}) async-start(f32[4,32,1664]{2,1,0:T(8,128)} %shard_map.52), calls=%async_computation.2 | async-start | bytes 1703936 | tf_op jit(solution)/shard_map/all_to_all | solution.py:21
  55.7 21.4 %collective-permute-start.4 = (bf16[128,1024]{1,0:T(8,128)(2,1)S(1)}, bf16[128,1024]{1,0:T(8,128)(2,1)S(1)}, u32[]{:S(2)}, u32[]{:S(2)}) collective-permute-start(bf16[128,1024]{1,0:T(8,128)(2,1)S(1)} %get-tuple-element.39), channel_id=1, source_target_pairs={{0,6},{2,0},{4,2},{6,4},{1,7},{3,1},{5,3},{7,5},{8,14},{10,8},{12,... | collective-permute-start | bytes 786440 | tf_op jit(solution)/shard_map/ppermute | solution.py:26
  60.1 17.1 %collective-permute-start.5 = (bf16[128,1024]{1,0:T(8,128)(2,1)S(1)}, bf16[128,1024]{1,0:T(8,128)(2,1)S(1)}, u32[]{:S(2)}, u32[]{:S(2)}) collective-permute-start(bf16[128,1024]{1,0:T(8,128)(2,1)S(1)} %get-tuple-element.40), channel_id=1, source_target_pairs={{0,4},{2,6},{4,0},{6,2},{1,5},{3,7},{5,1},{7,3},{8,12},{10,14},{12... | collective-permute-start | bytes 786440 | tf_op jit(solution)/shard_map/ppermute | solution.py:26
  62.6 16.7 %copy-start.1 = (bf16[128,1024]{1,0:T(8,128)(2,1)}, bf16[128,1024]{1,0:T(8,128)(2,1)S(1)}, u32[]{:S(2)}) copy-start(bf16[128,1024]{1,0:T(8,128)(2,1)S(1)} %pad_maximum_fusion.3) | copy-start | bytes 786436
  65.7 30.7 %all-to-all-start.3 = ((f32[16,2,1792]{2,1,0:T(2,128)}), f32[16,2,1792]{2,1,0:T(2,128)S(1)}, u32[]{:S(2)}, u32[]{:S(2)}) async-start(f32[16,2,1792]{2,1,0:T(2,128)} %shard_map.53), calls=%async_computation.3 | async-start | bytes 458752 | tf_op jit(solution)/shard_map/all_to_all | solution.py:21
  77.2 8.3 %collective-permute-start.6 = (bf16[128,1024]{1,0:T(8,128)(2,1)S(1)}, bf16[128,1024]{1,0:T(8,128)(2,1)S(1)}, u32[]{:S(2)}, u32[]{:S(2)}) collective-permute-start(bf16[128,1024]{1,0:T(8,128)(2,1)S(1)} %get-tuple-element.45), channel_id=1, source_target_pairs={{0,2},{2,4},{4,6},{6,0},{1,3},{3,5},{5,7},{7,1},{8,10},{10,12},{12... | collective-permute-start | bytes 786440 | tf_op jit(solution)/shard_map/ppermute | solution.py:26
  79.3 14.1 %copy-start.2 = (bf16[128,1024]{1,0:T(8,128)(2,1)S(1)}, bf16[128,1024]{1,0:T(8,128)(2,1)}, u32[]{:S(2)}) copy-start(bf16[128,1024]{1,0:T(8,128)(2,1)} %copy-done.1) | copy-start | bytes 786436
  85.8 9.7 %collective-permute-start.7 = (bf16[4,128,896]{2,1,0:T(8,128)(2,1)S(1)}, bf16[4,128,896]{2,1,0:T(8,128)(2,1)S(1)}, u32[]{:S(2)}, u32[]{:S(2)}) collective-permute-start(bf16[4,128,896]{2,1,0:T(8,128)(2,1)S(1)} %pad_maximum_fusion), channel_id=1, source_target_pairs={{0,8},{8,0},{1,9},{9,1},{2,10},{10,2},{3,11},{11,3},{4,12},{12,4},... | collective-permute-start | bytes 2752520 | tf_op jit(solution)/shard_map/ppermute | solution.py:26
  97.1 8.3 %all-to-all-start.4 = ((f32[8,4,128]{2,1,0:T(4,128)}), f32[8,4,128]{2,1,0:T(4,128)S(1)}, u32[]{:S(2)}, u32[]{:S(2)}) async-start(f32[8,4,128]{2,1,0:T(4,128)} %shard_map.55), calls=%async_computation.4 | async-start | bytes 32768 | tf_op jit(solution)/shard_map/all_to_all | solution.py:21

commit v14 on v12

--- a/solution.py
+++ b/solution.py
@@ -322,7 +322,7 @@
     block, high, low, stats, *rows = laid_out(got.reshape(count, -1), (ny, width, nc, nx, pool, dim))
     parts = local_parts(block, high, low, stats, near, far, ny)
 
-    for k in range(1, nx - 1):
+    for k in range(2, nx):
         rows[k] = from_next(rows[k], "x", k)
 
     z_at = lax.axis_index("y") * width + lax.axis_index(z_axes) * own
@@ -336,7 +336,7 @@
     got = exchange(sent, z_axes)
     rows[0] = jnp.concatenate([block, rows[0]], axis=1)
     *rows, _ = lax.optimization_barrier((*rows, sent))
-    rows[-1] = from_next(rows[-1], "x", nx - 1)
+    rows[1] = from_next(rows[1], "x", 1)
 
     kept = jnp.stack([r[:, : dim + pool] for r in rows])
     away = jnp.stack([jnp.concatenate([r[:, :dim], r[:, dim + pool :]], axis=1) for r in rows])

time: 108 us -> 109 us (level)
  starting transfers between devices: 69.4 us -> 72.1 us
  waiting for transfers between devices: 24.9 us -> 23 us
    all_to_all x5, starting transfers between devices: 38.9 us -> 41.2 us  [exchange(): return lax.all_to_all(values, axes, 0, 0, tiled=True)]
    ppermute x8, waiting for transfers between devices: 17 us -> 15.2 us  [from_next(): return lax.ppermute(values, axis, [(i, (i - step) % n) for i in range(n)])]
where the time goes in v14:
time: 109 us; the launch traced here: 108 us
  starting transfers between devices  72.1 us (66%)
  waiting for transfers between devices  23 us (21%)
  Pallas kernels  10.3 us (9%)
  other arithmetic  1.29 us (1%)
    all_to_all x5, starting transfers between devices, exchange(): return lax.all_to_all(values, axes, 0, 0, tiled=True)  41.2 us
    ppermute x8, starting transfers between devices, from_next(): return lax.ppermute(values, axis, [(i, (i - step) % n) for i in range(n)])  30.9 us
    ppermute x8, waiting for transfers between devices, from_next(): return lax.ppermute(values, axis, [(i, (i - step) % n) for i in range(n)])  15.2 us
    all_to_all x5, waiting for transfers between devices, exchange(): return lax.all_to_all(values, axes, 0, 0, tiled=True)  7.77 us
    pallas_call x5, Pallas kernels, simple_call(): pl.pallas_call(kernel, out_shape=out, in_specs=[smem] * len(scalars) + [v...  4.91 us
    pallas_call x1, Pallas kernels, local_parts(): pl.pallas_call(parts_kernel, out_shape=jax.ShapeDtypeStruct((ny, count //...  2.61 us
  transfers between devices with their start and end apart: 13, of which 7 were waited for; matrix products, arithmetic and copies ran while one was open for 1% of the time, Pallas kernels for 3%

profile of v14, /device:TPU:1, one launch (start us, length us, event | category | flops | bytes accessed | tf_op | source)
XLA Modules:
  0.0 108.2 jit_solution(990956079451247400)
XLA Ops:
  0.6 1.9 %shard_map.50 = bf16[16,2,4864]{2,1,0:T(2,128)(2,1)} custom-call(bf16[2,768]{1,0:T(2,128)(2,1)} %queries_in.1, bf16[2,65536]{1,0:T(2,128)(2,1)} %teacher_in.1), custom_call_target="tpu_custom_call" | custom-call | bytes 1048576 | tf_op jit(solution)/shard_map/pallas_call | solution.py:236
  2.5 15.8 %all-to-all-start = ((bf16[16,2,4864]{2,1,0:T(2,128)(2,1)}), bf16[16,2,4864]{2,1,0:T(2,128)(2,1)S(1)}, u32[]{:S(2)}, u32[]{:S(2)}) async-start(bf16[16,2,4864]{2,1,0:T(2,128)(2,1)} %shard_map.50), calls=%async_computation | async-start | bytes 622592 | tf_op jit(solution)/shard_map/all_to_all | solution.py:21
  18.3 0.0 copy-start
  18.3 4.5 %collective-permute-start = (bf16[128,768]{1,0:T(8,128)(2,1)}, bf16[128,768]{1,0:T(8,128)(2,1)S(1)}, u32[]{:S(2)}, u32[]{:S(2)}) collective-permute-start(bf16[128,768]{1,0:T(8,128)(2,1)} %passages.1), channel_id=1, source_target_pairs={{0,6},{2,0},{4,2},{6,4},{1,7},{3,1},{5,3},{7,5},{8,14},{10,8},{12,... | collective-permute-start | bytes 589832 | tf_op jit(solution)/shard_map/ppermute | solution.py:26
  22.8 2.4 %collective-permute-start.1 = (bf16[128,768]{1,0:T(8,128)(2,1)}, bf16[128,768]{1,0:T(8,128)(2,1)S(1)}, u32[]{:S(2)}, u32[]{:S(2)}) collective-permute-start(bf16[128,768]{1,0:T(8,128)(2,1)} %passages.1), channel_id=1, source_target_pairs={{0,4},{2,6},{4,0},{6,2},{1,5},{3,7},{5,1},{7,3},{8,12},{10,14},{12... | collective-permute-start | bytes 589832 | tf_op jit(solution)/shard_map/ppermute | solution.py:26
  25.2 2.5 %collective-permute-start.2 = (bf16[128,768]{1,0:T(8,128)(2,1)}, bf16[128,768]{1,0:T(8,128)(2,1)S(1)}, u32[]{:S(2)}, u32[]{:S(2)}) collective-permute-start(bf16[128,768]{1,0:T(8,128)(2,1)} %passages.1), channel_id=1, source_target_pairs={{0,2},{2,4},{4,6},{6,0},{1,3},{3,5},{5,7},{7,1},{8,10},{10,12},{12... | collective-permute-start | bytes 589832 | tf_op jit(solution)/shard_map/ppermute | solution.py:26
  27.8 0.0 collective-permute-done
  27.8 3.8 %collective-permute-done.1 = bf16[128,768]{1,0:T(8,128)(2,1)S(1)} collective-permute-done((bf16[128,768]{1,0:T(8,128)(2,1)}, bf16[128,768]{1,0:T(8,128)(2,1)S(1)}, u32[]{:S(2)}, u32[]{:S(2)}) %collective-permute-start.1) | collective-permute-done | bytes 196640 | tf_op jit(solution)/shard_map/ppermute | solution.py:26
  31.6 5.1 %collective-permute-done.2 = bf16[128,768]{1,0:T(8,128)(2,1)S(1)} collective-permute-done((bf16[128,768]{1,0:T(8,128)(2,1)}, bf16[128,768]{1,0:T(8,128)(2,1)S(1)}, u32[]{:S(2)}, u32[]{:S(2)}) %collective-permute-start.2) | collective-permute-done | bytes 196640 | tf_op jit(solution)/shard_map/ppermute | solution.py:26
  36.7 0.0 all-to-all-done
  36.7 0.1 reshape.19
  36.9 0.8 pad_maximum_fusion.2
  37.7 4.2 %all-to-all-start.1 = ((bf16[4,32,1792]{2,1,0:T(8,128)(2,1)}), bf16[4,32,1792]{2,1,0:T(8,128)(2,1)S(1)}, u32[]{:S(2)}, u32[]{:S(2)}) async-start(bf16[4,32,1792]{2,1,0:T(8,128)(2,1)} %pad_maximum_fusion.2), calls=%async_computation.1 | async-start | bytes 917504 | tf_op jit(solution)/shard_map/all_to_all | solution.py:21
  41.9 0.1 pad_add_fusion.place
  42.0 0.0 copy-done
  42.0 0.1 pad_maximum_fusion.1
  42.1 4.7 %collective-permute-start.3 = (bf16[4,128,768]{2,1,0:T(8,128)(2,1)S(1)}, bf16[4,128,768]{2,1,0:T(8,128)(2,1)S(1)}, u32[]{:S(2)}, u32[]{:S(2)}) collective-permute-start(bf16[4,128,768]{2,1,0:T(8,128)(2,1)S(1)} %pad_maximum_fusion.1), channel_id=1, source_target_pairs={{0,8},{8,0},{1,9},{9,1},{2,10},{10,2},{3,11},{11,3},{4,12},{12,4},... | collective-permute-start | bytes 2359304 | tf_op jit(solution)/shard_map/ppermute | solution.py:26
  46.8 1.7 %all-to-all-done.1 = bf16[4,32,1792]{2,1,0:T(8,128)(2,1)S(1)} async-done(((bf16[4,32,1792]{2,1,0:T(8,128)(2,1)}), bf16[4,32,1792]{2,1,0:T(8,128)(2,1)S(1)}, u32[]{:S(2)}, u32[]{:S(2)}) %all-to-all-start.1) | async-done | bytes 458784 | tf_op jit(solution)/shard_map/all_to_all | solution.py:21
  48.5 0.9 shard_map.51
  49.4 0.0 collective-permute-done.3
  49.4 2.6 %shard_map.52 = f32[4,32,1664]{2,1,0:T(8,128)} custom-call(bf16[128,768]{1,0:T(8,128)(2,1)S(1)} %get-tuple-element.28.block, bf16[128,1024]{1,0:T(8,128)(2,1)S(1)} %get-tuple-element.29.high, bf16[128,1024]{1,0:T(8,128)(2,1)S(1)} %get-tuple-element.30.low, f32[32,128]{1,0:T(8,128)S(1)} %get-tuple-element.31.taught, bf16[512,768]{1,0:T(8,128)(2,1)S(1)} %bitcast.40, ...), custom_call_target="tpu_custom_call" | custom-call | flops 1006632960 | bytes 4194304 | tf_op jit(solution)/shard_map/pallas_call | solution.py:278
  52.0 3.8 %all-to-all-start.2 = ((f32[4,32,1664]{2,1,0:T(8,128)}), f32[4,32,1664]{2,1,0:T(8,128)S(1)}, u32[]{:S(2)}, u32[]{:S(2)}) async-start(f32[4,32,1664]{2,1,0:T(8,128)} %shard_map.52), calls=%async_computation.2 | async-start | bytes 1703936 | tf_op jit(solution)/shard_map/all_to_all | solution.py:21
  55.8 4.6 %collective-permute-start.4 = (bf16[128,1024]{1,0:T(8,128)(2,1)S(1)}, bf16[128,1024]{1,0:T(8,128)(2,1)S(1)}, u32[]{:S(2)}, u32[]{:S(2)}) collective-permute-start(bf16[128,1024]{1,0:T(8,128)(2,1)S(1)} %get-tuple-element.40), channel_id=1, source_target_pairs={{0,4},{2,6},{4,0},{6,2},{1,5},{3,7},{5,1},{7,3},{8,12},{10,14},{12... | collective-permute-start | bytes 786440 | tf_op jit(solution)/shard_map/ppermute | solution.py:26
  60.5 2.2 %collective-permute-start.5 = (bf16[128,1024]{1,0:T(8,128)(2,1)S(1)}, bf16[128,1024]{1,0:T(8,128)(2,1)S(1)}, u32[]{:S(2)}, u32[]{:S(2)}) collective-permute-start(bf16[128,1024]{1,0:T(8,128)(2,1)S(1)} %get-tuple-element.41), channel_id=1, source_target_pairs={{0,2},{2,4},{4,6},{6,0},{1,3},{3,5},{5,7},{7,1},{8,10},{10,12},{12... | collective-permute-start | bytes 786440 | tf_op jit(solution)/shard_map/ppermute | solution.py:26
  62.7 0.0 copy-start.1
  62.7 2.2 %all-to-all-done.2.got = f32[4,32,1664]{2,1,0:T(8,128)S(1)} async-done(((f32[4,32,1664]{2,1,0:T(8,128)}), f32[4,32,1664]{2,1,0:T(8,128)S(1)}, u32[]{:S(2)}, u32[]{:S(2)}) %all-to-all-start.2) | async-done | bytes 852000 | tf_op jit(solution)/shard_map/all_to_all | solution.py:21
  64.9 0.9 shard_map.53
  65.8 11.8 %all-to-all-start.3 = ((f32[16,2,1792]{2,1,0:T(2,128)}), f32[16,2,1792]{2,1,0:T(2,128)S(1)}, u32[]{:S(2)}, u32[]{:S(2)}) async-start(f32[16,2,1792]{2,1,0:T(2,128)} %shard_map.53), calls=%async_computation.3 | async-start | bytes 458752 | tf_op jit(solution)/shard_map/all_to_all | solution.py:21
  77.5 0.0 collective-permute-done.4
  77.5 0.0 collective-permute-done.5
  77.6 2.5 %collective-permute-start.6 = (bf16[128,1024]{1,0:T(8,128)(2,1)S(1)}, bf16[128,1024]{1,0:T(8,128)(2,1)S(1)}, u32[]{:S(2)}, u32[]{:S(2)}) collective-permute-start(bf16[128,1024]{1,0:T(8,128)(2,1)S(1)} %get-tuple-element.43), channel_id=1, source_target_pairs={{0,6},{2,0},{4,2},{6,4},{1,7},{3,1},{5,3},{7,5},{8,14},{10,8},{12,... | collective-permute-start | bytes 786440 | tf_op jit(solution)/shard_map/ppermute | solution.py:26
  80.2 0.0 copy-done.1
  80.3 0.0 copy-start.2
  80.3 4.4 %collective-permute-done.6 = bf16[128,1024]{1,0:T(8,128)(2,1)S(1)} collective-permute-done((bf16[128,1024]{1,0:T(8,128)(2,1)S(1)}, bf16[128,1024]{1,0:T(8,128)(2,1)S(1)}, u32[]{:S(2)}, u32[]{:S(2)}) %collective-permute-start.6) | collective-permute-done | bytes 262176 | tf_op jit(solution)/shard_map/ppermute | solution.py:26
  84.8 0.1 pad_maximum_fusion
  84.9 7.3 %collective-permute-start.7 = (bf16[4,128,896]{2,1,0:T(8,128)(2,1)S(1)}, bf16[4,128,896]{2,1,0:T(8,128)(2,1)S(1)}, u32[]{:S(2)}, u32[]{:S(2)}) collective-permute-start(bf16[4,128,896]{2,1,0:T(8,128)(2,1)S(1)} %pad_maximum_fusion), channel_id=1, source_target_pairs={{0,8},{8,0},{1,9},{9,1},{2,10},{10,2},{3,11},{11,3},{4,12},{12,4},... | collective-permute-start | bytes 2752520 | tf_op jit(solution)/shard_map/ppermute | solution.py:26
  92.3 0.0 copy-done.2
  92.4 1.9 %collective-permute-done.7 = bf16[4,128,896]{2,1,0:T(8,128)(2,1)S(1)} collective-permute-done((bf16[4,128,896]{2,1,0:T(8,128)(2,1)S(1)}, bf16[4,128,896]{2,1,0:T(8,128)(2,1)S(1)}, u32[]{:S(2)}, u32[]{:S(2)}) %collective-permute-start.7) | collective-permute-done | bytes 917536 | tf_op jit(solution)/shard_map/ppermute | solution.py:26
  94.3 0.1 constant_dynamic-update-slice_fusion
  94.5 0.7 shard_map.54
  95.2 0.0 all-to-all-done.3.got
  95.3 0.7 shard_map.55
  95.9 5.7 %all-to-all-start.4 = ((f32[8,4,128]{2,1,0:T(4,128)}), f32[8,4,128]{2,1,0:T(4,128)S(1)}, u32[]{:S(2)}, u32[]{:S(2)}) async-start(f32[8,4,128]{2,1,0:T(4,128)} %shard_map.55), calls=%async_computation.4 | async-start | bytes 32768 | tf_op jit(solution)/shard_map/all_to_all | solution.py:21
  101.6 0.8 shard_map.56
  102.4 3.9 %all-to-all-done.4.got = f32[8,4,128]{2,1,0:T(4,128)S(1)} async-done(((f32[8,4,128]{2,1,0:T(4,128)}), f32[8,4,128]{2,1,0:T(4,128)S(1)}, u32[]{:S(2)}, u32[]{:S(2)}) %all-to-all-start.4) | async-done | bytes 16416 | tf_op jit(solution)/shard_map/all_to_all | solution.py:21
  106.3 1.9 %shard_map.57 = f32[128,768]{1,0:T(8,128)} custom-call(s32[2]{0:T(128)S(1)} %pad_add_fusion.place, f32[8,4,128]{2,1,0:T(4,128)S(1)} %all-to-all-done.4.got, f32[2,128,1024]{2,1,0:T(8,128)S(1)} %get-tuple-element.50.lifted, f32[2,1024]{1,0:T(2,128)S(1)} %get-tuple-element.51.tops, bf16[1024,896]{1,0:T(8,128)(2,1)S(1)} %bitcast.39), custom_call_target="tpu_custom_call" | custom-call | bytes 65536 | tf_op jit(solution)/shard_map/pallas_call | solution.py:294
  (20 shorter events, 0.4 us)
Async XLA Ops:
  2.5 34.2 %all-to-all-start = ((bf16[16,2,4864]{2,1,0:T(2,128)(2,1)}), bf16[16,2,4864]{2,1,0:T(2,128)(2,1)S(1)}, u32[]{:S(2)}, u32[]{:S(2)}) async-start(bf16[16,2,4864]{2,1,0:T(2,128)(2,1)} %shard_map.50), calls=%async_computation | async-start | bytes 622592 | tf_op jit(solution)/shard_map/all_to_all | solution.py:21
  18.3 23.7 %copy-start = (bf16[128,768]{1,0:T(8,128)(2,1)S(1)}, bf16[128,768]{1,0:T(8,128)(2,1)}, u32[]{:S(2)}) copy-start(bf16[128,768]{1,0:T(8,128)(2,1)} %passages.1) | copy-start | bytes 589828
  18.3 9.5 %collective-permute-start = (bf16[128,768]{1,0:T(8,128)(2,1)}, bf16[128,768]{1,0:T(8,128)(2,1)S(1)}, u32[]{:S(2)}, u32[]{:S(2)}) collective-permute-start(bf16[128,768]{1,0:T(8,128)(2,1)} %passages.1), channel_id=1, source_target_pairs={{0,6},{2,0},{4,2},{6,4},{1,7},{3,1},{5,3},{7,5},{8,14},{10,8},{12,... | collective-permute-start | bytes 589832 | tf_op jit(solution)/shard_map/ppermute | solution.py:26
  22.8 8.8 %collective-permute-start.1 = (bf16[128,768]{1,0:T(8,128)(2,1)}, bf16[128,768]{1,0:T(8,128)(2,1)S(1)}, u32[]{:S(2)}, u32[]{:S(2)}) collective-permute-start(bf16[128,768]{1,0:T(8,128)(2,1)} %passages.1), channel_id=1, source_target_pairs={{0,4},{2,6},{4,0},{6,2},{1,5},{3,7},{5,1},{7,3},{8,12},{10,14},{12... | collective-permute-start | bytes 589832 | tf_op jit(solution)/shard_map/ppermute | solution.py:26
  25.2 11.4 %collective-permute-start.2 = (bf16[128,768]{1,0:T(8,128)(2,1)}, bf16[128,768]{1,0:T(8,128)(2,1)S(1)}, u32[]{:S(2)}, u32[]{:S(2)}) collective-permute-start(bf16[128,768]{1,0:T(8,128)(2,1)} %passages.1), channel_id=1, source_target_pairs={{0,2},{2,4},{4,6},{6,0},{1,3},{3,5},{5,7},{7,1},{8,10},{10,12},{12... | collective-permute-start | bytes 589832 | tf_op jit(solution)/shard_map/ppermute | solution.py:26
  37.7 10.8 %all-to-all-start.1 = ((bf16[4,32,1792]{2,1,0:T(8,128)(2,1)}), bf16[4,32,1792]{2,1,0:T(8,128)(2,1)S(1)}, u32[]{:S(2)}, u32[]{:S(2)}) async-start(bf16[4,32,1792]{2,1,0:T(8,128)(2,1)} %pad_maximum_fusion.2), calls=%async_computation.1 | async-start | bytes 917504 | tf_op jit(solution)/shard_map/all_to_all | solution.py:21
  42.1 7.3 %collective-permute-start.3 = (bf16[4,128,768]{2,1,0:T(8,128)(2,1)S(1)}, bf16[4,128,768]{2,1,0:T(8,128)(2,1)S(1)}, u32[]{:S(2)}, u32[]{:S(2)}) collective-permute-start(bf16[4,128,768]{2,1,0:T(8,128)(2,1)S(1)} %pad_maximum_fusion.1), channel_id=1, source_target_pairs={{0,8},{8,0},{1,9},{9,1},{2,10},{10,2},{3,11},{11,3},{4,12},{12,4},... | collective-permute-start | bytes 2359304 | tf_op jit(solution)/shard_map/ppermute | solution.py:26
  52.0 12.9 %all-to-all-start.2 = ((f32[4,32,1664]{2,1,0:T(8,128)}), f32[4,32,1664]{2,1,0:T(8,128)S(1)}, u32[]{:S(2)}, u32[]{:S(2)}) async-start(f32[4,32,1664]{2,1,0:T(8,128)} %shard_map.52), calls=%async_computation.2 | async-start | bytes 1703936 | tf_op jit(solution)/shard_map/all_to_all | solution.py:21
  55.8 21.7 %collective-permute-start.4 = (bf16[128,1024]{1,0:T(8,128)(2,1)S(1)}, bf16[128,1024]{1,0:T(8,128)(2,1)S(1)}, u32[]{:S(2)}, u32[]{:S(2)}) collective-permute-start(bf16[128,1024]{1,0:T(8,128)(2,1)S(1)} %get-tuple-element.40), channel_id=1, source_target_pairs={{0,4},{2,6},{4,0},{6,2},{1,5},{3,7},{5,1},{7,3},{8,12},{10,14},{12... | collective-permute-start | bytes 786440 | tf_op jit(solution)/shard_map/ppermute | solution.py:26
  60.5 17.1 %collective-permute-start.5 = (bf16[128,1024]{1,0:T(8,128)(2,1)S(1)}, bf16[128,1024]{1,0:T(8,128)(2,1)S(1)}, u32[]{:S(2)}, u32[]{:S(2)}) collective-permute-start(bf16[128,1024]{1,0:T(8,128)(2,1)S(1)} %get-tuple-element.41), channel_id=1, source_target_pairs={{0,2},{2,4},{4,6},{6,0},{1,3},{3,5},{5,7},{7,1},{8,10},{10,12},{12... | collective-permute-start | bytes 786440 | tf_op jit(solution)/shard_map/ppermute | solution.py:26
  62.7 17.5 %copy-start.1 = (bf16[128,1024]{1,0:T(8,128)(2,1)}, bf16[128,1024]{1,0:T(8,128)(2,1)S(1)}, u32[]{:S(2)}) copy-start(bf16[128,1024]{1,0:T(8,128)(2,1)S(1)} %pad_maximum_fusion.3) | copy-start | bytes 786436
  65.8 29.5 %all-to-all-start.3 = ((f32[16,2,1792]{2,1,0:T(2,128)}), f32[16,2,1792]{2,1,0:T(2,128)S(1)}, u32[]{:S(2)}, u32[]{:S(2)}) async-start(f32[16,2,1792]{2,1,0:T(2,128)} %shard_map.53), calls=%async_computation.3 | async-start | bytes 458752 | tf_op jit(solution)/shard_map/all_to_all | solution.py:21
  77.6 7.1 %collective-permute-start.6 = (bf16[128,1024]{1,0:T(8,128)(2,1)S(1)}, bf16[128,1024]{1,0:T(8,128)(2,1)S(1)}, u32[]{:S(2)}, u32[]{:S(2)}) collective-permute-start(bf16[128,1024]{1,0:T(8,128)(2,1)S(1)} %get-tuple-element.43), channel_id=1, source_target_pairs={{0,6},{2,0},{4,2},{6,4},{1,7},{3,1},{5,3},{7,5},{8,14},{10,8},{12,... | collective-permute-start | bytes 786440 | tf_op jit(solution)/shard_map/ppermute | solution.py:26
  80.3 12.0 %copy-start.2 = (bf16[128,1024]{1,0:T(8,128)(2,1)S(1)}, bf16[128,1024]{1,0:T(8,128)(2,1)}, u32[]{:S(2)}) copy-start(bf16[128,1024]{1,0:T(8,128)(2,1)} %copy-done.1) | copy-start | bytes 786436
  84.9 9.4 %collective-permute-start.7 = (bf16[4,128,896]{2,1,0:T(8,128)(2,1)S(1)}, bf16[4,128,896]{2,1,0:T(8,128)(2,1)S(1)}, u32[]{:S(2)}, u32[]{:S(2)}) collective-permute-start(bf16[4,128,896]{2,1,0:T(8,128)(2,1)S(1)} %pad_maximum_fusion), channel_id=1, source_target_pairs={{0,8},{8,0},{1,9},{9,1},{2,10},{10,2},{3,11},{11,3},{4,12},{12,4},... | collective-permute-start | bytes 2752520 | tf_op jit(solution)/shard_map/ppermute | solution.py:26
  95.9 10.4 %all-to-all-start.4 = ((f32[8,4,128]{2,1,0:T(4,128)}), f32[8,4,128]{2,1,0:T(4,128)S(1)}, u32[]{:S(2)}, u32[]{:S(2)}) async-start(f32[8,4,128]{2,1,0:T(4,128)} %shard_map.55), calls=%async_computation.4 | async-start | bytes 32768 | tf_op jit(solution)/shard_map/all_to_all | solution.py:21
